TPU v7x, 32 devices: a whole 2x2x4 slice. The times are simulated.
32 devices in a mesh: groups: 2 (over y), ep: 16 (over z, x, core).
Axes of the slice: x: 2, y: 2, z: 4, core: 2. Of those that a mesh axis runs over, the one named last changes fastest.
Arguments:
- handoff_rows: bfloat16 [32, 256, 576], P(('groups', 'ep')), parts along dimension 0, may hold values from -6 to 6
- handoff_dest: int32 [32], P('groups'), parts along dimension 0, may hold values from 0 to 15, as said below
- handoff_len: int32 [32], P('groups'), parts along dimension 0, may hold values from 128 to 256, as said below
- resident_cache: bfloat16 [32, 2048, 576], P(('groups', 'ep')), parts along dimension 0, may hold values from -6 to 6
- resident_len: int32 [32], P(('groups', 'ep')), parts along dimension 0, may hold values from 512 to 2048, as said below
- queries: bfloat16 [1, 64, 128, 576], P(None, ('groups', 'ep')), parts along dimension 1
- new_latent: bfloat16 [1, 64, 576], P(None, ('groups', 'ep')), parts along dimension 1
- residual_in: bfloat16 [1, 64, 7168], P(None, ('groups', 'ep')), parts along dimension 1, may hold values from -3 to 3
- value_upward: bfloat16 [128, 512, 128], P('ep'), may hold values from -1 to 1
- out_proj: bfloat16 [128, 128, 7168], P('ep'), may hold values from -0.046875 to 0.046875
- norm_gain: bfloat16 [7168], replicated, may hold values from 0.099609375 to 1.8984375
- expert_ids: int32 [1, 64, 1], P(None, ('groups', 'ep')), parts along dimension 1, may hold values from 0 to 1
- expert_gates: float32 [1, 64, 1], P(None, ('groups', 'ep')), parts along dimension 1, may hold values from 0.1 to 0.6
- gate_proj: bfloat16 [2048, 7168], P('ep'), may hold values from -0.0625 to 0.0625
- up_proj: bfloat16 [2048, 7168], P('ep'), may hold values from -0.0625 to 0.0625
- down_proj: bfloat16 [2048, 7168], P('ep'), may hold values from -0.1875 to 0.1875
Outputs:
- hidden_leaving: bfloat16 [1, 64, 7168], P(None, ('groups', 'ep')), parts along dimension 1
There are 2 independent parts, one for each index of `groups`. A program takes and returns all parts, laid end to end along the dimension named above; an argument that names none is the same for every part. Nothing has to cross between parts.
Inputs may be any that keep to these rules, and one draw needn't show every extreme that they name: `handoff_dest`: no decode device is named by more than two prefill devices; some is named by two, some by none. `handoff_len`: some decode device receives two prompts of 256 rows. `resident_len`: some resident cache is full.
All inputs are finite; a program needn't handle non-finite values.
Results may differ from a plain program's by a relative error of at most 0.006.
Values may be sent and summed in bfloat16 or wider, within the bound.
No kernel may reach another device: no remote copies, remote signals or barrier semaphores. Data moves between devices by JAX's collectives and lax.ppermute only.
A program may use at most 128 MiB of HBM per device.

v0:
```python
import jax
import jax.numpy as jnp
from jax import lax
from jax.sharding import PartitionSpec as P

KVR = 512
MOE_FF = 1024
UNITS = 128


softmax_scale = 192.0 ** (-0.5)
norm_epsilon = 1e-06
contract_last = (((1,), (1,)), ((), ()))


def expert_rows(rows, gate_rows, up_rows, down_rows):
    flat_rows = rows.reshape(-1, rows.shape[-1])
    gate = lax.dot_general(flat_rows, gate_rows, contract_last, preferred_element_type=jnp.float32)
    up_value = lax.dot_general(
        flat_rows, up_rows, contract_last, preferred_element_type=jnp.float32
    )
    act = (jax.nn.silu(gate) * up_value).astype(jnp.bfloat16)
    produced = jnp.dot(act, down_rows, preferred_element_type=jnp.float32).astype(jnp.bfloat16)
    return produced.reshape(rows.shape)


def attend(query, key_rows, live_keys, fresh_rows):
    scores = (
        lax.dot_general(query, key_rows, contract_last, preferred_element_type=jnp.float32)
        * softmax_scale
    )
    scores = jnp.where(live_keys[None, :], scores, -jnp.inf)
    fresh_scores = (
        lax.dot_general(query, fresh_rows, contract_last, preferred_element_type=jnp.float32)
        * softmax_scale
    )
    peak_score = jnp.maximum(
        jnp.max(scores, axis=1, keepdims=True), jnp.max(fresh_scores, axis=1, keepdims=True)
    )
    cache_terms = jnp.exp(scores - peak_score)
    fresh_terms = jnp.exp(fresh_scores - peak_score)
    denominator = jnp.sum(cache_terms, axis=1, keepdims=True) + jnp.sum(
        fresh_terms, axis=1, keepdims=True
    )
    cache_probs = (cache_terms / denominator).astype(jnp.bfloat16)
    fresh_probs = (fresh_terms / denominator).astype(jnp.bfloat16)
    mixed = jnp.dot(cache_probs, key_rows, preferred_element_type=jnp.float32) + jnp.dot(
        fresh_probs, fresh_rows, preferred_element_type=jnp.float32
    )
    return mixed[:, :KVR].astype(jnp.bfloat16)


def shards(
    handoff_rows,
    handoff_dest,
    handoff_len,
    resident_cache,
    resident_len,
    queries,
    new_latent,
    residual_in,
    value_upward,
    out_proj,
    norm_gain,
    expert_ids,
    expert_gates,
    gate_proj,
    up_proj,
    down_proj,
):
    devices = lax.axis_size("ep")
    device = lax.axis_index("ep")
    slice_count = MOE_FF // UNITS
    expert_banks = devices // slice_count
    prompt_rows = handoff_rows.shape[1]
    width = handoff_rows.shape[2]
    per_peer = prompt_rows // devices
    spread_out = jnp.transpose(handoff_rows[0].reshape(per_peer, devices, width), (1, 0, 2))
    spread_in = lax.all_to_all(spread_out, "ep", split_axis=0, concat_axis=0, tiled=True)
    source_prompts = jnp.arange(devices, dtype=jnp.int32)
    same_dest = handoff_dest[:, None] == handoff_dest[None, :]
    earlier = source_prompts[None, :] < source_prompts[:, None]
    rank = jnp.sum((same_dest & earlier).astype(jnp.int32), axis=1)
    slot_of = handoff_dest * 2 + rank
    placing = (slot_of[None, :] == jnp.arange(2 * devices, dtype=jnp.int32)[:, None]).astype(
        jnp.bfloat16
    )
    outgoing = (
        jnp.dot(placing, spread_in.reshape(devices, -1), preferred_element_type=jnp.float32)
        .astype(jnp.bfloat16)
        .reshape(devices, 2, per_peer, width)
    )
    delivered = lax.all_to_all(outgoing, "ep", split_axis=0, concat_axis=0, tiled=True)
    new_keys = delivered.reshape(-1, width)
    own_match = slot_of[:, None] == (device * 2 + jnp.arange(2, dtype=jnp.int32))[None, :]
    slot_len = jnp.sum(jnp.where(own_match, handoff_len[:, None], 0), axis=0)
    peer_index = jnp.arange(devices, dtype=jnp.int32)[:, None, None]
    row_index = jnp.arange(per_peer, dtype=jnp.int32)[None, None, :]
    position = row_index * devices + peer_index
    new_live = (position < slot_len[None, :, None]).reshape(-1)
    cache_keys = resident_cache[0]
    cache_live = jnp.arange(cache_keys.shape[0], dtype=jnp.int32) < resident_len[0]
    resident_out = attend(queries[0, 0], cache_keys, cache_live, new_latent[:, 0])
    arrived_out = attend(queries[0, 1], new_keys, new_live, new_latent[:, 1])
    step_outputs = [jnp.stack([resident_out, arrived_out])]
    latent_result = jnp.stack(step_outputs)
    residual_rows = jnp.transpose(residual_in, (1, 0, 2))
    chosen_ids = jnp.transpose(expert_ids, (1, 0, 2))
    chosen_gates = jnp.transpose(expert_gates, (1, 0, 2))
    flat_weight = out_proj.reshape(-1, out_proj.shape[2])
    step_count = latent_result.shape[0]
    incoming_heads = lax.all_to_all(latent_result, "ep", split_axis=2, concat_axis=1, tiled=True)
    value_rows = jnp.einsum(
        "dfpl,pln->fdpn", incoming_heads, value_upward, preferred_element_type=jnp.float32
    ).astype(jnp.bfloat16)
    flat_values = value_rows.reshape(value_rows.shape[0] * step_count, -1)
    attention = lax.psum_scatter(
        jnp.dot(flat_values, flat_weight, preferred_element_type=jnp.float32),
        "ep",
        scatter_dimension=0,
        tiled=True,
    ).reshape(2, step_count, -1)
    hidden = residual_rows.astype(jnp.float32) + attention
    inverse_rms = lax.rsqrt(jnp.mean(hidden * hidden, axis=-1, keepdims=True) + norm_epsilon)
    normed = (hidden * inverse_rms * norm_gain.astype(jnp.float32)).astype(jnp.bfloat16)
    chosen = (chosen_ids[..., None] == jnp.arange(expert_banks, dtype=jnp.int32)).astype(
        jnp.float32
    )
    weights = jnp.sum(chosen_gates[..., None] * chosen, axis=2)
    slice_weights = jnp.repeat(weights, slice_count, axis=2)
    member = jnp.repeat(jnp.sum(chosen, axis=2), slice_count, axis=2)
    outgoing_rows = jnp.where(
        jnp.transpose(member, (2, 0, 1))[..., None] > 0.5, normed[None], jnp.zeros((), jnp.bfloat16)
    )
    produced = expert_rows(
        lax.all_to_all(outgoing_rows, "ep", split_axis=0, concat_axis=0, tiled=True),
        gate_proj,
        up_proj,
        down_proj,
    )
    returned = lax.all_to_all(produced, "ep", split_axis=0, concat_axis=0, tiled=True)
    mixed = jnp.einsum("bsq,qbsd->bsd", slice_weights, returned, preferred_element_type=jnp.float32)
    finished = (hidden + mixed).astype(jnp.bfloat16)
    return jnp.transpose(finished, (1, 0, 2))


def solution(mesh):
    placed = (
        P(("groups", "ep"), None, None),
        P("groups"),
        P("groups"),
        P(("groups", "ep"), None, None),
        P(("groups", "ep")),
        P(None, ("groups", "ep"), None, None),
        P(None, ("groups", "ep"), None),
        P(None, ("groups", "ep"), None),
        P("ep", None, None),
        P("ep", None, None),
        P(),
        P(None, ("groups", "ep"), None),
        P(None, ("groups", "ep"), None),
        P("ep", None),
        P("ep", None),
        P("ep", None),
    )
    return jax.shard_map(
        shards,
        mesh=mesh,
        in_specs=placed,
        out_specs=P(None, ("groups", "ep"), None),
        check_vma=False,
    )
```

profile of v0, /device:TPU:0, one launch (start us, length us, event | category | flops | bytes accessed | tf_op | source)
XLA Modules:
  0.0 230.3 jit_solution(9277103714243073976)
XLA Ops:
  6.5 1.3 copy.31
  7.9 0.8 copy.32
  8.6 7.4 %all-to-all-start = ((bf16[16,16,576]{2,1,0:T(8,128)(2,1)}), bf16[16,16,576]{2,1,0:T(8,128)(2,1)}, u32[]{:S(2)}, u32[]{:S(2)}) async-start(bf16[16,16,576]{2,1,0:T(8,128)(2,1)} %copy.32), calls=%async_computation | async-start | bytes 655360 | tf_op jit(solution)/shard_map/all_to_all | solution.py:79
  16.1 0.2 convert_reduce_fusion
  16.9 0.2 fusion.47
  17.1 1.6 fusion.54
  18.7 8.5 %all-to-all-done = bf16[16,16,576]{2,1,0:T(8,128)(2,1)} async-done(((bf16[16,16,576]{2,1,0:T(8,128)(2,1)}), bf16[16,16,576]{2,1,0:T(8,128)(2,1)}, u32[]{:S(2)}, u32[]{:S(2)}) %all-to-all-start) | async-done | bytes 294944 | tf_op jit(solution)/shard_map/all_to_all | solution.py:79
  27.2 2.0 reshape.250
  29.2 2.1 convolution_convert_fusion
  31.3 2.5 %reshape.251 = bf16[16,2,16,576]{3,2,1,0:T(8,128)(2,1)} reshape(bf16[32,9216]{1,0:T(8,128)(2,1)} %convolution_convert_fusion) | data formatting | bytes 1179648 | tf_op jit(solution)/shard_map/reshape | solution.py:91
  33.7 4.3 %all-to-all-start.1 = ((bf16[16,2,16,576]{3,2,1,0:T(8,128)(2,1)}), bf16[16,2,16,576]{3,2,1,0:T(8,128)(2,1)}, u32[]{:S(2)}, u32[]{:S(2)}) async-start(bf16[16,2,16,576]{3,2,1,0:T(8,128)(2,1)} %reshape.251), calls=%async_computation.1 | async-start | bytes 1310720 | tf_op jit(solution)/shard_map/all_to_all | solution.py:93
  38.0 0.1 broadcast_compare_fusion
  38.1 0.1 lt.51
  38.3 1.0 fusion.55
  39.3 0.3 fusion.9
  39.6 1.7 fusion.1
  41.4 13.2 %all-to-all-done.1 = bf16[16,2,16,576]{3,2,1,0:T(8,128)(2,1)} async-done(((bf16[16,2,16,576]{3,2,1,0:T(8,128)(2,1)}), bf16[16,2,16,576]{3,2,1,0:T(8,128)(2,1)}, u32[]{:S(2)}, u32[]{:S(2)}) %all-to-all-start.1) | async-done | bytes 589856 | tf_op jit(solution)/shard_map/all_to_all | solution.py:93
  54.6 1.5 fusion.52
  56.1 1.0 fusion.53
  57.2 0.1 fusion.16
  57.3 1.4 fusion.21
  58.7 0.1 fusion.22
  58.9 0.3 copy.33
  59.1 14.6 %all_to_all.35 = bf16[1,2,128,512]{3,1,0,2:T(2,128)(2,1)S(1)} all-to-all(bf16[1,2,128,512]{3,1,0,2:T(2,128)(2,1)S(1)} %copy.33), channel_id=1, replica_groups=mesh['groups'=2,'ep'=16] {'ep'}, dimensions={2} | all-to-all | bytes 524288 | tf_op jit(solution)/shard_map/all_to_all | solution.py:112
  73.7 0.9 copy.52
  74.6 1.7 reshape.254
  76.4 1.2 fusion.5
  77.7 8.8 %fusion.30 = f32[32,7168]{1,0:T(8,128)} fusion(bf16[1024,7168]{1,0:T(8,128)(2,1)} %bitcast.114, bf16[4,8,8,128]{3,2,1,0:T(8,128)(2,1)S(1)} %bitcast.119), kind=kOutput, calls=%fused_computation.47 | convolution fusion | flops 469762048 | bytes 15663104 | tf_op jit(solution)/shard_map/dot_general | solution.py:118
  86.5 0.1 convert_compare_fusion
  86.6 0.1 broadcast_in_dim.98
  86.7 0.1 gt.23
  86.8 0.1 copy.36
  86.9 0.6 dynamic-slice
  88.1 88.9 %all-reduce.3.cloned.1.call-done = f32[32,7168]{1,0:T(8,128)} async-done(((f32[32,7168]{1,0:T(8,128)}), f32[32,7168]{1,0:T(8,128)}) %all-reduce.3.cloned.1.call-update) | async-done | bytes 917520
  177.0 1.1 multiply_reduce_fusion
  178.1 1.0 multiply_convert_fusion
  179.2 0.4 broadcast_select_fusion
  179.5 18.1 %all_to_all.36 = bf16[16,2,1,7168]{3,1,2,0:T(2,128)(2,1)S(1)} all-to-all(bf16[16,2,1,7168]{3,1,2,0:T(2,128)(2,1)S(1)} %broadcast_select_fusion), channel_id=1, replica_groups=mesh['groups'=2,'ep'=16] {'ep'}, dimensions={0} | all-to-all | bytes 917504 | tf_op jit(solution)/shard_map/all_to_all | solution.py:136
  197.7 0.2 reshape.257
  197.9 2.2 fusion.56
  200.1 3.5 %convolution_convert_fusion.1 = bf16[32,7168]{1,0:T(8,128)(2,1)S(1)} fusion(bf16[128,7168]{1,0:T(8,128)(2,1)} %param.31, bf16[32,7168]{1,0:T(8,128)(2,1)S(1)} %reshape.257, bf16[128,7168]{1,0:T(8,128)(2,1)} %param.30, f32[32,128]{1,0:T(8,128)S(1)} %fusion.56), kind=kOutput, calls=%fused_computation.1 | convolution fusion | flops 117694464 | bytes 4603904 | tf_op jit(solution)/shard_map/dot_general | solution.py:23
  203.5 0.9 reshape.258
  204.5 3.9 %all-to-all-start.4 = ((bf16[16,2,1,7168]{3,1,2,0:T(2,128)(2,1)}), bf16[16,2,1,7168]{3,1,2,0:T(2,128)(2,1)S(1)}, u32[]{:S(2)}, u32[]{:S(2)}) async-start(bf16[16,2,1,7168]{3,1,2,0:T(2,128)(2,1)} %bitcast.24), calls=%async_computation.4 | async-start | bytes 917504 | tf_op jit(solution)/shard_map/all_to_all | solution.py:141
  208.5 0.1 broadcast_in_dim.96
  208.6 0.1 reshape.265
  208.6 13.0 %all-to-all-done.4 = bf16[16,2,1,7168]{3,1,2,0:T(2,128)(2,1)S(1)} async-done(((bf16[16,2,1,7168]{3,1,2,0:T(2,128)(2,1)}), bf16[16,2,1,7168]{3,1,2,0:T(2,128)(2,1)S(1)}, u32[]{:S(2)}, u32[]{:S(2)}) %all-to-all-start.4) | async-done | bytes 458784 | tf_op jit(solution)/shard_map/all_to_all | solution.py:141
  221.6 0.2 fusion.12
  221.9 1.6 fusion.34
  (39 shorter events, 0.4 us)
Async XLA Ops:
  6.5 10.6 %copy-start = (bf16[1,2048,576]{1,2,0:T(8,128)(2,1)S(1)}, bf16[1,2048,576]{1,2,0:T(8,128)(2,1)}, u32[]{:S(2)}) copy-start(bf16[1,2048,576]{1,2,0:T(8,128)(2,1)} %param.19) | copy-start | bytes 7077892
  6.5 9.5 %copy-start.9 = (s32[16]{0:T(128)S(1)}, s32[16]{0:T(128)}, u32[]{:S(2)}) copy-start(s32[16]{0:T(128)} %param.17) | copy-start | bytes 196
  6.5 10.4 %copy-start.6 = (s32[16]{0:T(128)S(1)}, s32[16]{0:T(128)}, u32[]{:S(2)}) copy-start(s32[16]{0:T(128)} %param.18) | copy-start | bytes 196
  8.6 18.6 %all-to-all-start = ((bf16[16,16,576]{2,1,0:T(8,128)(2,1)}), bf16[16,16,576]{2,1,0:T(8,128)(2,1)}, u32[]{:S(2)}, u32[]{:S(2)}) async-start(bf16[16,16,576]{2,1,0:T(8,128)(2,1)} %copy.32), calls=%async_computation | async-start | bytes 655360 | tf_op jit(solution)/shard_map/all_to_all | solution.py:79
  29.2 9.1 %copy-start.5 = (bf16[1,2,576]{2,1,0:T(2,128)(2,1)S(1)}, bf16[1,2,576]{2,1,0:T(2,128)(2,1)}, u32[]{:S(2)}) copy-start(bf16[1,2,576]{2,1,0:T(2,128)(2,1)} %param.22) | copy-start | bytes 6916
  33.7 20.9 %all-to-all-start.1 = ((bf16[16,2,16,576]{3,2,1,0:T(8,128)(2,1)}), bf16[16,2,16,576]{3,2,1,0:T(8,128)(2,1)}, u32[]{:S(2)}, u32[]{:S(2)}) async-start(bf16[16,2,16,576]{3,2,1,0:T(8,128)(2,1)} %reshape.251), calls=%async_computation.1 | async-start | bytes 1310720 | tf_op jit(solution)/shard_map/all_to_all | solution.py:93
  38.0 139.0 %all-reduce.3.cloned.1.call-start = ((), (), s32[]{:S(2)}) async-start(), calls=%async_computation.5 | async-start | bytes 1835008
  54.6 4.1 %copy-start.3 = (f32[128,576]{1,0:T(8,128)S(1)}, f32[128,576]{1,0:T(8,128)}, u32[]{:S(2)}) copy-start(f32[128,576]{1,0:T(8,128)} %fusion.1) | copy-start | bytes 884740
  58.7 17.7 %copy-start.1 = (bf16[8,512,128]{2,1,0:T(8,128)(2,1)S(1)}, bf16[8,512,128]{2,1,0:T(8,128)(2,1)}, u32[]{:S(2)}) copy-start(bf16[8,512,128]{2,1,0:T(8,128)(2,1)} %param.24) | copy-start | bytes 3145732
  77.6 8.9 %copy-start.4 = (bf16[7168]{0:T(1024)(128)(2,1)S(1)}, bf16[7168]{0:T(1024)(128)(2,1)}, u32[]{:S(2)}) copy-start(bf16[7168]{0:T(1024)(128)(2,1)} %param.26) | copy-start | bytes 43012
  77.6 8.9 %copy-start.8 = (s32[1,2,1]{1,2,0:T(1,128)S(1)}, s32[1,2,1]{1,2,0:T(1,128)}, u32[]{:S(2)}) copy-start(s32[1,2,1]{1,2,0:T(1,128)} %param.27) | copy-start | bytes 28
  77.7 9.2 %copy-start.10 = (u32[32]{0:T(128)S(1)}, u32[32]{0:T(128)}, u32[]{:S(2)}) copy-start(u32[32]{0:T(128)} %constant.44) | copy-start | bytes 388
  77.7 99.3 %copy-start.2 = (bf16[1,2,7168]{2,1,0:T(2,128)(2,1)S(1)}, bf16[1,2,7168]{2,1,0:T(2,128)(2,1)}, u32[]{:S(2)}) copy-start(bf16[1,2,7168]{2,1,0:T(2,128)(2,1)} %param.23) | copy-start | bytes 86020
  203.5 4.9 %copy-start.7 = (f32[1,2,1]{1,2,0:T(1,128)S(1)}, f32[1,2,1]{1,2,0:T(1,128)}, u32[]{:S(2)}) copy-start(f32[1,2,1]{1,2,0:T(1,128)} %param.28) | copy-start | bytes 28
  204.5 17.2 %all-to-all-start.4 = ((bf16[16,2,1,7168]{3,1,2,0:T(2,128)(2,1)}), bf16[16,2,1,7168]{3,1,2,0:T(2,128)(2,1)S(1)}, u32[]{:S(2)}, u32[]{:S(2)}) async-start(bf16[16,2,1,7168]{3,1,2,0:T(2,128)(2,1)} %bitcast.24), calls=%async_computation.4 | async-start | bytes 917504 | tf_op jit(solution)/shard_map/all_to_all | solution.py:141
Sparse Core Ops, SparseCore 0:
  86.6 90.3 all-reduce.2
where the time goes:
time: 231 us; the launch traced here: 230 us
  waiting for transfers between devices  124 us (54%)
  blocking collectives  32.7 us (14%)
  matrix products  26.3 us (11%)
  starting transfers between devices  15.6 us (7%)
  between operations  15 us (6%)
  local copies, waits for them, and re-layouts  11.8 us (5%)
  other arithmetic  5.33 us (2%)
    unnamed x2, waiting for transfers between devices  88.9 us
    all_to_all x1, blocking collectives, shards(): lax.all_to_all(outgoing_rows, 'ep', split_axis=0, concat_axis=0, tiled=True)  18.1 us
    all_to_all x1, blocking collectives, shards(): lax.all_to_all(latent_result, 'ep', split_axis=2, concat_axis=1, tiled=True)  14.6 us
    all_to_all x1, waiting for transfers between devices, shards(): lax.all_to_all(outgoing, 'ep', split_axis=0, concat_axis=0, tiled=True)  13.2 us
    all_to_all x1, waiting for transfers between devices, shards(): lax.all_to_all(produced, 'ep', split_axis=0, concat_axis=0, tiled=True)  13 us
    dot_general x1, matrix products, shards(): jnp.dot(flat_values, flat_weight, preferred_element_type=jnp.float32)  8.78 us
    all_to_all x1, waiting for transfers between devices, shards(): lax.all_to_all(spread_out, 'ep', split_axis=0, concat_axis=0, tiled=True)  8.47 us
    all_to_all x1, starting transfers between devices, shards(): lax.all_to_all(spread_out, 'ep', split_axis=0, concat_axis=0, tiled=True)  7.4 us
  transfers between devices with their start and end apart: 4, of which 4 were waited for; matrix products, arithmetic and copies ran while one was open for 3% of the time, Pallas kernels for 0%

commit v1 on v0

--- a/solution.py
+++ b/solution.py
@@ -114,12 +114,13 @@
         "dfpl,pln->fdpn", incoming_heads, value_upward, preferred_element_type=jnp.float32
     ).astype(jnp.bfloat16)
     flat_values = value_rows.reshape(value_rows.shape[0] * step_count, -1)
-    attention = lax.psum_scatter(
-        jnp.dot(flat_values, flat_weight, preferred_element_type=jnp.float32),
-        "ep",
-        scatter_dimension=0,
-        tiled=True,
-    ).reshape(2, step_count, -1)
+    partial = jnp.dot(flat_values, flat_weight, preferred_element_type=jnp.float32).astype(
+        jnp.bfloat16
+    )
+    partials = lax.all_to_all(
+        partial.reshape(devices, -1, partial.shape[1]), "ep", split_axis=0, concat_axis=0, tiled=True
+    )
+    attention = jnp.sum(partials.astype(jnp.float32), axis=0).reshape(2, step_count, -1)
     hidden = residual_rows.astype(jnp.float32) + attention
     inverse_rms = lax.rsqrt(jnp.mean(hidden * hidden, axis=-1, keepdims=True) + norm_epsilon)
     normed = (hidden * inverse_rms * norm_gain.astype(jnp.float32)).astype(jnp.bfloat16)

time: 231 us -> 140 us (0.61)
  waiting for transfers between devices: 124 us -> 47.6 us
  between operations: 15 us -> 0.93 us
  starting transfers between devices: 15.6 us -> 19.1 us
  other arithmetic: 5.33 us -> 2.89 us
    unnamed x2 -> x0, waiting for transfers between devices: 88.9 us -> none
    all_to_all x0 -> x1, waiting for transfers between devices: none -> 12.8 us  [shards(): lax.all_to_all(partial.reshape(devices, -1, partial.shape[1]), 'ep', spli...]
    all_to_all x0 -> x1, starting transfers between devices: none -> 3.56 us  [shards(): lax.all_to_all(partial.reshape(devices, -1, partial.shape[1]), 'ep', spli...]
  transfers between devices with their start and end apart: 4 -> 4, of which waited for: 4 -> 4; matrix products, arithmetic and copies ran while one was open for 3% -> 4% of each run, Pallas kernels for 0% -> 0%
where the time goes in v1:
time: 140 us; the launch traced here: 139 us
  waiting for transfers between devices  47.6 us (34%)
  blocking collectives  31.4 us (22%)
  matrix products  25.3 us (18%)
  starting transfers between devices  19.1 us (14%)
  local copies, waits for them, and re-layouts  12.1 us (9%)
  other arithmetic  2.89 us (2%)
    all_to_all x1, blocking collectives, shards(): lax.all_to_all(outgoing_rows, 'ep', split_axis=0, concat_axis=0, tiled=True)  16.9 us
    all_to_all x1, blocking collectives, shards(): lax.all_to_all(latent_result, 'ep', split_axis=2, concat_axis=1, tiled=True)  14.6 us
    all_to_all x1, waiting for transfers between devices, shards(): lax.all_to_all(outgoing, 'ep', split_axis=0, concat_axis=0, tiled=True)  13.3 us
    all_to_all x1, waiting for transfers between devices, shards(): lax.all_to_all(produced, 'ep', split_axis=0, concat_axis=0, tiled=True)  13 us
    all_to_all x1, waiting for transfers between devices, shards(): lax.all_to_all(partial.reshape(devices, -1, partial.shape[1]), 'ep', spli...  12.8 us
    all_to_all x1, waiting for transfers between devices, shards(): lax.all_to_all(spread_out, 'ep', split_axis=0, concat_axis=0, tiled=True)  8.41 us
    dot_general x1, matrix products, shards(): jnp.dot(flat_values, flat_weight, preferred_element_type=jnp.float32)  7.79 us
    all_to_all x1, starting transfers between devices, shards(): lax.all_to_all(spread_out, 'ep', split_axis=0, concat_axis=0, tiled=True)  7.41 us
  transfers between devices with their start and end apart: 4, of which 4 were waited for; matrix products, arithmetic and copies ran while one was open for 4% of the time, Pallas kernels for 0%

profile of v1, /device:TPU:0, one launch (start us, length us, event | category | flops | bytes accessed | tf_op | source)
XLA Modules:
  0.0 139.4 jit_solution(11002786628058515997)
XLA Ops:
  0.0 1.3 copy.31
  1.3 0.8 copy.32
  2.1 7.4 %all-to-all-start = ((bf16[16,16,576]{2,1,0:T(8,128)(2,1)}), bf16[16,16,576]{2,1,0:T(8,128)(2,1)}, u32[]{:S(2)}, u32[]{:S(2)}) async-start(bf16[16,16,576]{2,1,0:T(8,128)(2,1)} %copy.32), calls=%async_computation | async-start | bytes 655360 | tf_op jit(solution)/shard_map/all_to_all | solution.py:79
  10.2 0.2 convert_reduce_fusion.1
  10.5 0.2 fusion.46
  10.7 1.6 %fusion.53 = (f32[128]{0:T(128)S(1)}, f32[128,2048]{1,0:T(8,128)S(1)}) fusion(bf16[1,2048,576]{1,2,0:T(8,128)(2,1)S(1)} %copy-done, bf16[1,2,128,576]{2,3,1,0:T(8,128)(2,1)} %param.21, pred[2048]{0:T(1024)(128)(4,1)S(1)} %iota_compare_fusion.3), kind=kOutput, calls=%fused_computation.95 | convolution fusion | flops 302776192 | bytes 3557888 | tf_op jit(solution)/shard_map/dot_general | solution.py:29
  12.3 8.4 %all-to-all-done = bf16[16,16,576]{2,1,0:T(8,128)(2,1)} async-done(((bf16[16,16,576]{2,1,0:T(8,128)(2,1)}), bf16[16,16,576]{2,1,0:T(8,128)(2,1)}, u32[]{:S(2)}, u32[]{:S(2)}) %all-to-all-start) | async-done | bytes 294944 | tf_op jit(solution)/shard_map/all_to_all | solution.py:79
  20.7 2.0 %reshape.293 = bf16[16,9216]{1,0:T(8,128)(2,1)} reshape(bf16[16,16,576]{2,1,0:T(8,128)(2,1)} %all-to-all-done) | data formatting | bytes 589824 | tf_op jit(solution)/shard_map/reshape | solution.py:89
  22.7 2.1 %convolution_convert_fusion = bf16[32,9216]{1,0:T(8,128)(2,1)} fusion(bf16[16,9216]{1,0:T(8,128)(2,1)} %reshape.293, s32[16]{0:T(128)S(1)} %multiply_add_fusion), kind=kOutput, calls=%fused_computation | convolution fusion | flops 9732608 | bytes 884800 | tf_op jit(solution)/shard_map/dot_general | solution.py:89
  24.7 2.5 %reshape.294 = bf16[16,2,16,576]{3,2,1,0:T(8,128)(2,1)} reshape(bf16[32,9216]{1,0:T(8,128)(2,1)} %convolution_convert_fusion) | data formatting | bytes 1179648 | tf_op jit(solution)/shard_map/reshape | solution.py:91
  27.2 4.3 %all-to-all-start.1 = ((bf16[16,2,16,576]{3,2,1,0:T(8,128)(2,1)}), bf16[16,2,16,576]{3,2,1,0:T(8,128)(2,1)}, u32[]{:S(2)}, u32[]{:S(2)}) async-start(bf16[16,2,16,576]{3,2,1,0:T(8,128)(2,1)} %reshape.294), calls=%async_computation.1 | async-start | bytes 1310720 | tf_op jit(solution)/shard_map/all_to_all | solution.py:93
  31.5 0.1 broadcast_compare_fusion
  31.5 0.1 lt.51
  31.6 1.0 fusion.54
  32.7 0.3 fusion.9
  33.0 1.7 %fusion.1 = f32[128,576]{1,0:T(8,128)} fusion(bf16[1,2048,576]{1,2,0:T(8,128)(2,1)S(1)} %copy-done, f32[128,2048]{1,0:T(8,128)S(1)} %get-tuple-element.16, f32[128]{0:T(128)S(1)} %get-tuple-element.8, f32[128]{0:T(128)S(1)} %get-tuple-element.17), kind=kOutput, calls=%fused_computation.5 | convolution fusion | flops 302776320 | bytes 3703808 | tf_op jit(solution)/shard_map/dot_general | solution.py:47
  34.7 13.3 %all-to-all-done.1 = bf16[16,2,16,576]{3,2,1,0:T(8,128)(2,1)} async-done(((bf16[16,2,16,576]{3,2,1,0:T(8,128)(2,1)}), bf16[16,2,16,576]{3,2,1,0:T(8,128)(2,1)}, u32[]{:S(2)}, u32[]{:S(2)}) %all-to-all-start.1) | async-done | bytes 589856 | tf_op jit(solution)/shard_map/all_to_all | solution.py:93
  48.1 1.5 %fusion.51 = (f32[128]{0:T(128)S(1)}, f32[512,128]{1,0:T(8,128)S(1)}) fusion(bf16[512,576]{1,0:T(8,128)(2,1)} %bitcast.8, bf16[1,2,128,576]{2,3,1,0:T(8,128)(2,1)} %param.21, pred[512]{0:T(512)(128)(4,1)S(1)} %lt.51), kind=kOutput, calls=%fused_computation.93 | convolution fusion | flops 75693952 | bytes 1065984 | tf_op jit(solution)/shard_map/dot_general | solution.py:29
  49.6 1.0 fusion.52
  50.6 0.1 fusion.16
  50.7 1.4 %fusion.21 = f32[128,576]{1,0:T(8,128)S(1)} fusion(bf16[512,576]{1,0:T(8,128)(2,1)} %bitcast.8, f32[512,128]{1,0:T(8,128)S(1)} %get-tuple-element.12, f32[128]{0:T(128)S(1)} %get-tuple-element.10, f32[128]{0:T(128)S(1)} %get-tuple-element.13), kind=kOutput, calls=%fused_computation.40 | convolution fusion | flops 75694080 | bytes 1147904 | tf_op jit(solution)/shard_map/dot_general | solution.py:47
  52.2 0.1 fusion.22
  52.3 0.3 copy.33
  52.6 14.6 %all_to_all.40 = bf16[1,2,128,512]{3,1,0,2:T(2,128)(2,1)S(1)} all-to-all(bf16[1,2,128,512]{3,1,0,2:T(2,128)(2,1)S(1)} %copy.33), channel_id=1, replica_groups=mesh['groups'=2,'ep'=16] {'ep'}, dimensions={2} | all-to-all | bytes 524288 | tf_op jit(solution)/shard_map/all_to_all | solution.py:112
  67.2 0.9 copy.52
  68.1 1.7 %reshape.297 = bf16[32,8,512]{2,0,1:T(8,128)(2,1)} reshape(bf16[1,16,2,8,512]{4,2,1,3,0:T(2,128)(2,1)} %bitcast.117) | data formatting | bytes 524288 | tf_op jit(solution)/shard_map/reshape.29
  69.8 1.2 fusion.5
  71.1 7.8 %convolution_convert_fusion.2 = bf16[32,7168]{1,0:T(8,128)(2,1)S(1)} fusion(bf16[1024,7168]{1,0:T(8,128)(2,1)} %bitcast.113, bf16[4,8,8,128]{3,2,1,0:T(8,128)(2,1)S(1)} %bitcast.118), kind=kOutput, calls=%fused_computation.2 | convolution fusion | flops 469991424 | bytes 15204352 | tf_op jit(solution)/shard_map/dot_general | solution.py:117
  78.9 0.9 reshape.300
  79.9 3.6 %all-to-all-start.3 = ((bf16[16,2,7168]{2,1,0:T(2,128)(2,1)}), bf16[16,2,7168]{2,1,0:T(2,128)(2,1)S(1)}, u32[]{:S(2)}, u32[]{:S(2)}) async-start(bf16[16,2,7168]{2,1,0:T(2,128)(2,1)} %reshape.300), calls=%async_computation.3 | async-start | bytes 917504 | tf_op jit(solution)/shard_map/all_to_all | solution.py:120
  83.5 0.1 broadcast_in_dim.98
  83.6 0.1 gt.23
  83.7 0.1 copy.36
  83.8 12.8 %all-to-all-done.3 = bf16[16,2,7168]{2,1,0:T(2,128)(2,1)S(1)} async-done(((bf16[16,2,7168]{2,1,0:T(2,128)(2,1)}), bf16[16,2,7168]{2,1,0:T(2,128)(2,1)S(1)}, u32[]{:S(2)}, u32[]{:S(2)}) %all-to-all-start.3) | async-done | bytes 458784 | tf_op jit(solution)/shard_map/all_to_all | solution.py:120
  96.7 0.4 convert_reduce_fusion
  97.0 0.2 multiply_reduce_fusion
  97.2 0.1 multiply_convert_fusion
  97.3 0.4 broadcast_select_fusion
  97.7 16.9 %all_to_all.41 = bf16[16,2,1,7168]{3,1,2,0:T(2,128)(2,1)S(1)} all-to-all(bf16[16,2,1,7168]{3,1,2,0:T(2,128)(2,1)S(1)} %broadcast_select_fusion), channel_id=1, replica_groups=mesh['groups'=2,'ep'=16] {'ep'}, dimensions={0} | all-to-all | bytes 917504 | tf_op jit(solution)/shard_map/all_to_all | solution.py:137
  114.6 0.2 reshape.301
  114.8 2.2 %fusion.55 = f32[32,128]{1,0:T(8,128)S(1)} fusion(bf16[32,7168]{1,0:T(8,128)(2,1)S(1)} %reshape.301, bf16[128,7168]{1,0:T(8,128)(2,1)} %param.29), kind=kOutput, calls=%fused_computation.97 | convolution fusion | flops 58720256 | bytes 2310144 | tf_op jit(solution)/shard_map/dot_general | solution.py:18
  117.0 3.5 %convolution_convert_fusion.1 = bf16[32,7168]{1,0:T(8,128)(2,1)S(1)} fusion(bf16[128,7168]{1,0:T(8,128)(2,1)} %param.31, bf16[32,7168]{1,0:T(8,128)(2,1)S(1)} %reshape.301, bf16[128,7168]{1,0:T(8,128)(2,1)} %param.30, f32[32,128]{1,0:T(8,128)S(1)} %fusion.55), kind=kOutput, calls=%fused_computation.1 | convolution fusion | flops 117694464 | bytes 4603904 | tf_op jit(solution)/shard_map/dot_general | solution.py:23
  120.4 0.9 reshape.302
  121.4 3.9 %all-to-all-start.5 = ((bf16[16,2,1,7168]{3,1,2,0:T(2,128)(2,1)}), bf16[16,2,1,7168]{3,1,2,0:T(2,128)(2,1)S(1)}, u32[]{:S(2)}, u32[]{:S(2)}) async-start(bf16[16,2,1,7168]{3,1,2,0:T(2,128)(2,1)} %bitcast.24), calls=%async_computation.5 | async-start | bytes 917504 | tf_op jit(solution)/shard_map/all_to_all | solution.py:142
  125.4 0.1 reshape.309
  125.5 13.0 %all-to-all-done.5 = bf16[16,2,1,7168]{3,1,2,0:T(2,128)(2,1)S(1)} async-done(((bf16[16,2,1,7168]{3,1,2,0:T(2,128)(2,1)}), bf16[16,2,1,7168]{3,1,2,0:T(2,128)(2,1)S(1)}, u32[]{:S(2)}, u32[]{:S(2)}) %all-to-all-start.5) | async-done | bytes 458784 | tf_op jit(solution)/shard_map/all_to_all | solution.py:142
  138.5 0.2 fusion.12
  138.8 0.7 fusion.33
  (37 shorter events, 0.4 us)
Async XLA Ops:
  0.0 10.7 %copy-start = (bf16[1,2048,576]{1,2,0:T(8,128)(2,1)S(1)}, bf16[1,2048,576]{1,2,0:T(8,128)(2,1)}, u32[]{:S(2)}) copy-start(bf16[1,2048,576]{1,2,0:T(8,128)(2,1)} %param.19) | copy-start | bytes 7077892
  0.0 10.2 %copy-start.5 = (bf16[1,2,576]{2,1,0:T(2,128)(2,1)S(1)}, bf16[1,2,576]{2,1,0:T(2,128)(2,1)}, u32[]{:S(2)}) copy-start(bf16[1,2,576]{2,1,0:T(2,128)(2,1)} %param.22) | copy-start | bytes 6916
  0.0 10.2 %copy-start.9 = (s32[16]{0:T(128)S(1)}, s32[16]{0:T(128)}, u32[]{:S(2)}) copy-start(s32[16]{0:T(128)} %param.17) | copy-start | bytes 196
  0.0 10.4 %copy-start.6 = (s32[16]{0:T(128)S(1)}, s32[16]{0:T(128)}, u32[]{:S(2)}) copy-start(s32[16]{0:T(128)} %param.18) | copy-start | bytes 196
  2.1 18.6 %all-to-all-start = ((bf16[16,16,576]{2,1,0:T(8,128)(2,1)}), bf16[16,16,576]{2,1,0:T(8,128)(2,1)}, u32[]{:S(2)}, u32[]{:S(2)}) async-start(bf16[16,16,576]{2,1,0:T(8,128)(2,1)} %copy.32), calls=%async_computation | async-start | bytes 655360 | tf_op jit(solution)/shard_map/all_to_all | solution.py:79
  27.2 20.9 %all-to-all-start.1 = ((bf16[16,2,16,576]{3,2,1,0:T(8,128)(2,1)}), bf16[16,2,16,576]{3,2,1,0:T(8,128)(2,1)}, u32[]{:S(2)}, u32[]{:S(2)}) async-start(bf16[16,2,16,576]{3,2,1,0:T(8,128)(2,1)} %reshape.294), calls=%async_computation.1 | async-start | bytes 1310720 | tf_op jit(solution)/shard_map/all_to_all | solution.py:93
  48.1 4.1 %copy-start.3 = (f32[128,576]{1,0:T(8,128)S(1)}, f32[128,576]{1,0:T(8,128)}, u32[]{:S(2)}) copy-start(f32[128,576]{1,0:T(8,128)} %fusion.1) | copy-start | bytes 884740
  52.2 17.7 %copy-start.1 = (bf16[8,512,128]{2,1,0:T(8,128)(2,1)S(1)}, bf16[8,512,128]{2,1,0:T(8,128)(2,1)}, u32[]{:S(2)}) copy-start(bf16[8,512,128]{2,1,0:T(8,128)(2,1)} %param.24) | copy-start | bytes 3145732
  78.9 4.6 %copy-start.8 = (s32[1,2,1]{1,2,0:T(1,128)S(1)}, s32[1,2,1]{1,2,0:T(1,128)}, u32[]{:S(2)}) copy-start(s32[1,2,1]{1,2,0:T(1,128)} %param.27) | copy-start | bytes 28
  78.9 4.9 %copy-start.4 = (bf16[7168]{0:T(1024)(128)(2,1)S(1)}, bf16[7168]{0:T(1024)(128)(2,1)}, u32[]{:S(2)}) copy-start(bf16[7168]{0:T(1024)(128)(2,1)} %param.26) | copy-start | bytes 43012
  78.9 18.1 %copy-start.2 = (bf16[1,2,7168]{2,1,0:T(2,128)(2,1)S(1)}, bf16[1,2,7168]{2,1,0:T(2,128)(2,1)}, u32[]{:S(2)}) copy-start(bf16[1,2,7168]{2,1,0:T(2,128)(2,1)} %param.23) | copy-start | bytes 86020
  79.9 16.8 %all-to-all-start.3 = ((bf16[16,2,7168]{2,1,0:T(2,128)(2,1)}), bf16[16,2,7168]{2,1,0:T(2,128)(2,1)S(1)}, u32[]{:S(2)}, u32[]{:S(2)}) async-start(bf16[16,2,7168]{2,1,0:T(2,128)(2,1)} %reshape.300), calls=%async_computation.3 | async-start | bytes 917504 | tf_op jit(solution)/shard_map/all_to_all | solution.py:120
  120.4 4.9 %copy-start.7 = (f32[1,2,1]{1,2,0:T(1,128)S(1)}, f32[1,2,1]{1,2,0:T(1,128)}, u32[]{:S(2)}) copy-start(f32[1,2,1]{1,2,0:T(1,128)} %param.28) | copy-start | bytes 28
  121.4 17.2 %all-to-all-start.5 = ((bf16[16,2,1,7168]{3,1,2,0:T(2,128)(2,1)}), bf16[16,2,1,7168]{3,1,2,0:T(2,128)(2,1)S(1)}, u32[]{:S(2)}, u32[]{:S(2)}) async-start(bf16[16,2,1,7168]{3,1,2,0:T(2,128)(2,1)} %bitcast.24), calls=%async_computation.5 | async-start | bytes 917504 | tf_op jit(solution)/shard_map/all_to_all | solution.py:142

commit v2 on v1

v2 whole, which is shorter than its diff:
```python
import functools

import jax
import jax.numpy as jnp
from jax import lax
from jax.experimental import pallas as pl
from jax.experimental.pallas import tpu as pltpu
from jax.sharding import PartitionSpec as P

KVR = 512
MOE_FF = 1024
UNITS = 128
LANES = 128

softmax_scale = 192.0 ** (-0.5)
norm_epsilon = 1e-06
contract_last = (((1,), (1,)), ((), ()))
f32 = jnp.float32
bf16 = jnp.bfloat16
whole = pl.BlockSpec(memory_space=pltpu.VMEM)
scalars = pl.BlockSpec(memory_space=pltpu.SMEM)


def attend(query, key_rows, live_keys, fresh_rows):
    scores = (
        lax.dot_general(query, key_rows, contract_last, preferred_element_type=f32) * softmax_scale
    )
    scores = jnp.where(live_keys[None, :], scores, -jnp.inf)
    fresh_scores = (
        lax.dot_general(query, fresh_rows, contract_last, preferred_element_type=f32)
        * softmax_scale
    )
    peak_score = jnp.maximum(
        jnp.max(scores, axis=1, keepdims=True), jnp.max(fresh_scores, axis=1, keepdims=True)
    )
    cache_terms = jnp.exp(scores - peak_score)
    fresh_terms = jnp.exp(fresh_scores - peak_score)
    denominator = jnp.sum(cache_terms, axis=1, keepdims=True) + jnp.sum(
        fresh_terms, axis=1, keepdims=True
    )
    cache_probs = (cache_terms / denominator).astype(bf16)
    fresh_probs = (fresh_terms / denominator).astype(bf16)
    mixed = jnp.dot(cache_probs, key_rows, preferred_element_type=f32) + jnp.dot(
        fresh_probs, fresh_rows, preferred_element_type=f32
    )
    return mixed[:, :KVR].astype(bf16)


def three_parts(value):
    first = value.astype(bf16).astype(f32)
    second = (value - first).astype(bf16).astype(f32)
    third = value - first - second
    return first, second, third


def pick_kernel(dest_ref, spread_ref, picked_ref):
    for prompt in range(spread_ref.shape[0]):
        picked_ref[prompt] = spread_ref[dest_ref[prompt]]


def prompt_kernel(
    length_ref, query_ref, key_ref, resident_ref, own_query_ref, fresh_ref, fresh_rows_ref, out_ref
):
    peers, rows, width = out_ref.shape
    per_peer = rows // 2
    heads = peers * per_peer
    query = query_ref[...].reshape(heads, query_ref.shape[2])
    keys = key_ref[...]
    scores = lax.dot_general(query, keys, contract_last, preferred_element_type=f32)
    position = lax.broadcasted_iota(jnp.int32, scores.shape, 1)
    scores = jnp.where(position < length_ref[0], scores * softmax_scale, -jnp.inf)
    peak = jnp.max(scores, axis=1, keepdims=True)
    terms = jnp.exp(scores - peak)
    total = jnp.sum(terms, axis=1, keepdims=True)
    mixed = jnp.dot(terms.astype(bf16), keys[:, :KVR], preferred_element_type=f32) / total
    log_sum = peak + jnp.log(total)
    fresh_score = softmax_scale * jnp.sum(
        own_query_ref[...].astype(f32) * fresh_ref[...].astype(f32), axis=1, keepdims=True
    )
    lane = lax.broadcasted_iota(jnp.int32, (heads, width - KVR), 1)
    stats = jnp.zeros((heads, width - KVR), f32)
    for at, column in enumerate(three_parts(log_sum) + three_parts(fresh_score)):
        stats = jnp.where(lane == at, column, stats)
    fold = lambda value: value.reshape(peers, per_peer, value.shape[1])
    out_ref[:, :, :KVR] = jnp.concatenate(
        [fold(mixed), fold(resident_ref[...].astype(f32))], axis=1
    ).astype(bf16)
    fresh_rows = jnp.broadcast_to(
        fresh_rows_ref[...].astype(f32)[None], (peers, per_peer, width - KVR)
    )
    out_ref[:, :, KVR:] = jnp.concatenate([fold(stats), fresh_rows], axis=1).astype(bf16)


def heads_kernel(row_ref, column_ref, rows_ref, upward_ref, proj_ref, keep_ref, send_ref):
    peers, rows, width = rows_ref.shape
    per_peer = rows // 2
    columns = peers * rows
    both = 2 * peers
    row_head, row_device, row_new = row_ref[:, 0:1], row_ref[:, 1:2], row_ref[:, 2:3]
    col_peer, col_row, col_dest = column_ref[0:1, :], column_ref[1:2, :], column_ref[2:3, :]
    stats = rows_ref[:, :, KVR : KVR + LANES].astype(f32).reshape(columns, LANES).T
    log_sum = stats[0:1] + stats[1:2] + stats[2:3]
    fresh_score = stats[3:4] + stats[4:5] + stats[5:6]
    same_head = col_row == row_head
    own = col_peer == row_device
    new_row = row_new == 1
    arrives = same_head & (col_dest == row_device) & new_row
    fresh = jnp.sum(jnp.where(same_head & own, fresh_score, 0.0), axis=1, keepdims=True)
    scored = jnp.where(arrives, log_sum, -jnp.inf)
    peak = jnp.maximum(jnp.max(scored, axis=1, keepdims=True), fresh)
    terms = jnp.exp(scored - peak)
    fresh_term = jnp.exp(fresh - peak)
    scale = 1.0 / (jnp.sum(terms, axis=1, keepdims=True) + fresh_term)
    resident = jnp.where(own & (col_row == row_head + per_peer), 1.0, 0.0)
    mixing = jnp.where(new_row, terms * scale, resident)
    peer = lax.broadcasted_iota(jnp.int32, (row_ref.shape[0], peers), 1)
    fresh_mixing = jnp.where((peer == row_device) & new_row, fresh_term * scale, 0.0)
    chunk = width - KVR
    fresh_rows = jnp.concatenate(
        [rows_ref[:, per_peer + at, KVR:] for at in range(KVR // chunk)], axis=1
    )
    latents = rows_ref[:, :, :KVR].reshape(columns, KVR)
    mixed = jnp.zeros((row_ref.shape[0], KVR), f32)
    for weights, values in ((mixing, latents), (fresh_mixing, fresh_rows)):
        high = weights.astype(bf16)
        low = (weights - high.astype(f32)).astype(bf16)
        mixed = mixed + jnp.dot(high, values, preferred_element_type=f32)
        mixed = mixed + jnp.dot(low, values, preferred_element_type=f32)
    mixed = mixed.astype(bf16)
    value_rows = jnp.concatenate(
        [
            jnp.dot(
                mixed[head * both : (head + 1) * both], upward_ref[head], preferred_element_type=f32
            ).astype(bf16)
            for head in range(per_peer)
        ],
        axis=1,
    )
    step = 1024
    for start in range(0, proj_ref.shape[1], step):
        part = jnp.dot(value_rows, proj_ref[:, start : start + step], preferred_element_type=f32)
        keep_ref[:, start : start + step] = part[:peers]
        send_ref[:, start : start + step] = part[peers:].astype(bf16)


def expert_kernel(own_ref, sibling_ref, gate_ref, up_ref, down_ref, keep_ref, send_ref):
    half = own_ref.shape[0]
    rows = jnp.concatenate([own_ref[...], sibling_ref[...]], axis=0)
    gate = lax.dot_general(rows, gate_ref[...], contract_last, preferred_element_type=f32)
    up_value = lax.dot_general(rows, up_ref[...], contract_last, preferred_element_type=f32)
    act = (gate / (1.0 + jnp.exp(-gate)) * up_value).astype(bf16)
    step = 1024
    for start in range(0, down_ref.shape[1], step):
        part = jnp.dot(act, down_ref[:, start : start + step], preferred_element_type=f32)
        keep_ref[:, start : start + step] = part[:half]
        send_ref[:, start : start + step] = part[half:].astype(bf16)


def call(kernel, shapes, specs, limit=32):
    return pl.pallas_call(
        kernel,
        out_shape=shapes,
        in_specs=specs,
        out_specs=jax.tree.map(lambda _: whole, shapes),
        compiler_params=pltpu.CompilerParams(vmem_limit_bytes=limit << 20),
    )


def shards(
    handoff_rows,
    handoff_dest,
    handoff_len,
    resident_cache,
    resident_len,
    queries,
    new_latent,
    residual_in,
    value_upward,
    out_proj,
    norm_gain,
    expert_ids,
    expert_gates,
    gate_proj,
    up_proj,
    down_proj,
):
    devices = lax.axis_size("ep")
    device = lax.axis_index("ep")
    core = device % 2
    chips = devices // 2
    siblings = [(i, i ^ 1) for i in range(devices)]
    same_core = [[2 * chip + k for chip in range(chips)] for k in range(2)]
    slice_count = MOE_FF // UNITS
    heads, width = queries.shape[2], queries.shape[3]
    per_peer = heads // devices
    model = residual_in.shape[2]

    exchange = functools.partial(
        lax.all_to_all, axis_name="ep", split_axis=0, concat_axis=0, tiled=True
    )
    exchange_core = functools.partial(exchange, axis_index_groups=same_core)

    spread = exchange(queries[0, 1].reshape(devices, per_peer, width))
    picked = call(
        pick_kernel,
        jax.ShapeDtypeStruct(spread.shape, bf16),
        [scalars, whole],
    )(handoff_dest, spread)
    arrived = exchange(picked)

    cache_keys = resident_cache[0]
    cache_live = jnp.arange(cache_keys.shape[0], dtype=jnp.int32) < resident_len[0]
    resident_out = attend(queries[0, 0], cache_keys, cache_live, new_latent[:, 0])

    chunk = max(LANES, KVR // per_peer)
    fresh_rows = new_latent[0, 1, :KVR].reshape(KVR // chunk, chunk)
    fresh_rows = jnp.pad(fresh_rows, ((0, per_peer - KVR // chunk), (0, 0)))
    own_len = lax.dynamic_slice(handoff_len, (device,), (1,))
    payload = call(
        prompt_kernel,
        jax.ShapeDtypeStruct((devices, 2 * per_peer, KVR + chunk), bf16),
        [scalars] + [whole] * 6,
    )(
        own_len,
        arrived,
        handoff_rows[0],
        resident_out,
        queries[0, 1],
        new_latent[0, 1:2],
        fresh_rows,
    )
    by_head = exchange(payload)

    row = jnp.arange(per_peer * 2 * devices, dtype=jnp.int32)
    row_core = (row // devices % 2) ^ core
    row_device = row // 2 % chips * 2 + row_core
    row_table = jnp.stack([row // (2 * devices), row_device, row % 2], axis=1)
    column = jnp.arange(devices * 2 * per_peer, dtype=jnp.int32)
    col_peer = column // (2 * per_peer)
    column_table = jnp.stack(
        [col_peer, column % (2 * per_peer), jnp.repeat(handoff_dest, 2 * per_peer)], axis=0
    )
    half_f32 = jax.ShapeDtypeStruct((devices, model), f32)
    half_bf16 = jax.ShapeDtypeStruct((devices, model), bf16)
    keep, send = call(heads_kernel, (half_f32, half_bf16), [whole] * 5, 48)(
        row_table,
        column_table,
        by_head,
        value_upward,
        out_proj.reshape(-1, model),
    )

    def reduce_rows(keep, send):
        other = lax.ppermute(send, "ep", siblings)
        pair = (keep + other.astype(f32)).astype(bf16).reshape(chips, 2, model)
        return exchange_core(pair)

    attention = jnp.sum(reduce_rows(keep, send).astype(f32), axis=0)
    hidden = residual_in[0].astype(f32) + attention
    inverse_rms = lax.rsqrt(jnp.mean(hidden * hidden, axis=-1, keepdims=True) + norm_epsilon)
    normed = (hidden * inverse_rms * norm_gain.astype(f32)).astype(bf16)

    own_rows = exchange_core(jnp.broadcast_to(normed[None], (chips, 2, model)))
    own_rows = own_rows.reshape(devices, model)
    sibling_rows = lax.ppermute(own_rows, "ep", siblings)
    keep, send = call(expert_kernel, (half_f32, half_bf16), [whole] * 5)(
        own_rows, sibling_rows, gate_proj, up_proj, down_proj
    )
    returned = reduce_rows(keep, send)

    chip_expert = jnp.arange(chips, dtype=jnp.int32) * 2 // slice_count
    chosen = (expert_ids[0][..., None] == chip_expert).astype(f32)
    weights = jnp.sum(expert_gates[0][..., None] * chosen, axis=1)
    mixed = jnp.sum(weights.T[..., None] * returned.astype(f32), axis=0)
    return (hidden + mixed).astype(bf16)[None]


def solution(mesh):
    placed = (
        P(("groups", "ep"), None, None),
        P("groups"),
        P("groups"),
        P(("groups", "ep"), None, None),
        P(("groups", "ep")),
        P(None, ("groups", "ep"), None, None),
        P(None, ("groups", "ep"), None),
        P(None, ("groups", "ep"), None),
        P("ep", None, None),
        P("ep", None, None),
        P(),
        P(None, ("groups", "ep"), None),
        P(None, ("groups", "ep"), None),
        P("ep", None),
        P("ep", None),
        P("ep", None),
    )
    return jax.shard_map(
        shards,
        mesh=mesh,
        in_specs=placed,
        out_specs=P(None, ("groups", "ep"), None),
        check_vma=False,
    )
```

time: 140 us -> 110 us (0.79)
  matrix products: 25.3 us -> 3.44 us
  blocking collectives: 31.4 us -> 11.6 us
  Pallas kernels: 0 us -> 14.8 us
  waiting for transfers between devices: 47.6 us -> 43.2 us
  starting transfers between devices: 19.1 us -> 21.5 us
  local copies, waits for them, and re-layouts: 12.1 us -> 10.5 us
    dot_general x10 -> x2, matrix products: 23.2 us -> 3.3 us  [the longest x1 1.71 us: attend(): jnp.dot(cache_probs, key_rows, preferred_element_type=f32)]
    all_to_all x2 -> x1, blocking collectives: 31.4 us -> 11.6 us  [shards(): own_rows = exchange_core(jnp.broadcast_to(normed[None], (chips, 2, model)))]
    pallas_call x0 -> x4, Pallas kernels: none -> 14.8 us  [the longest x1 9.05 us: shards(): call(heads_kernel, (half_f32, half_bf16), [whole] * 5, 48)]
    all_to_all x4 -> x5, waiting for transfers between devices: 47.6 us -> 38.9 us  [the longest x2 17.8 us: reduce_rows(): return exchange_core(pair)]
    unnamed x21 -> x30, local copies, waits for them, and re-layouts: 1.37 us -> 6.77 us
    reshape x5 -> x3, local copies, waits for them, and re-layouts: 6.49 us -> 1.64 us  [the longest x2 1.55 us: reduce_rows(): pair = (keep + other.astype(f32)).astype(bf16).reshape(chips, 2, model)]
    ppermute x0 -> x3, waiting for transfers between devices: none -> 4.31 us  [the longest x2 2.84 us: reduce_rows(): other = lax.ppermute(send, 'ep', siblings)]
    all_to_all x4 -> x5, starting transfers between devices: 19.1 us -> 21.2 us  [the longest x1 7.36 us: shards(): spread = exchange(queries[0, 1].reshape(devices, per_peer, width))]
  transfers between devices with their start and end apart: 4 -> 8, of which waited for: 4 -> 8; matrix products, arithmetic and copies ran while one was open for 4% -> 6% of each run, Pallas kernels for 0% -> 0%
where the time goes in v2:
time: 110 us; the launch traced here: 109 us
  waiting for transfers between devices  43.2 us (39%)
  starting transfers between devices  21.5 us (20%)
  Pallas kernels  14.8 us (13%)
  blocking collectives  11.6 us (11%)
  local copies, waits for them, and re-layouts  10.5 us (10%)
  matrix products  3.44 us (3%)
  other arithmetic  3.04 us (3%)
    all_to_all x2, waiting for transfers between devices, reduce_rows(): return exchange_core(pair)  17.8 us
    all_to_all x1, blocking collectives, shards(): own_rows = exchange_core(jnp.broadcast_to(normed[None], (chips, 2, model)))  11.6 us
    all_to_all x1, waiting for transfers between devices, shards(): by_head = exchange(payload)  10.7 us
    pallas_call x1, Pallas kernels, shards(): call(heads_kernel, (half_f32, half_bf16), [whole] * 5, 48)  9.05 us
    all_to_all x1, starting transfers between devices, shards(): spread = exchange(queries[0, 1].reshape(devices, per_peer, width))  7.36 us
    all_to_all x2, starting transfers between devices, reduce_rows(): return exchange_core(pair)  6.8 us
    unnamed x30, local copies, waits for them, and re-layouts  6.77 us
    all_to_all x1, waiting for transfers between devices, shards(): arrived = exchange(picked)  6.52 us
  transfers between devices with their start and end apart: 8, of which 8 were waited for; matrix products, arithmetic and copies ran while one was open for 6% of the time, Pallas kernels for 0%

profile of v2, /device:TPU:0, one launch (start us, length us, event | category | flops | bytes accessed | tf_op | source)
XLA Modules:
  0.0 109.1 jit_solution(4990622676646957216)
XLA Ops:
  0.0 1.1 slice.20
  1.1 0.8 copy.22
  1.9 7.4 %all-to-all-start = ((bf16[16,8,576]{2,1,0:T(8,128)(2,1)}), bf16[16,8,576]{2,1,0:T(8,128)(2,1)S(1)}, u32[]{:S(2)}, u32[]{:S(2)}) async-start(bf16[16,8,576]{2,1,0:T(8,128)(2,1)} %bitcast), calls=%async_computation | async-start | bytes 327680 | tf_op jit(solution)/shard_map/all_to_all | solution.py:203
  9.9 1.6 %fusion.27 = (f32[128]{0:T(128)S(1)}, f32[128,2048]{1,0:T(8,128)S(1)}) fusion(bf16[1,2048,576]{1,2,0:T(8,128)(2,1)S(1)} %copy-done, bf16[1,2,128,576]{2,3,1,0:T(8,128)(2,1)} %param.21, pred[2048]{0:T(1024)(128)(4,1)S(1)} %iota_compare_fusion), kind=kOutput, calls=%fused_computation.76 | convolution fusion | flops 302776192 | bytes 3557888 | tf_op jit(solution)/shard_map/dot_general | solution.py:26
  11.5 0.1 fusion.28
  11.7 0.3 fusion.5
  12.0 1.7 %fusion.1 = f32[128,576]{1,0:T(8,128)} fusion(bf16[1,2048,576]{1,2,0:T(8,128)(2,1)S(1)} %copy-done, f32[128,2048]{1,0:T(8,128)S(1)} %get-tuple-element.18, f32[128]{0:T(128)S(1)} %get-tuple-element.16, f32[128]{0:T(128)S(1)} %get-tuple-element.19), kind=kOutput, calls=%fused_computation.2 | convolution fusion | flops 302776320 | bytes 3703808 | tf_op jit(solution)/shard_map/dot_general | solution.py:43
  13.8 4.0 %all-to-all-done.spread_ref = bf16[16,8,576]{2,1,0:T(8,128)(2,1)S(1)} async-done(((bf16[16,8,576]{2,1,0:T(8,128)(2,1)}), bf16[16,8,576]{2,1,0:T(8,128)(2,1)S(1)}, u32[]{:S(2)}, u32[]{:S(2)}) %all-to-all-start) | async-done | bytes 147488 | tf_op jit(solution)/shard_map/all_to_all | solution.py:203
  17.7 1.2 %shard_map.154 = bf16[16,8,576]{2,1,0:T(8,128)(2,1)} custom-call(s32[16]{0:T(128)S(1)} %copy-done.5, bf16[16,8,576]{2,1,0:T(8,128)(2,1)S(1)} %all-to-all-done.spread_ref), custom_call_target="tpu_custom_call" | custom-call | tf_op jit(solution)/shard_map/pallas_call | solution.py:204
  19.0 3.5 %all-to-all-start.1 = ((bf16[16,8,576]{2,1,0:T(8,128)(2,1)}), bf16[16,8,576]{2,1,0:T(8,128)(2,1)S(1)}, u32[]{:S(2)}, u32[]{:S(2)}) async-start(bf16[16,8,576]{2,1,0:T(8,128)(2,1)} %shard_map.154), calls=%async_computation.1 | async-start | bytes 327680 | tf_op jit(solution)/shard_map/all_to_all | solution.py:209
  22.5 0.2 copy.20
  22.7 0.6 dynamic_slice.3.length_ref
  23.3 1.0 fusion.8.resident_ref
  24.4 6.5 %all-to-all-done.1.query_ref = bf16[16,8,576]{2,1,0:T(8,128)(2,1)S(1)} async-done(((bf16[16,8,576]{2,1,0:T(8,128)(2,1)}), bf16[16,8,576]{2,1,0:T(8,128)(2,1)S(1)}, u32[]{:S(2)}, u32[]{:S(2)}) %all-to-all-start.1) | async-done | bytes 147488 | tf_op jit(solution)/shard_map/all_to_all | solution.py:209
  30.9 2.8 %shard_map.155 = bf16[16,16,640]{2,1,0:T(8,128)(2,1)} custom-call(s32[1]{0:T(128)} %dynamic_slice.3.length_ref, bf16[16,8,576]{2,1,0:T(8,128)(2,1)S(1)} %all-to-all-done.1.query_ref, bf16[256,576]{1,0:T(8,128)(2,1)S(1)} %bitcast.58, bf16[128,512]{1,0:T(8,128)(2,1)S(1)} %fusion.8.resident_ref, bf16[128,576]{1,0:T(8,128)(2,1)} %bitcast.6.own_query_ref, ...), custom_call_target="tpu_custom_call" | custom-call | tf_op jit(solution)/shard_map/pallas_call | solution.py:219
  33.7 3.5 %all-to-all-start.2 = ((bf16[16,16,640]{2,1,0:T(8,128)(2,1)}), bf16[16,16,640]{2,1,0:T(8,128)(2,1)S(1)}, u32[]{:S(2)}, u32[]{:S(2)}) async-start(bf16[16,16,640]{2,1,0:T(8,128)(2,1)} %shard_map.155), calls=%async_computation.2 | async-start | bytes 655360 | tf_op jit(solution)/shard_map/all_to_all | solution.py:232
  37.3 0.1 copy.21.row_ref
  37.4 0.1 broadcast_in_dim.18
  37.5 0.1 stack_reshape.3
  37.6 10.7 %all-to-all-done.2.rows_ref = bf16[16,16,640]{2,1,0:T(8,128)(2,1)S(1)} async-done(((bf16[16,16,640]{2,1,0:T(8,128)(2,1)}), bf16[16,16,640]{2,1,0:T(8,128)(2,1)S(1)}, u32[]{:S(2)}, u32[]{:S(2)}) %all-to-all-start.2) | async-done | bytes 327712 | tf_op jit(solution)/shard_map/all_to_all | solution.py:232
  48.3 1.2 %copy-done.4 = bf16[8,512,128]{2,1,0:T(8,128)(2,1)S(1)} copy-done((bf16[8,512,128]{2,1,0:T(8,128)(2,1)S(1)}, bf16[8,512,128]{2,1,0:T(8,128)(2,1)}, u32[]{:S(2)}) %copy-start.4) | copy-done | bytes 1048600
  49.5 9.1 %shard_map.156 = (f32[16,7168]{1,0:T(8,128)S(1)}, bf16[16,7168]{1,0:T(8,128)(2,1)S(1)}) custom-call(s32[256,3]{1,0:T(8,128)S(1)} %copy.21.row_ref, s32[3,256]{1,0:T(4,128)S(1)} %pad_add_fusion.1.column_ref, bf16[16,16,640]{2,1,0:T(8,128)(2,1)S(1)} %all-to-all-done.2.rows_ref, bf16[8,512,128]{2,1,0:T(8,128)(2,1)S(1)} %copy-done.4, bf16[1024,7168]{1,0:T(8,128)(2,1)} %bitcast.59), custom_call_target="tpu_custom_call" | custom-call | tf_op jit(solution)/shard_map/pallas_call | solution.py:245
  58.6 0.0 collective-permute-start
  58.6 1.5 %collective-permute-done = bf16[16,7168]{1,0:T(8,128)(2,1)S(1)} collective-permute-done((bf16[16,7168]{1,0:T(8,128)(2,1)S(1)}, bf16[16,7168]{1,0:T(8,128)(2,1)S(1)}, u32[]{:S(2)}, u32[]{:S(2)}) %collective-permute-start) | collective-permute-done | bytes 229408 | tf_op jit(solution)/shard_map/ppermute | solution.py:254
  60.1 0.8 reshape.348
  60.9 3.4 %all-to-all-start.3 = ((bf16[8,2,7168]{2,1,0:T(2,128)(2,1)}), bf16[8,2,7168]{2,1,0:T(2,128)(2,1)S(1)}, u32[]{:S(2)}, u32[]{:S(2)}) async-start(bf16[8,2,7168]{2,1,0:T(2,128)(2,1)} %reshape.348), calls=%async_computation.3 | async-start | bytes 458752 | tf_op jit(solution)/shard_map/all_to_all | solution.py:256
  64.3 8.9 %all-to-all-done.3 = bf16[8,2,7168]{2,1,0:T(2,128)(2,1)S(1)} async-done(((bf16[8,2,7168]{2,1,0:T(2,128)(2,1)}), bf16[8,2,7168]{2,1,0:T(2,128)(2,1)S(1)}, u32[]{:S(2)}, u32[]{:S(2)}) %all-to-all-start.3) | async-done | bytes 229408 | tf_op jit(solution)/shard_map/all_to_all | solution.py:256
  73.3 0.2 convert_reduce_fusion
  73.5 0.2 fusion.15
  73.6 0.1 fusion.17
  73.8 0.1 broadcast_in_dim.22
  73.9 11.6 %all_to_all.30 = bf16[8,2,7168]{2,1,0:T(2,128)(2,1)S(1)} all-to-all(bf16[8,2,7168]{2,1,0:T(2,128)(2,1)S(1)} %broadcast_in_dim.22), channel_id=1, replica_groups={{0,2,4,6,8,10,12,14},{1,3,5,7,9,11,13,15},{16,18,20,22,24,26,28,30},{17..., dimensions={0} | all-to-all | bytes 458752 | tf_op jit(solution)/shard_map/all_to_all | solution.py:263
  85.5 0.1 reshape.349.own_ref
  85.6 0.1 collective-permute-start.1
  85.7 1.5 %collective-permute-done.1.sibling_ref = bf16[16,7168]{1,0:T(8,128)(2,1)S(1)} collective-permute-done((bf16[16,7168]{1,0:T(8,128)(2,1)S(1)}, bf16[16,7168]{1,0:T(8,128)(2,1)S(1)}, u32[]{:S(2)}, u32[]{:S(2)}) %collective-permute-start.1) | collective-permute-done | bytes 229408 | tf_op jit(solution)/shard_map/ppermute | solution.py:265
  87.2 1.5 %copy-done.1 = bf16[128,7168]{1,0:T(8,128)(2,1)S(1)} copy-done((bf16[128,7168]{1,0:T(8,128)(2,1)S(1)}, bf16[128,7168]{1,0:T(8,128)(2,1)}, u32[]{:S(2)}) %copy-start.1) | copy-done | bytes 1835032
  88.7 1.5 %copy-done.2 = bf16[128,7168]{1,0:T(8,128)(2,1)S(1)} copy-done((bf16[128,7168]{1,0:T(8,128)(2,1)S(1)}, bf16[128,7168]{1,0:T(8,128)(2,1)}, u32[]{:S(2)}) %copy-start.2) | copy-done | bytes 1835032
  90.2 1.5 %copy-done.3 = bf16[128,7168]{1,0:T(8,128)(2,1)S(1)} copy-done((bf16[128,7168]{1,0:T(8,128)(2,1)S(1)}, bf16[128,7168]{1,0:T(8,128)(2,1)}, u32[]{:S(2)}) %copy-start.3) | copy-done | bytes 1835032
  91.7 1.7 %shard_map.157 = (f32[16,7168]{1,0:T(8,128)S(1)}, bf16[16,7168]{1,0:T(8,128)(2,1)S(1)}) custom-call(bf16[16,7168]{1,0:T(8,128)(2,1)S(1)} %reshape.349.own_ref, bf16[16,7168]{1,0:T(8,128)(2,1)S(1)} %collective-permute-done.1.sibling_ref, bf16[128,7168]{1,0:T(8,128)(2,1)S(1)} %copy-done.1, bf16[128,7168]{1,0:T(8,128)(2,1)S(1)} %copy-done.2, ...), custom_call_target="tpu_custom_call" | custom-call | tf_op jit(solution)/shard_map/pallas_call | solution.py:266
  93.4 0.2 collective-permute-start.2
  93.6 1.4 %collective-permute-done.2 = bf16[16,7168]{1,0:T(8,128)(2,1)S(1)} collective-permute-done((bf16[16,7168]{1,0:T(8,128)(2,1)S(1)}, bf16[16,7168]{1,0:T(8,128)(2,1)S(1)}, u32[]{:S(2)}, u32[]{:S(2)}) %collective-permute-start.2) | collective-permute-done | bytes 229408 | tf_op jit(solution)/shard_map/ppermute | solution.py:254
  94.9 0.1 add_convert_fusion
  95.0 0.8 reshape.350
  95.7 3.4 %all-to-all-start.5 = ((bf16[8,2,7168]{2,1,0:T(2,128)(2,1)}), bf16[8,2,7168]{2,1,0:T(2,128)(2,1)S(1)}, u32[]{:S(2)}, u32[]{:S(2)}) async-start(bf16[8,2,7168]{2,1,0:T(2,128)(2,1)} %reshape.350), calls=%async_computation.5 | async-start | bytes 458752 | tf_op jit(solution)/shard_map/all_to_all | solution.py:256
  99.2 0.1 compare_select_fusion.4
  99.3 8.8 %all-to-all-done.5 = bf16[8,2,7168]{2,1,0:T(2,128)(2,1)S(1)} async-done(((bf16[8,2,7168]{2,1,0:T(2,128)(2,1)}), bf16[8,2,7168]{2,1,0:T(2,128)(2,1)S(1)}, u32[]{:S(2)}, u32[]{:S(2)}) %all-to-all-start.5) | async-done | bytes 229408 | tf_op jit(solution)/shard_map/all_to_all | solution.py:256
  108.1 0.3 multiply_reduce_fusion
  108.4 0.7 fusion.16
  (39 shorter events, 0.2 us)
Async XLA Ops:
  0.0 9.9 %copy-start = (bf16[1,2048,576]{1,2,0:T(8,128)(2,1)S(1)}, bf16[1,2048,576]{1,2,0:T(8,128)(2,1)}, u32[]{:S(2)}) copy-start(bf16[1,2048,576]{1,2,0:T(8,128)(2,1)} %param.19) | copy-start | bytes 7077892
  0.0 11.5 %copy-start.6 = (bf16[1,2,128,576]{2,3,1,0:T(8,128)(2,1)S(1)}, bf16[1,2,128,576]{2,3,1,0:T(8,128)(2,1)}, u32[]{:S(2)}) copy-start(bf16[1,2,128,576]{2,3,1,0:T(8,128)(2,1)} %param.21) | copy-start | bytes 884740
  0.0 11.5 %copy-start.9 = (bf16[1,2,576]{2,1,0:T(2,128)(2,1)S(1)}, bf16[1,2,576]{2,1,0:T(2,128)(2,1)}, u32[]{:S(2)}) copy-start(bf16[1,2,576]{2,1,0:T(2,128)(2,1)} %param.22) | copy-start | bytes 6916
  1.9 15.8 %all-to-all-start = ((bf16[16,8,576]{2,1,0:T(8,128)(2,1)}), bf16[16,8,576]{2,1,0:T(8,128)(2,1)S(1)}, u32[]{:S(2)}, u32[]{:S(2)}) async-start(bf16[16,8,576]{2,1,0:T(8,128)(2,1)} %bitcast), calls=%async_computation | async-start | bytes 327680 | tf_op jit(solution)/shard_map/all_to_all | solution.py:203
  12.0 5.7 %copy-start.5 = (s32[16]{0:T(128)S(1)}, s32[16]{0:T(128)}, u32[]{:S(2)}) copy-start(s32[16]{0:T(128)} %dest_ref.1) | copy-start | bytes 196
  12.0 10.5 %copy-start.7 = (bf16[1,256,576]{1,2,0:T(8,128)(2,1)S(1)}, bf16[1,256,576]{1,2,0:T(8,128)(2,1)}, u32[]{:S(2)}) copy-start(bf16[1,256,576]{1,2,0:T(8,128)(2,1)} %param.16) | copy-start | bytes 884740
  12.0 10.7 %copy-start.13 = (s32[16]{0:T(128)S(1)}, s32[16]{0:T(128)}, u32[]{:S(2)}) copy-start(s32[16]{0:T(128)} %param.18) | copy-start | bytes 196
  19.0 11.9 %all-to-all-start.1 = ((bf16[16,8,576]{2,1,0:T(8,128)(2,1)}), bf16[16,8,576]{2,1,0:T(8,128)(2,1)S(1)}, u32[]{:S(2)}, u32[]{:S(2)}) async-start(bf16[16,8,576]{2,1,0:T(8,128)(2,1)} %shard_map.154), calls=%async_computation.1 | async-start | bytes 327680 | tf_op jit(solution)/shard_map/all_to_all | solution.py:209
  33.7 14.6 %all-to-all-start.2 = ((bf16[16,16,640]{2,1,0:T(8,128)(2,1)}), bf16[16,16,640]{2,1,0:T(8,128)(2,1)S(1)}, u32[]{:S(2)}, u32[]{:S(2)}) async-start(bf16[16,16,640]{2,1,0:T(8,128)(2,1)} %shard_map.155), calls=%async_computation.2 | async-start | bytes 655360 | tf_op jit(solution)/shard_map/all_to_all | solution.py:232
  48.3 1.2 %copy-start.4 = (bf16[8,512,128]{2,1,0:T(8,128)(2,1)S(1)}, bf16[8,512,128]{2,1,0:T(8,128)(2,1)}, u32[]{:S(2)}) copy-start(bf16[8,512,128]{2,1,0:T(8,128)(2,1)} %upward_ref.1) | copy-start | bytes 3145732
  49.5 14.8 %copy-start.10 = (bf16[7168]{0:T(1024)(128)(2,1)S(1)}, bf16[7168]{0:T(1024)(128)(2,1)}, u32[]{:S(2)}) copy-start(bf16[7168]{0:T(1024)(128)(2,1)} %param.26) | copy-start | bytes 43012
  49.5 23.9 %copy-start.8 = (bf16[1,2,7168]{2,1,0:T(2,128)(2,1)S(1)}, bf16[1,2,7168]{2,1,0:T(2,128)(2,1)}, u32[]{:S(2)}) copy-start(bf16[1,2,7168]{2,1,0:T(2,128)(2,1)} %param.23) | copy-start | bytes 86020
  58.6 1.5 %collective-permute-start = (bf16[16,7168]{1,0:T(8,128)(2,1)S(1)}, bf16[16,7168]{1,0:T(8,128)(2,1)S(1)}, u32[]{:S(2)}, u32[]{:S(2)}) collective-permute-start(bf16[16,7168]{1,0:T(8,128)(2,1)S(1)} %get-tuple-element.10), channel_id=1, source_target_pairs={{0,1},{1,0},{2,3},{3,2},{4,5},{5,4},{6,7},{7,6},{8,9},{9,8},{10,11... | collective-permute-start | bytes 688136 | tf_op jit(solution)/shard_map/ppermute | solution.py:254
  60.9 12.4 %all-to-all-start.3 = ((bf16[8,2,7168]{2,1,0:T(2,128)(2,1)}), bf16[8,2,7168]{2,1,0:T(2,128)(2,1)S(1)}, u32[]{:S(2)}, u32[]{:S(2)}) async-start(bf16[8,2,7168]{2,1,0:T(2,128)(2,1)} %reshape.348), calls=%async_computation.3 | async-start | bytes 458752 | tf_op jit(solution)/shard_map/all_to_all | solution.py:256
  85.5 13.7 %copy-start.11 = (f32[1,2,1]{1,2,0:T(1,128)S(1)}, f32[1,2,1]{1,2,0:T(1,128)}, u32[]{:S(2)}) copy-start(f32[1,2,1]{1,2,0:T(1,128)} %param.28) | copy-start | bytes 28
  85.5 13.7 %copy-start.12 = (s32[1,2,1]{1,2,0:T(1,128)S(1)}, s32[1,2,1]{1,2,0:T(1,128)}, u32[]{:S(2)}) copy-start(s32[1,2,1]{1,2,0:T(1,128)} %param.27) | copy-start | bytes 28
  85.6 1.6 %collective-permute-start.1 = (bf16[16,7168]{1,0:T(8,128)(2,1)S(1)}, bf16[16,7168]{1,0:T(8,128)(2,1)S(1)}, u32[]{:S(2)}, u32[]{:S(2)}) collective-permute-start(bf16[16,7168]{1,0:T(8,128)(2,1)S(1)} %reshape.349.own_ref), channel_id=1, source_target_pairs={{0,1},{1,0},{2,3},{3,2},{4,5},{5,4},{6,7},{7,6},{8,9},{9,8},{10,11... | collective-permute-start | bytes 688136 | tf_op jit(solution)/shard_map/ppermute | solution.py:265
  87.2 1.5 %copy-start.1 = (bf16[128,7168]{1,0:T(8,128)(2,1)S(1)}, bf16[128,7168]{1,0:T(8,128)(2,1)}, u32[]{:S(2)}) copy-start(bf16[128,7168]{1,0:T(8,128)(2,1)} %gate_ref.1) | copy-start | bytes 5505028
  88.7 1.5 %copy-start.2 = (bf16[128,7168]{1,0:T(8,128)(2,1)S(1)}, bf16[128,7168]{1,0:T(8,128)(2,1)}, u32[]{:S(2)}) copy-start(bf16[128,7168]{1,0:T(8,128)(2,1)} %up_ref.1) | copy-start | bytes 5505028
  90.2 1.5 %copy-start.3 = (bf16[128,7168]{1,0:T(8,128)(2,1)S(1)}, bf16[128,7168]{1,0:T(8,128)(2,1)}, u32[]{:S(2)}) copy-start(bf16[128,7168]{1,0:T(8,128)(2,1)} %down_ref.1) | copy-start | bytes 5505028
  93.4 1.6 %collective-permute-start.2 = (bf16[16,7168]{1,0:T(8,128)(2,1)S(1)}, bf16[16,7168]{1,0:T(8,128)(2,1)S(1)}, u32[]{:S(2)}, u32[]{:S(2)}) collective-permute-start(bf16[16,7168]{1,0:T(8,128)(2,1)S(1)} %get-tuple-element.12), channel_id=1, source_target_pairs={{0,1},{1,0},{2,3},{3,2},{4,5},{5,4},{6,7},{7,6},{8,9},{9,8},{10,11... | collective-permute-start | bytes 688136 | tf_op jit(solution)/shard_map/ppermute | solution.py:254
  95.7 12.4 %all-to-all-start.5 = ((bf16[8,2,7168]{2,1,0:T(2,128)(2,1)}), bf16[8,2,7168]{2,1,0:T(2,128)(2,1)S(1)}, u32[]{:S(2)}, u32[]{:S(2)}) async-start(bf16[8,2,7168]{2,1,0:T(2,128)(2,1)} %reshape.350), calls=%async_computation.5 | async-start | bytes 458752 | tf_op jit(solution)/shard_map/all_to_all | solution.py:256

commit v3 on v2

--- a/solution.py
+++ b/solution.py
@@ -11,6 +11,7 @@
 MOE_FF = 1024
 UNITS = 128
 LANES = 128
+BLOCK = 1024
 
 softmax_scale = 192.0 ** (-0.5)
 norm_epsilon = 1e-06
@@ -53,13 +54,30 @@
     return first, second, third
 
 
+def spread_kernel(query_ref, spread_ref):
+    peers, per_peer, width = spread_ref.shape
+    rows = query_ref[0].astype(f32).T.reshape(peers, per_peer, width)
+    spread_ref[...] = rows.astype(bf16)
+
+
 def pick_kernel(dest_ref, spread_ref, picked_ref):
     for prompt in range(spread_ref.shape[0]):
         picked_ref[prompt] = spread_ref[dest_ref[prompt]]
 
 
+def fresh_kernel(query_ref, fresh_ref, stats_ref):
+    score = softmax_scale * jnp.sum(
+        query_ref[...].astype(f32) * fresh_ref[...].astype(f32), axis=1, keepdims=True
+    )
+    lane = lax.broadcasted_iota(jnp.int32, stats_ref.shape, 1)
+    stats = jnp.zeros(stats_ref.shape, f32)
+    for at, column in enumerate(three_parts(score)):
+        stats = jnp.where(lane == 3 + at, column, stats)
+    stats_ref[...] = stats
+
+
 def prompt_kernel(
-    length_ref, query_ref, key_ref, resident_ref, own_query_ref, fresh_ref, fresh_rows_ref, out_ref
+    length_ref, query_ref, key_ref, resident_ref, stats_ref, fresh_rows_ref, out_ref
 ):
     peers, rows, width = out_ref.shape
     per_peer = rows // 2
@@ -73,13 +91,9 @@
     terms = jnp.exp(scores - peak)
     total = jnp.sum(terms, axis=1, keepdims=True)
     mixed = jnp.dot(terms.astype(bf16), keys[:, :KVR], preferred_element_type=f32) / total
-    log_sum = peak + jnp.log(total)
-    fresh_score = softmax_scale * jnp.sum(
-        own_query_ref[...].astype(f32) * fresh_ref[...].astype(f32), axis=1, keepdims=True
-    )
     lane = lax.broadcasted_iota(jnp.int32, (heads, width - KVR), 1)
-    stats = jnp.zeros((heads, width - KVR), f32)
-    for at, column in enumerate(three_parts(log_sum) + three_parts(fresh_score)):
+    stats = stats_ref[...]
+    for at, column in enumerate(three_parts(peak + jnp.log(total))):
         stats = jnp.where(lane == at, column, stats)
     fold = lambda value: value.reshape(peers, per_peer, value.shape[1])
     out_ref[:, :, :KVR] = jnp.concatenate(
@@ -91,7 +105,36 @@
     out_ref[:, :, KVR:] = jnp.concatenate([fold(stats), fresh_rows], axis=1).astype(bf16)
 
 
-def heads_kernel(row_ref, column_ref, rows_ref, upward_ref, proj_ref, keep_ref, send_ref):
+def pair_kernel(keep_ref, other_ref, pair_ref):
+    total = keep_ref[...] + other_ref[...].astype(f32)
+    pair_ref[...] = total.reshape(pair_ref.shape).astype(bf16)
+
+
+def heads_kernel(
+    row_ref,
+    column_ref,
+    rows_ref,
+    upward_hbm,
+    proj_hbm,
+    keep_ref,
+    send_ref,
+    upward_ref,
+    proj_ref,
+    arrived,
+):
+    upward_copy = pltpu.make_async_copy(upward_hbm, upward_ref, arrived.at[0])
+    upward_copy.start()
+    blocks = range(0, proj_ref.shape[1], BLOCK)
+    proj_copies = [
+        pltpu.make_async_copy(
+            proj_hbm.at[:, start : start + BLOCK],
+            proj_ref.at[:, start : start + BLOCK],
+            arrived.at[1 + at],
+        )
+        for at, start in enumerate(blocks)
+    ]
+    for copy in proj_copies:
+        copy.start()
     peers, rows, width = rows_ref.shape
     per_peer = rows // 2
     columns = peers * rows
@@ -127,6 +170,7 @@
         mixed = mixed + jnp.dot(high, values, preferred_element_type=f32)
         mixed = mixed + jnp.dot(low, values, preferred_element_type=f32)
     mixed = mixed.astype(bf16)
+    upward_copy.wait()
     value_rows = jnp.concatenate(
         [
             jnp.dot(
@@ -136,33 +180,57 @@
         ],
         axis=1,
     )
-    step = 1024
-    for start in range(0, proj_ref.shape[1], step):
-        part = jnp.dot(value_rows, proj_ref[:, start : start + step], preferred_element_type=f32)
-        keep_ref[:, start : start + step] = part[:peers]
-        send_ref[:, start : start + step] = part[peers:].astype(bf16)
-
-
-def expert_kernel(own_ref, sibling_ref, gate_ref, up_ref, down_ref, keep_ref, send_ref):
-    half = own_ref.shape[0]
-    rows = jnp.concatenate([own_ref[...], sibling_ref[...]], axis=0)
+    for copy, start in zip(proj_copies, blocks):
+        copy.wait()
+        part = jnp.dot(value_rows, proj_ref[:, start : start + BLOCK], preferred_element_type=f32)
+        keep_ref[:, start : start + BLOCK] = part[:peers]
+        send_ref[:, start : start + BLOCK] = part[peers:].astype(bf16)
+
+
+def expert_kernel(rows_ref, *refs):
+    out_ref, arrived = refs[6], refs[10]
+    units = refs[0].shape[0]
+    copies = [
+        pltpu.make_async_copy(
+            refs[at], refs[7 + at // 2].at[pl.ds(at % 2 * units, units)], arrived.at[at]
+        )
+        for at in range(6)
+    ]
+    for copy in copies:
+        copy.start()
+    gate_ref, up_ref, down_ref = refs[7:10]
+    rows = rows_ref[...]
+    copies[0].wait()
+    copies[1].wait()
     gate = lax.dot_general(rows, gate_ref[...], contract_last, preferred_element_type=f32)
+    copies[2].wait()
+    copies[3].wait()
     up_value = lax.dot_general(rows, up_ref[...], contract_last, preferred_element_type=f32)
     act = (gate / (1.0 + jnp.exp(-gate)) * up_value).astype(bf16)
-    step = 1024
-    for start in range(0, down_ref.shape[1], step):
-        part = jnp.dot(act, down_ref[:, start : start + step], preferred_element_type=f32)
-        keep_ref[:, start : start + step] = part[:half]
-        send_ref[:, start : start + step] = part[half:].astype(bf16)
-
-
-def call(kernel, shapes, specs, limit=32):
+    copies[4].wait()
+    copies[5].wait()
+    chips, pair = out_ref.shape[:2]
+    for start in range(0, down_ref.shape[1], BLOCK):
+        part = jnp.dot(act, down_ref[:, start : start + BLOCK], preferred_element_type=f32)
+        out_ref[:, :, start : start + BLOCK] = part.reshape(chips, pair, BLOCK).astype(bf16)
+
+
+def near(value):
+    return pltpu.with_memory_space_constraint(value, pltpu.VMEM)
+
+
+def call(kernel, outputs, operands, far=(), scratch=()):
+    specs = [scalars if operand.ndim == 1 else whole for operand in operands]
     return pl.pallas_call(
         kernel,
-        out_shape=shapes,
-        in_specs=specs,
-        out_specs=jax.tree.map(lambda _: whole, shapes),
-        compiler_params=pltpu.CompilerParams(vmem_limit_bytes=limit << 20),
+        out_shape=[pltpu.VMEM(shape, dtype) for shape, dtype in outputs],
+        in_specs=specs + [pl.BlockSpec(memory_space=pl.ANY)] * len(far),
+        out_specs=[whole] * len(outputs),
+        scratch_shapes=scratch,
+        compiler_params=pltpu.CompilerParams(vmem_limit_bytes=32 << 20),
+    )(
+        *[operand if operand.ndim == 1 else near(operand) for operand in operands],
+        *[pltpu.with_memory_space_constraint(operand, pltpu.HBM) for operand in far],
     )
 
 
@@ -200,12 +268,17 @@
     )
     exchange_core = functools.partial(exchange, axis_index_groups=same_core)
 
-    spread = exchange(queries[0, 1].reshape(devices, per_peer, width))
-    picked = call(
-        pick_kernel,
-        jax.ShapeDtypeStruct(spread.shape, bf16),
-        [scalars, whole],
-    )(handoff_dest, spread)
+    flipped = jnp.swapaxes(queries[0], 1, 2)
+    spread_rows = pl.pallas_call(
+        spread_kernel,
+        out_shape=pltpu.VMEM((devices, per_peer, width), bf16),
+        grid=(1,),
+        in_specs=[pl.BlockSpec((1, width, heads), lambda step: (1, 0, 0))],
+        out_specs=pl.BlockSpec((devices, per_peer, width), lambda step: (0, 0, 0)),
+        compiler_params=pltpu.CompilerParams(vmem_limit_bytes=16 << 20),
+    )(pltpu.with_memory_space_constraint(flipped, pltpu.HBM))
+    spread = exchange(spread_rows)
+    (picked,) = call(pick_kernel, [(spread.shape, bf16)], [handoff_dest, spread])
     arrived = exchange(picked)
 
     cache_keys = resident_cache[0]
@@ -216,18 +289,11 @@
     fresh_rows = new_latent[0, 1, :KVR].reshape(KVR // chunk, chunk)
     fresh_rows = jnp.pad(fresh_rows, ((0, per_peer - KVR // chunk), (0, 0)))
     own_len = lax.dynamic_slice(handoff_len, (device,), (1,))
-    payload = call(
+    (stats,) = call(fresh_kernel, [((heads, chunk), f32)], [queries[0, 1], new_latent[0, 1:2]])
+    (payload,) = call(
         prompt_kernel,
-        jax.ShapeDtypeStruct((devices, 2 * per_peer, KVR + chunk), bf16),
-        [scalars] + [whole] * 6,
-    )(
-        own_len,
-        arrived,
-        handoff_rows[0],
-        resident_out,
-        queries[0, 1],
-        new_latent[0, 1:2],
-        fresh_rows,
+        [((devices, 2 * per_peer, KVR + chunk), bf16)],
+        [own_len, arrived, handoff_rows[0], resident_out, stats, fresh_rows],
     )
     by_head = exchange(payload)
 
@@ -240,33 +306,39 @@
     column_table = jnp.stack(
         [col_peer, column % (2 * per_peer), jnp.repeat(handoff_dest, 2 * per_peer)], axis=0
     )
-    half_f32 = jax.ShapeDtypeStruct((devices, model), f32)
-    half_bf16 = jax.ShapeDtypeStruct((devices, model), bf16)
-    keep, send = call(heads_kernel, (half_f32, half_bf16), [whole] * 5, 48)(
-        row_table,
-        column_table,
-        by_head,
-        value_upward,
-        out_proj.reshape(-1, model),
-    )
-
-    def reduce_rows(keep, send):
-        other = lax.ppermute(send, "ep", siblings)
-        pair = (keep + other.astype(f32)).astype(bf16).reshape(chips, 2, model)
-        return exchange_core(pair)
-
-    attention = jnp.sum(reduce_rows(keep, send).astype(f32), axis=0)
+    projection = out_proj.reshape(-1, model)
+    keep, send = call(
+        heads_kernel,
+        [((devices, model), f32), ((devices, model), bf16)],
+        [row_table, column_table, by_head],
+        [value_upward, projection],
+        [
+            pltpu.VMEM(value_upward.shape, bf16),
+            pltpu.VMEM(projection.shape, bf16),
+            pltpu.SemaphoreType.DMA((1 + model // BLOCK,)),
+        ],
+    )
+
+    other = lax.ppermute(send, "ep", siblings)
+    (pair,) = call(pair_kernel, [((chips, 2, model), bf16)], [keep, other])
+    attention = jnp.sum(exchange_core(pair).astype(f32), axis=0)
     hidden = residual_in[0].astype(f32) + attention
     inverse_rms = lax.rsqrt(jnp.mean(hidden * hidden, axis=-1, keepdims=True) + norm_epsilon)
     normed = (hidden * inverse_rms * norm_gain.astype(f32)).astype(bf16)
 
     own_rows = exchange_core(jnp.broadcast_to(normed[None], (chips, 2, model)))
-    own_rows = own_rows.reshape(devices, model)
-    sibling_rows = lax.ppermute(own_rows, "ep", siblings)
-    keep, send = call(expert_kernel, (half_f32, half_bf16), [whole] * 5)(
-        own_rows, sibling_rows, gate_proj, up_proj, down_proj
-    )
-    returned = reduce_rows(keep, send)
+    experts = []
+    for matrix in (gate_proj, up_proj, down_proj):
+        experts += [matrix, lax.ppermute(matrix, "ep", siblings)]
+    (part,) = call(
+        expert_kernel,
+        [((chips, 2, model), bf16)],
+        [own_rows.reshape(devices, model)],
+        experts,
+        [pltpu.VMEM((2 * gate_proj.shape[0], model), bf16)] * 3
+        + [pltpu.SemaphoreType.DMA((6,))],
+    )
+    returned = exchange_core(part)
 
     chip_expert = jnp.arange(chips, dtype=jnp.int32) * 2 // slice_count
     chosen = (expert_ids[0][..., None] == chip_expert).astype(f32)

time: 110 us -> 102 us (0.927)
  local copies, waits for them, and re-layouts: 10.5 us -> 1.57 us
  Pallas kernels: 14.8 us -> 20.4 us
  waiting for transfers between devices: 43.2 us -> 38.5 us
    unnamed x30 -> x22, local copies, waits for them, and re-layouts: 6.77 us -> 0.42 us
    pallas_call x4 -> x7, Pallas kernels: 14.8 us -> 20.4 us  [the longest x6 18.6 us: call(): pl.pallas_call(kernel, out_shape=[pltpu.VMEM(shape, dtype) for shape, dty...]
    ppermute x3 -> x4, waiting for transfers between devices: 4.31 us -> 1.48 us  [the longest x1 1.48 us: shards(): other = lax.ppermute(send, 'ep', siblings)]
    all_to_all x3, waiting for transfers between devices: 21.7 us -> 20.2 us  [the longest x1 8.23 us: shards(): attention = jnp.sum(exchange_core(pair).astype(f32), axis=0)]
    reshape x3 -> x1, local copies, waits for them, and re-layouts: 1.64 us -> 0.09 us  [shards(): own_rows.reshape(devices, model)]
  transfers between devices with their start and end apart: 8 -> 9, of which waited for: 8 -> 6; matrix products, arithmetic and copies ran while one was open for 6% -> 7% of each run, Pallas kernels for 0% -> 0%
where the time goes in v3:
time: 102 us
  waiting for transfers between devices  38.5 us (38%)
  starting transfers between devices  22 us (22%)
  Pallas kernels  20.4 us (20%)
  blocking collectives  11.6 us (11%)
  matrix products  3.45 us (3%)
  other arithmetic  2.95 us (3%)
  local copies, waits for them, and re-layouts  1.57 us (2%)
    pallas_call x6, Pallas kernels, call(): pl.pallas_call(kernel, out_shape=[pltpu.VMEM(shape, dtype) for shape, dty...  18.6 us
    all_to_all x1, blocking collectives, shards(): own_rows = exchange_core(jnp.broadcast_to(normed[None], (chips, 2, model)))  11.6 us
    all_to_all x1, waiting for transfers between devices, shards(): by_head = exchange(payload)  10.7 us
    all_to_all x1, waiting for transfers between devices, shards(): attention = jnp.sum(exchange_core(pair).astype(f32), axis=0)  8.23 us
    all_to_all x1, waiting for transfers between devices, shards(): returned = exchange_core(part)  7.98 us
    all_to_all x1, starting transfers between devices, shards(): spread = exchange(spread_rows)  7.36 us
    all_to_all x1, waiting for transfers between devices, shards(): arrived = exchange(picked)  6.2 us
    all_to_all x1, waiting for transfers between devices, shards(): spread = exchange(spread_rows)  3.95 us
  transfers between devices with their start and end apart: 9, of which 6 were waited for; matrix products, arithmetic and copies ran while one was open for 7% of the time, Pallas kernels for 0%

profile of v3, /device:TPU:0, one launch (start us, length us, event | category | flops | bytes accessed | tf_op | source)
XLA Modules:
  0.0 101.5 jit_solution(1725745299162800164)
XLA Ops:
  0.0 1.9 %shard_map.154 = bf16[16,8,576]{2,1,0:T(8,128)(2,1)} custom-call(bf16[2,576,128]{2,1,0:T(8,128)(2,1)} %bitcast.63), custom_call_target="tpu_custom_call" | custom-call | tf_op jit(solution)/shard_map/pallas_call | solution.py:272
  1.9 7.4 %all-to-all-start = ((bf16[16,8,576]{2,1,0:T(8,128)(2,1)}), bf16[16,8,576]{2,1,0:T(8,128)(2,1)S(1)}, u32[]{:S(2)}, u32[]{:S(2)}) async-start(bf16[16,8,576]{2,1,0:T(8,128)(2,1)} %shard_map.154), calls=%async_computation | async-start | bytes 327680 | tf_op jit(solution)/shard_map/all_to_all | solution.py:280
  9.9 1.6 %fusion.27 = (f32[128]{0:T(128)S(1)}, f32[128,2048]{1,0:T(8,128)S(1)}) fusion(bf16[1,2048,576]{1,2,0:T(8,128)(2,1)S(1)} %copy-done, bf16[1,2,128,576]{2,3,1,0:T(8,128)(2,1)} %param.21, pred[2048]{0:T(1024)(128)(4,1)S(1)} %iota_compare_fusion), kind=kOutput, calls=%fused_computation.74 | convolution fusion | flops 302776192 | bytes 3557888 | tf_op jit(solution)/shard_map/dot_general | solution.py:27
  11.5 0.1 fusion.28
  11.7 0.3 fusion.5
  12.0 0.0 copy-start.1
  12.0 0.0 copy-start.3
  12.0 0.0 copy-start.9
  12.0 1.7 %fusion.1 = f32[128,576]{1,0:T(8,128)} fusion(bf16[1,2048,576]{1,2,0:T(8,128)(2,1)S(1)} %copy-done, f32[128,2048]{1,0:T(8,128)S(1)} %get-tuple-element.14, f32[128]{0:T(128)S(1)} %get-tuple-element.12, f32[128]{0:T(128)S(1)} %get-tuple-element.15), kind=kOutput, calls=%fused_computation.2 | convolution fusion | flops 302776320 | bytes 3703808 | tf_op jit(solution)/shard_map/dot_general | solution.py:44
  13.8 3.9 %all-to-all-done.spread_ref = bf16[16,8,576]{2,1,0:T(8,128)(2,1)S(1)} async-done(((bf16[16,8,576]{2,1,0:T(8,128)(2,1)}), bf16[16,8,576]{2,1,0:T(8,128)(2,1)S(1)}, u32[]{:S(2)}, u32[]{:S(2)}) %all-to-all-start) | async-done | bytes 147488 | tf_op jit(solution)/shard_map/all_to_all | solution.py:280
  17.7 1.2 %shard_map.155 = bf16[16,8,576]{2,1,0:T(8,128)(2,1)} custom-call(s32[16]{0:T(128)S(1)} %copy-done.1, bf16[16,8,576]{2,1,0:T(8,128)(2,1)S(1)} %all-to-all-done.spread_ref), custom_call_target="tpu_custom_call" | custom-call | tf_op jit(solution)/shard_map/pallas_call | solution.py:224
  18.9 3.5 %all-to-all-start.1 = ((bf16[16,8,576]{2,1,0:T(8,128)(2,1)}), bf16[16,8,576]{2,1,0:T(8,128)(2,1)S(1)}, u32[]{:S(2)}, u32[]{:S(2)}) async-start(bf16[16,8,576]{2,1,0:T(8,128)(2,1)} %shard_map.155), calls=%async_computation.1 | async-start | bytes 327680 | tf_op jit(solution)/shard_map/all_to_all | solution.py:282
  22.5 0.2 copy.22
  22.7 0.2 copy.19
  22.9 0.6 dynamic_slice.3.length_ref
  23.5 0.1 shard_map.156.stats_ref
  23.6 1.0 %fusion.8.resident_ref = bf16[128,512]{1,0:T(8,128)(2,1)S(1)} fusion(f32[128,576]{1,0:T(8,128)} %fusion.1, f32[512]{0:T(512)S(1)} %slice.25, f32[128]{0:T(128)S(1)} %get-tuple-element.11), kind=kLoop, calls=%fused_computation.15 | loop fusion | flops 196608 | bytes 395776 | tf_op jit(solution)/shard_map/convert.3
  24.7 6.2 %all-to-all-done.1.query_ref = bf16[16,8,576]{2,1,0:T(8,128)(2,1)S(1)} async-done(((bf16[16,8,576]{2,1,0:T(8,128)(2,1)}), bf16[16,8,576]{2,1,0:T(8,128)(2,1)S(1)}, u32[]{:S(2)}, u32[]{:S(2)}) %all-to-all-start.1) | async-done | bytes 147488 | tf_op jit(solution)/shard_map/all_to_all | solution.py:282
  30.9 1.9 %shard_map.157 = bf16[16,16,640]{2,1,0:T(8,128)(2,1)} custom-call(s32[1]{0:T(128)} %dynamic_slice.3.length_ref, bf16[16,8,576]{2,1,0:T(8,128)(2,1)S(1)} %all-to-all-done.1.query_ref, bf16[256,576]{1,0:T(8,128)(2,1)S(1)} %bitcast.60, bf16[128,512]{1,0:T(8,128)(2,1)S(1)} %fusion.8.resident_ref, f32[128,128]{1,0:T(8,128)S(1)} %shard_map.156.stats_ref, ...), custom_call_target="tpu_custom_call" | custom-call | tf_op jit(solution)/shard_map/pallas_call | solution.py:224
  32.8 3.5 %all-to-all-start.2 = ((bf16[16,16,640]{2,1,0:T(8,128)(2,1)}), bf16[16,16,640]{2,1,0:T(8,128)(2,1)S(1)}, u32[]{:S(2)}, u32[]{:S(2)}) async-start(bf16[16,16,640]{2,1,0:T(8,128)(2,1)} %shard_map.157), calls=%async_computation.2 | async-start | bytes 655360 | tf_op jit(solution)/shard_map/all_to_all | solution.py:298
  36.4 0.1 copy.21.row_ref
  36.5 0.1 broadcast_in_dim.18
  36.6 0.1 stack_reshape.3
  36.7 10.7 %all-to-all-done.2.rows_ref = bf16[16,16,640]{2,1,0:T(8,128)(2,1)S(1)} async-done(((bf16[16,16,640]{2,1,0:T(8,128)(2,1)}), bf16[16,16,640]{2,1,0:T(8,128)(2,1)S(1)}, u32[]{:S(2)}, u32[]{:S(2)}) %all-to-all-start.2) | async-done | bytes 327712 | tf_op jit(solution)/shard_map/all_to_all | solution.py:298
  47.4 7.0 %shard_map.158 = (f32[16,7168]{1,0:T(8,128)S(1)}, bf16[16,7168]{1,0:T(8,128)(2,1)S(1)}) custom-call(s32[256,3]{1,0:T(8,128)S(1)} %copy.21.row_ref, s32[3,256]{1,0:T(4,128)S(1)} %pad_add_fusion.1.column_ref, bf16[16,16,640]{2,1,0:T(8,128)(2,1)S(1)} %all-to-all-done.2.rows_ref, bf16[8,512,128]{2,1,0:T(8,128)(2,1)} %upward_hbm.1, bf16[1024,7168]{1,0:T(8,128)(2,1)} %bitcast.62), custom_call_target="tpu_custom_call" | custom-call | tf_op jit(solution)/shard_map/pallas_call | solution.py:224
  54.3 0.1 collective-permute-start
  54.4 1.5 %collective-permute-done.other_ref = bf16[16,7168]{1,0:T(8,128)(2,1)S(1)} collective-permute-done((bf16[16,7168]{1,0:T(8,128)(2,1)S(1)}, bf16[16,7168]{1,0:T(8,128)(2,1)S(1)}, u32[]{:S(2)}, u32[]{:S(2)}) %collective-permute-start) | collective-permute-done | bytes 229408 | tf_op jit(solution)/shard_map/ppermute | solution.py:322
  55.9 0.9 shard_map.159
  56.8 3.4 %all-to-all-start.3 = ((bf16[8,2,7168]{2,1,0:T(2,128)(2,1)}), bf16[8,2,7168]{2,1,0:T(2,128)(2,1)S(1)}, u32[]{:S(2)}, u32[]{:S(2)}) async-start(bf16[8,2,7168]{2,1,0:T(2,128)(2,1)} %shard_map.159), calls=%async_computation.3 | async-start | bytes 458752 | tf_op jit(solution)/shard_map/all_to_all | solution.py:324
  60.3 0.2 collective-permute-start.1
  60.5 0.4 collective-permute-start.2
  60.8 0.1 collective-permute-start.3
  61.0 8.2 %all-to-all-done.3 = bf16[8,2,7168]{2,1,0:T(2,128)(2,1)S(1)} async-done(((bf16[8,2,7168]{2,1,0:T(2,128)(2,1)}), bf16[8,2,7168]{2,1,0:T(2,128)(2,1)S(1)}, u32[]{:S(2)}, u32[]{:S(2)}) %all-to-all-start.3) | async-done | bytes 229408 | tf_op jit(solution)/shard_map/all_to_all | solution.py:324
  69.2 0.2 convert_reduce_fusion
  69.4 0.2 fusion.15
  69.6 0.1 fusion.17
  69.7 0.1 broadcast_in_dim.22
  69.8 11.6 %all_to_all.30 = bf16[8,2,7168]{2,1,0:T(2,128)(2,1)S(1)} all-to-all(bf16[8,2,7168]{2,1,0:T(2,128)(2,1)S(1)} %broadcast_in_dim.22), channel_id=1, replica_groups={{0,2,4,6,8,10,12,14},{1,3,5,7,9,11,13,15},{16,18,20,22,24,26,28,30},{17..., dimensions={0} | all-to-all | bytes 458752 | tf_op jit(solution)/shard_map/all_to_all | solution.py:329
  81.5 0.1 reshape.342.rows_ref
  81.5 0.0 copy-start.7
  81.6 0.0 copy-start.8
  81.6 0.0 collective-permute-done.2.refs_3_
  81.6 7.4 %shard_map.160 = bf16[8,2,7168]{2,1,0:T(2,128)(2,1)} custom-call(bf16[16,7168]{1,0:T(8,128)(2,1)S(1)} %reshape.342.rows_ref, bf16[128,7168]{1,0:T(8,128)(2,1)} %refs_0_.1, bf16[128,7168]{1,0:T(8,128)(2,1)} %collective-permute-done.1.refs_1_, bf16[128,7168]{1,0:T(8,128)(2,1)} %refs_2_.1, bf16[128,7168]{1,0:T(8,128)(2,1)} %collective-permute-done.2.refs_3_, ...), custom_call_target="tpu_custom_call" | custom-call | tf_op jit(solution)/shard_map/pallas_call | solution.py:224
  89.0 3.4 %all-to-all-start.5 = ((bf16[8,2,7168]{2,1,0:T(2,128)(2,1)}), bf16[8,2,7168]{2,1,0:T(2,128)(2,1)S(1)}, u32[]{:S(2)}, u32[]{:S(2)}) async-start(bf16[8,2,7168]{2,1,0:T(2,128)(2,1)} %shard_map.160), calls=%async_computation.5 | async-start | bytes 458752 | tf_op jit(solution)/shard_map/all_to_all | solution.py:341
  92.5 0.1 compare_select_fusion.4
  92.6 8.0 %all-to-all-done.5 = bf16[8,2,7168]{2,1,0:T(2,128)(2,1)S(1)} async-done(((bf16[8,2,7168]{2,1,0:T(2,128)(2,1)}), bf16[8,2,7168]{2,1,0:T(2,128)(2,1)S(1)}, u32[]{:S(2)}, u32[]{:S(2)}) %all-to-all-start.5) | async-done | bytes 229408 | tf_op jit(solution)/shard_map/all_to_all | solution.py:341
  100.6 0.3 multiply_reduce_fusion
  100.9 0.7 fusion.16
  (32 shorter events, 0.2 us)
Async XLA Ops:
  0.0 9.9 %copy-start = (bf16[1,2048,576]{1,2,0:T(8,128)(2,1)S(1)}, bf16[1,2048,576]{1,2,0:T(8,128)(2,1)}, u32[]{:S(2)}) copy-start(bf16[1,2048,576]{1,2,0:T(8,128)(2,1)} %param.19) | copy-start | bytes 7077892
  0.0 11.5 %copy-start.2 = (bf16[1,2,128,576]{2,3,1,0:T(8,128)(2,1)S(1)}, bf16[1,2,128,576]{2,3,1,0:T(8,128)(2,1)}, u32[]{:S(2)}) copy-start(bf16[1,2,128,576]{2,3,1,0:T(8,128)(2,1)} %param.21) | copy-start | bytes 884740
  0.0 11.5 %copy-start.5 = (bf16[1,2,576]{2,1,0:T(2,128)(2,1)S(1)}, bf16[1,2,576]{2,1,0:T(2,128)(2,1)}, u32[]{:S(2)}) copy-start(bf16[1,2,576]{2,1,0:T(2,128)(2,1)} %param.22) | copy-start | bytes 6916
  1.9 15.8 %all-to-all-start = ((bf16[16,8,576]{2,1,0:T(8,128)(2,1)}), bf16[16,8,576]{2,1,0:T(8,128)(2,1)S(1)}, u32[]{:S(2)}, u32[]{:S(2)}) async-start(bf16[16,8,576]{2,1,0:T(8,128)(2,1)} %shard_map.154), calls=%async_computation | async-start | bytes 327680 | tf_op jit(solution)/shard_map/all_to_all | solution.py:280
  12.0 5.7 %copy-start.1 = (s32[16]{0:T(128)S(1)}, s32[16]{0:T(128)}, u32[]{:S(2)}) copy-start(s32[16]{0:T(128)} %dest_ref.1) | copy-start | bytes 196
  12.0 10.7 %copy-start.3 = (bf16[1,256,576]{1,2,0:T(8,128)(2,1)S(1)}, bf16[1,256,576]{1,2,0:T(8,128)(2,1)}, u32[]{:S(2)}) copy-start(bf16[1,256,576]{1,2,0:T(8,128)(2,1)} %param.16) | copy-start | bytes 884740
  12.0 10.9 %copy-start.9 = (s32[16]{0:T(128)S(1)}, s32[16]{0:T(128)}, u32[]{:S(2)}) copy-start(s32[16]{0:T(128)} %param.18) | copy-start | bytes 196
  18.9 11.9 %all-to-all-start.1 = ((bf16[16,8,576]{2,1,0:T(8,128)(2,1)}), bf16[16,8,576]{2,1,0:T(8,128)(2,1)S(1)}, u32[]{:S(2)}, u32[]{:S(2)}) async-start(bf16[16,8,576]{2,1,0:T(8,128)(2,1)} %shard_map.155), calls=%async_computation.1 | async-start | bytes 327680 | tf_op jit(solution)/shard_map/all_to_all | solution.py:282
  32.8 14.6 %all-to-all-start.2 = ((bf16[16,16,640]{2,1,0:T(8,128)(2,1)}), bf16[16,16,640]{2,1,0:T(8,128)(2,1)S(1)}, u32[]{:S(2)}, u32[]{:S(2)}) async-start(bf16[16,16,640]{2,1,0:T(8,128)(2,1)} %shard_map.157), calls=%async_computation.2 | async-start | bytes 655360 | tf_op jit(solution)/shard_map/all_to_all | solution.py:298
  47.4 13.6 %copy-start.6 = (bf16[7168]{0:T(1024)(128)(2,1)S(1)}, bf16[7168]{0:T(1024)(128)(2,1)}, u32[]{:S(2)}) copy-start(bf16[7168]{0:T(1024)(128)(2,1)} %param.26) | copy-start | bytes 43012
  47.4 22.0 %copy-start.4 = (bf16[1,2,7168]{2,1,0:T(2,128)(2,1)S(1)}, bf16[1,2,7168]{2,1,0:T(2,128)(2,1)}, u32[]{:S(2)}) copy-start(bf16[1,2,7168]{2,1,0:T(2,128)(2,1)} %param.23) | copy-start | bytes 86020
  54.3 1.6 %collective-permute-start = (bf16[16,7168]{1,0:T(8,128)(2,1)S(1)}, bf16[16,7168]{1,0:T(8,128)(2,1)S(1)}, u32[]{:S(2)}, u32[]{:S(2)}) collective-permute-start(bf16[16,7168]{1,0:T(8,128)(2,1)S(1)} %get-tuple-element.8), channel_id=1, source_target_pairs={{0,1},{1,0},{2,3},{3,2},{4,5},{5,4},{6,7},{7,6},{8,9},{9,8},{10,11... | collective-permute-start | bytes 688136 | tf_op jit(solution)/shard_map/ppermute | solution.py:322
  56.8 12.4 %all-to-all-start.3 = ((bf16[8,2,7168]{2,1,0:T(2,128)(2,1)}), bf16[8,2,7168]{2,1,0:T(2,128)(2,1)S(1)}, u32[]{:S(2)}, u32[]{:S(2)}) async-start(bf16[8,2,7168]{2,1,0:T(2,128)(2,1)} %shard_map.159), calls=%async_computation.3 | async-start | bytes 458752 | tf_op jit(solution)/shard_map/all_to_all | solution.py:324
  60.3 21.3 %collective-permute-start.1 = (bf16[128,7168]{1,0:T(8,128)(2,1)}, bf16[128,7168]{1,0:T(8,128)(2,1)}, u32[]{:S(2)}, u32[]{:S(2)}) collective-permute-start(bf16[128,7168]{1,0:T(8,128)(2,1)} %refs_0_.1), channel_id=1, source_target_pairs={{0,1},{1,0},{2,3},{3,2},{4,5},{5,4},{6,7},{7,6},{8,9},{9,8},{10,11... | collective-permute-start | bytes 5505032 | tf_op jit(solution)/shard_map/ppermute | solution.py:332
  60.5 21.1 %collective-permute-start.2 = (bf16[128,7168]{1,0:T(8,128)(2,1)}, bf16[128,7168]{1,0:T(8,128)(2,1)}, u32[]{:S(2)}, u32[]{:S(2)}) collective-permute-start(bf16[128,7168]{1,0:T(8,128)(2,1)} %refs_2_.1), channel_id=1, source_target_pairs={{0,1},{1,0},{2,3},{3,2},{4,5},{5,4},{6,7},{7,6},{8,9},{9,8},{10,11... | collective-permute-start | bytes 5505032 | tf_op jit(solution)/shard_map/ppermute | solution.py:332
  60.8 20.8 %collective-permute-start.3 = (bf16[128,7168]{1,0:T(8,128)(2,1)}, bf16[128,7168]{1,0:T(8,128)(2,1)}, u32[]{:S(2)}, u32[]{:S(2)}) collective-permute-start(bf16[128,7168]{1,0:T(8,128)(2,1)} %refs_4_.1), channel_id=1, source_target_pairs={{0,1},{1,0},{2,3},{3,2},{4,5},{5,4},{6,7},{7,6},{8,9},{9,8},{10,11... | collective-permute-start | bytes 5505032 | tf_op jit(solution)/shard_map/ppermute | solution.py:332
  81.5 10.9 %copy-start.7 = (f32[1,2,1]{1,2,0:T(1,128)S(1)}, f32[1,2,1]{1,2,0:T(1,128)}, u32[]{:S(2)}) copy-start(f32[1,2,1]{1,2,0:T(1,128)} %param.28) | copy-start | bytes 28
  81.6 10.9 %copy-start.8 = (s32[1,2,1]{1,2,0:T(1,128)S(1)}, s32[1,2,1]{1,2,0:T(1,128)}, u32[]{:S(2)}) copy-start(s32[1,2,1]{1,2,0:T(1,128)} %param.27) | copy-start | bytes 28
  89.0 11.5 %all-to-all-start.5 = ((bf16[8,2,7168]{2,1,0:T(2,128)(2,1)}), bf16[8,2,7168]{2,1,0:T(2,128)(2,1)S(1)}, u32[]{:S(2)}, u32[]{:S(2)}) async-start(bf16[8,2,7168]{2,1,0:T(2,128)(2,1)} %shard_map.160), calls=%async_computation.5 | async-start | bytes 458752 | tf_op jit(solution)/shard_map/all_to_all | solution.py:341

commit v4 on v3

--- a/solution.py
+++ b/solution.py
@@ -12,6 +12,8 @@
 UNITS = 128
 LANES = 128
 BLOCK = 1024
+PLANE = 4
+FRESH_ROWS = 16
 
 softmax_scale = 192.0 ** (-0.5)
 norm_epsilon = 1e-06
@@ -44,7 +46,7 @@
     mixed = jnp.dot(cache_probs, key_rows, preferred_element_type=f32) + jnp.dot(
         fresh_probs, fresh_rows, preferred_element_type=f32
     )
-    return mixed[:, :KVR].astype(bf16)
+    return mixed[:, :KVR]
 
 
 def three_parts(value):
@@ -55,54 +57,72 @@
 
 
 def spread_kernel(query_ref, spread_ref):
-    peers, per_peer, width = spread_ref.shape
-    rows = query_ref[0].astype(f32).T.reshape(peers, per_peer, width)
-    spread_ref[...] = rows.astype(bf16)
-
-
-def pick_kernel(dest_ref, spread_ref, picked_ref):
-    for prompt in range(spread_ref.shape[0]):
-        picked_ref[prompt] = spread_ref[dest_ref[prompt]]
-
-
-def fresh_kernel(query_ref, fresh_ref, stats_ref):
-    score = softmax_scale * jnp.sum(
-        query_ref[...].astype(f32) * fresh_ref[...].astype(f32), axis=1, keepdims=True
-    )
-    lane = lax.broadcasted_iota(jnp.int32, stats_ref.shape, 1)
-    stats = jnp.zeros(stats_ref.shape, f32)
-    for at, column in enumerate(three_parts(score)):
-        stats = jnp.where(lane == 3 + at, column, stats)
-    stats_ref[...] = stats
-
-
-def prompt_kernel(
-    length_ref, query_ref, key_ref, resident_ref, stats_ref, fresh_rows_ref, out_ref
-):
-    peers, rows, width = out_ref.shape
-    per_peer = rows // 2
-    heads = peers * per_peer
-    query = query_ref[...].reshape(heads, query_ref.shape[2])
-    keys = key_ref[...]
-    scores = lax.dot_general(query, keys, contract_last, preferred_element_type=f32)
-    position = lax.broadcasted_iota(jnp.int32, scores.shape, 1)
-    scores = jnp.where(position < length_ref[0], scores * softmax_scale, -jnp.inf)
+    peers, rows, width = spread_ref.shape
+    planes = peers // PLANE
+    by_peer = query_ref[0].astype(f32).T.reshape(planes, PLANE, rows // planes, width)
+    for column in range(PLANE):
+        block = by_peer[:, column].reshape(rows, width).astype(bf16)
+        for plane in range(planes):
+            spread_ref[plane * PLANE + column] = block
+
+
+def column_kernel(device_ref, resident_ref, fresh_ref, *message_refs):
+    planes, _, per_peer, latent = resident_ref.shape
+    rows = planes * per_peer
+    column = device_ref[0] % PLANE
+    for at, message_ref in enumerate(message_refs):
+        message_ref[:rows, :latent] = resident_ref[:, column ^ at].reshape(rows, latent).astype(bf16)
+        message_ref[rows:] = jnp.broadcast_to(fresh_ref[...], message_ref[rows:].shape)
+
+
+def prompt_kernel(device_ref, dest_ref, length_ref, query_ref, *refs):
+    key_refs, message_refs = refs[:PLANE], refs[PLANE : 2 * PLANE]
+    out_refs, stage_ref = refs[2 * PLANE : -1], refs[-1]
+    planes, _, rows, width = stage_ref.shape
+    per_peer, chunk = rows // 2, width - KVR
+    heads = planes * per_peer
+    device = device_ref[0]
+    scores = []
+    for at in range(PLANE):
+        prompt = device ^ at
+        query = query_ref[dest_ref[prompt]]
+        score = jnp.dot(query, key_refs[at][...], preferred_element_type=f32) * softmax_scale
+        position = lax.broadcasted_iota(jnp.int32, score.shape, 1)
+        scores.append(jnp.where(position < length_ref[prompt], score, -jnp.inf))
+    scores = jnp.concatenate(scores, axis=0)
     peak = jnp.max(scores, axis=1, keepdims=True)
     terms = jnp.exp(scores - peak)
     total = jnp.sum(terms, axis=1, keepdims=True)
-    mixed = jnp.dot(terms.astype(bf16), keys[:, :KVR], preferred_element_type=f32) / total
-    lane = lax.broadcasted_iota(jnp.int32, (heads, width - KVR), 1)
-    stats = stats_ref[...]
-    for at, column in enumerate(three_parts(peak + jnp.log(total))):
-        stats = jnp.where(lane == at, column, stats)
-    fold = lambda value: value.reshape(peers, per_peer, value.shape[1])
-    out_ref[:, :, :KVR] = jnp.concatenate(
-        [fold(mixed), fold(resident_ref[...].astype(f32))], axis=1
-    ).astype(bf16)
-    fresh_rows = jnp.broadcast_to(
-        fresh_rows_ref[...].astype(f32)[None], (peers, per_peer, width - KVR)
-    )
-    out_ref[:, :, KVR:] = jnp.concatenate([fold(stats), fresh_rows], axis=1).astype(bf16)
+    log_sum = peak + jnp.log(total)
+    scale = 1.0 / total
+    terms = terms.astype(bf16)
+    lane = lax.broadcasted_iota(jnp.int32, (heads, chunk), 1)
+    fold = lambda value: value.reshape(planes, per_peer, value.shape[1])
+    for at in range(PLANE):
+        part = slice(at * heads, (at + 1) * heads)
+        mixed = lax.dot_general(
+            terms[part], key_refs[at][:KVR], contract_last, preferred_element_type=f32
+        )
+        resident = message_refs[at][:heads, :KVR].astype(f32)
+        stage_ref[:, at, :, :KVR] = jnp.concatenate(
+            [fold(mixed * scale[part]), fold(resident)], axis=1
+        ).astype(bf16)
+        fresh = message_refs[at][heads : heads + FRESH_ROWS].astype(f32)[:1]
+        fresh_score = softmax_scale * jnp.sum(
+            query_ref[device ^ at].astype(f32) * fresh, axis=1, keepdims=True
+        )
+        stats = jnp.zeros((heads, chunk), f32)
+        for lane_at, value in enumerate(three_parts(log_sum[part]) + three_parts(fresh_score)):
+            stats = jnp.where(lane == lane_at, value, stats)
+        fresh_rows = [fresh[:, start : start + chunk] for start in range(0, KVR, chunk)]
+        if len(fresh_rows) < per_peer:
+            fresh_rows.append(jnp.zeros((per_peer - len(fresh_rows), chunk), f32))
+        fresh_rows = jnp.concatenate(fresh_rows, axis=0)[None]
+        stage_ref[:, at, :, KVR:] = jnp.concatenate(
+            [fold(stats), jnp.broadcast_to(fresh_rows, (planes, per_peer, chunk))], axis=1
+        ).astype(bf16)
+    for at, out_ref in enumerate(out_refs):
+        out_ref[...] = stage_ref[(device // PLANE) ^ at]
 
 
 def pair_kernel(keep_ref, other_ref, pair_ref):
@@ -110,18 +130,9 @@
     pair_ref[...] = total.reshape(pair_ref.shape).astype(bf16)
 
 
-def heads_kernel(
-    row_ref,
-    column_ref,
-    rows_ref,
-    upward_hbm,
-    proj_hbm,
-    keep_ref,
-    send_ref,
-    upward_ref,
-    proj_ref,
-    arrived,
-):
+def heads_kernel(row_ref, column_ref, peer_ref, *refs):
+    payload_refs, rows_ref, arrived = refs[:-8], refs[-2], refs[-1]
+    upward_hbm, proj_hbm, keep_ref, send_ref, upward_ref, proj_ref = refs[-8:-2]
     upward_copy = pltpu.make_async_copy(upward_hbm, upward_ref, arrived.at[0])
     upward_copy.start()
     blocks = range(0, proj_ref.shape[1], BLOCK)
@@ -135,6 +146,8 @@
     ]
     for copy in proj_copies:
         copy.start()
+    for at, payload_ref in enumerate(payload_refs):
+        rows_ref[at * PLANE : (at + 1) * PLANE] = payload_ref[...]
     peers, rows, width = rows_ref.shape
     per_peer = rows // 2
     columns = peers * rows
@@ -156,8 +169,7 @@
     scale = 1.0 / (jnp.sum(terms, axis=1, keepdims=True) + fresh_term)
     resident = jnp.where(own & (col_row == row_head + per_peer), 1.0, 0.0)
     mixing = jnp.where(new_row, terms * scale, resident)
-    peer = lax.broadcasted_iota(jnp.int32, (row_ref.shape[0], peers), 1)
-    fresh_mixing = jnp.where((peer == row_device) & new_row, fresh_term * scale, 0.0)
+    fresh_mixing = jnp.where((peer_ref[...] == row_device) & new_row, fresh_term * scale, 0.0)
     chunk = width - KVR
     fresh_rows = jnp.concatenate(
         [rows_ref[:, per_peer + at, KVR:] for at in range(KVR // chunk)], axis=1
@@ -268,53 +280,75 @@
     )
     exchange_core = functools.partial(exchange, axis_index_groups=same_core)
 
+    planes = devices // PLANE
+    toward = lambda value, bits: (
+        lax.ppermute(value, "ep", [(i, i ^ bits) for i in range(devices)]) if bits else value
+    )
+    own_device = device.astype(jnp.int32)[None]
+
     flipped = jnp.swapaxes(queries[0], 1, 2)
+    spread_shape = (devices, planes * per_peer, width)
     spread_rows = pl.pallas_call(
         spread_kernel,
-        out_shape=pltpu.VMEM((devices, per_peer, width), bf16),
+        out_shape=pltpu.VMEM(spread_shape, bf16),
         grid=(1,),
         in_specs=[pl.BlockSpec((1, width, heads), lambda step: (1, 0, 0))],
-        out_specs=pl.BlockSpec((devices, per_peer, width), lambda step: (0, 0, 0)),
-        compiler_params=pltpu.CompilerParams(vmem_limit_bytes=16 << 20),
+        out_specs=pl.BlockSpec(spread_shape, lambda step: (0, 0, 0)),
+        compiler_params=pltpu.CompilerParams(vmem_limit_bytes=32 << 20),
     )(pltpu.with_memory_space_constraint(flipped, pltpu.HBM))
     spread = exchange(spread_rows)
-    (picked,) = call(pick_kernel, [(spread.shape, bf16)], [handoff_dest, spread])
-    arrived = exchange(picked)
-
+
+    flipped_keys = jnp.swapaxes(handoff_rows[0], 0, 1)
+    plane_keys = [toward(flipped_keys, at) for at in range(PLANE)]
     cache_keys = resident_cache[0]
     cache_live = jnp.arange(cache_keys.shape[0], dtype=jnp.int32) < resident_len[0]
     resident_out = attend(queries[0, 0], cache_keys, cache_live, new_latent[:, 0])
+    messages = call(
+        column_kernel,
+        [((planes * per_peer + FRESH_ROWS, width), bf16)] * PLANE,
+        [
+            own_device,
+            resident_out.reshape(planes, PLANE, per_peer, KVR),
+            new_latent[0, 1:2],
+        ],
+    )
+    messages = [toward(message, at) for at, message in enumerate(messages)]
 
     chunk = max(LANES, KVR // per_peer)
-    fresh_rows = new_latent[0, 1, :KVR].reshape(KVR // chunk, chunk)
-    fresh_rows = jnp.pad(fresh_rows, ((0, per_peer - KVR // chunk), (0, 0)))
-    own_len = lax.dynamic_slice(handoff_len, (device,), (1,))
-    (stats,) = call(fresh_kernel, [((heads, chunk), f32)], [queries[0, 1], new_latent[0, 1:2]])
-    (payload,) = call(
+    payloads = call(
         prompt_kernel,
-        [((devices, 2 * per_peer, KVR + chunk), bf16)],
-        [own_len, arrived, handoff_rows[0], resident_out, stats, fresh_rows],
-    )
-    by_head = exchange(payload)
+        [((PLANE, 2 * per_peer, KVR + chunk), bf16)] * planes,
+        [own_device, handoff_dest, handoff_len, spread, *plane_keys, *messages],
+        scratch=[pltpu.VMEM((planes, PLANE, 2 * per_peer, KVR + chunk), bf16)],
+    )
+    payloads = [toward(payload, at * PLANE) for at, payload in enumerate(payloads)]
 
     row = jnp.arange(per_peer * 2 * devices, dtype=jnp.int32)
     row_core = (row // devices % 2) ^ core
     row_device = row // 2 % chips * 2 + row_core
     row_table = jnp.stack([row // (2 * devices), row_device, row % 2], axis=1)
+    peers = device.astype(jnp.int32) ^ jnp.arange(devices, dtype=jnp.int32)
+    is_peer = peers[:, None] == jnp.arange(devices, dtype=jnp.int32)[None, :]
+    peer_dest = jnp.sum(jnp.where(is_peer, handoff_dest[None, :], 0), axis=1)
     column = jnp.arange(devices * 2 * per_peer, dtype=jnp.int32)
-    col_peer = column // (2 * per_peer)
     column_table = jnp.stack(
-        [col_peer, column % (2 * per_peer), jnp.repeat(handoff_dest, 2 * per_peer)], axis=0
+        [
+            jnp.repeat(peers, 2 * per_peer),
+            column % (2 * per_peer),
+            jnp.repeat(peer_dest, 2 * per_peer),
+        ],
+        axis=0,
     )
     projection = out_proj.reshape(-1, model)
     keep, send = call(
         heads_kernel,
         [((devices, model), f32), ((devices, model), bf16)],
-        [row_table, column_table, by_head],
+        [row_table, column_table, peers[None], *payloads],
         [value_upward, projection],
         [
             pltpu.VMEM(value_upward.shape, bf16),
             pltpu.VMEM(projection.shape, bf16),
+            pltpu.VMEM((devices, 2 * per_peer, KVR + chunk), bf16),
             pltpu.SemaphoreType.DMA((1 + model // BLOCK,)),
         ],
     )

time: 102 us -> 96.3 us (0.944)
  waiting for transfers between devices: 38.5 us -> 31.4 us
  starting transfers between devices: 22 us -> 24.3 us
  local copies, waits for them, and re-layouts: 1.57 us -> 3.01 us
  Pallas kernels: 20.4 us -> 19 us
    all_to_all x2 -> x0, waiting for transfers between devices: 16.9 us -> none  [the longest x1 10.7 us: shards(): by_head = exchange(payload)]
    ppermute x0 -> x9, waiting for transfers between devices: none -> 11.4 us  [shards(): lax.ppermute(value, 'ep', [(i, i ^ bits) for i in range(devices)])]
    ppermute x0 -> x9, starting transfers between devices: none -> 9.92 us  [shards(): lax.ppermute(value, 'ep', [(i, i ^ bits) for i in range(devices)])]
    all_to_all x2 -> x0, starting transfers between devices: 7.06 us -> none  [the longest x1 3.54 us: shards(): by_head = exchange(payload)]
    unnamed x22 -> x26, local copies, waits for them, and re-layouts: 0.42 us -> 2.34 us
    all_to_all x1, waiting for transfers between devices: 3.95 us -> 2.55 us  [shards(): spread = exchange(spread_rows)]
    all_to_all x1, starting transfers between devices: 7.36 us -> 6.28 us  [shards(): spread = exchange(spread_rows)]
    another operation x3 -> x2, other arithmetic: 1.06 us -> 0.02 us
  transfers between devices with their start and end apart: 9 -> 16, of which waited for: 6 -> 8; matrix products, arithmetic and copies ran while one was open for 7% -> 6% of each run, Pallas kernels for 0% -> 2%
where the time goes in v4:
time: 96.3 us; the launch traced here: 95.7 us
  waiting for transfers between devices  31.4 us (33%)
  starting transfers between devices  24.3 us (25%)
  Pallas kernels  19 us (20%)
  blocking collectives  11.3 us (12%)
  other arithmetic  3.13 us (3%)
  local copies, waits for them, and re-layouts  3.01 us (3%)
  matrix products  2.55 us (3%)
    pallas_call x5, Pallas kernels, call(): pl.pallas_call(kernel, out_shape=[pltpu.VMEM(shape, dtype) for shape, dty...  17.9 us
    ppermute x9, waiting for transfers between devices, shards(): lax.ppermute(value, 'ep', [(i, i ^ bits) for i in range(devices)])  11.4 us
    all_to_all x1, blocking collectives, shards(): own_rows = exchange_core(jnp.broadcast_to(normed[None], (chips, 2, model)))  11.3 us
    ppermute x9, starting transfers between devices, shards(): lax.ppermute(value, 'ep', [(i, i ^ bits) for i in range(devices)])  9.92 us
    all_to_all x1, waiting for transfers between devices, shards(): attention = jnp.sum(exchange_core(pair).astype(f32), axis=0)  8.14 us
    all_to_all x1, waiting for transfers between devices, shards(): returned = exchange_core(part)  7.9 us
    all_to_all x1, starting transfers between devices, shards(): spread = exchange(spread_rows)  6.28 us
    all_to_all x1, starting transfers between devices, shards(): attention = jnp.sum(exchange_core(pair).astype(f32), axis=0)  4.09 us
  transfers between devices with their start and end apart: 16, of which 8 were waited for; matrix products, arithmetic and copies ran while one was open for 6% of the time, Pallas kernels for 2%

profile of v4, /device:TPU:0, one launch (start us, length us, event | category | flops | bytes accessed | tf_op | source)
XLA Modules:
  0.0 95.7 jit_solution(14025003795944599418)
XLA Ops:
  0.0 0.5 collective-permute-start
  0.5 2.6 %collective-permute-start.1 = (bf16[576,256]{1,0:T(8,128)(2,1)}, bf16[576,256]{1,0:T(8,128)(2,1)}, u32[]{:S(2)}, u32[]{:S(2)}) collective-permute-start(bf16[576,256]{1,0:T(8,128)(2,1)} %bitcast.64), channel_id=1, source_target_pairs={{0,2},{1,3},{2,0},{3,1},{4,6},{5,7},{6,4},{7,5},{8,10},{9,11},{10,... | collective-permute-start | bytes 884744 | tf_op jit(solution)/shard_map/ppermute | solution.py:285
  3.1 1.0 %shard_map.154 = bf16[16,32,576]{2,1,0:T(8,128)(2,1)S(1)} custom-call(bf16[2,576,128]{2,1,0:T(8,128)(2,1)} %bitcast.68), custom_call_target="tpu_custom_call" | custom-call | tf_op jit(solution)/shard_map/pallas_call | solution.py:291
  4.2 0.8 copy-done.1
  5.0 6.3 %all-to-all-start = ((bf16[16,32,576]{2,1,0:T(8,128)(2,1)}), bf16[16,32,576]{2,1,0:T(8,128)(2,1)S(1)}, u32[]{:S(2)}, u32[]{:S(2)}) async-start(bf16[16,32,576]{2,1,0:T(8,128)(2,1)} %copy-done.1), calls=%async_computation | async-start | bytes 1310720 | tf_op jit(solution)/shard_map/all_to_all | solution.py:299
  12.0 0.7 fusion.26
  12.7 0.1 fusion.27
  12.8 0.3 fusion.5
  13.2 1.7 %fusion.1 = f32[128,576]{1,0:T(8,128)} fusion(bf16[1,2048,576]{1,2,0:T(8,128)(2,1)S(1)} %copy-done, f32[128,2048]{1,0:T(8,128)S(1)} %get-tuple-element.30, f32[128]{0:T(128)S(1)} %get-tuple-element.28, f32[128]{0:T(128)S(1)} %get-tuple-element.31), kind=kOutput, calls=%fused_computation.2 | convolution fusion | flops 302776320 | bytes 3703808 | tf_op jit(solution)/shard_map/dot_general | solution.py:46
  14.9 1.0 %slice_add_fusion = f32[128,512]{1,0:T(8,128)S(1)} fusion(f32[128,576]{1,0:T(8,128)} %fusion.1, f32[512]{0:T(512)S(1)} %slice.16, f32[128]{0:T(128)S(1)} %get-tuple-element.27), kind=kLoop, calls=%fused_computation.14 | loop fusion | flops 131072 | bytes 526848 | tf_op jit(solution)/shard_map/add | solution.py:46
  16.0 0.7 shard_map.155
  16.6 0.4 collective-permute-start.3
  17.0 1.7 %collective-permute-start.4 = (bf16[48,576]{1,0:T(8,128)(2,1)}, bf16[48,576]{1,0:T(8,128)(2,1)}, u32[]{:S(2)}, u32[]{:S(2)}) collective-permute-start(bf16[48,576]{1,0:T(8,128)(2,1)} %get-tuple-element.17), channel_id=1, source_target_pairs={{0,2},{1,3},{2,0},{3,1},{4,6},{5,7},{6,4},{7,5},{8,10},{9,11},{10,... | collective-permute-start | bytes 165896 | tf_op jit(solution)/shard_map/ppermute | solution.py:285
  18.8 0.2 select_reduce_fusion
  19.0 0.1 stack_reshape.7
  19.2 0.1 stack_reshape.6
  19.3 0.6 copy-done.3
  19.9 0.3 collective-permute-start.5
  20.2 0.1 copy.17.row_ref
  20.3 4.1 %collective-permute-done.4.refs_6_ = bf16[48,576]{1,0:T(8,128)(2,1)} collective-permute-done((bf16[48,576]{1,0:T(8,128)(2,1)}, bf16[48,576]{1,0:T(8,128)(2,1)}, u32[]{:S(2)}, u32[]{:S(2)}) %collective-permute-start.4) | collective-permute-done | bytes 55328 | tf_op jit(solution)/shard_map/ppermute | solution.py:285
  24.4 0.9 collective-permute-done.5.refs_7_
  25.3 2.6 %all-to-all-done.query_ref = bf16[16,32,576]{2,1,0:T(8,128)(2,1)S(1)} async-done(((bf16[16,32,576]{2,1,0:T(8,128)(2,1)}), bf16[16,32,576]{2,1,0:T(8,128)(2,1)S(1)}, u32[]{:S(2)}, u32[]{:S(2)}) %all-to-all-start) | async-done | bytes 589856 | tf_op jit(solution)/shard_map/all_to_all | solution.py:299
  27.9 0.8 copy-done.4
  28.7 1.9 %shard_map.156 = (bf16[4,16,640]{2,1,0:T(8,128)(2,1)S(1)}, bf16[4,16,640]{2,1,0:T(8,128)(2,1)S(1)}, bf16[4,16,640]{2,1,0:T(8,128)(2,1)S(1)}, bf16[4,16,640]{2,1,0:T(8,128)(2,1)S(1)}) custom-call(s32[1]{0:T(128)} %bitcast.device_ref, s32[16]{0:T(128)S(1)} %copy-done.5, s32[16]{0:T(128)S(1)} %copy-done.6, bf16[16,32,576]{2,1,0:T(8,128)(2,1)S(1)} %all-to-all-done.query_ref, ...), custom_call_target="tpu_custom_call" | custom-call | tf_op jit(solution)/shard_map/pallas_call | solution.py:236
  30.6 1.7 %collective-permute-start.6 = (bf16[4,16,640]{2,1,0:T(8,128)(2,1)S(1)}, bf16[4,16,640]{2,1,0:T(8,128)(2,1)S(1)}, u32[]{:S(2)}, u32[]{:S(2)}) collective-permute-start(bf16[4,16,640]{2,1,0:T(8,128)(2,1)S(1)} %get-tuple-element.20), channel_id=1, source_target_pairs={{0,4},{1,5},{2,6},{3,7},{4,0},{5,1},{6,2},{7,3},{8,12},{9,13},{10,... | collective-permute-start | bytes 245768 | tf_op jit(solution)/shard_map/ppermute | solution.py:285
  32.3 1.4 %collective-permute-start.7 = (bf16[4,16,640]{2,1,0:T(8,128)(2,1)S(1)}, bf16[4,16,640]{2,1,0:T(8,128)(2,1)S(1)}, u32[]{:S(2)}, u32[]{:S(2)}) collective-permute-start(bf16[4,16,640]{2,1,0:T(8,128)(2,1)S(1)} %get-tuple-element.21), channel_id=1, source_target_pairs={{0,8},{1,9},{2,10},{3,11},{4,12},{5,13},{6,14},{7,15},{8,0},{9,1},... | collective-permute-start | bytes 245768 | tf_op jit(solution)/shard_map/ppermute | solution.py:285
  33.7 1.4 %collective-permute-start.8 = (bf16[4,16,640]{2,1,0:T(8,128)(2,1)S(1)}, bf16[4,16,640]{2,1,0:T(8,128)(2,1)S(1)}, u32[]{:S(2)}, u32[]{:S(2)}) collective-permute-start(bf16[4,16,640]{2,1,0:T(8,128)(2,1)S(1)} %get-tuple-element.22), channel_id=1, source_target_pairs={{0,12},{1,13},{2,14},{3,15},{4,8},{5,9},{6,10},{7,11},{8,4},{9,5},... | collective-permute-start | bytes 245768 | tf_op jit(solution)/shard_map/ppermute | solution.py:285
  35.1 0.6 collective-permute-done.6.refs_1_
  35.6 5.8 %collective-permute-done.7.refs_2_ = bf16[4,16,640]{2,1,0:T(8,128)(2,1)S(1)} collective-permute-done((bf16[4,16,640]{2,1,0:T(8,128)(2,1)S(1)}, bf16[4,16,640]{2,1,0:T(8,128)(2,1)S(1)}, u32[]{:S(2)}, u32[]{:S(2)}) %collective-permute-start.7) | collective-permute-done | bytes 81952 | tf_op jit(solution)/shard_map/ppermute | solution.py:285
  41.4 7.0 %shard_map.157 = (f32[16,7168]{1,0:T(8,128)S(1)}, bf16[16,7168]{1,0:T(8,128)(2,1)S(1)}) custom-call(s32[256,3]{1,0:T(8,128)S(1)} %copy.17.row_ref, s32[3,256]{1,0:T(4,128)S(1)} %pad_add_fusion.1.column_ref, s32[1,16]{1,0:T(1,128)S(1)} %iota_xor_fusion.peer_ref, bf16[4,16,640]{2,1,0:T(8,128)(2,1)S(1)} %get-tuple-element.19.refs_0_, ...), custom_call_target="tpu_custom_call" | custom-call | tf_op jit(solution)/shard_map/pallas_call | solution.py:236
  48.5 1.5 %collective-permute-done.9.other_ref = bf16[16,7168]{1,0:T(8,128)(2,1)S(1)} collective-permute-done((bf16[16,7168]{1,0:T(8,128)(2,1)S(1)}, bf16[16,7168]{1,0:T(8,128)(2,1)S(1)}, u32[]{:S(2)}, u32[]{:S(2)}) %collective-permute-start.9) | collective-permute-done | bytes 229408 | tf_op jit(solution)/shard_map/ppermute | solution.py:356
  50.0 1.0 %shard_map.158 = bf16[8,2,7168]{2,1,0:T(2,128)(2,1)} custom-call(f32[16,7168]{1,0:T(8,128)S(1)} %get-tuple-element.23.keep_ref, bf16[16,7168]{1,0:T(8,128)(2,1)S(1)} %collective-permute-done.9.other_ref), custom_call_target="tpu_custom_call" | custom-call | tf_op jit(solution)/shard_map/pallas_call | solution.py:236
  50.9 4.1 %all-to-all-start.1 = ((bf16[8,2,7168]{2,1,0:T(2,128)(2,1)}), bf16[8,2,7168]{2,1,0:T(2,128)(2,1)S(1)}, u32[]{:S(2)}, u32[]{:S(2)}) async-start(bf16[8,2,7168]{2,1,0:T(2,128)(2,1)} %shard_map.158), calls=%async_computation.1 | async-start | bytes 458752 | tf_op jit(solution)/shard_map/all_to_all | solution.py:358
  55.0 0.5 collective-permute-start.11
  55.5 0.1 collective-permute-start.12
  55.6 8.1 %all-to-all-done.1 = bf16[8,2,7168]{2,1,0:T(2,128)(2,1)S(1)} async-done(((bf16[8,2,7168]{2,1,0:T(2,128)(2,1)}), bf16[8,2,7168]{2,1,0:T(2,128)(2,1)S(1)}, u32[]{:S(2)}, u32[]{:S(2)}) %all-to-all-start.1) | async-done | bytes 229408 | tf_op jit(solution)/shard_map/all_to_all | solution.py:358
  63.8 0.2 convert_reduce_fusion
  64.0 0.2 fusion.14
  64.1 0.1 fusion.16
  64.3 0.1 broadcast_in_dim.63
  64.4 11.3 %all_to_all.20 = bf16[8,2,7168]{2,1,0:T(2,128)(2,1)S(1)} all-to-all(bf16[8,2,7168]{2,1,0:T(2,128)(2,1)S(1)} %broadcast_in_dim.63), channel_id=1, replica_groups={{0,2,4,6,8,10,12,14},{1,3,5,7,9,11,13,15},{16,18,20,22,24,26,28,30},{17..., dimensions={0} | all-to-all | bytes 458752 | tf_op jit(solution)/shard_map/all_to_all | solution.py:363
  75.7 0.1 reshape.330.rows_ref
  75.8 7.4 %shard_map.159 = bf16[8,2,7168]{2,1,0:T(2,128)(2,1)} custom-call(bf16[16,7168]{1,0:T(8,128)(2,1)S(1)} %reshape.330.rows_ref, bf16[128,7168]{1,0:T(8,128)(2,1)} %refs_0_.1, bf16[128,7168]{1,0:T(8,128)(2,1)} %collective-permute-done.10.refs_1_, bf16[128,7168]{1,0:T(8,128)(2,1)} %refs_2_.1, bf16[128,7168]{1,0:T(8,128)(2,1)} %collective-permute-done.11.refs_3_, ...), custom_call_target="tpu_custom_call" | custom-call | tf_op jit(solution)/shard_map/pallas_call | solution.py:236
  83.3 3.4 %all-to-all-start.3 = ((bf16[8,2,7168]{2,1,0:T(2,128)(2,1)}), bf16[8,2,7168]{2,1,0:T(2,128)(2,1)S(1)}, u32[]{:S(2)}, u32[]{:S(2)}) async-start(bf16[8,2,7168]{2,1,0:T(2,128)(2,1)} %shard_map.159), calls=%async_computation.3 | async-start | bytes 458752 | tf_op jit(solution)/shard_map/all_to_all | solution.py:375
  86.7 0.1 compare_select_fusion.4
  86.8 7.9 %all-to-all-done.3 = bf16[8,2,7168]{2,1,0:T(2,128)(2,1)S(1)} async-done(((bf16[8,2,7168]{2,1,0:T(2,128)(2,1)}), bf16[8,2,7168]{2,1,0:T(2,128)(2,1)S(1)}, u32[]{:S(2)}, u32[]{:S(2)}) %all-to-all-start.3) | async-done | bytes 229408 | tf_op jit(solution)/shard_map/all_to_all | solution.py:375
  94.7 0.3 multiply_reduce_fusion
  95.0 0.7 fusion.15
  (50 shorter events, 0.5 us)
Async XLA Ops:
  0.0 11.9 %copy-start = (bf16[1,2048,576]{1,2,0:T(8,128)(2,1)S(1)}, bf16[1,2048,576]{1,2,0:T(8,128)(2,1)}, u32[]{:S(2)}) copy-start(bf16[1,2048,576]{1,2,0:T(8,128)(2,1)} %param.19) | copy-start | bytes 7077892
  0.0 11.9 %copy-start.7 = (bf16[1,2,128,576]{2,3,1,0:T(8,128)(2,1)S(1)}, bf16[1,2,128,576]{2,3,1,0:T(8,128)(2,1)}, u32[]{:S(2)}) copy-start(bf16[1,2,128,576]{2,3,1,0:T(8,128)(2,1)} %param.21) | copy-start | bytes 884740
  0.0 25.3 %collective-permute-start = (bf16[576,256]{1,0:T(8,128)(2,1)}, bf16[576,256]{1,0:T(8,128)(2,1)}, u32[]{:S(2)}, u32[]{:S(2)}) collective-permute-start(bf16[576,256]{1,0:T(8,128)(2,1)} %bitcast.63), channel_id=1, source_target_pairs={{0,1},{1,0},{2,3},{3,2},{4,5},{5,4},{6,7},{7,6},{8,9},{9,8},{10,11... | collective-permute-start | bytes 884744 | tf_op jit(solution)/shard_map/ppermute | solution.py:285
  0.5 24.9 %collective-permute-start.1 = (bf16[576,256]{1,0:T(8,128)(2,1)}, bf16[576,256]{1,0:T(8,128)(2,1)}, u32[]{:S(2)}, u32[]{:S(2)}) collective-permute-start(bf16[576,256]{1,0:T(8,128)(2,1)} %bitcast.64), channel_id=1, source_target_pairs={{0,2},{1,3},{2,0},{3,1},{4,6},{5,7},{6,4},{7,5},{8,10},{9,11},{10,... | collective-permute-start | bytes 884744 | tf_op jit(solution)/shard_map/ppermute | solution.py:285
  3.0 22.3 %collective-permute-start.2 = (bf16[576,256]{1,0:T(8,128)(2,1)}, bf16[576,256]{1,0:T(8,128)(2,1)}, u32[]{:S(2)}, u32[]{:S(2)}) collective-permute-start(bf16[576,256]{1,0:T(8,128)(2,1)} %bitcast.65), channel_id=1, source_target_pairs={{0,3},{1,2},{2,1},{3,0},{4,7},{5,6},{6,5},{7,4},{8,11},{9,10},{10,... | collective-permute-start | bytes 884744 | tf_op jit(solution)/shard_map/ppermute | solution.py:285
  4.1 0.9 copy-start.1
  5.0 7.7 %copy-start.10 = (bf16[1,2,576]{2,1,0:T(2,128)(2,1)S(1)}, bf16[1,2,576]{2,1,0:T(2,128)(2,1)}, u32[]{:S(2)}) copy-start(bf16[1,2,576]{2,1,0:T(2,128)(2,1)} %param.22) | copy-start | bytes 6916
  5.0 22.9 %all-to-all-start = ((bf16[16,32,576]{2,1,0:T(8,128)(2,1)}), bf16[16,32,576]{2,1,0:T(8,128)(2,1)S(1)}, u32[]{:S(2)}, u32[]{:S(2)}) async-start(bf16[16,32,576]{2,1,0:T(8,128)(2,1)} %copy-done.1), calls=%async_computation | async-start | bytes 1310720 | tf_op jit(solution)/shard_map/all_to_all | solution.py:299
  13.1 5.6 %copy-start.5 = (s32[16]{0:T(128)S(1)}, s32[16]{0:T(128)}, u32[]{:S(2)}) copy-start(s32[16]{0:T(128)} %dest_ref.1) | copy-start | bytes 196
  13.1 14.8 %copy-start.2 = (bf16[1,256,576]{1,2,0:T(8,128)(2,1)S(1)}, bf16[1,256,576]{1,2,0:T(8,128)(2,1)}, u32[]{:S(2)}) copy-start(bf16[1,256,576]{1,2,0:T(8,128)(2,1)} %param.16) | copy-start | bytes 884740
  13.1 14.7 %copy-start.6 = (s32[16]{0:T(128)S(1)}, s32[16]{0:T(128)}, u32[]{:S(2)}) copy-start(s32[16]{0:T(128)} %length_ref.1) | copy-start | bytes 196
  16.6 2.7 %collective-permute-start.3 = (bf16[48,576]{1,0:T(8,128)(2,1)S(1)}, bf16[48,576]{1,0:T(8,128)(2,1)S(1)}, u32[]{:S(2)}, u32[]{:S(2)}) collective-permute-start(bf16[48,576]{1,0:T(8,128)(2,1)S(1)} %get-tuple-element.16), channel_id=1, source_target_pairs={{0,1},{1,0},{2,3},{3,2},{4,5},{5,4},{6,7},{7,6},{8,9},{9,8},{10,11... | collective-permute-start | bytes 165896 | tf_op jit(solution)/shard_map/ppermute | solution.py:285
  17.0 7.4 %collective-permute-start.4 = (bf16[48,576]{1,0:T(8,128)(2,1)}, bf16[48,576]{1,0:T(8,128)(2,1)}, u32[]{:S(2)}, u32[]{:S(2)}) collective-permute-start(bf16[48,576]{1,0:T(8,128)(2,1)} %get-tuple-element.17), channel_id=1, source_target_pairs={{0,2},{1,3},{2,0},{3,1},{4,6},{5,7},{6,4},{7,5},{8,10},{9,11},{10,... | collective-permute-start | bytes 165896 | tf_op jit(solution)/shard_map/ppermute | solution.py:285
  19.3 0.6 copy-start.3
  19.9 5.4 %collective-permute-start.5 = (bf16[48,576]{1,0:T(8,128)(2,1)}, bf16[48,576]{1,0:T(8,128)(2,1)}, u32[]{:S(2)}, u32[]{:S(2)}) collective-permute-start(bf16[48,576]{1,0:T(8,128)(2,1)} %get-tuple-element.18), channel_id=1, source_target_pairs={{0,3},{1,2},{2,1},{3,0},{4,7},{5,6},{6,5},{7,4},{8,11},{9,10},{10,... | collective-permute-start | bytes 165896 | tf_op jit(solution)/shard_map/ppermute | solution.py:285
  27.9 0.8 copy-start.4
  30.6 5.0 %collective-permute-start.6 = (bf16[4,16,640]{2,1,0:T(8,128)(2,1)S(1)}, bf16[4,16,640]{2,1,0:T(8,128)(2,1)S(1)}, u32[]{:S(2)}, u32[]{:S(2)}) collective-permute-start(bf16[4,16,640]{2,1,0:T(8,128)(2,1)S(1)} %get-tuple-element.20), channel_id=1, source_target_pairs={{0,4},{1,5},{2,6},{3,7},{4,0},{5,1},{6,2},{7,3},{8,12},{9,13},{10,... | collective-permute-start | bytes 245768 | tf_op jit(solution)/shard_map/ppermute | solution.py:285
  32.3 9.1 %collective-permute-start.7 = (bf16[4,16,640]{2,1,0:T(8,128)(2,1)S(1)}, bf16[4,16,640]{2,1,0:T(8,128)(2,1)S(1)}, u32[]{:S(2)}, u32[]{:S(2)}) collective-permute-start(bf16[4,16,640]{2,1,0:T(8,128)(2,1)S(1)} %get-tuple-element.21), channel_id=1, source_target_pairs={{0,8},{1,9},{2,10},{3,11},{4,12},{5,13},{6,14},{7,15},{8,0},{9,1},... | collective-permute-start | bytes 245768 | tf_op jit(solution)/shard_map/ppermute | solution.py:285
  33.7 7.8 %collective-permute-start.8 = (bf16[4,16,640]{2,1,0:T(8,128)(2,1)S(1)}, bf16[4,16,640]{2,1,0:T(8,128)(2,1)S(1)}, u32[]{:S(2)}, u32[]{:S(2)}) collective-permute-start(bf16[4,16,640]{2,1,0:T(8,128)(2,1)S(1)} %get-tuple-element.22), channel_id=1, source_target_pairs={{0,12},{1,13},{2,14},{3,15},{4,8},{5,9},{6,10},{7,11},{8,4},{9,5},... | collective-permute-start | bytes 245768 | tf_op jit(solution)/shard_map/ppermute | solution.py:285
  41.4 14.2 %copy-start.9 = (bf16[7168]{0:T(1024)(128)(2,1)S(1)}, bf16[7168]{0:T(1024)(128)(2,1)}, u32[]{:S(2)}) copy-start(bf16[7168]{0:T(1024)(128)(2,1)} %param.26) | copy-start | bytes 43012
  41.4 22.5 %copy-start.8 = (bf16[1,2,7168]{2,1,0:T(2,128)(2,1)S(1)}, bf16[1,2,7168]{2,1,0:T(2,128)(2,1)}, u32[]{:S(2)}) copy-start(bf16[1,2,7168]{2,1,0:T(2,128)(2,1)} %param.23) | copy-start | bytes 86020
  48.4 1.6 %collective-permute-start.9 = (bf16[16,7168]{1,0:T(8,128)(2,1)S(1)}, bf16[16,7168]{1,0:T(8,128)(2,1)S(1)}, u32[]{:S(2)}, u32[]{:S(2)}) collective-permute-start(bf16[16,7168]{1,0:T(8,128)(2,1)S(1)} %get-tuple-element.24), channel_id=1, source_target_pairs={{0,1},{1,0},{2,3},{3,2},{4,5},{5,4},{6,7},{7,6},{8,9},{9,8},{10,11... | collective-permute-start | bytes 688136 | tf_op jit(solution)/shard_map/ppermute | solution.py:356
  50.9 12.8 %all-to-all-start.1 = ((bf16[8,2,7168]{2,1,0:T(2,128)(2,1)}), bf16[8,2,7168]{2,1,0:T(2,128)(2,1)S(1)}, u32[]{:S(2)}, u32[]{:S(2)}) async-start(bf16[8,2,7168]{2,1,0:T(2,128)(2,1)} %shard_map.158), calls=%async_computation.1 | async-start | bytes 458752 | tf_op jit(solution)/shard_map/all_to_all | solution.py:358
  55.0 20.8 %collective-permute-start.10 = (bf16[128,7168]{1,0:T(8,128)(2,1)}, bf16[128,7168]{1,0:T(8,128)(2,1)}, u32[]{:S(2)}, u32[]{:S(2)}) collective-permute-start(bf16[128,7168]{1,0:T(8,128)(2,1)} %refs_0_.1), channel_id=1, source_target_pairs={{0,1},{1,0},{2,3},{3,2},{4,5},{5,4},{6,7},{7,6},{8,9},{9,8},{10,11... | collective-permute-start | bytes 5505032 | tf_op jit(solution)/shard_map/ppermute | solution.py:366
  55.0 20.8 %collective-permute-start.11 = (bf16[128,7168]{1,0:T(8,128)(2,1)}, bf16[128,7168]{1,0:T(8,128)(2,1)}, u32[]{:S(2)}, u32[]{:S(2)}) collective-permute-start(bf16[128,7168]{1,0:T(8,128)(2,1)} %refs_2_.1), channel_id=1, source_target_pairs={{0,1},{1,0},{2,3},{3,2},{4,5},{5,4},{6,7},{7,6},{8,9},{9,8},{10,11... | collective-permute-start | bytes 5505032 | tf_op jit(solution)/shard_map/ppermute | solution.py:366
  55.5 20.3 %collective-permute-start.12 = (bf16[128,7168]{1,0:T(8,128)(2,1)}, bf16[128,7168]{1,0:T(8,128)(2,1)}, u32[]{:S(2)}, u32[]{:S(2)}) collective-permute-start(bf16[128,7168]{1,0:T(8,128)(2,1)} %refs_4_.3), channel_id=1, source_target_pairs={{0,1},{1,0},{2,3},{3,2},{4,5},{5,4},{6,7},{7,6},{8,9},{9,8},{10,11... | collective-permute-start | bytes 5505032 | tf_op jit(solution)/shard_map/ppermute | solution.py:366
  75.8 10.9 %copy-start.11 = (f32[1,2,1]{1,2,0:T(1,128)S(1)}, f32[1,2,1]{1,2,0:T(1,128)}, u32[]{:S(2)}) copy-start(f32[1,2,1]{1,2,0:T(1,128)} %param.28) | copy-start | bytes 28
  75.8 10.9 %copy-start.12 = (s32[1,2,1]{1,2,0:T(1,128)S(1)}, s32[1,2,1]{1,2,0:T(1,128)}, u32[]{:S(2)}) copy-start(s32[1,2,1]{1,2,0:T(1,128)} %param.27) | copy-start | bytes 28
  83.3 11.4 %all-to-all-start.3 = ((bf16[8,2,7168]{2,1,0:T(2,128)(2,1)}), bf16[8,2,7168]{2,1,0:T(2,128)(2,1)S(1)}, u32[]{:S(2)}, u32[]{:S(2)}) async-start(bf16[8,2,7168]{2,1,0:T(2,128)(2,1)} %shard_map.159), calls=%async_computation.3 | async-start | bytes 458752 | tf_op jit(solution)/shard_map/all_to_all | solution.py:375

commit v5 on v4

--- a/solution.py
+++ b/solution.py
@@ -24,31 +24,6 @@
 scalars = pl.BlockSpec(memory_space=pltpu.SMEM)
 
 
-def attend(query, key_rows, live_keys, fresh_rows):
-    scores = (
-        lax.dot_general(query, key_rows, contract_last, preferred_element_type=f32) * softmax_scale
-    )
-    scores = jnp.where(live_keys[None, :], scores, -jnp.inf)
-    fresh_scores = (
-        lax.dot_general(query, fresh_rows, contract_last, preferred_element_type=f32)
-        * softmax_scale
-    )
-    peak_score = jnp.maximum(
-        jnp.max(scores, axis=1, keepdims=True), jnp.max(fresh_scores, axis=1, keepdims=True)
-    )
-    cache_terms = jnp.exp(scores - peak_score)
-    fresh_terms = jnp.exp(fresh_scores - peak_score)
-    denominator = jnp.sum(cache_terms, axis=1, keepdims=True) + jnp.sum(
-        fresh_terms, axis=1, keepdims=True
-    )
-    cache_probs = (cache_terms / denominator).astype(bf16)
-    fresh_probs = (fresh_terms / denominator).astype(bf16)
-    mixed = jnp.dot(cache_probs, key_rows, preferred_element_type=f32) + jnp.dot(
-        fresh_probs, fresh_rows, preferred_element_type=f32
-    )
-    return mixed[:, :KVR]
-
-
 def three_parts(value):
     first = value.astype(bf16).astype(f32)
     second = (value - first).astype(bf16).astype(f32)
@@ -56,36 +31,98 @@
     return first, second, third
 
 
-def spread_kernel(query_ref, spread_ref):
-    peers, rows, width = spread_ref.shape
+def spread_kernel(query_hbm, spread_hbm, query_ref, blocks_ref, sems):
+    peers, rows, width = spread_hbm.shape
     planes = peers // PLANE
-    by_peer = query_ref[0].astype(f32).T.reshape(planes, PLANE, rows // planes, width)
+    load = pltpu.make_async_copy(query_hbm.at[1], query_ref, sems.at[0])
+    load.start()
+    load.wait()
+    by_peer = query_ref[...].astype(f32).T.reshape(planes, PLANE, rows // planes, width)
+    copies = []
     for column in range(PLANE):
-        block = by_peer[:, column].reshape(rows, width).astype(bf16)
+        blocks_ref[column] = by_peer[:, column].reshape(rows, width).astype(bf16)
         for plane in range(planes):
-            spread_ref[plane * PLANE + column] = block
-
-
-def column_kernel(device_ref, resident_ref, fresh_ref, *message_refs):
-    planes, _, per_peer, latent = resident_ref.shape
+            peer = plane * PLANE + column
+            copies.append(
+                pltpu.make_async_copy(blocks_ref.at[column], spread_hbm.at[peer], sems.at[1 + peer])
+            )
+            copies[-1].start()
+    for copy in copies:
+        copy.wait()
+
+
+def stage_kernel(after_ref, keys_hbm, staged_hbm, sem):
+    del after_ref
+    copy = pltpu.make_async_copy(keys_hbm, staged_hbm, sem)
+    copy.start()
+    copy.wait()
+
+
+def prefetch_kernel(after_ref, *refs):
+    del after_ref
+    count = (len(refs) - 1) // 2
+    copies = [
+        pltpu.make_async_copy(refs[at], refs[count + at], refs[-1].at[at]) for at in range(count)
+    ]
+    for copy in copies:
+        copy.start()
+    for copy in copies:
+        copy.wait()
+
+
+def resident_kernel(device_ref, length_ref, fresh_ref, after_ref, query_hbm, cache_hbm, *refs):
+    message_refs, (query_ref, cache_ref, mixed_ref, sems) = refs[:-4], refs[-4:]
+    del after_ref
+    loads = [
+        pltpu.make_async_copy(query_hbm.at[0], query_ref, sems.at[0]),
+        pltpu.make_async_copy(cache_hbm, cache_ref, sems.at[1]),
+    ]
+    for load in loads:
+        load.start()
+    for load in loads:
+        load.wait()
+    query = query_ref[...].astype(f32).T
+    fresh = fresh_ref[0:1].astype(f32)
+    scores = jnp.dot(query.astype(bf16), cache_ref[...], preferred_element_type=f32)
+    position = lax.broadcasted_iota(jnp.int32, scores.shape, 1)
+    scores = jnp.where(position < length_ref[0], scores * softmax_scale, -jnp.inf)
+    fresh_score = softmax_scale * jnp.sum(query * fresh, axis=1, keepdims=True)
+    peak = jnp.maximum(jnp.max(scores, axis=1, keepdims=True), fresh_score)
+    terms = jnp.exp(scores - peak)
+    fresh_term = jnp.exp(fresh_score - peak)
+    scale = 1.0 / (jnp.sum(terms, axis=1, keepdims=True) + fresh_term)
+    mixed = lax.dot_general(
+        (terms * scale).astype(bf16), cache_ref[:KVR], contract_last, preferred_element_type=f32
+    )
+    mixed_ref[...] = (mixed + fresh_term * scale * fresh[:, :KVR]).reshape(mixed_ref.shape)
+    planes, _, per_peer, latent = mixed_ref.shape
     rows = planes * per_peer
     column = device_ref[0] % PLANE
     for at, message_ref in enumerate(message_refs):
-        message_ref[:rows, :latent] = resident_ref[:, column ^ at].reshape(rows, latent).astype(bf16)
-        message_ref[rows:] = jnp.broadcast_to(fresh_ref[...], message_ref[rows:].shape)
-
-
-def prompt_kernel(device_ref, dest_ref, length_ref, query_ref, *refs):
-    key_refs, message_refs = refs[:PLANE], refs[PLANE : 2 * PLANE]
-    out_refs, stage_ref = refs[2 * PLANE : -1], refs[-1]
+        message_ref[:rows, :latent] = mixed_ref[:, column ^ at].reshape(rows, latent).astype(bf16)
+        message_ref[rows:] = jnp.broadcast_to(fresh_ref[1:2], message_ref[rows:].shape)
+
+
+def prompt_kernel(device_ref, dest_ref, length_ref, *refs):
+    key_refs, message_refs, query_hbm = refs[:PLANE], refs[PLANE : 2 * PLANE], refs[2 * PLANE]
+    out_refs, (stage_ref, query_ref, sems) = refs[2 * PLANE + 1 : -3], refs[-3:]
     planes, _, rows, width = stage_ref.shape
     per_peer, chunk = rows // 2, width - KVR
     heads = planes * per_peer
     device = device_ref[0]
+    sources = [dest_ref[device ^ at] for at in range(PLANE)] + [device ^ at for at in range(PLANE)]
+    loads = [
+        pltpu.make_async_copy(query_hbm.at[source], query_ref.at[at], sems.at[at])
+        for at, source in enumerate(sources)
+    ]
+    for load in loads:
+        load.start()
+    for load in loads:
+        load.wait()
     scores = []
     for at in range(PLANE):
         prompt = device ^ at
-        query = query_ref[dest_ref[prompt]]
+        query = query_ref[at]
         score = jnp.dot(query, key_refs[at][...], preferred_element_type=f32) * softmax_scale
         position = lax.broadcasted_iota(jnp.int32, score.shape, 1)
         scores.append(jnp.where(position < length_ref[prompt], score, -jnp.inf))
@@ -109,7 +146,7 @@
         ).astype(bf16)
         fresh = message_refs[at][heads : heads + FRESH_ROWS].astype(f32)[:1]
         fresh_score = softmax_scale * jnp.sum(
-            query_ref[device ^ at].astype(f32) * fresh, axis=1, keepdims=True
+            query_ref[PLANE + at].astype(f32) * fresh, axis=1, keepdims=True
         )
         stats = jnp.zeros((heads, chunk), f32)
         for lane_at, value in enumerate(three_parts(log_sum[part]) + three_parts(fresh_score)):
@@ -130,22 +167,8 @@
     pair_ref[...] = total.reshape(pair_ref.shape).astype(bf16)
 
 
-def heads_kernel(row_ref, column_ref, peer_ref, *refs):
-    payload_refs, rows_ref, arrived = refs[:-8], refs[-2], refs[-1]
-    upward_hbm, proj_hbm, keep_ref, send_ref, upward_ref, proj_ref = refs[-8:-2]
-    upward_copy = pltpu.make_async_copy(upward_hbm, upward_ref, arrived.at[0])
-    upward_copy.start()
-    blocks = range(0, proj_ref.shape[1], BLOCK)
-    proj_copies = [
-        pltpu.make_async_copy(
-            proj_hbm.at[:, start : start + BLOCK],
-            proj_ref.at[:, start : start + BLOCK],
-            arrived.at[1 + at],
-        )
-        for at, start in enumerate(blocks)
-    ]
-    for copy in proj_copies:
-        copy.start()
+def heads_kernel(row_ref, column_ref, peer_ref, upward_ref, proj_ref, *refs):
+    payload_refs, (keep_ref, send_ref, rows_ref) = refs[:-3], refs[-3:]
     for at, payload_ref in enumerate(payload_refs):
         rows_ref[at * PLANE : (at + 1) * PLANE] = payload_ref[...]
     peers, rows, width = rows_ref.shape
@@ -182,7 +205,6 @@
         mixed = mixed + jnp.dot(high, values, preferred_element_type=f32)
         mixed = mixed + jnp.dot(low, values, preferred_element_type=f32)
     mixed = mixed.astype(bf16)
-    upward_copy.wait()
     value_rows = jnp.concatenate(
         [
             jnp.dot(
@@ -192,8 +214,7 @@
         ],
         axis=1,
     )
-    for copy, start in zip(proj_copies, blocks):
-        copy.wait()
+    for start in range(0, proj_ref.shape[1], BLOCK):
         part = jnp.dot(value_rows, proj_ref[:, start : start + BLOCK], preferred_element_type=f32)
         keep_ref[:, start : start + BLOCK] = part[:peers]
         send_ref[:, start : start + BLOCK] = part[peers:].astype(bf16)
@@ -201,37 +222,46 @@
 
 def expert_kernel(rows_ref, *refs):
     out_ref, arrived = refs[6], refs[10]
-    units = refs[0].shape[0]
-    copies = [
-        pltpu.make_async_copy(
-            refs[at], refs[7 + at // 2].at[pl.ds(at % 2 * units, units)], arrived.at[at]
-        )
-        for at in range(6)
-    ]
-    for copy in copies:
-        copy.start()
     gate_ref, up_ref, down_ref = refs[7:10]
-    rows = rows_ref[...]
-    copies[0].wait()
-    copies[1].wait()
-    gate = lax.dot_general(rows, gate_ref[...], contract_last, preferred_element_type=f32)
-    copies[2].wait()
-    copies[3].wait()
-    up_value = lax.dot_general(rows, up_ref[...], contract_last, preferred_element_type=f32)
-    act = (gate / (1.0 + jnp.exp(-gate)) * up_value).astype(bf16)
-    copies[4].wait()
-    copies[5].wait()
+    units, model = refs[0].shape
     chips, pair = out_ref.shape[:2]
-    for start in range(0, down_ref.shape[1], BLOCK):
-        part = jnp.dot(act, down_ref[:, start : start + BLOCK], preferred_element_type=f32)
-        out_ref[:, :, start : start + BLOCK] = part.reshape(chips, pair, BLOCK).astype(bf16)
+    first, second = model // 4, model // 2
+    steps = [(range(4), start, first) for start in range(0, model, first)]
+    steps += [(range(4, 6), start, second) for start in range(0, model, second)]
+    copies = []
+    for matrices, start, size in steps:
+        copies.append([])
+        for at in matrices:
+            place = refs[7 + at // 2].at[pl.ds(at % 2 * units, units), pl.ds(start, size)]
+            sem = arrived.at[sum(map(len, copies))]
+            copies[-1].append(
+                pltpu.make_async_copy(refs[at].at[:, pl.ds(start, size)], place, sem)
+            )
+            copies[-1][-1].start()
+    gate = up_value = jnp.zeros((rows_ref.shape[0], 2 * units), f32)
+    for step, (matrices, start, size) in enumerate(steps):
+        for copy in copies[step]:
+            copy.wait()
+        columns = slice(start, start + size)
+        if size == first:
+            rows = rows_ref[:, columns]
+            gate += lax.dot_general(
+                rows, gate_ref[:, columns], contract_last, preferred_element_type=f32
+            )
+            up_value += lax.dot_general(
+                rows, up_ref[:, columns], contract_last, preferred_element_type=f32
+            )
+        else:
+            act = (gate / (1.0 + jnp.exp(-gate)) * up_value).astype(bf16)
+            part = jnp.dot(act, down_ref[:, columns], preferred_element_type=f32)
+            out_ref[:, :, columns] = part.reshape(chips, pair, size).astype(bf16)
 
 
 def near(value):
     return pltpu.with_memory_space_constraint(value, pltpu.VMEM)
 
 
-def call(kernel, outputs, operands, far=(), scratch=()):
+def call(kernel, outputs, operands, far=(), scratch=(), cost=None):
     specs = [scalars if operand.ndim == 1 else whole for operand in operands]
     return pl.pallas_call(
         kernel,
@@ -240,10 +270,35 @@
         out_specs=[whole] * len(outputs),
         scratch_shapes=scratch,
         compiler_params=pltpu.CompilerParams(vmem_limit_bytes=32 << 20),
+        cost_estimate=cost,
     )(
         *[operand if operand.ndim == 1 else near(operand) for operand in operands],
         *[pltpu.with_memory_space_constraint(operand, pltpu.HBM) for operand in far],
     )
+
+
+def call_far(kernel, shapes, operands, scratch, cost=None):
+    far = pl.BlockSpec(memory_space=pltpu.HBM)
+    return pl.pallas_call(
+        kernel,
+        out_shape=shapes,
+        in_specs=[far] * len(operands),
+        out_specs=jax.tree.map(lambda _: far, shapes),
+        scratch_shapes=scratch,
+        compiler_params=pltpu.CompilerParams(vmem_limit_bytes=16 << 20),
+        cost_estimate=cost,
+    )(*operands)
+
+
+def prefetch(after, weights):
+    return pl.pallas_call(
+        prefetch_kernel,
+        out_shape=[pltpu.VMEM(weight.shape, weight.dtype) for weight in weights],
+        in_specs=[pl.BlockSpec(memory_space=pl.ANY)] * (1 + len(weights)),
+        out_specs=[whole] * len(weights),
+        scratch_shapes=[pltpu.SemaphoreType.DMA((len(weights),))],
+        compiler_params=pltpu.CompilerParams(vmem_limit_bytes=16 << 20),
+    )(after, *[pltpu.with_memory_space_constraint(weight, pltpu.HBM) for weight in weights])
 
 
 def shards(
@@ -288,29 +343,46 @@
 
     flipped = jnp.swapaxes(queries[0], 1, 2)
     spread_shape = (devices, planes * per_peer, width)
-    spread_rows = pl.pallas_call(
+    spread_rows = call_far(
         spread_kernel,
-        out_shape=pltpu.VMEM(spread_shape, bf16),
-        grid=(1,),
-        in_specs=[pl.BlockSpec((1, width, heads), lambda step: (1, 0, 0))],
-        out_specs=pl.BlockSpec(spread_shape, lambda step: (0, 0, 0)),
-        compiler_params=pltpu.CompilerParams(vmem_limit_bytes=32 << 20),
-    )(pltpu.with_memory_space_constraint(flipped, pltpu.HBM))
+        jax.ShapeDtypeStruct(spread_shape, bf16),
+        [flipped],
+        [
+            pltpu.VMEM((width, heads), bf16),
+            pltpu.VMEM((PLANE, *spread_shape[1:]), bf16),
+            pltpu.SemaphoreType.DMA((1 + devices,)),
+        ],
+    )
     spread = exchange(spread_rows)
 
+    short = pl.CostEstimate(flops=1, bytes_accessed=1, transcendentals=0)
     flipped_keys = jnp.swapaxes(handoff_rows[0], 0, 1)
-    plane_keys = [toward(flipped_keys, at) for at in range(PLANE)]
-    cache_keys = resident_cache[0]
-    cache_live = jnp.arange(cache_keys.shape[0], dtype=jnp.int32) < resident_len[0]
-    resident_out = attend(queries[0, 0], cache_keys, cache_live, new_latent[:, 0])
+    staged_keys = call_far(
+        stage_kernel,
+        jax.ShapeDtypeStruct(flipped_keys.shape, bf16),
+        [spread_rows, flipped_keys],
+        [pltpu.SemaphoreType.DMA],
+        short,
+    )
+    plane_keys = [staged_keys]
+    bit = PLANE // 2
+    while bit:
+        crossing = [toward(keys, bit) for keys in plane_keys]
+        plane_keys = [keys for pair in zip(plane_keys, crossing) for keys in pair]
+        bit //= 2
+    flipped_cache = jnp.swapaxes(resident_cache[0], 0, 1)
     messages = call(
-        column_kernel,
+        resident_kernel,
         [((planes * per_peer + FRESH_ROWS, width), bf16)] * PLANE,
+        [own_device, resident_len, new_latent[0]],
+        [spread_rows, flipped, flipped_cache],
         [
-            own_device,
-            resident_out.reshape(planes, PLANE, per_peer, KVR),
-            new_latent[0, 1:2],
+            pltpu.VMEM((width, heads), bf16),
+            pltpu.VMEM(flipped_cache.shape, bf16),
+            pltpu.VMEM((planes, PLANE, per_peer, KVR), f32),
+            pltpu.SemaphoreType.DMA((2,)),
         ],
+        short,
     )
     messages = [toward(message, at) for at, message in enumerate(messages)]
 
@@ -318,9 +390,15 @@
     payloads = call(
         prompt_kernel,
         [((PLANE, 2 * per_peer, KVR + chunk), bf16)] * planes,
-        [own_device, handoff_dest, handoff_len, spread, *plane_keys, *messages],
-        scratch=[pltpu.VMEM((planes, PLANE, 2 * per_peer, KVR + chunk), bf16)],
-    )
+        [own_device, handoff_dest, handoff_len, *plane_keys, *messages],
+        [spread],
+        [
+            pltpu.VMEM((planes, PLANE, 2 * per_peer, KVR + chunk), bf16),
+            pltpu.VMEM((2 * PLANE, *spread_shape[1:]), bf16),
+            pltpu.SemaphoreType.DMA((2 * PLANE,)),
+        ],
+    )
+    upward, projection = prefetch(payloads[0], [value_upward, out_proj.reshape(-1, model)])
     payloads = [toward(payload, at * PLANE) for at, payload in enumerate(payloads)]
 
     row = jnp.arange(per_peer * 2 * devices, dtype=jnp.int32)
@@ -339,18 +417,11 @@
         ],
         axis=0,
     )
-    projection = out_proj.reshape(-1, model)
     keep, send = call(
         heads_kernel,
         [((devices, model), f32), ((devices, model), bf16)],
-        [row_table, column_table, peers[None], *payloads],
-        [value_upward, projection],
-        [
-            pltpu.VMEM(value_upward.shape, bf16),
-            pltpu.VMEM(projection.shape, bf16),
-            pltpu.VMEM((devices, 2 * per_peer, KVR + chunk), bf16),
-            pltpu.SemaphoreType.DMA((1 + model // BLOCK,)),
-        ],
+        [row_table, column_table, peers[None], upward, projection, *payloads],
+        scratch=[pltpu.VMEM((devices, 2 * per_peer, KVR + chunk), bf16)],
     )
 
     other = lax.ppermute(send, "ep", siblings)
@@ -370,7 +441,7 @@
         [own_rows.reshape(devices, model)],
         experts,
         [pltpu.VMEM((2 * gate_proj.shape[0], model), bf16)] * 3
-        + [pltpu.SemaphoreType.DMA((6,))],
+        + [pltpu.SemaphoreType.DMA((20,))],
     )
     returned = exchange_core(part)
 

time: 96.3 us -> 92 us (0.955)
  Pallas kernels: 19 us -> 23 us
  waiting for transfers between devices: 31.4 us -> 28.3 us
  matrix products: 2.55 us -> 0 us
  other arithmetic: 3.13 us -> 1.77 us
    pallas_call x1 -> x3, Pallas kernels: 1.04 us -> 6.92 us  [the longest x1 5.53 us: prefetch(): pl.pallas_call(prefetch_kernel, out_shape=[pltpu.VMEM(weight.shape, weigh...]
    all_to_all x1, waiting for transfers between devices: 2.55 us -> 0.01 us  [shards(): spread = exchange(spread_rows)]
    dot_general x3 -> x0, matrix products: 2.55 us -> none  [the longest x1 1.72 us: attend(): jnp.dot(cache_probs, key_rows, preferred_element_type=f32)]
    pallas_call x5, Pallas kernels: 17.9 us -> 16.1 us  [call(): pl.pallas_call(kernel, out_shape=[pltpu.VMEM(shape, dtype) for shape, dty...]
    ppermute x9, starting transfers between devices: 9.92 us -> 8.45 us  [shards(): lax.ppermute(value, 'ep', [(i, i ^ bits) for i in range(devices)])]
    all_to_all x1, starting transfers between devices: 6.28 us -> 7.37 us  [shards(): spread = exchange(spread_rows)]
    add x1 -> x0, other arithmetic: 1.04 us -> none  [attend(): jnp.dot(cache_probs, key_rows, preferred_element_type=f32)]
    unnamed x26 -> x22, local copies, waits for them, and re-layouts: 2.34 us -> 1.87 us
  transfers between devices with their start and end apart: 16 -> 16, of which waited for: 8 -> 7; matrix products, arithmetic and copies ran while one was open for 6% -> 2% of each run, Pallas kernels for 2% -> 10%
where the time goes in v5:
time: 92 us; the launch traced here: 91.4 us
  waiting for transfers between devices  28.3 us (31%)
  starting transfers between devices  23.6 us (26%)
  Pallas kernels  23 us (25%)
  blocking collectives  11.3 us (12%)
  local copies, waits for them, and re-layouts  2.51 us (3%)
  other arithmetic  1.77 us (2%)
  between operations  0.95 us (1%)
    pallas_call x5, Pallas kernels, call(): pl.pallas_call(kernel, out_shape=[pltpu.VMEM(shape, dtype) for shape, dty...  16.1 us
    all_to_all x1, blocking collectives, shards(): own_rows = exchange_core(jnp.broadcast_to(normed[None], (chips, 2, model)))  11.3 us
    ppermute x9, waiting for transfers between devices, shards(): lax.ppermute(value, 'ep', [(i, i ^ bits) for i in range(devices)])  10.8 us
    ppermute x9, starting transfers between devices, shards(): lax.ppermute(value, 'ep', [(i, i ^ bits) for i in range(devices)])  8.45 us
    all_to_all x1, waiting for transfers between devices, shards(): attention = jnp.sum(exchange_core(pair).astype(f32), axis=0)  8.07 us
    all_to_all x1, waiting for transfers between devices, shards(): returned = exchange_core(part)  7.9 us
    all_to_all x1, starting transfers between devices, shards(): spread = exchange(spread_rows)  7.37 us
    pallas_call x1, Pallas kernels, prefetch(): pl.pallas_call(prefetch_kernel, out_shape=[pltpu.VMEM(weight.shape, weigh...  5.53 us
  transfers between devices with their start and end apart: 16, of which 7 were waited for; matrix products, arithmetic and copies ran while one was open for 2% of the time, Pallas kernels for 10%

profile of v5, /device:TPU:0, one launch (start us, length us, event | category | flops | bytes accessed | tf_op | source)
XLA Modules:
  0.0 91.4 jit_solution(17338257043802471616)
XLA Ops:
  0.0 1.0 %copy-done = bf16[1,2,128,576]{2,3,1,0:T(8,128)(2,1)S(1)} copy-done((bf16[1,2,128,576]{2,3,1,0:T(8,128)(2,1)S(1)}, bf16[1,2,128,576]{2,3,1,0:T(8,128)(2,1)}, u32[]{:S(2)}) %copy-start) | copy-done | bytes 294936
  1.0 1.3 %shard_map.154.after_ref = bf16[16,32,576]{2,1,0:T(8,128)(2,1)} custom-call(bf16[2,576,128]{2,1,0:T(8,128)(2,1)S(1)} %bitcast.37), custom_call_target="tpu_custom_call" | custom-call | tf_op jit(solution)/shard_map/pallas_call | solution.py:282
  2.3 7.4 %all-to-all-start = ((bf16[16,32,576]{2,1,0:T(8,128)(2,1)}), bf16[16,32,576]{2,1,0:T(8,128)(2,1)S(1)}, u32[]{:S(2)}, u32[]{:S(2)}) async-start(bf16[16,32,576]{2,1,0:T(8,128)(2,1)} %shard_map.154.after_ref), calls=%async_computation | async-start | bytes 1310720 | tf_op jit(solution)/shard_map/all_to_all | solution.py:356
  9.7 0.1 shard_map.155.refs_0_
  9.8 0.0 copy-start.4
  9.8 2.0 %collective-permute-start.1 = (bf16[576,256]{1,0:T(8,128)(2,1)S(1)}, bf16[576,256]{1,0:T(8,128)(2,1)S(1)}, u32[]{:S(2)}, u32[]{:S(2)}) collective-permute-start(bf16[576,256]{1,0:T(8,128)(2,1)S(1)} %shard_map.155.refs_0_), channel_id=1, source_target_pairs={{0,2},{1,3},{2,0},{3,1},{4,6},{5,7},{6,4},{7,5},{8,10},{9,11},{10,... | collective-permute-start | bytes 884744 | tf_op jit(solution)/shard_map/ppermute | solution.py:340
  12.4 3.4 %shard_map.156 = (bf16[48,576]{1,0:T(8,128)(2,1)S(1)}, bf16[48,576]{1,0:T(8,128)(2,1)S(1)}, bf16[48,576]{1,0:T(8,128)(2,1)S(1)}, bf16[48,576]{1,0:T(8,128)(2,1)S(1)}) custom-call(s32[1]{0:T(128)} %bitcast.device_ref, s32[1]{0:T(128)S(6)} %copy.18.length_ref, bf16[2,576]{1,0:T(2,128)(2,1)S(1)} %bitcast.39, bf16[16,32,576]{2,1,0:T(8,128)(2,1)} %shard_map.154.after_ref, ...), custom_call_target="tpu_custom_call" | custom-call | flops 1 | bytes 1 | tf_op jit(solution)/shard_map/pallas_call | solution.py:266
  15.8 0.6 collective-permute-start.3
  16.4 0.1 collective-permute-start.4
  16.5 1.3 %collective-permute-start.5 = (bf16[48,576]{1,0:T(8,128)(2,1)S(1)}, bf16[48,576]{1,0:T(8,128)(2,1)S(1)}, u32[]{:S(2)}, u32[]{:S(2)}) collective-permute-start(bf16[48,576]{1,0:T(8,128)(2,1)S(1)} %get-tuple-element.20), channel_id=1, source_target_pairs={{0,3},{1,2},{2,1},{3,0},{4,7},{5,6},{6,5},{7,4},{8,11},{9,10},{10,... | collective-permute-start | bytes 165896 | tf_op jit(solution)/shard_map/ppermute | solution.py:340
  17.9 0.2 select_reduce_fusion
  18.0 0.1 broadcast_in_dim.41
  18.1 0.1 stack_reshape.7
  18.2 0.1 broadcast_in_dim.22
  18.3 0.1 stack_reshape.6
  18.4 8.2 %collective-permute-done.1.refs_2_ = bf16[576,256]{1,0:T(8,128)(2,1)S(1)} collective-permute-done((bf16[576,256]{1,0:T(8,128)(2,1)S(1)}, bf16[576,256]{1,0:T(8,128)(2,1)S(1)}, u32[]{:S(2)}, u32[]{:S(2)}) %collective-permute-start.1) | collective-permute-done | bytes 294944 | tf_op jit(solution)/shard_map/ppermute | solution.py:340
  26.7 0.1 copy.17.row_ref
  26.8 1.1 %collective-permute-done.4.refs_6_ = bf16[48,576]{1,0:T(8,128)(2,1)S(1)} collective-permute-done((bf16[48,576]{1,0:T(8,128)(2,1)S(1)}, bf16[48,576]{1,0:T(8,128)(2,1)S(1)}, u32[]{:S(2)}, u32[]{:S(2)}) %collective-permute-start.4) | collective-permute-done | bytes 55328 | tf_op jit(solution)/shard_map/ppermute | solution.py:340
  27.9 0.4 collective-permute-done.5.refs_7_
  28.3 0.9 copy-done.5
  29.2 2.3 %shard_map.157 = (bf16[4,16,640]{2,1,0:T(8,128)(2,1)S(1)}, bf16[4,16,640]{2,1,0:T(8,128)(2,1)S(1)}, bf16[4,16,640]{2,1,0:T(8,128)(2,1)S(1)}, bf16[4,16,640]{2,1,0:T(8,128)(2,1)S(1)}) custom-call(s32[1]{0:T(128)} %bitcast.device_ref, s32[16]{0:T(128)S(1)} %copy-done.3, s32[16]{0:T(128)S(1)} %copy-done.4, bf16[576,256]{1,0:T(8,128)(2,1)S(1)} %shard_map.155.refs_0_, ...), custom_call_target="tpu_custom_call" | custom-call | tf_op jit(solution)/shard_map/pallas_call | solution.py:266
  31.5 1.5 %collective-permute-start.6 = (bf16[4,16,640]{2,1,0:T(8,128)(2,1)S(1)}, bf16[4,16,640]{2,1,0:T(8,128)(2,1)S(1)}, u32[]{:S(2)}, u32[]{:S(2)}) collective-permute-start(bf16[4,16,640]{2,1,0:T(8,128)(2,1)S(1)} %get-tuple-element.24), channel_id=1, source_target_pairs={{0,4},{1,5},{2,6},{3,7},{4,0},{5,1},{6,2},{7,3},{8,12},{9,13},{10,... | collective-permute-start | bytes 245768 | tf_op jit(solution)/shard_map/ppermute | solution.py:340
  33.0 2.4 %collective-permute-start.7 = (bf16[4,16,640]{2,1,0:T(8,128)(2,1)S(1)}, bf16[4,16,640]{2,1,0:T(8,128)(2,1)S(1)}, u32[]{:S(2)}, u32[]{:S(2)}) collective-permute-start(bf16[4,16,640]{2,1,0:T(8,128)(2,1)S(1)} %get-tuple-element.25), channel_id=1, source_target_pairs={{0,8},{1,9},{2,10},{3,11},{4,12},{5,13},{6,14},{7,15},{8,0},{9,1},... | collective-permute-start | bytes 245768 | tf_op jit(solution)/shard_map/ppermute | solution.py:340
  35.4 0.5 collective-permute-start.8
  35.9 5.5 %shard_map.158 = (bf16[8,512,128]{2,1,0:T(8,128)(2,1)S(1)}, bf16[1024,7168]{1,0:T(8,128)(2,1)S(1)}) custom-call(bf16[4,16,640]{2,1,0:T(8,128)(2,1)S(1)} %get-tuple-element.21.after_ref.refs_0_, bf16[8,512,128]{2,1,0:T(8,128)(2,1)} %refs_0_.2, bf16[1024,7168]{1,0:T(8,128)(2,1)} %bitcast.40), custom_call_target="tpu_custom_call" | custom-call | tf_op jit(solution)/shard_map/pallas_call | solution.py:294
  41.5 1.1 %collective-permute-done.7.refs_2_ = bf16[4,16,640]{2,1,0:T(8,128)(2,1)S(1)} collective-permute-done((bf16[4,16,640]{2,1,0:T(8,128)(2,1)S(1)}, bf16[4,16,640]{2,1,0:T(8,128)(2,1)S(1)}, u32[]{:S(2)}, u32[]{:S(2)}) %collective-permute-start.7) | collective-permute-done | bytes 81952 | tf_op jit(solution)/shard_map/ppermute | solution.py:340
  42.5 3.9 %shard_map.159 = (f32[16,7168]{1,0:T(8,128)S(1)}, bf16[16,7168]{1,0:T(8,128)(2,1)S(1)}) custom-call(s32[256,3]{1,0:T(8,128)S(1)} %copy.17.row_ref, s32[3,256]{1,0:T(4,128)S(1)} %pad_add_fusion.1.column_ref, s32[1,16]{1,0:T(1,128)S(1)} %iota_xor_fusion.peer_ref, bf16[8,512,128]{2,1,0:T(8,128)(2,1)S(1)} %get-tuple-element.22.upward_ref, ...), custom_call_target="tpu_custom_call" | custom-call | tf_op jit(solution)/shard_map/pallas_call | solution.py:266
  46.4 0.0 collective-permute-start.9
  46.4 1.5 %collective-permute-done.9.other_ref = bf16[16,7168]{1,0:T(8,128)(2,1)S(1)} collective-permute-done((bf16[16,7168]{1,0:T(8,128)(2,1)S(1)}, bf16[16,7168]{1,0:T(8,128)(2,1)S(1)}, u32[]{:S(2)}, u32[]{:S(2)}) %collective-permute-start.9) | collective-permute-done | bytes 229408 | tf_op jit(solution)/shard_map/ppermute | solution.py:427
  47.9 0.9 %shard_map.160 = bf16[8,2,7168]{2,1,0:T(2,128)(2,1)} custom-call(f32[16,7168]{1,0:T(8,128)S(1)} %get-tuple-element.27.keep_ref, bf16[16,7168]{1,0:T(8,128)(2,1)S(1)} %collective-permute-done.9.other_ref), custom_call_target="tpu_custom_call" | custom-call | tf_op jit(solution)/shard_map/pallas_call | solution.py:266
  48.8 3.7 %all-to-all-start.1 = ((bf16[8,2,7168]{2,1,0:T(2,128)(2,1)}), bf16[8,2,7168]{2,1,0:T(2,128)(2,1)S(1)}, u32[]{:S(2)}, u32[]{:S(2)}) async-start(bf16[8,2,7168]{2,1,0:T(2,128)(2,1)} %shard_map.160), calls=%async_computation.1 | async-start | bytes 458752 | tf_op jit(solution)/shard_map/all_to_all | solution.py:429
  52.6 0.1 collective-permute-start.10
  52.7 0.5 collective-permute-start.11
  53.2 0.1 collective-permute-start.12
  53.3 8.1 %all-to-all-done.1 = bf16[8,2,7168]{2,1,0:T(2,128)(2,1)S(1)} async-done(((bf16[8,2,7168]{2,1,0:T(2,128)(2,1)}), bf16[8,2,7168]{2,1,0:T(2,128)(2,1)S(1)}, u32[]{:S(2)}, u32[]{:S(2)}) %all-to-all-start.1) | async-done | bytes 229408 | tf_op jit(solution)/shard_map/all_to_all | solution.py:429
  61.3 0.2 convert_reduce_fusion
  61.5 0.2 fusion.2
  61.7 0.1 fusion.4
  61.8 0.1 broadcast_in_dim.44
  62.0 11.3 %all_to_all.20 = bf16[8,2,7168]{2,1,0:T(2,128)(2,1)S(1)} all-to-all(bf16[8,2,7168]{2,1,0:T(2,128)(2,1)S(1)} %broadcast_in_dim.44), channel_id=1, replica_groups={{0,2,4,6,8,10,12,14},{1,3,5,7,9,11,13,15},{16,18,20,22,24,26,28,30},{17..., dimensions={0} | all-to-all | bytes 458752 | tf_op jit(solution)/shard_map/all_to_all | solution.py:434
  73.2 0.1 reshape.291.rows_ref
  73.3 0.0 copy-start.10
  73.4 5.6 %shard_map.161 = bf16[8,2,7168]{2,1,0:T(2,128)(2,1)} custom-call(bf16[16,7168]{1,0:T(8,128)(2,1)S(1)} %reshape.291.rows_ref, bf16[128,7168]{1,0:T(8,128)(2,1)} %refs_0_.3, bf16[128,7168]{1,0:T(8,128)(2,1)} %collective-permute-done.10.refs_1_, bf16[128,7168]{1,0:T(8,128)(2,1)} %refs_2_.1, bf16[128,7168]{1,0:T(8,128)(2,1)} %collective-permute-done.11.refs_3_, ...), custom_call_target="tpu_custom_call" | custom-call | tf_op jit(solution)/shard_map/pallas_call | solution.py:266
  79.0 3.4 %all-to-all-start.3 = ((bf16[8,2,7168]{2,1,0:T(2,128)(2,1)}), bf16[8,2,7168]{2,1,0:T(2,128)(2,1)S(1)}, u32[]{:S(2)}, u32[]{:S(2)}) async-start(bf16[8,2,7168]{2,1,0:T(2,128)(2,1)} %shard_map.161), calls=%async_computation.3 | async-start | bytes 458752 | tf_op jit(solution)/shard_map/all_to_all | solution.py:446
  82.5 0.1 compare_select_fusion.4
  82.6 7.9 %all-to-all-done.3 = bf16[8,2,7168]{2,1,0:T(2,128)(2,1)S(1)} async-done(((bf16[8,2,7168]{2,1,0:T(2,128)(2,1)}), bf16[8,2,7168]{2,1,0:T(2,128)(2,1)S(1)}, u32[]{:S(2)}, u32[]{:S(2)}) %all-to-all-start.3) | async-done | bytes 229408 | tf_op jit(solution)/shard_map/all_to_all | solution.py:446
  90.5 0.3 multiply_reduce_fusion
  90.8 0.7 fusion.3
  (39 shorter events, 0.1 us)
Async XLA Ops:
  0.0 1.0 %copy-start = (bf16[1,2,128,576]{2,3,1,0:T(8,128)(2,1)S(1)}, bf16[1,2,128,576]{2,3,1,0:T(8,128)(2,1)}, u32[]{:S(2)}) copy-start(bf16[1,2,128,576]{2,3,1,0:T(8,128)(2,1)} %param.21) | copy-start | bytes 884740
  1.0 8.7 %copy-start.1 = (bf16[1,256,576]{1,2,0:T(8,128)(2,1)S(1)}, bf16[1,256,576]{1,2,0:T(8,128)(2,1)}, u32[]{:S(2)}) copy-start(bf16[1,256,576]{1,2,0:T(8,128)(2,1)} %param.16) | copy-start | bytes 884740
  1.0 11.5 %copy-start.2 = (bf16[1,2,576]{2,1,0:T(2,128)(2,1)S(1)}, bf16[1,2,576]{2,1,0:T(2,128)(2,1)}, u32[]{:S(2)}) copy-start(bf16[1,2,576]{2,1,0:T(2,128)(2,1)} %param.22) | copy-start | bytes 6916
  2.3 26.0 %all-to-all-start = ((bf16[16,32,576]{2,1,0:T(8,128)(2,1)}), bf16[16,32,576]{2,1,0:T(8,128)(2,1)S(1)}, u32[]{:S(2)}, u32[]{:S(2)}) async-start(bf16[16,32,576]{2,1,0:T(8,128)(2,1)} %shard_map.154.after_ref), calls=%async_computation | async-start | bytes 1310720 | tf_op jit(solution)/shard_map/all_to_all | solution.py:356
  9.8 8.1 %copy-start.3 = (s32[16]{0:T(128)S(1)}, s32[16]{0:T(128)}, u32[]{:S(2)}) copy-start(s32[16]{0:T(128)} %dest_ref.1) | copy-start | bytes 196
  9.8 19.4 %copy-start.4 = (s32[16]{0:T(128)S(1)}, s32[16]{0:T(128)}, u32[]{:S(2)}) copy-start(s32[16]{0:T(128)} %length_ref.2) | copy-start | bytes 196
  9.8 16.8 %collective-permute-start.1 = (bf16[576,256]{1,0:T(8,128)(2,1)S(1)}, bf16[576,256]{1,0:T(8,128)(2,1)S(1)}, u32[]{:S(2)}, u32[]{:S(2)}) collective-permute-start(bf16[576,256]{1,0:T(8,128)(2,1)S(1)} %shard_map.155.refs_0_), channel_id=1, source_target_pairs={{0,2},{1,3},{2,0},{3,1},{4,6},{5,7},{6,4},{7,5},{8,10},{9,11},{10,... | collective-permute-start | bytes 884744 | tf_op jit(solution)/shard_map/ppermute | solution.py:340
  11.8 16.5 %collective-permute-start = (bf16[576,256]{1,0:T(8,128)(2,1)S(1)}, bf16[576,256]{1,0:T(8,128)(2,1)S(1)}, u32[]{:S(2)}, u32[]{:S(2)}) collective-permute-start(bf16[576,256]{1,0:T(8,128)(2,1)S(1)} %shard_map.155.refs_0_), channel_id=1, source_target_pairs={{0,1},{1,0},{2,3},{3,2},{4,5},{5,4},{6,7},{7,6},{8,9},{9,8},{10,11... | collective-permute-start | bytes 884744 | tf_op jit(solution)/shard_map/ppermute | solution.py:340
  15.8 11.0 %collective-permute-start.3 = (bf16[48,576]{1,0:T(8,128)(2,1)S(1)}, bf16[48,576]{1,0:T(8,128)(2,1)S(1)}, u32[]{:S(2)}, u32[]{:S(2)}) collective-permute-start(bf16[48,576]{1,0:T(8,128)(2,1)S(1)} %get-tuple-element.18), channel_id=1, source_target_pairs={{0,1},{1,0},{2,3},{3,2},{4,5},{5,4},{6,7},{7,6},{8,9},{9,8},{10,11... | collective-permute-start | bytes 165896 | tf_op jit(solution)/shard_map/ppermute | solution.py:340
  16.4 11.5 %collective-permute-start.4 = (bf16[48,576]{1,0:T(8,128)(2,1)S(1)}, bf16[48,576]{1,0:T(8,128)(2,1)S(1)}, u32[]{:S(2)}, u32[]{:S(2)}) collective-permute-start(bf16[48,576]{1,0:T(8,128)(2,1)S(1)} %get-tuple-element.19), channel_id=1, source_target_pairs={{0,2},{1,3},{2,0},{3,1},{4,6},{5,7},{6,4},{7,5},{8,10},{9,11},{10,... | collective-permute-start | bytes 165896 | tf_op jit(solution)/shard_map/ppermute | solution.py:340
  16.5 11.8 %collective-permute-start.5 = (bf16[48,576]{1,0:T(8,128)(2,1)S(1)}, bf16[48,576]{1,0:T(8,128)(2,1)S(1)}, u32[]{:S(2)}, u32[]{:S(2)}) collective-permute-start(bf16[48,576]{1,0:T(8,128)(2,1)S(1)} %get-tuple-element.20), channel_id=1, source_target_pairs={{0,3},{1,2},{2,1},{3,0},{4,7},{5,6},{6,5},{7,4},{8,11},{9,10},{10,... | collective-permute-start | bytes 165896 | tf_op jit(solution)/shard_map/ppermute | solution.py:340
  26.6 1.7 %collective-permute-start.2 = (bf16[576,256]{1,0:T(8,128)(2,1)S(1)}, bf16[576,256]{1,0:T(8,128)(2,1)S(1)}, u32[]{:S(2)}, u32[]{:S(2)}) collective-permute-start(bf16[576,256]{1,0:T(8,128)(2,1)S(1)} %collective-permute-done.1.refs_2_), channel_id=1, source_target_pairs={{0,1},{1,0},{2,3},{3,2},{4,5},{5,4},{6,7},{7,6},{8,9},{9,8},{10,11... | collective-permute-start | bytes 884744 | tf_op jit(solution)/shard_map/ppermute | solution.py:340
  28.3 0.9 copy-start.5
  31.5 10.0 %collective-permute-start.6 = (bf16[4,16,640]{2,1,0:T(8,128)(2,1)S(1)}, bf16[4,16,640]{2,1,0:T(8,128)(2,1)S(1)}, u32[]{:S(2)}, u32[]{:S(2)}) collective-permute-start(bf16[4,16,640]{2,1,0:T(8,128)(2,1)S(1)} %get-tuple-element.24), channel_id=1, source_target_pairs={{0,4},{1,5},{2,6},{3,7},{4,0},{5,1},{6,2},{7,3},{8,12},{9,13},{10,... | collective-permute-start | bytes 245768 | tf_op jit(solution)/shard_map/ppermute | solution.py:340
  33.0 9.5 %collective-permute-start.7 = (bf16[4,16,640]{2,1,0:T(8,128)(2,1)S(1)}, bf16[4,16,640]{2,1,0:T(8,128)(2,1)S(1)}, u32[]{:S(2)}, u32[]{:S(2)}) collective-permute-start(bf16[4,16,640]{2,1,0:T(8,128)(2,1)S(1)} %get-tuple-element.25), channel_id=1, source_target_pairs={{0,8},{1,9},{2,10},{3,11},{4,12},{5,13},{6,14},{7,15},{8,0},{9,1},... | collective-permute-start | bytes 245768 | tf_op jit(solution)/shard_map/ppermute | solution.py:340
  35.4 7.2 %collective-permute-start.8 = (bf16[4,16,640]{2,1,0:T(8,128)(2,1)S(1)}, bf16[4,16,640]{2,1,0:T(8,128)(2,1)S(1)}, u32[]{:S(2)}, u32[]{:S(2)}) collective-permute-start(bf16[4,16,640]{2,1,0:T(8,128)(2,1)S(1)} %get-tuple-element.26), channel_id=1, source_target_pairs={{0,12},{1,13},{2,14},{3,15},{4,8},{5,9},{6,10},{7,11},{8,4},{9,5},... | collective-permute-start | bytes 245768 | tf_op jit(solution)/shard_map/ppermute | solution.py:340
  42.5 10.1 %copy-start.6 = (bf16[128,7168]{1,0:T(8,128)(2,1)S(1)}, bf16[128,7168]{1,0:T(8,128)(2,1)}, u32[]{:S(2)}) copy-start(bf16[128,7168]{1,0:T(8,128)(2,1)} %refs_0_.3) | copy-start | bytes 5505028
  42.5 10.7 %copy-start.8 = (bf16[7168]{0:T(1024)(128)(2,1)S(1)}, bf16[7168]{0:T(1024)(128)(2,1)}, u32[]{:S(2)}) copy-start(bf16[7168]{0:T(1024)(128)(2,1)} %param.26) | copy-start | bytes 43012
  42.5 19.0 %copy-start.7 = (bf16[1,2,7168]{2,1,0:T(2,128)(2,1)S(1)}, bf16[1,2,7168]{2,1,0:T(2,128)(2,1)}, u32[]{:S(2)}) copy-start(bf16[1,2,7168]{2,1,0:T(2,128)(2,1)} %param.23) | copy-start | bytes 86020
  46.4 1.5 %collective-permute-start.9 = (bf16[16,7168]{1,0:T(8,128)(2,1)S(1)}, bf16[16,7168]{1,0:T(8,128)(2,1)S(1)}, u32[]{:S(2)}, u32[]{:S(2)}) collective-permute-start(bf16[16,7168]{1,0:T(8,128)(2,1)S(1)} %get-tuple-element.28), channel_id=1, source_target_pairs={{0,1},{1,0},{2,3},{3,2},{4,5},{5,4},{6,7},{7,6},{8,9},{9,8},{10,11... | collective-permute-start | bytes 688136 | tf_op jit(solution)/shard_map/ppermute | solution.py:427
  48.8 12.5 %all-to-all-start.1 = ((bf16[8,2,7168]{2,1,0:T(2,128)(2,1)}), bf16[8,2,7168]{2,1,0:T(2,128)(2,1)S(1)}, u32[]{:S(2)}, u32[]{:S(2)}) async-start(bf16[8,2,7168]{2,1,0:T(2,128)(2,1)} %shard_map.160), calls=%async_computation.1 | async-start | bytes 458752 | tf_op jit(solution)/shard_map/all_to_all | solution.py:429
  52.6 20.8 %collective-permute-start.10 = (bf16[128,7168]{1,0:T(8,128)(2,1)S(1)}, bf16[128,7168]{1,0:T(8,128)(2,1)}, u32[]{:S(2)}, u32[]{:S(2)}) collective-permute-start(bf16[128,7168]{1,0:T(8,128)(2,1)S(1)} %copy-done.6), channel_id=1, source_target_pairs={{0,1},{1,0},{2,3},{3,2},{4,5},{5,4},{6,7},{7,6},{8,9},{9,8},{10,11... | collective-permute-start | bytes 5505032 | tf_op jit(solution)/shard_map/ppermute | solution.py:437
  52.7 20.7 %collective-permute-start.11 = (bf16[128,7168]{1,0:T(8,128)(2,1)}, bf16[128,7168]{1,0:T(8,128)(2,1)}, u32[]{:S(2)}, u32[]{:S(2)}) collective-permute-start(bf16[128,7168]{1,0:T(8,128)(2,1)} %refs_2_.1), channel_id=1, source_target_pairs={{0,1},{1,0},{2,3},{3,2},{4,5},{5,4},{6,7},{7,6},{8,9},{9,8},{10,11... | collective-permute-start | bytes 5505032 | tf_op jit(solution)/shard_map/ppermute | solution.py:437
  53.2 20.2 %collective-permute-start.12 = (bf16[128,7168]{1,0:T(8,128)(2,1)}, bf16[128,7168]{1,0:T(8,128)(2,1)}, u32[]{:S(2)}, u32[]{:S(2)}) collective-permute-start(bf16[128,7168]{1,0:T(8,128)(2,1)} %refs_4_.1), channel_id=1, source_target_pairs={{0,1},{1,0},{2,3},{3,2},{4,5},{5,4},{6,7},{7,6},{8,9},{9,8},{10,11... | collective-permute-start | bytes 5505032 | tf_op jit(solution)/shard_map/ppermute | solution.py:437
  73.3 9.1 %copy-start.9 = (f32[1,2,1]{1,2,0:T(1,128)S(1)}, f32[1,2,1]{1,2,0:T(1,128)}, u32[]{:S(2)}) copy-start(f32[1,2,1]{1,2,0:T(1,128)} %param.28) | copy-start | bytes 28
  73.3 9.1 %copy-start.10 = (s32[1,2,1]{1,2,0:T(1,128)S(1)}, s32[1,2,1]{1,2,0:T(1,128)}, u32[]{:S(2)}) copy-start(s32[1,2,1]{1,2,0:T(1,128)} %param.27) | copy-start | bytes 28
  79.0 11.4 %all-to-all-start.3 = ((bf16[8,2,7168]{2,1,0:T(2,128)(2,1)}), bf16[8,2,7168]{2,1,0:T(2,128)(2,1)S(1)}, u32[]{:S(2)}, u32[]{:S(2)}) async-start(bf16[8,2,7168]{2,1,0:T(2,128)(2,1)} %shard_map.161), calls=%async_computation.3 | async-start | bytes 458752 | tf_op jit(solution)/shard_map/all_to_all | solution.py:446

commit v6 on v5

--- a/solution.py
+++ b/solution.py
@@ -31,16 +31,37 @@
     return first, second, third
 
 
+def pack(rows):
+    heads, width = rows.shape
+    tail = width - KVR
+    beside = LANES // tail
+    high = heads // beside
+    pieces = [rows[:, start : start + LANES] for start in range(0, KVR, LANES)]
+    pieces.append(
+        jnp.concatenate([rows[at * high : (at + 1) * high, KVR:] for at in range(beside)], axis=1)
+    )
+    return jnp.concatenate(pieces, axis=0)
+
+
+def unpack(packed, heads, tail):
+    pieces = [packed[at * heads : (at + 1) * heads] for at in range(KVR // LANES)]
+    rest = packed[heads * (KVR // LANES) :]
+    tails = [rest[:, start : start + tail] for start in range(0, LANES, tail)]
+    return jnp.concatenate(pieces, axis=1), jnp.concatenate(tails, axis=0)
+
+
 def spread_kernel(query_hbm, spread_hbm, query_ref, blocks_ref, sems):
-    peers, rows, width = spread_hbm.shape
+    peers = spread_hbm.shape[0]
     planes = peers // PLANE
+    width, heads = query_ref.shape
     load = pltpu.make_async_copy(query_hbm.at[1], query_ref, sems.at[0])
     load.start()
     load.wait()
-    by_peer = query_ref[...].astype(f32).T.reshape(planes, PLANE, rows // planes, width)
+    by_peer = query_ref[...].astype(f32).T.reshape(planes, PLANE, heads // peers, width)
     copies = []
     for column in range(PLANE):
-        blocks_ref[column] = by_peer[:, column].reshape(rows, width).astype(bf16)
+        rows = by_peer[:, column].reshape(heads // PLANE, width)
+        blocks_ref[column] = pack(rows).astype(bf16)
         for plane in range(planes):
             peer = plane * PLANE + column
             copies.append(
@@ -49,13 +70,6 @@
             copies[-1].start()
     for copy in copies:
         copy.wait()
-
-
-def stage_kernel(after_ref, keys_hbm, staged_hbm, sem):
-    del after_ref
-    copy = pltpu.make_async_copy(keys_hbm, staged_hbm, sem)
-    copy.start()
-    copy.wait()
 
 
 def prefetch_kernel(after_ref, *refs):
@@ -98,9 +112,15 @@
     planes, _, per_peer, latent = mixed_ref.shape
     rows = planes * per_peer
     column = device_ref[0] % PLANE
+    new_key = fresh_ref[1:2].astype(f32)
+    rest = jnp.concatenate(
+        [new_key[:, KVR:], jnp.zeros((1, 2 * KVR - new_key.shape[1]), f32)], axis=1
+    )
+    line = lax.broadcasted_iota(jnp.int32, (FRESH_ROWS, KVR), 0)
+    key_rows = jnp.where(line == 0, new_key[:, :KVR], jnp.where(line == 1, rest, 0.0)).astype(bf16)
     for at, message_ref in enumerate(message_refs):
-        message_ref[:rows, :latent] = mixed_ref[:, column ^ at].reshape(rows, latent).astype(bf16)
-        message_ref[rows:] = jnp.broadcast_to(fresh_ref[1:2], message_ref[rows:].shape)
+        message_ref[:rows] = mixed_ref[:, column ^ at].reshape(rows, latent).astype(bf16)
+        message_ref[rows:] = key_rows
 
 
 def prompt_kernel(device_ref, dest_ref, length_ref, *refs):
@@ -109,6 +129,7 @@
     planes, _, rows, width = stage_ref.shape
     per_peer, chunk = rows // 2, width - KVR
     heads = planes * per_peer
+    tail = key_refs[0].shape[0] - KVR
     device = device_ref[0]
     sources = [dest_ref[device ^ at] for at in range(PLANE)] + [device ^ at for at in range(PLANE)]
     loads = [
@@ -122,8 +143,10 @@
     scores = []
     for at in range(PLANE):
         prompt = device ^ at
-        query = query_ref[at]
-        score = jnp.dot(query, key_refs[at][...], preferred_element_type=f32) * softmax_scale
+        latent, rest = unpack(query_ref[at], heads, tail)
+        score = jnp.dot(latent, key_refs[at][:KVR], preferred_element_type=f32)
+        score += jnp.dot(rest, key_refs[at][KVR:], preferred_element_type=f32)
+        score *= softmax_scale
         position = lax.broadcasted_iota(jnp.int32, score.shape, 1)
         scores.append(jnp.where(position < length_ref[prompt], score, -jnp.inf))
     scores = jnp.concatenate(scores, axis=0)
@@ -144,9 +167,12 @@
         stage_ref[:, at, :, :KVR] = jnp.concatenate(
             [fold(mixed * scale[part]), fold(resident)], axis=1
         ).astype(bf16)
-        fresh = message_refs[at][heads : heads + FRESH_ROWS].astype(f32)[:1]
-        fresh_score = softmax_scale * jnp.sum(
-            query_ref[PLANE + at].astype(f32) * fresh, axis=1, keepdims=True
+        fresh = message_refs[at][heads : heads + FRESH_ROWS].astype(f32)
+        fresh, fresh_rest = fresh[0:1], fresh[1:2, :tail]
+        latent, rest = unpack(query_ref[PLANE + at], heads, tail)
+        fresh_score = softmax_scale * (
+            jnp.sum(latent.astype(f32) * fresh, axis=1, keepdims=True)
+            + jnp.sum(rest.astype(f32) * fresh_rest, axis=1, keepdims=True)
         )
         stats = jnp.zeros((heads, chunk), f32)
         for lane_at, value in enumerate(three_parts(log_sum[part]) + three_parts(fresh_score)):
@@ -163,8 +189,7 @@
 
 
 def pair_kernel(keep_ref, other_ref, pair_ref):
-    total = keep_ref[...] + other_ref[...].astype(f32)
-    pair_ref[...] = total.reshape(pair_ref.shape).astype(bf16)
+    pair_ref[...] = (keep_ref[...] + other_ref[...].astype(f32)).astype(bf16)
 
 
 def heads_kernel(row_ref, column_ref, peer_ref, upward_ref, proj_ref, *refs):
@@ -216,8 +241,9 @@
     )
     for start in range(0, proj_ref.shape[1], BLOCK):
         part = jnp.dot(value_rows, proj_ref[:, start : start + BLOCK], preferred_element_type=f32)
-        keep_ref[:, start : start + BLOCK] = part[:peers]
-        send_ref[:, start : start + BLOCK] = part[peers:].astype(bf16)
+        columns = slice(start, start + BLOCK)
+        keep_ref[:, :, columns] = part[:peers].reshape(peers // 2, 2, BLOCK)
+        send_ref[:, :, columns] = part[peers:].reshape(peers // 2, 2, BLOCK).astype(bf16)
 
 
 def expert_kernel(rows_ref, *refs):
@@ -261,6 +287,10 @@
     return pltpu.with_memory_space_constraint(value, pltpu.VMEM)
 
 
+def distant(value):
+    return pltpu.with_memory_space_constraint(value, pltpu.HBM)
+
+
 def call(kernel, outputs, operands, far=(), scratch=(), cost=None):
     specs = [scalars if operand.ndim == 1 else whole for operand in operands]
     return pl.pallas_call(
@@ -273,7 +303,7 @@
         cost_estimate=cost,
     )(
         *[operand if operand.ndim == 1 else near(operand) for operand in operands],
-        *[pltpu.with_memory_space_constraint(operand, pltpu.HBM) for operand in far],
+        *far,
     )
 
 
@@ -287,7 +317,7 @@
         scratch_shapes=scratch,
         compiler_params=pltpu.CompilerParams(vmem_limit_bytes=16 << 20),
         cost_estimate=cost,
-    )(*operands)
+    )(*map(distant, operands))
 
 
 def prefetch(after, weights):
@@ -298,7 +328,7 @@
         out_specs=[whole] * len(weights),
         scratch_shapes=[pltpu.SemaphoreType.DMA((len(weights),))],
         compiler_params=pltpu.CompilerParams(vmem_limit_bytes=16 << 20),
-    )(after, *[pltpu.with_memory_space_constraint(weight, pltpu.HBM) for weight in weights])
+    )(after, *map(distant, weights))
 
 
 def shards(
@@ -342,7 +372,7 @@
     own_device = device.astype(jnp.int32)[None]
 
     flipped = jnp.swapaxes(queries[0], 1, 2)
-    spread_shape = (devices, planes * per_peer, width)
+    spread_shape = (devices, heads // PLANE * width // LANES, LANES)
     spread_rows = call_far(
         spread_kernel,
         jax.ShapeDtypeStruct(spread_shape, bf16),
@@ -357,14 +387,7 @@
 
     short = pl.CostEstimate(flops=1, bytes_accessed=1, transcendentals=0)
     flipped_keys = jnp.swapaxes(handoff_rows[0], 0, 1)
-    staged_keys = call_far(
-        stage_kernel,
-        jax.ShapeDtypeStruct(flipped_keys.shape, bf16),
-        [spread_rows, flipped_keys],
-        [pltpu.SemaphoreType.DMA],
-        short,
-    )
-    plane_keys = [staged_keys]
+    plane_keys = [flipped_keys]
     bit = PLANE // 2
     while bit:
         crossing = [toward(keys, bit) for keys in plane_keys]
@@ -373,9 +396,9 @@
     flipped_cache = jnp.swapaxes(resident_cache[0], 0, 1)
     messages = call(
         resident_kernel,
-        [((planes * per_peer + FRESH_ROWS, width), bf16)] * PLANE,
+        [((planes * per_peer + FRESH_ROWS, KVR), bf16)] * PLANE,
         [own_device, resident_len, new_latent[0]],
-        [spread_rows, flipped, flipped_cache],
+        [spread_rows, distant(flipped), distant(flipped_cache)],
         [
             pltpu.VMEM((width, heads), bf16),
             pltpu.VMEM(flipped_cache.shape, bf16),
@@ -419,7 +442,7 @@
     )
     keep, send = call(
         heads_kernel,
-        [((devices, model), f32), ((devices, model), bf16)],
+        [((chips, 2, model), f32), ((chips, 2, model), bf16)],
         [row_table, column_table, peers[None], upward, projection, *payloads],
         scratch=[pltpu.VMEM((devices, 2 * per_peer, KVR + chunk), bf16)],
     )
@@ -439,7 +462,7 @@
         expert_kernel,
         [((chips, 2, model), bf16)],
         [own_rows.reshape(devices, model)],
-        experts,
+        [matrix if at == 1 else distant(matrix) for at, matrix in enumerate(experts)],
         [pltpu.VMEM((2 * gate_proj.shape[0], model), bf16)] * 3
         + [pltpu.SemaphoreType.DMA((20,))],
     )

time: 92 us -> 89.3 us (0.971)
  local copies, waits for them, and re-layouts: 2.51 us -> 0.69 us
    unnamed x22 -> x16, local copies, waits for them, and re-layouts: 1.87 us -> 0.04 us
    ppermute x9, waiting for transfers between devices: 10.8 us -> 9.84 us  [shards(): lax.ppermute(value, 'ep', [(i, i ^ bits) for i in range(devices)])]
    pallas_call x2 -> x1, Pallas kernels: 1.39 us -> 2.11 us  [call_far(): pl.pallas_call(kernel, out_shape=shapes, in_specs=[far] * len(operands),...]
  transfers between devices with their start and end apart: 16 -> 16, of which waited for: 7 -> 8; matrix products, arithmetic and copies ran while one was open for 2% -> 2% of each run, Pallas kernels for 10% -> 10%
where the time goes in v6:
time: 89.3 us; the launch traced here: 88.7 us
  waiting for transfers between devices  27.4 us (31%)
  starting transfers between devices  23.7 us (27%)
  Pallas kernels  23 us (26%)
  blocking collectives  11.3 us (13%)
  other arithmetic  1.77 us (2%)
  between operations  0.93 us (1%)
    pallas_call x5, Pallas kernels, call(): pl.pallas_call(kernel, out_shape=[pltpu.VMEM(shape, dtype) for shape, dty...  15.4 us
    all_to_all x1, blocking collectives, shards(): own_rows = exchange_core(jnp.broadcast_to(normed[None], (chips, 2, model)))  11.3 us
    ppermute x9, waiting for transfers between devices, shards(): lax.ppermute(value, 'ep', [(i, i ^ bits) for i in range(devices)])  9.84 us
    ppermute x9, starting transfers between devices, shards(): lax.ppermute(value, 'ep', [(i, i ^ bits) for i in range(devices)])  8.45 us
    all_to_all x1, waiting for transfers between devices, shards(): attention = jnp.sum(exchange_core(pair).astype(f32), axis=0)  8.14 us
    all_to_all x1, waiting for transfers between devices, shards(): returned = exchange_core(part)  7.9 us
    all_to_all x1, starting transfers between devices, shards(): spread = exchange(spread_rows)  7.37 us
    pallas_call x1, Pallas kernels, prefetch(): pl.pallas_call(prefetch_kernel, out_shape=[pltpu.VMEM(weight.shape, weigh...  5.53 us
  transfers between devices with their start and end apart: 16, of which 8 were waited for; matrix products, arithmetic and copies ran while one was open for 2% of the time, Pallas kernels for 10%

profile of v6, /device:TPU:0, one launch (start us, length us, event | category | flops | bytes accessed | tf_op | source)
XLA Modules:
  0.0 88.7 jit_solution(4928986652990235790)
XLA Ops:
  0.0 2.1 %shard_map.154.after_ref = bf16[16,144,128]{2,1,0:T(8,128)(2,1)} custom-call(bf16[2,576,128]{2,1,0:T(8,128)(2,1)} %bitcast.42), custom_call_target="tpu_custom_call" | custom-call | tf_op jit(solution)/shard_map/pallas_call | solution.py:312
  2.1 7.4 %all-to-all-start = ((bf16[16,144,128]{2,1,0:T(8,128)(2,1)}), bf16[16,144,128]{2,1,0:T(8,128)(2,1)S(1)}, u32[]{:S(2)}, u32[]{:S(2)}) async-start(bf16[16,144,128]{2,1,0:T(8,128)(2,1)} %shard_map.154.after_ref), calls=%async_computation | async-start | bytes 1179648 | tf_op jit(solution)/shard_map/all_to_all | solution.py:386
  9.5 0.0 copy-start.2
  9.5 0.0 copy-start.3
  9.5 2.0 %collective-permute-start.1 = (bf16[576,256]{1,0:T(8,128)(2,1)S(1)}, bf16[576,256]{1,0:T(8,128)(2,1)S(1)}, u32[]{:S(2)}, u32[]{:S(2)}) collective-permute-start(bf16[576,256]{1,0:T(8,128)(2,1)S(1)} %bitcast.36), channel_id=1, source_target_pairs={{0,2},{1,3},{2,0},{3,1},{4,6},{5,7},{6,4},{7,5},{8,10},{9,11},{10,... | collective-permute-start | bytes 884744 | tf_op jit(solution)/shard_map/ppermute | solution.py:370
  12.2 3.4 %shard_map.155 = (bf16[48,512]{1,0:T(8,128)(2,1)S(1)}, bf16[48,512]{1,0:T(8,128)(2,1)S(1)}, bf16[48,512]{1,0:T(8,128)(2,1)S(1)}, bf16[48,512]{1,0:T(8,128)(2,1)S(1)}) custom-call(s32[1]{0:T(128)} %bitcast.device_ref, s32[1]{0:T(128)S(6)} %copy.18.length_ref, bf16[2,576]{1,0:T(2,128)(2,1)S(1)} %bitcast.39, bf16[16,144,128]{2,1,0:T(8,128)(2,1)} %shard_map.154.after_ref, ...), custom_call_target="tpu_custom_call" | custom-call | flops 1 | bytes 1 | tf_op jit(solution)/shard_map/pallas_call | solution.py:296
  15.6 0.6 collective-permute-start.3
  16.2 0.1 collective-permute-start.4
  16.3 1.3 %collective-permute-start.5 = (bf16[48,512]{1,0:T(8,128)(2,1)S(1)}, bf16[48,512]{1,0:T(8,128)(2,1)S(1)}, u32[]{:S(2)}, u32[]{:S(2)}) collective-permute-start(bf16[48,512]{1,0:T(8,128)(2,1)S(1)} %get-tuple-element.20), channel_id=1, source_target_pairs={{0,3},{1,2},{2,1},{3,0},{4,7},{5,6},{6,5},{7,4},{8,11},{9,10},{10,... | collective-permute-start | bytes 147464 | tf_op jit(solution)/shard_map/ppermute | solution.py:370
  17.6 0.2 select_reduce_fusion
  17.8 0.1 broadcast_in_dim.41
  17.9 0.1 stack_reshape.7
  17.9 0.1 broadcast_in_dim.22
  18.0 0.1 stack_reshape.6
  18.1 7.6 %collective-permute-done.1.refs_2_ = bf16[576,256]{1,0:T(8,128)(2,1)S(1)} collective-permute-done((bf16[576,256]{1,0:T(8,128)(2,1)S(1)}, bf16[576,256]{1,0:T(8,128)(2,1)S(1)}, u32[]{:S(2)}, u32[]{:S(2)}) %collective-permute-start.1) | collective-permute-done | bytes 294944 | tf_op jit(solution)/shard_map/ppermute | solution.py:370
  25.8 0.1 copy.17.row_ref
  25.9 0.8 collective-permute-done.4.refs_6_
  26.8 0.1 collective-permute-done.5.refs_7_
  26.9 0.4 collective-permute-done.2.refs_3_
  27.3 1.8 %shard_map.156 = (bf16[4,16,640]{2,1,0:T(8,128)(2,1)S(1)}, bf16[4,16,640]{2,1,0:T(8,128)(2,1)S(1)}, bf16[4,16,640]{2,1,0:T(8,128)(2,1)S(1)}, bf16[4,16,640]{2,1,0:T(8,128)(2,1)S(1)}) custom-call(s32[1]{0:T(128)} %bitcast.device_ref, s32[16]{0:T(128)S(1)} %copy-done.2, s32[16]{0:T(128)S(1)} %copy-done.3, bf16[576,256]{1,0:T(8,128)(2,1)S(1)} %bitcast.38, ...), custom_call_target="tpu_custom_call" | custom-call | tf_op jit(solution)/shard_map/pallas_call | solution.py:296
  29.1 1.4 %collective-permute-start.6 = (bf16[4,16,640]{2,1,0:T(8,128)(2,1)S(1)}, bf16[4,16,640]{2,1,0:T(8,128)(2,1)S(1)}, u32[]{:S(2)}, u32[]{:S(2)}) collective-permute-start(bf16[4,16,640]{2,1,0:T(8,128)(2,1)S(1)} %get-tuple-element.24), channel_id=1, source_target_pairs={{0,4},{1,5},{2,6},{3,7},{4,0},{5,1},{6,2},{7,3},{8,12},{9,13},{10,... | collective-permute-start | bytes 245768 | tf_op jit(solution)/shard_map/ppermute | solution.py:370
  30.5 2.5 %collective-permute-start.7 = (bf16[4,16,640]{2,1,0:T(8,128)(2,1)S(1)}, bf16[4,16,640]{2,1,0:T(8,128)(2,1)S(1)}, u32[]{:S(2)}, u32[]{:S(2)}) collective-permute-start(bf16[4,16,640]{2,1,0:T(8,128)(2,1)S(1)} %get-tuple-element.25), channel_id=1, source_target_pairs={{0,8},{1,9},{2,10},{3,11},{4,12},{5,13},{6,14},{7,15},{8,0},{9,1},... | collective-permute-start | bytes 245768 | tf_op jit(solution)/shard_map/ppermute | solution.py:370
  33.0 0.6 collective-permute-start.8
  33.6 5.5 %shard_map.157 = (bf16[8,512,128]{2,1,0:T(8,128)(2,1)S(1)}, bf16[1024,7168]{1,0:T(8,128)(2,1)S(1)}) custom-call(bf16[4,16,640]{2,1,0:T(8,128)(2,1)S(1)} %get-tuple-element.21.after_ref.refs_0_, bf16[8,512,128]{2,1,0:T(8,128)(2,1)} %refs_0_.2, bf16[1024,7168]{1,0:T(8,128)(2,1)} %bitcast.40), custom_call_target="tpu_custom_call" | custom-call | tf_op jit(solution)/shard_map/pallas_call | solution.py:324
  39.1 0.8 collective-permute-done.7.refs_2_
  40.0 4.0 %shard_map.158 = (f32[8,2,7168]{2,1,0:T(2,128)S(1)}, bf16[8,2,7168]{2,1,0:T(2,128)(2,1)S(1)}) custom-call(s32[256,3]{1,0:T(8,128)S(1)} %copy.17.row_ref, s32[3,256]{1,0:T(4,128)S(1)} %pad_add_fusion.1.column_ref, s32[1,16]{1,0:T(1,128)S(1)} %iota_xor_fusion.peer_ref, bf16[8,512,128]{2,1,0:T(8,128)(2,1)S(1)} %get-tuple-element.22.upward_ref, ...), custom_call_target="tpu_custom_call" | custom-call | tf_op jit(solution)/shard_map/pallas_call | solution.py:296
  43.9 0.1 collective-permute-start.9
  44.0 1.5 %collective-permute-done.9.other_ref = bf16[8,2,7168]{2,1,0:T(2,128)(2,1)S(1)} collective-permute-done((bf16[8,2,7168]{2,1,0:T(2,128)(2,1)S(1)}, bf16[8,2,7168]{2,1,0:T(2,128)(2,1)S(1)}, u32[]{:S(2)}, u32[]{:S(2)}) %collective-permute-start.9) | collective-permute-done | bytes 229408 | tf_op jit(solution)/shard_map/ppermute | solution.py:450
  45.5 0.9 %shard_map.159 = bf16[8,2,7168]{2,1,0:T(2,128)(2,1)} custom-call(f32[8,2,7168]{2,1,0:T(2,128)S(1)} %get-tuple-element.27.keep_ref, bf16[8,2,7168]{2,1,0:T(2,128)(2,1)S(1)} %collective-permute-done.9.other_ref), custom_call_target="tpu_custom_call" | custom-call | tf_op jit(solution)/shard_map/pallas_call | solution.py:296
  46.4 3.8 %all-to-all-start.1 = ((bf16[8,2,7168]{2,1,0:T(2,128)(2,1)}), bf16[8,2,7168]{2,1,0:T(2,128)(2,1)S(1)}, u32[]{:S(2)}, u32[]{:S(2)}) async-start(bf16[8,2,7168]{2,1,0:T(2,128)(2,1)} %shard_map.159), calls=%async_computation.1 | async-start | bytes 458752 | tf_op jit(solution)/shard_map/all_to_all | solution.py:452
  50.1 0.0 collective-permute-start.10
  50.2 0.5 collective-permute-start.11
  50.7 0.1 collective-permute-start.12
  50.7 8.1 %all-to-all-done.1 = bf16[8,2,7168]{2,1,0:T(2,128)(2,1)S(1)} async-done(((bf16[8,2,7168]{2,1,0:T(2,128)(2,1)}), bf16[8,2,7168]{2,1,0:T(2,128)(2,1)S(1)}, u32[]{:S(2)}, u32[]{:S(2)}) %all-to-all-start.1) | async-done | bytes 229408 | tf_op jit(solution)/shard_map/all_to_all | solution.py:452
  58.9 0.2 convert_reduce_fusion
  59.1 0.2 fusion.2
  59.3 0.1 fusion.4
  59.4 0.1 broadcast_in_dim.44
  59.5 11.3 %all_to_all.20 = bf16[8,2,7168]{2,1,0:T(2,128)(2,1)S(1)} all-to-all(bf16[8,2,7168]{2,1,0:T(2,128)(2,1)S(1)} %broadcast_in_dim.44), channel_id=1, replica_groups={{0,2,4,6,8,10,12,14},{1,3,5,7,9,11,13,15},{16,18,20,22,24,26,28,30},{17..., dimensions={0} | all-to-all | bytes 458752 | tf_op jit(solution)/shard_map/all_to_all | solution.py:457
  70.8 0.1 reshape.291.rows_ref
  70.9 0.0 copy-start.6
  70.9 0.0 copy-start.7
  70.9 5.4 %shard_map.160 = bf16[8,2,7168]{2,1,0:T(2,128)(2,1)} custom-call(bf16[16,7168]{1,0:T(8,128)(2,1)S(1)} %reshape.291.rows_ref, bf16[128,7168]{1,0:T(8,128)(2,1)} %refs_0_.3, bf16[128,7168]{1,0:T(8,128)(2,1)S(1)} %collective-permute-done.10.refs_1_, bf16[128,7168]{1,0:T(8,128)(2,1)} %refs_2_.1, bf16[128,7168]{1,0:T(8,128)(2,1)} %collective-permute-done.11.refs_3_, ...), custom_call_target="tpu_custom_call" | custom-call | tf_op jit(solution)/shard_map/pallas_call | solution.py:296
  76.3 3.4 %all-to-all-start.3 = ((bf16[8,2,7168]{2,1,0:T(2,128)(2,1)}), bf16[8,2,7168]{2,1,0:T(2,128)(2,1)S(1)}, u32[]{:S(2)}, u32[]{:S(2)}) async-start(bf16[8,2,7168]{2,1,0:T(2,128)(2,1)} %shard_map.160), calls=%async_computation.3 | async-start | bytes 458752 | tf_op jit(solution)/shard_map/all_to_all | solution.py:469
  79.8 0.1 compare_select_fusion.4
  79.9 7.9 %all-to-all-done.3 = bf16[8,2,7168]{2,1,0:T(2,128)(2,1)S(1)} async-done(((bf16[8,2,7168]{2,1,0:T(2,128)(2,1)}), bf16[8,2,7168]{2,1,0:T(2,128)(2,1)S(1)}, u32[]{:S(2)}, u32[]{:S(2)}) %all-to-all-start.3) | async-done | bytes 229408 | tf_op jit(solution)/shard_map/all_to_all | solution.py:469
  87.8 0.3 multiply_reduce_fusion
  88.1 0.7 fusion.3
  (32 shorter events, 0.1 us)
Async XLA Ops:
  0.0 9.5 %copy-start = (bf16[1,256,576]{1,2,0:T(8,128)(2,1)S(1)}, bf16[1,256,576]{1,2,0:T(8,128)(2,1)}, u32[]{:S(2)}) copy-start(bf16[1,256,576]{1,2,0:T(8,128)(2,1)} %param.16) | copy-start | bytes 884740
  0.0 12.2 %copy-start.1 = (bf16[1,2,576]{2,1,0:T(2,128)(2,1)S(1)}, bf16[1,2,576]{2,1,0:T(2,128)(2,1)}, u32[]{:S(2)}) copy-start(bf16[1,2,576]{2,1,0:T(2,128)(2,1)} %param.22) | copy-start | bytes 6916
  2.1 25.2 %all-to-all-start = ((bf16[16,144,128]{2,1,0:T(8,128)(2,1)}), bf16[16,144,128]{2,1,0:T(8,128)(2,1)S(1)}, u32[]{:S(2)}, u32[]{:S(2)}) async-start(bf16[16,144,128]{2,1,0:T(8,128)(2,1)} %shard_map.154.after_ref), calls=%async_computation | async-start | bytes 1179648 | tf_op jit(solution)/shard_map/all_to_all | solution.py:386
  9.5 8.1 %copy-start.2 = (s32[16]{0:T(128)S(1)}, s32[16]{0:T(128)}, u32[]{:S(2)}) copy-start(s32[16]{0:T(128)} %dest_ref.1) | copy-start | bytes 196
  9.5 17.8 %copy-start.3 = (s32[16]{0:T(128)S(1)}, s32[16]{0:T(128)}, u32[]{:S(2)}) copy-start(s32[16]{0:T(128)} %length_ref.2) | copy-start | bytes 196
  9.5 16.2 %collective-permute-start.1 = (bf16[576,256]{1,0:T(8,128)(2,1)S(1)}, bf16[576,256]{1,0:T(8,128)(2,1)S(1)}, u32[]{:S(2)}, u32[]{:S(2)}) collective-permute-start(bf16[576,256]{1,0:T(8,128)(2,1)S(1)} %bitcast.36), channel_id=1, source_target_pairs={{0,2},{1,3},{2,0},{3,1},{4,6},{5,7},{6,4},{7,5},{8,10},{9,11},{10,... | collective-permute-start | bytes 884744 | tf_op jit(solution)/shard_map/ppermute | solution.py:370
  11.5 15.4 %collective-permute-start = (bf16[576,256]{1,0:T(8,128)(2,1)S(1)}, bf16[576,256]{1,0:T(8,128)(2,1)S(1)}, u32[]{:S(2)}, u32[]{:S(2)}) collective-permute-start(bf16[576,256]{1,0:T(8,128)(2,1)S(1)} %bitcast.37), channel_id=1, source_target_pairs={{0,1},{1,0},{2,3},{3,2},{4,5},{5,4},{6,7},{7,6},{8,9},{9,8},{10,11... | collective-permute-start | bytes 884744 | tf_op jit(solution)/shard_map/ppermute | solution.py:370
  15.6 10.3 %collective-permute-start.3 = (bf16[48,512]{1,0:T(8,128)(2,1)S(1)}, bf16[48,512]{1,0:T(8,128)(2,1)S(1)}, u32[]{:S(2)}, u32[]{:S(2)}) collective-permute-start(bf16[48,512]{1,0:T(8,128)(2,1)S(1)} %get-tuple-element.18), channel_id=1, source_target_pairs={{0,1},{1,0},{2,3},{3,2},{4,5},{5,4},{6,7},{7,6},{8,9},{9,8},{10,11... | collective-permute-start | bytes 147464 | tf_op jit(solution)/shard_map/ppermute | solution.py:370
  16.2 10.6 %collective-permute-start.4 = (bf16[48,512]{1,0:T(8,128)(2,1)S(1)}, bf16[48,512]{1,0:T(8,128)(2,1)S(1)}, u32[]{:S(2)}, u32[]{:S(2)}) collective-permute-start(bf16[48,512]{1,0:T(8,128)(2,1)S(1)} %get-tuple-element.19), channel_id=1, source_target_pairs={{0,2},{1,3},{2,0},{3,1},{4,6},{5,7},{6,4},{7,5},{8,10},{9,11},{10,... | collective-permute-start | bytes 147464 | tf_op jit(solution)/shard_map/ppermute | solution.py:370
  16.3 10.6 %collective-permute-start.5 = (bf16[48,512]{1,0:T(8,128)(2,1)S(1)}, bf16[48,512]{1,0:T(8,128)(2,1)S(1)}, u32[]{:S(2)}, u32[]{:S(2)}) collective-permute-start(bf16[48,512]{1,0:T(8,128)(2,1)S(1)} %get-tuple-element.20), channel_id=1, source_target_pairs={{0,3},{1,2},{2,1},{3,0},{4,7},{5,6},{6,5},{7,4},{8,11},{9,10},{10,... | collective-permute-start | bytes 147464 | tf_op jit(solution)/shard_map/ppermute | solution.py:370
  25.7 1.6 %collective-permute-start.2 = (bf16[576,256]{1,0:T(8,128)(2,1)S(1)}, bf16[576,256]{1,0:T(8,128)(2,1)S(1)}, u32[]{:S(2)}, u32[]{:S(2)}) collective-permute-start(bf16[576,256]{1,0:T(8,128)(2,1)S(1)} %collective-permute-done.1.refs_2_), channel_id=1, source_target_pairs={{0,1},{1,0},{2,3},{3,2},{4,5},{5,4},{6,7},{7,6},{8,9},{9,8},{10,11... | collective-permute-start | bytes 884744 | tf_op jit(solution)/shard_map/ppermute | solution.py:370
  29.1 10.0 %collective-permute-start.6 = (bf16[4,16,640]{2,1,0:T(8,128)(2,1)S(1)}, bf16[4,16,640]{2,1,0:T(8,128)(2,1)S(1)}, u32[]{:S(2)}, u32[]{:S(2)}) collective-permute-start(bf16[4,16,640]{2,1,0:T(8,128)(2,1)S(1)} %get-tuple-element.24), channel_id=1, source_target_pairs={{0,4},{1,5},{2,6},{3,7},{4,0},{5,1},{6,2},{7,3},{8,12},{9,13},{10,... | collective-permute-start | bytes 245768 | tf_op jit(solution)/shard_map/ppermute | solution.py:370
  30.5 9.5 %collective-permute-start.7 = (bf16[4,16,640]{2,1,0:T(8,128)(2,1)S(1)}, bf16[4,16,640]{2,1,0:T(8,128)(2,1)S(1)}, u32[]{:S(2)}, u32[]{:S(2)}) collective-permute-start(bf16[4,16,640]{2,1,0:T(8,128)(2,1)S(1)} %get-tuple-element.25), channel_id=1, source_target_pairs={{0,8},{1,9},{2,10},{3,11},{4,12},{5,13},{6,14},{7,15},{8,0},{9,1},... | collective-permute-start | bytes 245768 | tf_op jit(solution)/shard_map/ppermute | solution.py:370
  33.0 7.0 %collective-permute-start.8 = (bf16[4,16,640]{2,1,0:T(8,128)(2,1)S(1)}, bf16[4,16,640]{2,1,0:T(8,128)(2,1)S(1)}, u32[]{:S(2)}, u32[]{:S(2)}) collective-permute-start(bf16[4,16,640]{2,1,0:T(8,128)(2,1)S(1)} %get-tuple-element.26), channel_id=1, source_target_pairs={{0,12},{1,13},{2,14},{3,15},{4,8},{5,9},{6,10},{7,11},{8,4},{9,5},... | collective-permute-start | bytes 245768 | tf_op jit(solution)/shard_map/ppermute | solution.py:370
  39.9 10.8 %copy-start.5 = (bf16[7168]{0:T(1024)(128)(2,1)S(1)}, bf16[7168]{0:T(1024)(128)(2,1)}, u32[]{:S(2)}) copy-start(bf16[7168]{0:T(1024)(128)(2,1)} %param.26) | copy-start | bytes 43012
  39.9 19.1 %copy-start.4 = (bf16[1,2,7168]{2,1,0:T(2,128)(2,1)S(1)}, bf16[1,2,7168]{2,1,0:T(2,128)(2,1)}, u32[]{:S(2)}) copy-start(bf16[1,2,7168]{2,1,0:T(2,128)(2,1)} %param.23) | copy-start | bytes 86020
  43.9 1.6 %collective-permute-start.9 = (bf16[8,2,7168]{2,1,0:T(2,128)(2,1)S(1)}, bf16[8,2,7168]{2,1,0:T(2,128)(2,1)S(1)}, u32[]{:S(2)}, u32[]{:S(2)}) collective-permute-start(bf16[8,2,7168]{2,1,0:T(2,128)(2,1)S(1)} %get-tuple-element.28), channel_id=1, source_target_pairs={{0,1},{1,0},{2,3},{3,2},{4,5},{5,4},{6,7},{7,6},{8,9},{9,8},{10,11... | collective-permute-start | bytes 688136 | tf_op jit(solution)/shard_map/ppermute | solution.py:450
  46.4 12.5 %all-to-all-start.1 = ((bf16[8,2,7168]{2,1,0:T(2,128)(2,1)}), bf16[8,2,7168]{2,1,0:T(2,128)(2,1)S(1)}, u32[]{:S(2)}, u32[]{:S(2)}) async-start(bf16[8,2,7168]{2,1,0:T(2,128)(2,1)} %shard_map.159), calls=%async_computation.1 | async-start | bytes 458752 | tf_op jit(solution)/shard_map/all_to_all | solution.py:452
  50.1 20.8 %collective-permute-start.10 = (bf16[128,7168]{1,0:T(8,128)(2,1)}, bf16[128,7168]{1,0:T(8,128)(2,1)S(1)}, u32[]{:S(2)}, u32[]{:S(2)}) collective-permute-start(bf16[128,7168]{1,0:T(8,128)(2,1)} %refs_0_.3), channel_id=1, source_target_pairs={{0,1},{1,0},{2,3},{3,2},{4,5},{5,4},{6,7},{7,6},{8,9},{9,8},{10,11... | collective-permute-start | bytes 5505032 | tf_op jit(solution)/shard_map/ppermute | solution.py:460
  50.2 20.8 %collective-permute-start.11 = (bf16[128,7168]{1,0:T(8,128)(2,1)}, bf16[128,7168]{1,0:T(8,128)(2,1)}, u32[]{:S(2)}, u32[]{:S(2)}) collective-permute-start(bf16[128,7168]{1,0:T(8,128)(2,1)} %refs_2_.1), channel_id=1, source_target_pairs={{0,1},{1,0},{2,3},{3,2},{4,5},{5,4},{6,7},{7,6},{8,9},{9,8},{10,11... | collective-permute-start | bytes 5505032 | tf_op jit(solution)/shard_map/ppermute | solution.py:460
  50.7 20.3 %collective-permute-start.12 = (bf16[128,7168]{1,0:T(8,128)(2,1)}, bf16[128,7168]{1,0:T(8,128)(2,1)}, u32[]{:S(2)}, u32[]{:S(2)}) collective-permute-start(bf16[128,7168]{1,0:T(8,128)(2,1)} %refs_4_.1), channel_id=1, source_target_pairs={{0,1},{1,0},{2,3},{3,2},{4,5},{5,4},{6,7},{7,6},{8,9},{9,8},{10,11... | collective-permute-start | bytes 5505032 | tf_op jit(solution)/shard_map/ppermute | solution.py:460
  70.9 8.9 %copy-start.6 = (f32[1,2,1]{1,2,0:T(1,128)S(1)}, f32[1,2,1]{1,2,0:T(1,128)}, u32[]{:S(2)}) copy-start(f32[1,2,1]{1,2,0:T(1,128)} %param.28) | copy-start | bytes 28
  70.9 8.9 %copy-start.7 = (s32[1,2,1]{1,2,0:T(1,128)S(1)}, s32[1,2,1]{1,2,0:T(1,128)}, u32[]{:S(2)}) copy-start(s32[1,2,1]{1,2,0:T(1,128)} %param.27) | copy-start | bytes 28
  76.3 11.4 %all-to-all-start.3 = ((bf16[8,2,7168]{2,1,0:T(2,128)(2,1)}), bf16[8,2,7168]{2,1,0:T(2,128)(2,1)S(1)}, u32[]{:S(2)}, u32[]{:S(2)}) async-start(bf16[8,2,7168]{2,1,0:T(2,128)(2,1)} %shard_map.160), calls=%async_computation.3 | async-start | bytes 458752 | tf_op jit(solution)/shard_map/all_to_all | solution.py:469

commit v7 on v6

--- a/solution.py
+++ b/solution.py
@@ -50,7 +50,7 @@
     return jnp.concatenate(pieces, axis=1), jnp.concatenate(tails, axis=0)
 
 
-def spread_kernel(query_hbm, spread_hbm, query_ref, blocks_ref, sems):
+def spread_kernel(slots, query_hbm, spread_hbm, query_ref, blocks_ref, sems):
     peers = spread_hbm.shape[0]
     planes = peers // PLANE
     width, heads = query_ref.shape
@@ -63,7 +63,7 @@
         rows = by_peer[:, column].reshape(heads // PLANE, width)
         blocks_ref[column] = pack(rows).astype(bf16)
         for plane in range(planes):
-            peer = plane * PLANE + column
+            peer = slots[plane * PLANE + column]
             copies.append(
                 pltpu.make_async_copy(blocks_ref.at[column], spread_hbm.at[peer], sems.at[1 + peer])
             )
@@ -123,7 +123,7 @@
         message_ref[rows:] = key_rows
 
 
-def prompt_kernel(device_ref, dest_ref, length_ref, *refs):
+def prompt_kernel(device_ref, dest_ref, length_ref, slot_ref, *refs):
     key_refs, message_refs, query_hbm = refs[:PLANE], refs[PLANE : 2 * PLANE], refs[2 * PLANE]
     out_refs, (stage_ref, query_ref, sems) = refs[2 * PLANE + 1 : -3], refs[-3:]
     planes, _, rows, width = stage_ref.shape
@@ -133,7 +133,7 @@
     device = device_ref[0]
     sources = [dest_ref[device ^ at] for at in range(PLANE)] + [device ^ at for at in range(PLANE)]
     loads = [
-        pltpu.make_async_copy(query_hbm.at[source], query_ref.at[at], sems.at[at])
+        pltpu.make_async_copy(query_hbm.at[slot_ref[source]], query_ref.at[at], sems.at[at])
         for at, source in enumerate(sources)
     ]
     for load in loads:
@@ -331,6 +331,10 @@
     )(after, *map(distant, weights))
 
 
+def middle_first(count):
+    return sorted(range(count), key=lambda at: abs(4 * at - 2 * count + 1))
+
+
 def shards(
     handoff_rows,
     handoff_dest,
@@ -354,16 +358,20 @@
     core = device % 2
     chips = devices // 2
     siblings = [(i, i ^ 1) for i in range(devices)]
-    same_core = [[2 * chip + k for chip in range(chips)] for k in range(2)]
+    chip_order = middle_first(chips)
+    same_core = [[2 * chip + k for chip in chip_order] for k in range(2)]
+    device_order = [2 * chip + k for k in range(2) for chip in chip_order]
+    slots = sorted(range(devices), key=device_order.__getitem__)
     slice_count = MOE_FF // UNITS
     heads, width = queries.shape[2], queries.shape[3]
     per_peer = heads // devices
     model = residual_in.shape[2]
 
-    exchange = functools.partial(
-        lax.all_to_all, axis_name="ep", split_axis=0, concat_axis=0, tiled=True
-    )
-    exchange_core = functools.partial(exchange, axis_index_groups=same_core)
+    def exchange(value, groups):
+        return lax.all_to_all(
+            value, "ep", split_axis=0, concat_axis=0, tiled=True, axis_index_groups=groups
+        )
+
 
     planes = devices // PLANE
     toward = lambda value, bits: (
@@ -374,7 +382,7 @@
     flipped = jnp.swapaxes(queries[0], 1, 2)
     spread_shape = (devices, heads // PLANE * width // LANES, LANES)
     spread_rows = call_far(
-        spread_kernel,
+        functools.partial(spread_kernel, slots),
         jax.ShapeDtypeStruct(spread_shape, bf16),
         [flipped],
         [
@@ -383,7 +391,7 @@
             pltpu.SemaphoreType.DMA((1 + devices,)),
         ],
     )
-    spread = exchange(spread_rows)
+    spread = exchange(spread_rows, [device_order])
 
     short = pl.CostEstimate(flops=1, bytes_accessed=1, transcendentals=0)
     flipped_keys = jnp.swapaxes(handoff_rows[0], 0, 1)
@@ -405,7 +413,7 @@
             pltpu.VMEM((planes, PLANE, per_peer, KVR), f32),
             pltpu.SemaphoreType.DMA((2,)),
         ],
-        short,
+        pl.CostEstimate(flops=6000000000, bytes_accessed=30000000, transcendentals=262144),
     )
     messages = [toward(message, at) for at, message in enumerate(messages)]
 
@@ -413,7 +421,7 @@
     payloads = call(
         prompt_kernel,
         [((PLANE, 2 * per_peer, KVR + chunk), bf16)] * planes,
-        [own_device, handoff_dest, handoff_len, *plane_keys, *messages],
+        [own_device, handoff_dest, handoff_len, jnp.array(slots, jnp.int32), *plane_keys, *messages],
         [spread],
         [
             pltpu.VMEM((planes, PLANE, 2 * per_peer, KVR + chunk), bf16),
@@ -426,7 +434,8 @@
 
     row = jnp.arange(per_peer * 2 * devices, dtype=jnp.int32)
     row_core = (row // devices % 2) ^ core
-    row_device = row // 2 % chips * 2 + row_core
+    chip_at = jnp.array(chip_order, jnp.int32)
+    row_device = chip_at[row // 2 % chips] * 2 + row_core
     row_table = jnp.stack([row // (2 * devices), row_device, row % 2], axis=1)
     peers = device.astype(jnp.int32) ^ jnp.arange(devices, dtype=jnp.int32)
     is_peer = peers[:, None] == jnp.arange(devices, dtype=jnp.int32)[None, :]
@@ -449,12 +458,12 @@
 
     other = lax.ppermute(send, "ep", siblings)
     (pair,) = call(pair_kernel, [((chips, 2, model), bf16)], [keep, other])
-    attention = jnp.sum(exchange_core(pair).astype(f32), axis=0)
+    attention = jnp.sum(exchange(pair, same_core).astype(f32), axis=0)
     hidden = residual_in[0].astype(f32) + attention
     inverse_rms = lax.rsqrt(jnp.mean(hidden * hidden, axis=-1, keepdims=True) + norm_epsilon)
     normed = (hidden * inverse_rms * norm_gain.astype(f32)).astype(bf16)
 
-    own_rows = exchange_core(jnp.broadcast_to(normed[None], (chips, 2, model)))
+    own_rows = exchange(jnp.broadcast_to(normed[None], (chips, 2, model)), same_core)
     experts = []
     for matrix in (gate_proj, up_proj, down_proj):
         experts += [matrix, lax.ppermute(matrix, "ep", siblings)]
@@ -466,9 +475,9 @@
         [pltpu.VMEM((2 * gate_proj.shape[0], model), bf16)] * 3
         + [pltpu.SemaphoreType.DMA((20,))],
     )
-    returned = exchange_core(part)
-
-    chip_expert = jnp.arange(chips, dtype=jnp.int32) * 2 // slice_count
+    returned = exchange(part, same_core)
+
+    chip_expert = chip_at * 2 // slice_count
     chosen = (expert_ids[0][..., None] == chip_expert).astype(f32)
     weights = jnp.sum(expert_gates[0][..., None] * chosen, axis=1)
     mixed = jnp.sum(weights.T[..., None] * returned.astype(f32), axis=0)

time: 89.3 us -> 83.7 us (0.937)
  waiting for transfers between devices: 27.4 us -> 20.1 us
  starting transfers between devices: 23.7 us -> 26.9 us
  blocking collectives: 11.3 us -> 9.64 us
    ppermute x9, waiting for transfers between devices: 9.84 us -> 3.24 us  [shards(): lax.ppermute(value, 'ep', [(i, i ^ bits) for i in range(devices)])]
    all_to_all x3, starting transfers between devices: 14.6 us -> 16.4 us  [exchange(): lax.all_to_all(value, 'ep', split_axis=0, concat_axis=0, tiled=True, axis...]
    all_to_all x1, blocking collectives: 11.3 us -> 9.64 us  [exchange(): lax.all_to_all(value, 'ep', split_axis=0, concat_axis=0, tiled=True, axis...]
    ppermute x9, starting transfers between devices: 8.45 us -> 9.86 us  [shards(): lax.ppermute(value, 'ep', [(i, i ^ bits) for i in range(devices)])]
  transfers between devices with their start and end apart: 16 -> 16, of which waited for: 8 -> 6; matrix products, arithmetic and copies ran while one was open for 2% -> 2% of each run, Pallas kernels for 10% -> 13%
where the time goes in v7:
time: 83.7 us; the launch traced here: 83.2 us
  starting transfers between devices  26.9 us (32%)
  Pallas kernels  23 us (27%)
  waiting for transfers between devices  20.1 us (24%)
  blocking collectives  9.64 us (12%)
  other arithmetic  1.83 us (2%)
  between operations  0.96 us (1%)
    all_to_all x3, starting transfers between devices, exchange(): lax.all_to_all(value, 'ep', split_axis=0, concat_axis=0, tiled=True, axis...  16.4 us
    pallas_call x5, Pallas kernels, call(): pl.pallas_call(kernel, out_shape=[pltpu.VMEM(shape, dtype) for shape, dty...  15.4 us
    all_to_all x3, waiting for transfers between devices, exchange(): lax.all_to_all(value, 'ep', split_axis=0, concat_axis=0, tiled=True, axis...  15.4 us
    ppermute x9, starting transfers between devices, shards(): lax.ppermute(value, 'ep', [(i, i ^ bits) for i in range(devices)])  9.86 us
    all_to_all x1, blocking collectives, exchange(): lax.all_to_all(value, 'ep', split_axis=0, concat_axis=0, tiled=True, axis...  9.64 us
    pallas_call x1, Pallas kernels, prefetch(): pl.pallas_call(prefetch_kernel, out_shape=[pltpu.VMEM(weight.shape, weigh...  5.53 us
    ppermute x9, waiting for transfers between devices, shards(): lax.ppermute(value, 'ep', [(i, i ^ bits) for i in range(devices)])  3.24 us
    pallas_call x1, Pallas kernels, call_far(): pl.pallas_call(kernel, out_shape=shapes, in_specs=[far] * len(operands),...  2.06 us
  transfers between devices with their start and end apart: 16, of which 6 were waited for; matrix products, arithmetic and copies ran while one was open for 2% of the time, Pallas kernels for 13%

profile of v7, /device:TPU:0, one launch (start us, length us, event | category | flops | bytes accessed | tf_op | source)
XLA Modules:
  0.0 83.2 jit_solution(7135583999556864050)
XLA Ops:
  0.0 2.9 %collective-permute-start.1 = (bf16[576,256]{1,0:T(8,128)(2,1)}, bf16[576,256]{1,0:T(8,128)(2,1)S(1)}, u32[]{:S(2)}, u32[]{:S(2)}) collective-permute-start(bf16[576,256]{1,0:T(8,128)(2,1)} %bitcast.38), channel_id=1, source_target_pairs={{0,2},{1,3},{2,0},{3,1},{4,6},{5,7},{6,4},{7,5},{8,10},{9,11},{10,... | collective-permute-start | bytes 884744 | tf_op jit(solution)/shard_map/ppermute | solution.py:378
  2.9 2.1 %shard_map.172.after_ref = bf16[16,144,128]{2,1,0:T(8,128)(2,1)} custom-call(bf16[2,576,128]{2,1,0:T(8,128)(2,1)} %bitcast.43), custom_call_target="tpu_custom_call" | custom-call | tf_op jit(solution)/shard_map/pallas_call | solution.py:312
  5.0 6.0 %all-to-all-start = ((bf16[16,144,128]{2,1,0:T(8,128)(2,1)}), bf16[16,144,128]{2,1,0:T(8,128)(2,1)S(1)}, u32[]{:S(2)}, u32[]{:S(2)}) async-start(bf16[16,144,128]{2,1,0:T(8,128)(2,1)} %shard_map.172.after_ref), calls=%async_computation | async-start | bytes 1179648 | tf_op jit(solution)/shard_map/all_to_all | solution.py:371
  11.7 0.0 copy-start.1
  11.7 0.0 copy-start
  11.7 0.0 copy-start.2
  11.7 0.0 copy-start.3
  11.7 3.4 %shard_map.173 = (bf16[48,512]{1,0:T(8,128)(2,1)S(1)}, bf16[48,512]{1,0:T(8,128)(2,1)S(1)}, bf16[48,512]{1,0:T(8,128)(2,1)S(1)}, bf16[48,512]{1,0:T(8,128)(2,1)S(1)}) custom-call(s32[1]{0:T(128)} %bitcast.2.device_ref, s32[1]{0:T(128)S(6)} %copy.21.length_ref, bf16[2,576]{1,0:T(2,128)(2,1)S(1)} %bitcast.41, bf16[16,144,128]{2,1,0:T(8,128)(2,1)} %shard_map.172.after_ref, ...), custom_call_target="tpu_custom_call" | custom-call | flops 6000000000 | bytes 30000000 | tf_op jit(solution)/shard_map/pallas_call | solution.py:296
  15.2 0.2 collective-permute-start.3
  15.4 1.4 %collective-permute-start.4 = (bf16[48,512]{1,0:T(8,128)(2,1)S(1)}, bf16[48,512]{1,0:T(8,128)(2,1)S(1)}, u32[]{:S(2)}, u32[]{:S(2)}) collective-permute-start(bf16[48,512]{1,0:T(8,128)(2,1)S(1)} %get-tuple-element.19), channel_id=1, source_target_pairs={{0,2},{1,3},{2,0},{3,1},{4,6},{5,7},{6,4},{7,5},{8,10},{9,11},{10,... | collective-permute-start | bytes 147464 | tf_op jit(solution)/shard_map/ppermute | solution.py:378
  16.9 0.2 collective-permute-start.5
  17.1 0.2 select_reduce_fusion
  17.3 0.1 broadcast_in_dim.42
  17.4 0.1 stack_reshape.7
  17.4 0.1 broadcast_in_dim.22
  17.5 0.1 stack_reshape.6
  17.7 0.5 collective-permute-start.2
  18.3 0.1 copy.20.row_ref
  18.4 2.1 %collective-permute-done.4.refs_6_ = bf16[48,512]{1,0:T(8,128)(2,1)S(1)} collective-permute-done((bf16[48,512]{1,0:T(8,128)(2,1)S(1)}, bf16[48,512]{1,0:T(8,128)(2,1)S(1)}, u32[]{:S(2)}, u32[]{:S(2)}) %collective-permute-start.4) | collective-permute-done | bytes 49184 | tf_op jit(solution)/shard_map/ppermute | solution.py:378
  20.6 1.1 %collective-permute-done.5.refs_7_ = bf16[48,512]{1,0:T(8,128)(2,1)S(1)} collective-permute-done((bf16[48,512]{1,0:T(8,128)(2,1)S(1)}, bf16[48,512]{1,0:T(8,128)(2,1)S(1)}, u32[]{:S(2)}, u32[]{:S(2)}) %collective-permute-start.5) | collective-permute-done | bytes 49184 | tf_op jit(solution)/shard_map/ppermute | solution.py:378
  21.7 3.4 %all-to-all-done.refs_8_ = bf16[16,144,128]{2,1,0:T(8,128)(2,1)S(1)} async-done(((bf16[16,144,128]{2,1,0:T(8,128)(2,1)}), bf16[16,144,128]{2,1,0:T(8,128)(2,1)S(1)}, u32[]{:S(2)}, u32[]{:S(2)}) %all-to-all-start) | async-done | bytes 589856 | tf_op jit(solution)/shard_map/all_to_all | solution.py:371
  25.1 1.8 %shard_map.174 = (bf16[4,16,640]{2,1,0:T(8,128)(2,1)S(1)}, bf16[4,16,640]{2,1,0:T(8,128)(2,1)S(1)}, bf16[4,16,640]{2,1,0:T(8,128)(2,1)S(1)}, bf16[4,16,640]{2,1,0:T(8,128)(2,1)S(1)}) custom-call(s32[1]{0:T(128)} %bitcast.2.device_ref, s32[16]{0:T(128)S(1)} %copy-done.1, s32[16]{0:T(128)S(1)} %copy-done.2, s32[16]{0:T(128)S(1)} %copy-done.3, ...), custom_call_target="tpu_custom_call" | custom-call | tf_op jit(solution)/shard_map/pallas_call | solution.py:296
  26.9 0.1 collective-permute-start.6
  27.0 2.7 %collective-permute-start.7 = (bf16[4,16,640]{2,1,0:T(8,128)(2,1)S(1)}, bf16[4,16,640]{2,1,0:T(8,128)(2,1)S(1)}, u32[]{:S(2)}, u32[]{:S(2)}) collective-permute-start(bf16[4,16,640]{2,1,0:T(8,128)(2,1)S(1)} %get-tuple-element.25), channel_id=1, source_target_pairs={{0,8},{1,9},{2,10},{3,11},{4,12},{5,13},{6,14},{7,15},{8,0},{9,1},... | collective-permute-start | bytes 245768 | tf_op jit(solution)/shard_map/ppermute | solution.py:378
  29.7 1.6 %collective-permute-start.8 = (bf16[4,16,640]{2,1,0:T(8,128)(2,1)S(1)}, bf16[4,16,640]{2,1,0:T(8,128)(2,1)S(1)}, u32[]{:S(2)}, u32[]{:S(2)}) collective-permute-start(bf16[4,16,640]{2,1,0:T(8,128)(2,1)S(1)} %get-tuple-element.26), channel_id=1, source_target_pairs={{0,12},{1,13},{2,14},{3,15},{4,8},{5,9},{6,10},{7,11},{8,4},{9,5},... | collective-permute-start | bytes 245768 | tf_op jit(solution)/shard_map/ppermute | solution.py:378
  31.4 5.5 %shard_map.175 = (bf16[8,512,128]{2,1,0:T(8,128)(2,1)S(1)}, bf16[1024,7168]{1,0:T(8,128)(2,1)S(1)}) custom-call(bf16[4,16,640]{2,1,0:T(8,128)(2,1)S(1)} %get-tuple-element.21.after_ref.refs_0_, bf16[8,512,128]{2,1,0:T(8,128)(2,1)} %refs_0_.2, bf16[1024,7168]{1,0:T(8,128)(2,1)} %bitcast.42), custom_call_target="tpu_custom_call" | custom-call | tf_op jit(solution)/shard_map/pallas_call | solution.py:324
  36.9 0.0 copy-start.5
  36.9 4.0 %shard_map.176 = (f32[8,2,7168]{2,1,0:T(2,128)S(1)}, bf16[8,2,7168]{2,1,0:T(2,128)(2,1)S(1)}) custom-call(s32[256,3]{1,0:T(8,128)S(1)} %copy.20.row_ref, s32[3,256]{1,0:T(4,128)S(1)} %pad_add_fusion.1.column_ref, s32[1,16]{1,0:T(1,128)S(1)} %iota_xor_fusion.peer_ref, bf16[8,512,128]{2,1,0:T(8,128)(2,1)S(1)} %get-tuple-element.22.upward_ref, ...), custom_call_target="tpu_custom_call" | custom-call | tf_op jit(solution)/shard_map/pallas_call | solution.py:296
  40.9 0.1 collective-permute-start.9
  41.0 1.5 %collective-permute-done.9.other_ref = bf16[8,2,7168]{2,1,0:T(2,128)(2,1)S(1)} collective-permute-done((bf16[8,2,7168]{2,1,0:T(2,128)(2,1)S(1)}, bf16[8,2,7168]{2,1,0:T(2,128)(2,1)S(1)}, u32[]{:S(2)}, u32[]{:S(2)}) %collective-permute-start.9) | collective-permute-done | bytes 229408 | tf_op jit(solution)/shard_map/ppermute | solution.py:459
  42.5 0.9 %shard_map.177 = bf16[8,2,7168]{2,1,0:T(2,128)(2,1)} custom-call(f32[8,2,7168]{2,1,0:T(2,128)S(1)} %get-tuple-element.27.keep_ref, bf16[8,2,7168]{2,1,0:T(2,128)(2,1)S(1)} %collective-permute-done.9.other_ref), custom_call_target="tpu_custom_call" | custom-call | tf_op jit(solution)/shard_map/pallas_call | solution.py:296
  43.4 6.2 %all-to-all-start.1 = ((bf16[8,2,7168]{2,1,0:T(2,128)(2,1)}), bf16[8,2,7168]{2,1,0:T(2,128)(2,1)S(1)}, u32[]{:S(2)}, u32[]{:S(2)}) async-start(bf16[8,2,7168]{2,1,0:T(2,128)(2,1)} %shard_map.177), calls=%async_computation.1 | async-start | bytes 458752 | tf_op jit(solution)/shard_map/all_to_all | solution.py:371
  49.6 0.5 collective-permute-start.11
  50.1 6.4 %all-to-all-done.1 = bf16[8,2,7168]{2,1,0:T(2,128)(2,1)S(1)} async-done(((bf16[8,2,7168]{2,1,0:T(2,128)(2,1)}), bf16[8,2,7168]{2,1,0:T(2,128)(2,1)S(1)}, u32[]{:S(2)}, u32[]{:S(2)}) %all-to-all-start.1) | async-done | bytes 229408 | tf_op jit(solution)/shard_map/all_to_all | solution.py:371
  56.5 0.2 convert_reduce_fusion
  56.7 0.2 fusion.2
  56.9 0.1 fusion.4
  57.0 0.1 broadcast_in_dim.45
  57.1 9.6 %all_to_all.20 = bf16[8,2,7168]{2,1,0:T(2,128)(2,1)S(1)} all-to-all(bf16[8,2,7168]{2,1,0:T(2,128)(2,1)S(1)} %broadcast_in_dim.45), channel_id=1, replica_groups={{8,6,10,4,12,2,14,0},{9,7,11,5,13,3,15,1},{24,22,26,20,28,18,30,16},{25..., dimensions={0} | all-to-all | bytes 458752 | tf_op jit(solution)/shard_map/all_to_all | solution.py:371
  66.8 0.1 reshape.289.rows_ref
  66.9 0.0 copy-start.8
  66.9 0.0 copy-start.9
  66.9 5.4 %shard_map.178 = bf16[8,2,7168]{2,1,0:T(2,128)(2,1)} custom-call(bf16[16,7168]{1,0:T(8,128)(2,1)S(1)} %reshape.289.rows_ref, bf16[128,7168]{1,0:T(8,128)(2,1)} %refs_0_.3, bf16[128,7168]{1,0:T(8,128)(2,1)S(1)} %collective-permute-done.10.refs_1_, bf16[128,7168]{1,0:T(8,128)(2,1)} %refs_2_.1, bf16[128,7168]{1,0:T(8,128)(2,1)} %collective-permute-done.11.refs_3_, ...), custom_call_target="tpu_custom_call" | custom-call | tf_op jit(solution)/shard_map/pallas_call | solution.py:296
  72.3 4.2 %all-to-all-start.3 = ((bf16[8,2,7168]{2,1,0:T(2,128)(2,1)}), bf16[8,2,7168]{2,1,0:T(2,128)(2,1)S(1)}, u32[]{:S(2)}, u32[]{:S(2)}) async-start(bf16[8,2,7168]{2,1,0:T(2,128)(2,1)} %shard_map.178), calls=%async_computation.3 | async-start | bytes 458752 | tf_op jit(solution)/shard_map/all_to_all | solution.py:371
  76.6 0.1 compare_select_fusion.11
  76.6 5.6 %all-to-all-done.3 = bf16[8,2,7168]{2,1,0:T(2,128)(2,1)S(1)} async-done(((bf16[8,2,7168]{2,1,0:T(2,128)(2,1)}), bf16[8,2,7168]{2,1,0:T(2,128)(2,1)S(1)}, u32[]{:S(2)}, u32[]{:S(2)}) %all-to-all-start.3) | async-done | bytes 229408 | tf_op jit(solution)/shard_map/all_to_all | solution.py:371
  82.2 0.3 multiply_reduce_fusion
  82.5 0.7 fusion.3
  (38 shorter events, 0.2 us)
Async XLA Ops:
  0.0 11.7 %copy-start.4 = (bf16[1,2,576]{2,1,0:T(2,128)(2,1)S(1)}, bf16[1,2,576]{2,1,0:T(2,128)(2,1)}, u32[]{:S(2)}) copy-start(bf16[1,2,576]{2,1,0:T(2,128)(2,1)} %param.24) | copy-start | bytes 6916
  0.0 17.7 %collective-permute-start.1 = (bf16[576,256]{1,0:T(8,128)(2,1)}, bf16[576,256]{1,0:T(8,128)(2,1)S(1)}, u32[]{:S(2)}, u32[]{:S(2)}) collective-permute-start(bf16[576,256]{1,0:T(8,128)(2,1)} %bitcast.38), channel_id=1, source_target_pairs={{0,2},{1,3},{2,0},{3,1},{4,6},{5,7},{6,4},{7,5},{8,10},{9,11},{10,... | collective-permute-start | bytes 884744 | tf_op jit(solution)/shard_map/ppermute | solution.py:378
  2.9 18.7 %collective-permute-start = (bf16[576,256]{1,0:T(8,128)(2,1)}, bf16[576,256]{1,0:T(8,128)(2,1)S(1)}, u32[]{:S(2)}, u32[]{:S(2)}) collective-permute-start(bf16[576,256]{1,0:T(8,128)(2,1)} %bitcast.39), channel_id=1, source_target_pairs={{0,1},{1,0},{2,3},{3,2},{4,5},{5,4},{6,7},{7,6},{8,9},{9,8},{10,11... | collective-permute-start | bytes 884744 | tf_op jit(solution)/shard_map/ppermute | solution.py:378
  5.0 20.1 %all-to-all-start = ((bf16[16,144,128]{2,1,0:T(8,128)(2,1)}), bf16[16,144,128]{2,1,0:T(8,128)(2,1)S(1)}, u32[]{:S(2)}, u32[]{:S(2)}) async-start(bf16[16,144,128]{2,1,0:T(8,128)(2,1)} %shard_map.172.after_ref), calls=%async_computation | async-start | bytes 1179648 | tf_op jit(solution)/shard_map/all_to_all | solution.py:371
  11.7 5.4 %copy-start.1 = (s32[16]{0:T(128)S(1)}, s32[16]{0:T(128)}, u32[]{:S(2)}) copy-start(s32[16]{0:T(128)} %dest_ref.1) | copy-start | bytes 196
  11.7 13.4 %copy-start = (bf16[1,256,576]{1,2,0:T(8,128)(2,1)S(1)}, bf16[1,256,576]{1,2,0:T(8,128)(2,1)}, u32[]{:S(2)}) copy-start(bf16[1,256,576]{1,2,0:T(8,128)(2,1)} %param.18) | copy-start | bytes 884740
  11.7 13.4 %copy-start.2 = (s32[16]{0:T(128)S(1)}, s32[16]{0:T(128)}, u32[]{:S(2)}) copy-start(s32[16]{0:T(128)} %length_ref.2) | copy-start | bytes 196
  11.7 13.4 %copy-start.3 = (s32[16]{0:T(128)S(1)}, s32[16]{0:T(128)}, u32[]{:S(2)}) copy-start(s32[16]{0:T(128)} %constant.119.clone.slot_ref) | copy-start | bytes 196
  15.2 3.2 %collective-permute-start.3 = (bf16[48,512]{1,0:T(8,128)(2,1)S(1)}, bf16[48,512]{1,0:T(8,128)(2,1)S(1)}, u32[]{:S(2)}, u32[]{:S(2)}) collective-permute-start(bf16[48,512]{1,0:T(8,128)(2,1)S(1)} %get-tuple-element.18), channel_id=1, source_target_pairs={{0,1},{1,0},{2,3},{3,2},{4,5},{5,4},{6,7},{7,6},{8,9},{9,8},{10,11... | collective-permute-start | bytes 147464 | tf_op jit(solution)/shard_map/ppermute | solution.py:378
  15.4 5.2 %collective-permute-start.4 = (bf16[48,512]{1,0:T(8,128)(2,1)S(1)}, bf16[48,512]{1,0:T(8,128)(2,1)S(1)}, u32[]{:S(2)}, u32[]{:S(2)}) collective-permute-start(bf16[48,512]{1,0:T(8,128)(2,1)S(1)} %get-tuple-element.19), channel_id=1, source_target_pairs={{0,2},{1,3},{2,0},{3,1},{4,6},{5,7},{6,4},{7,5},{8,10},{9,11},{10,... | collective-permute-start | bytes 147464 | tf_op jit(solution)/shard_map/ppermute | solution.py:378
  16.9 4.8 %collective-permute-start.5 = (bf16[48,512]{1,0:T(8,128)(2,1)S(1)}, bf16[48,512]{1,0:T(8,128)(2,1)S(1)}, u32[]{:S(2)}, u32[]{:S(2)}) collective-permute-start(bf16[48,512]{1,0:T(8,128)(2,1)S(1)} %get-tuple-element.20), channel_id=1, source_target_pairs={{0,3},{1,2},{2,1},{3,0},{4,7},{5,6},{6,5},{7,4},{8,11},{9,10},{10,... | collective-permute-start | bytes 147464 | tf_op jit(solution)/shard_map/ppermute | solution.py:378
  17.7 3.9 %collective-permute-start.2 = (bf16[576,256]{1,0:T(8,128)(2,1)S(1)}, bf16[576,256]{1,0:T(8,128)(2,1)S(1)}, u32[]{:S(2)}, u32[]{:S(2)}) collective-permute-start(bf16[576,256]{1,0:T(8,128)(2,1)S(1)} %collective-permute-done.1.refs_2_), channel_id=1, source_target_pairs={{0,1},{1,0},{2,3},{3,2},{4,5},{5,4},{6,7},{7,6},{8,9},{9,8},{10,11... | collective-permute-start | bytes 884744 | tf_op jit(solution)/shard_map/ppermute | solution.py:378
  26.9 10.0 %collective-permute-start.6 = (bf16[4,16,640]{2,1,0:T(8,128)(2,1)S(1)}, bf16[4,16,640]{2,1,0:T(8,128)(2,1)S(1)}, u32[]{:S(2)}, u32[]{:S(2)}) collective-permute-start(bf16[4,16,640]{2,1,0:T(8,128)(2,1)S(1)} %get-tuple-element.24), channel_id=1, source_target_pairs={{0,4},{1,5},{2,6},{3,7},{4,0},{5,1},{6,2},{7,3},{8,12},{9,13},{10,... | collective-permute-start | bytes 245768 | tf_op jit(solution)/shard_map/ppermute | solution.py:378
  27.0 9.9 %collective-permute-start.7 = (bf16[4,16,640]{2,1,0:T(8,128)(2,1)S(1)}, bf16[4,16,640]{2,1,0:T(8,128)(2,1)S(1)}, u32[]{:S(2)}, u32[]{:S(2)}) collective-permute-start(bf16[4,16,640]{2,1,0:T(8,128)(2,1)S(1)} %get-tuple-element.25), channel_id=1, source_target_pairs={{0,8},{1,9},{2,10},{3,11},{4,12},{5,13},{6,14},{7,15},{8,0},{9,1},... | collective-permute-start | bytes 245768 | tf_op jit(solution)/shard_map/ppermute | solution.py:378
  29.7 7.2 %collective-permute-start.8 = (bf16[4,16,640]{2,1,0:T(8,128)(2,1)S(1)}, bf16[4,16,640]{2,1,0:T(8,128)(2,1)S(1)}, u32[]{:S(2)}, u32[]{:S(2)}) collective-permute-start(bf16[4,16,640]{2,1,0:T(8,128)(2,1)S(1)} %get-tuple-element.26), channel_id=1, source_target_pairs={{0,12},{1,13},{2,14},{3,15},{4,8},{5,9},{6,10},{7,11},{8,4},{9,5},... | collective-permute-start | bytes 245768 | tf_op jit(solution)/shard_map/ppermute | solution.py:378
  36.9 13.2 %copy-start.6 = (bf16[7168]{0:T(1024)(128)(2,1)S(1)}, bf16[7168]{0:T(1024)(128)(2,1)}, u32[]{:S(2)}) copy-start(bf16[7168]{0:T(1024)(128)(2,1)} %param.28) | copy-start | bytes 43012
  36.9 19.8 %copy-start.5 = (bf16[1,2,7168]{2,1,0:T(2,128)(2,1)S(1)}, bf16[1,2,7168]{2,1,0:T(2,128)(2,1)}, u32[]{:S(2)}) copy-start(bf16[1,2,7168]{2,1,0:T(2,128)(2,1)} %param.25) | copy-start | bytes 86020
  40.9 1.6 %collective-permute-start.9 = (bf16[8,2,7168]{2,1,0:T(2,128)(2,1)S(1)}, bf16[8,2,7168]{2,1,0:T(2,128)(2,1)S(1)}, u32[]{:S(2)}, u32[]{:S(2)}) collective-permute-start(bf16[8,2,7168]{2,1,0:T(2,128)(2,1)S(1)} %get-tuple-element.28), channel_id=1, source_target_pairs={{0,1},{1,0},{2,3},{3,2},{4,5},{5,4},{6,7},{7,6},{8,9},{9,8},{10,11... | collective-permute-start | bytes 688136 | tf_op jit(solution)/shard_map/ppermute | solution.py:459
  43.4 13.1 %all-to-all-start.1 = ((bf16[8,2,7168]{2,1,0:T(2,128)(2,1)}), bf16[8,2,7168]{2,1,0:T(2,128)(2,1)S(1)}, u32[]{:S(2)}, u32[]{:S(2)}) async-start(bf16[8,2,7168]{2,1,0:T(2,128)(2,1)} %shard_map.177), calls=%async_computation.1 | async-start | bytes 458752 | tf_op jit(solution)/shard_map/all_to_all | solution.py:371
  49.6 17.3 %collective-permute-start.10 = (bf16[128,7168]{1,0:T(8,128)(2,1)}, bf16[128,7168]{1,0:T(8,128)(2,1)S(1)}, u32[]{:S(2)}, u32[]{:S(2)}) collective-permute-start(bf16[128,7168]{1,0:T(8,128)(2,1)} %refs_0_.3), channel_id=1, source_target_pairs={{0,1},{1,0},{2,3},{3,2},{4,5},{5,4},{6,7},{7,6},{8,9},{9,8},{10,11... | collective-permute-start | bytes 5505032 | tf_op jit(solution)/shard_map/ppermute | solution.py:469
  49.6 17.4 %collective-permute-start.11 = (bf16[128,7168]{1,0:T(8,128)(2,1)}, bf16[128,7168]{1,0:T(8,128)(2,1)}, u32[]{:S(2)}, u32[]{:S(2)}) collective-permute-start(bf16[128,7168]{1,0:T(8,128)(2,1)} %refs_2_.1), channel_id=1, source_target_pairs={{0,1},{1,0},{2,3},{3,2},{4,5},{5,4},{6,7},{7,6},{8,9},{9,8},{10,11... | collective-permute-start | bytes 5505032 | tf_op jit(solution)/shard_map/ppermute | solution.py:469
  50.1 16.9 %collective-permute-start.12 = (bf16[128,7168]{1,0:T(8,128)(2,1)}, bf16[128,7168]{1,0:T(8,128)(2,1)}, u32[]{:S(2)}, u32[]{:S(2)}) collective-permute-start(bf16[128,7168]{1,0:T(8,128)(2,1)} %refs_4_.1), channel_id=1, source_target_pairs={{0,1},{1,0},{2,3},{3,2},{4,5},{5,4},{6,7},{7,6},{8,9},{9,8},{10,11... | collective-permute-start | bytes 5505032 | tf_op jit(solution)/shard_map/ppermute | solution.py:469
  66.9 9.7 %copy-start.7 = (f32[1,2,1]{1,2,0:T(1,128)S(1)}, f32[1,2,1]{1,2,0:T(1,128)}, u32[]{:S(2)}) copy-start(f32[1,2,1]{1,2,0:T(1,128)} %param.30) | copy-start | bytes 28
  66.9 9.7 %copy-start.8 = (s32[1,2,1]{1,2,0:T(1,128)S(1)}, s32[1,2,1]{1,2,0:T(1,128)}, u32[]{:S(2)}) copy-start(s32[1,2,1]{1,2,0:T(1,128)} %param.29) | copy-start | bytes 28
  66.9 9.7 %copy-start.9 = (s32[8]{0:T(128)S(1)}, s32[8]{0:T(128)}, u32[]{:S(2)}) copy-start(s32[8]{0:T(128)} %constant.146) | copy-start | bytes 100
  72.3 9.9 %all-to-all-start.3 = ((bf16[8,2,7168]{2,1,0:T(2,128)(2,1)}), bf16[8,2,7168]{2,1,0:T(2,128)(2,1)S(1)}, u32[]{:S(2)}, u32[]{:S(2)}) async-start(bf16[8,2,7168]{2,1,0:T(2,128)(2,1)} %shard_map.178), calls=%async_computation.3 | async-start | bytes 458752 | tf_op jit(solution)/shard_map/all_to_all | solution.py:371

commit v8 on v7

--- a/solution.py
+++ b/solution.py
@@ -12,8 +12,8 @@
 UNITS = 128
 LANES = 128
 BLOCK = 1024
+EARLY = 5120
 PLANE = 4
-FRESH_ROWS = 16
 
 softmax_scale = 192.0 ** (-0.5)
 norm_epsilon = 1e-06
@@ -72,11 +72,11 @@
         copy.wait()
 
 
-def prefetch_kernel(after_ref, *refs):
+def prefetch_kernel(after_ref, upward_hbm, proj_hbm, upward_ref, early_ref, sems):
     del after_ref
-    count = (len(refs) - 1) // 2
     copies = [
-        pltpu.make_async_copy(refs[at], refs[count + at], refs[-1].at[at]) for at in range(count)
+        pltpu.make_async_copy(proj_hbm.at[:, :EARLY], early_ref, sems.at[0]),
+        pltpu.make_async_copy(upward_hbm, upward_ref, sems.at[1]),
     ]
     for copy in copies:
         copy.start()
@@ -109,25 +109,44 @@
         (terms * scale).astype(bf16), cache_ref[:KVR], contract_last, preferred_element_type=f32
     )
     mixed_ref[...] = (mixed + fresh_term * scale * fresh[:, :KVR]).reshape(mixed_ref.shape)
-    planes, _, per_peer, latent = mixed_ref.shape
-    rows = planes * per_peer
+    planes, _, per_peer, _ = mixed_ref.shape
     column = device_ref[0] % PLANE
     new_key = fresh_ref[1:2].astype(f32)
     rest = jnp.concatenate(
         [new_key[:, KVR:], jnp.zeros((1, 2 * KVR - new_key.shape[1]), f32)], axis=1
     )
-    line = lax.broadcasted_iota(jnp.int32, (FRESH_ROWS, KVR), 0)
-    key_rows = jnp.where(line == 0, new_key[:, :KVR], jnp.where(line == 1, rest, 0.0)).astype(bf16)
+    shape = message_refs[0].shape[1:]
+    blocks = message_refs[0].shape[0] - planes
     for at, message_ref in enumerate(message_refs):
-        message_ref[:rows] = mixed_ref[:, column ^ at].reshape(rows, latent).astype(bf16)
-        message_ref[rows:] = key_rows
+        message_ref[:planes] = mixed_ref[:, column ^ at].astype(bf16)
+        for block in range(blocks):
+            line = lax.broadcasted_iota(jnp.int32, shape, 0) + block * per_peer
+            key_rows = jnp.where(line == 0, new_key[:, :KVR], jnp.where(line == 1, rest, 0.0))
+            message_ref[planes + block] = key_rows.astype(bf16)
+
+
+def regroup_kernel(device_ref, *refs):
+    message_refs, out_refs = refs[:PLANE], refs[PLANE:]
+    per_peer = out_refs[0].shape[1]
+    plane = device_ref[0] // PLANE
+    planes = len(out_refs)
+    fresh = [message_ref[planes].astype(f32)[0:1] for message_ref in message_refs]
+    blocks = out_refs[0].shape[0] - PLANE
+    for at, out_ref in enumerate(out_refs):
+        for source, message_ref in enumerate(message_refs):
+            out_ref[source] = message_ref[plane ^ at]
+        for block in range(blocks):
+            line = lax.broadcasted_iota(jnp.int32, (per_peer, KVR), 0) + block * per_peer
+            rows = jnp.zeros((per_peer, KVR), f32)
+            for source, row in enumerate(fresh):
+                rows = jnp.where(line == source, row, rows)
+            out_ref[PLANE + block] = rows.astype(bf16)
 
 
 def prompt_kernel(device_ref, dest_ref, length_ref, slot_ref, *refs):
     key_refs, message_refs, query_hbm = refs[:PLANE], refs[PLANE : 2 * PLANE], refs[2 * PLANE]
     out_refs, (stage_ref, query_ref, sems) = refs[2 * PLANE + 1 : -3], refs[-3:]
-    planes, _, rows, width = stage_ref.shape
-    per_peer, chunk = rows // 2, width - KVR
+    planes, _, per_peer, width = stage_ref.shape
     heads = planes * per_peer
     tail = key_refs[0].shape[0] - KVR
     device = device_ref[0]
@@ -156,34 +175,27 @@
     log_sum = peak + jnp.log(total)
     scale = 1.0 / total
     terms = terms.astype(bf16)
-    lane = lax.broadcasted_iota(jnp.int32, (heads, chunk), 1)
-    fold = lambda value: value.reshape(planes, per_peer, value.shape[1])
+    lane = lax.broadcasted_iota(jnp.int32, (heads, width - KVR), 1)
     for at in range(PLANE):
         part = slice(at * heads, (at + 1) * heads)
         mixed = lax.dot_general(
             terms[part], key_refs[at][:KVR], contract_last, preferred_element_type=f32
         )
-        resident = message_refs[at][:heads, :KVR].astype(f32)
-        stage_ref[:, at, :, :KVR] = jnp.concatenate(
-            [fold(mixed * scale[part]), fold(resident)], axis=1
-        ).astype(bf16)
-        fresh = message_refs[at][heads : heads + FRESH_ROWS].astype(f32)
+        mixed = (mixed * scale[part]).reshape(planes, per_peer, KVR)
+        stage_ref[:, at, :, :KVR] = mixed.astype(bf16)
+        fresh = message_refs[at][planes:].astype(f32)
+        fresh = fresh.reshape(fresh.shape[0] * per_peer, KVR)
         fresh, fresh_rest = fresh[0:1], fresh[1:2, :tail]
         latent, rest = unpack(query_ref[PLANE + at], heads, tail)
         fresh_score = softmax_scale * (
             jnp.sum(latent.astype(f32) * fresh, axis=1, keepdims=True)
             + jnp.sum(rest.astype(f32) * fresh_rest, axis=1, keepdims=True)
         )
-        stats = jnp.zeros((heads, chunk), f32)
+        stats = jnp.zeros((heads, width - KVR), f32)
         for lane_at, value in enumerate(three_parts(log_sum[part]) + three_parts(fresh_score)):
             stats = jnp.where(lane == lane_at, value, stats)
-        fresh_rows = [fresh[:, start : start + chunk] for start in range(0, KVR, chunk)]
-        if len(fresh_rows) < per_peer:
-            fresh_rows.append(jnp.zeros((per_peer - len(fresh_rows), chunk), f32))
-        fresh_rows = jnp.concatenate(fresh_rows, axis=0)[None]
-        stage_ref[:, at, :, KVR:] = jnp.concatenate(
-            [fold(stats), jnp.broadcast_to(fresh_rows, (planes, per_peer, chunk))], axis=1
-        ).astype(bf16)
+        stats = stats.reshape(planes, per_peer, width - KVR)
+        stage_ref[:, at, :, KVR:] = stats.astype(bf16)
     for at, out_ref in enumerate(out_refs):
         out_ref[...] = stage_ref[(device // PLANE) ^ at]
 
@@ -192,39 +204,48 @@
     pair_ref[...] = (keep_ref[...] + other_ref[...].astype(f32)).astype(bf16)
 
 
-def heads_kernel(row_ref, column_ref, peer_ref, upward_ref, proj_ref, *refs):
-    payload_refs, (keep_ref, send_ref, rows_ref) = refs[:-3], refs[-3:]
-    for at, payload_ref in enumerate(payload_refs):
-        rows_ref[at * PLANE : (at + 1) * PLANE] = payload_ref[...]
-    peers, rows, width = rows_ref.shape
-    per_peer = rows // 2
-    columns = peers * rows
+def heads_kernel(row_ref, column_ref, peer_ref, upward_ref, early_ref, *refs):
+    proj_hbm, keep_ref, send_ref, partial_ref, resident_ref, fresh_ref, late_ref, sems = refs[-8:]
+    planes = (len(refs) - 8) // 2
+    depth, model = proj_hbm.shape
+    loads = []
+    for at in range(2):
+        part = slice(at * depth // 2, (at + 1) * depth // 2)
+        loads.append(
+            pltpu.make_async_copy(proj_hbm.at[part, EARLY:], late_ref.at[part], sems.at[at])
+        )
+        loads[at].start()
+    for at in range(planes):
+        places = slice(at * PLANE, (at + 1) * PLANE)
+        partial_ref[places] = refs[at][...]
+        arrived = refs[planes + at]
+        resident_ref[places] = arrived[:PLANE]
+        fresh = arrived[PLANE:].astype(f32)
+        fresh_ref[places] = fresh.reshape(fresh.shape[0] * fresh.shape[1], KVR)[:PLANE]
+    peers, per_peer, _ = partial_ref.shape
+    columns = peers * per_peer
     both = 2 * peers
     row_head, row_device, row_new = row_ref[:, 0:1], row_ref[:, 1:2], row_ref[:, 2:3]
-    col_peer, col_row, col_dest = column_ref[0:1, :], column_ref[1:2, :], column_ref[2:3, :]
-    stats = rows_ref[:, :, KVR : KVR + LANES].astype(f32).reshape(columns, LANES).T
+    col_peer, col_head, col_dest = column_ref[0:1, :], column_ref[1:2, :], column_ref[2:3, :]
+    stats = partial_ref[:, :, KVR:].astype(f32).reshape(columns, LANES).T
     log_sum = stats[0:1] + stats[1:2] + stats[2:3]
     fresh_score = stats[3:4] + stats[4:5] + stats[5:6]
-    same_head = col_row == row_head
-    own = col_peer == row_device
+    same_head = col_head == row_head
+    own = same_head & (col_peer == row_device)
     new_row = row_new == 1
     arrives = same_head & (col_dest == row_device) & new_row
-    fresh = jnp.sum(jnp.where(same_head & own, fresh_score, 0.0), axis=1, keepdims=True)
+    fresh = jnp.sum(jnp.where(own, fresh_score, 0.0), axis=1, keepdims=True)
     scored = jnp.where(arrives, log_sum, -jnp.inf)
     peak = jnp.maximum(jnp.max(scored, axis=1, keepdims=True), fresh)
     terms = jnp.exp(scored - peak)
     fresh_term = jnp.exp(fresh - peak)
     scale = 1.0 / (jnp.sum(terms, axis=1, keepdims=True) + fresh_term)
-    resident = jnp.where(own & (col_row == row_head + per_peer), 1.0, 0.0)
-    mixing = jnp.where(new_row, terms * scale, resident)
     fresh_mixing = jnp.where((peer_ref[...] == row_device) & new_row, fresh_term * scale, 0.0)
-    chunk = width - KVR
-    fresh_rows = jnp.concatenate(
-        [rows_ref[:, per_peer + at, KVR:] for at in range(KVR // chunk)], axis=1
-    )
-    latents = rows_ref[:, :, :KVR].reshape(columns, KVR)
-    mixed = jnp.zeros((row_ref.shape[0], KVR), f32)
-    for weights, values in ((mixing, latents), (fresh_mixing, fresh_rows)):
+    resident_mixing = jnp.where(own & (row_new == 0), 1.0, 0.0).astype(bf16)
+    resident = resident_ref[...].reshape(columns, KVR)
+    mixed = jnp.dot(resident_mixing, resident, preferred_element_type=f32)
+    latents = partial_ref[:, :, :KVR].reshape(columns, KVR)
+    for weights, values in ((terms * scale, latents), (fresh_mixing, fresh_ref[...].astype(bf16))):
         high = weights.astype(bf16)
         low = (weights - high.astype(f32)).astype(bf16)
         mixed = mixed + jnp.dot(high, values, preferred_element_type=f32)
@@ -239,8 +260,15 @@
         ],
         axis=1,
     )
-    for start in range(0, proj_ref.shape[1], BLOCK):
-        part = jnp.dot(value_rows, proj_ref[:, start : start + BLOCK], preferred_element_type=f32)
+    for start in range(0, model, BLOCK):
+        if start == EARLY - BLOCK:
+            for load in loads:
+                load.wait()
+        if start < EARLY:
+            weights = early_ref[:, start : start + BLOCK]
+        else:
+            weights = late_ref[:, start - EARLY : start - EARLY + BLOCK]
+        part = jnp.dot(value_rows, weights, preferred_element_type=f32)
         columns = slice(start, start + BLOCK)
         keep_ref[:, :, columns] = part[:peers].reshape(peers // 2, 2, BLOCK)
         send_ref[:, :, columns] = part[peers:].reshape(peers // 2, 2, BLOCK).astype(bf16)
@@ -320,19 +348,25 @@
     )(*map(distant, operands))
 
 
-def prefetch(after, weights):
+def prefetch(after, upward, projection):
     return pl.pallas_call(
         prefetch_kernel,
-        out_shape=[pltpu.VMEM(weight.shape, weight.dtype) for weight in weights],
-        in_specs=[pl.BlockSpec(memory_space=pl.ANY)] * (1 + len(weights)),
-        out_specs=[whole] * len(weights),
-        scratch_shapes=[pltpu.SemaphoreType.DMA((len(weights),))],
+        out_shape=[pltpu.VMEM(upward.shape, bf16), pltpu.VMEM((len(projection), EARLY), bf16)],
+        in_specs=[pl.BlockSpec(memory_space=pl.ANY)] * 3,
+        out_specs=[whole] * 2,
+        scratch_shapes=[pltpu.SemaphoreType.DMA((2,))],
         compiler_params=pltpu.CompilerParams(vmem_limit_bytes=16 << 20),
-    )(after, *map(distant, weights))
-
-
-def middle_first(count):
-    return sorted(range(count), key=lambda at: abs(4 * at - 2 * count + 1))
+    )(after, distant(upward), distant(projection))
+
+
+def middle_first(chips):
+    middle = chips // 4
+    return [
+        2 * plane + chip
+        for ring in range(middle)
+        for chip in range(2)
+        for plane in (middle + ring, middle - 1 - ring)
+    ]
 
 
 def shards(
@@ -404,7 +438,7 @@
     flipped_cache = jnp.swapaxes(resident_cache[0], 0, 1)
     messages = call(
         resident_kernel,
-        [((planes * per_peer + FRESH_ROWS, KVR), bf16)] * PLANE,
+        [((planes + -(-2 // per_peer), per_peer, KVR), bf16)] * PLANE,
         [own_device, resident_len, new_latent[0]],
         [spread_rows, distant(flipped), distant(flipped_cache)],
         [
@@ -417,19 +451,27 @@
     )
     messages = [toward(message, at) for at, message in enumerate(messages)]
 
-    chunk = max(LANES, KVR // per_peer)
+    residents = call(
+        regroup_kernel,
+        [((PLANE + -(-PLANE // per_peer), per_peer, KVR), bf16)] * planes,
+        [own_device, *messages],
+        cost=short,
+    )
+    residents = [toward(resident, at * PLANE) for at, resident in enumerate(residents)]
+
     payloads = call(
         prompt_kernel,
-        [((PLANE, 2 * per_peer, KVR + chunk), bf16)] * planes,
+        [((PLANE, per_peer, KVR + LANES), bf16)] * planes,
         [own_device, handoff_dest, handoff_len, jnp.array(slots, jnp.int32), *plane_keys, *messages],
         [spread],
         [
-            pltpu.VMEM((planes, PLANE, 2 * per_peer, KVR + chunk), bf16),
+            pltpu.VMEM((planes, PLANE, per_peer, KVR + LANES), bf16),
             pltpu.VMEM((2 * PLANE, *spread_shape[1:]), bf16),
             pltpu.SemaphoreType.DMA((2 * PLANE,)),
         ],
     )
-    upward, projection = prefetch(payloads[0], [value_upward, out_proj.reshape(-1, model)])
+    projection = out_proj.reshape(-1, model)
+    upward, early = prefetch(payloads[0], value_upward, projection)
     payloads = [toward(payload, at * PLANE) for at, payload in enumerate(payloads)]
 
     row = jnp.arange(per_peer * 2 * devices, dtype=jnp.int32)
@@ -440,20 +482,22 @@
     peers = device.astype(jnp.int32) ^ jnp.arange(devices, dtype=jnp.int32)
     is_peer = peers[:, None] == jnp.arange(devices, dtype=jnp.int32)[None, :]
     peer_dest = jnp.sum(jnp.where(is_peer, handoff_dest[None, :], 0), axis=1)
-    column = jnp.arange(devices * 2 * per_peer, dtype=jnp.int32)
+    column = jnp.arange(devices * per_peer, dtype=jnp.int32)
     column_table = jnp.stack(
-        [
-            jnp.repeat(peers, 2 * per_peer),
-            column % (2 * per_peer),
-            jnp.repeat(peer_dest, 2 * per_peer),
-        ],
-        axis=0,
+        [jnp.repeat(peers, per_peer), column % per_peer, jnp.repeat(peer_dest, per_peer)], axis=0
     )
     keep, send = call(
         heads_kernel,
         [((chips, 2, model), f32), ((chips, 2, model), bf16)],
-        [row_table, column_table, peers[None], upward, projection, *payloads],
-        scratch=[pltpu.VMEM((devices, 2 * per_peer, KVR + chunk), bf16)],
+        [row_table, column_table, peers[None], upward, early, *payloads, *residents],
+        [distant(projection)],
+        [
+            pltpu.VMEM((devices, per_peer, KVR + LANES), bf16),
+            pltpu.VMEM((devices, per_peer, KVR), bf16),
+            pltpu.VMEM((devices, KVR), f32),
+            pltpu.VMEM((len(projection), model - EARLY), bf16),
+            pltpu.SemaphoreType.DMA((2,)),
+        ],
     )
 
     other = lax.ppermute(send, "ep", siblings)

time: 83.7 us -> 82.8 us (0.989)
  waiting for transfers between devices: 20.1 us -> 14.7 us
  starting transfers between devices: 26.9 us -> 32.3 us
  Pallas kernels: 23 us -> 21.8 us
    ppermute x9 -> x12, starting transfers between devices: 9.86 us -> 15.7 us  [shards(): lax.ppermute(value, 'ep', [(i, i ^ bits) for i in range(devices)])]
    all_to_all x3, waiting for transfers between devices: 15.4 us -> 10.3 us  [exchange(): lax.all_to_all(value, 'ep', split_axis=0, concat_axis=0, tiled=True, axis...]
    pallas_call x1, Pallas kernels: 5.53 us -> 4.23 us  [prefetch(): pl.pallas_call(prefetch_kernel, out_shape=[pltpu.VMEM(upward.shape, bf16)...]
    ppermute x9 -> x12, waiting for transfers between devices: 3.24 us -> 2.98 us  [shards(): lax.ppermute(value, 'ep', [(i, i ^ bits) for i in range(devices)])]
    pallas_call x5 -> x6, Pallas kernels: 15.4 us -> 15.5 us  [call(): pl.pallas_call(kernel, out_shape=[pltpu.VMEM(shape, dtype) for shape, dty...]
  transfers between devices with their start and end apart: 16 -> 19, of which waited for: 6 -> 5; matrix products, arithmetic and copies ran while one was open for 2% -> 2% of each run, Pallas kernels for 13% -> 14%
where the time goes in v8:
time: 82.8 us; the launch traced here: 82.3 us
  starting transfers between devices  32.3 us (39%)
  Pallas kernels  21.8 us (26%)
  waiting for transfers between devices  14.7 us (18%)
  blocking collectives  9.86 us (12%)
  other arithmetic  1.83 us (2%)
  between operations  1.02 us (1%)
    all_to_all x3, starting transfers between devices, exchange(): lax.all_to_all(value, 'ep', split_axis=0, concat_axis=0, tiled=True, axis...  16.1 us
    ppermute x12, starting transfers between devices, shards(): lax.ppermute(value, 'ep', [(i, i ^ bits) for i in range(devices)])  15.7 us
    pallas_call x6, Pallas kernels, call(): pl.pallas_call(kernel, out_shape=[pltpu.VMEM(shape, dtype) for shape, dty...  15.5 us
    all_to_all x3, waiting for transfers between devices, exchange(): lax.all_to_all(value, 'ep', split_axis=0, concat_axis=0, tiled=True, axis...  10.3 us
    all_to_all x1, blocking collectives, exchange(): lax.all_to_all(value, 'ep', split_axis=0, concat_axis=0, tiled=True, axis...  9.86 us
    pallas_call x1, Pallas kernels, prefetch(): pl.pallas_call(prefetch_kernel, out_shape=[pltpu.VMEM(upward.shape, bf16)...  4.23 us
    ppermute x12, waiting for transfers between devices, shards(): lax.ppermute(value, 'ep', [(i, i ^ bits) for i in range(devices)])  2.98 us
    pallas_call x1, Pallas kernels, call_far(): pl.pallas_call(kernel, out_shape=shapes, in_specs=[far] * len(operands),...  2.05 us
  transfers between devices with their start and end apart: 19, of which 5 were waited for; matrix products, arithmetic and copies ran while one was open for 2% of the time, Pallas kernels for 14%

profile of v8, /device:TPU:0, one launch (start us, length us, event | category | flops | bytes accessed | tf_op | source)
XLA Modules:
  0.0 82.3 jit_solution(5000678874554352495)
XLA Ops:
  0.0 2.9 %collective-permute-start.1 = (bf16[576,256]{1,0:T(8,128)(2,1)}, bf16[576,256]{1,0:T(8,128)(2,1)S(1)}, u32[]{:S(2)}, u32[]{:S(2)}) collective-permute-start(bf16[576,256]{1,0:T(8,128)(2,1)} %bitcast.38), channel_id=1, source_target_pairs={{0,2},{1,3},{2,0},{3,1},{4,6},{5,7},{6,4},{7,5},{8,10},{9,11},{10,... | collective-permute-start | bytes 884744 | tf_op jit(solution)/shard_map/ppermute | solution.py:412
  2.9 2.1 %shard_map.172.after_ref = bf16[16,144,128]{2,1,0:T(8,128)(2,1)} custom-call(bf16[2,576,128]{2,1,0:T(8,128)(2,1)} %bitcast.44), custom_call_target="tpu_custom_call" | custom-call | tf_op jit(solution)/shard_map/pallas_call | solution.py:340
  5.0 6.0 %all-to-all-start = ((bf16[16,144,128]{2,1,0:T(8,128)(2,1)}), bf16[16,144,128]{2,1,0:T(8,128)(2,1)S(1)}, u32[]{:S(2)}, u32[]{:S(2)}) async-start(bf16[16,144,128]{2,1,0:T(8,128)(2,1)} %shard_map.172.after_ref), calls=%async_computation | async-start | bytes 1179648 | tf_op jit(solution)/shard_map/all_to_all | solution.py:405
  11.7 0.0 copy-start.1
  11.7 0.0 copy-start.2
  11.7 0.0 copy-start.3
  11.7 3.4 %shard_map.173 = (bf16[5,8,512]{2,1,0:T(8,128)(2,1)S(1)}, bf16[5,8,512]{2,1,0:T(8,128)(2,1)S(1)}, bf16[5,8,512]{2,1,0:T(8,128)(2,1)S(1)}, bf16[5,8,512]{2,1,0:T(8,128)(2,1)S(1)}) custom-call(s32[1]{0:T(128)} %bitcast.2.device_ref, s32[1]{0:T(128)S(6)} %copy.22.length_ref, bf16[2,576]{1,0:T(2,128)(2,1)S(1)} %bitcast.41, ...), custom_call_target="tpu_custom_call" | custom-call | flops 6000000000 | bytes 30000000 | tf_op jit(solution)/shard_map/pallas_call | solution.py:324
  15.2 0.2 collective-permute-start.3
  15.4 1.5 %collective-permute-start.4 = (bf16[5,8,512]{2,1,0:T(8,128)(2,1)S(1)}, bf16[5,8,512]{2,1,0:T(8,128)(2,1)S(1)}, u32[]{:S(2)}, u32[]{:S(2)}) collective-permute-start(bf16[5,8,512]{2,1,0:T(8,128)(2,1)S(1)} %get-tuple-element.23), channel_id=1, source_target_pairs={{0,2},{1,3},{2,0},{3,1},{4,6},{5,7},{6,4},{7,5},{8,10},{9,11},{10,... | collective-permute-start | bytes 122888 | tf_op jit(solution)/shard_map/ppermute | solution.py:412
  16.9 0.2 collective-permute-start.5
  17.2 0.2 select_reduce_fusion
  17.4 0.5 collective-permute-start.2
  17.9 0.1 broadcast_in_dim.42
  18.0 0.1 stack_reshape.7
  18.1 0.1 broadcast_in_dim.22
  18.2 0.1 stack_reshape.6
  18.3 2.6 %collective-permute-done.4.refs_6_.refs_2_ = bf16[5,8,512]{2,1,0:T(8,128)(2,1)S(1)} collective-permute-done((bf16[5,8,512]{2,1,0:T(8,128)(2,1)S(1)}, bf16[5,8,512]{2,1,0:T(8,128)(2,1)S(1)}, u32[]{:S(2)}, u32[]{:S(2)}) %collective-permute-start.4) | collective-permute-done | bytes 40992 | tf_op jit(solution)/shard_map/ppermute | solution.py:412
  20.9 0.3 collective-permute-done.5.refs_7_.refs_3_
  21.3 0.1 collective-permute-start.10
  21.3 2.1 %collective-permute-start.11 = (bf16[5,8,512]{2,1,0:T(8,128)(2,1)S(1)}, bf16[5,8,512]{2,1,0:T(8,128)(2,1)S(1)}, u32[]{:S(2)}, u32[]{:S(2)}) collective-permute-start(bf16[5,8,512]{2,1,0:T(8,128)(2,1)S(1)} %get-tuple-element.34), channel_id=1, source_target_pairs={{0,12},{1,13},{2,14},{3,15},{4,8},{5,9},{6,10},{7,11},{8,4},{9,5},... | collective-permute-start | bytes 122888 | tf_op jit(solution)/shard_map/ppermute | solution.py:412
  23.5 1.3 %collective-permute-start.9 = (bf16[5,8,512]{2,1,0:T(8,128)(2,1)S(1)}, bf16[5,8,512]{2,1,0:T(8,128)(2,1)S(1)}, u32[]{:S(2)}, u32[]{:S(2)}) collective-permute-start(bf16[5,8,512]{2,1,0:T(8,128)(2,1)S(1)} %get-tuple-element.32), channel_id=1, source_target_pairs={{0,4},{1,5},{2,6},{3,7},{4,0},{5,1},{6,2},{7,3},{8,12},{9,13},{10,... | collective-permute-start | bytes 122888 | tf_op jit(solution)/shard_map/ppermute | solution.py:412
  24.9 1.8 %shard_map.174 = (bf16[4,8,640]{2,1,0:T(8,128)(2,1)S(1)}, bf16[4,8,640]{2,1,0:T(8,128)(2,1)S(1)}, bf16[4,8,640]{2,1,0:T(8,128)(2,1)S(1)}, bf16[4,8,640]{2,1,0:T(8,128)(2,1)S(1)}) custom-call(s32[1]{0:T(128)} %bitcast.2.device_ref, s32[16]{0:T(128)S(1)} %copy-done.1, s32[16]{0:T(128)S(1)} %copy-done.2, s32[16]{0:T(128)S(1)} %copy-done.3, ...), custom_call_target="tpu_custom_call" | custom-call | tf_op jit(solution)/shard_map/pallas_call | solution.py:324
  26.6 4.3 %collective-permute-start.6 = (bf16[4,8,640]{2,1,0:T(8,128)(2,1)S(1)}, bf16[4,8,640]{2,1,0:T(8,128)(2,1)S(1)}, u32[]{:S(2)}, u32[]{:S(2)}) collective-permute-start(bf16[4,8,640]{2,1,0:T(8,128)(2,1)S(1)} %get-tuple-element.28), channel_id=1, source_target_pairs={{0,4},{1,5},{2,6},{3,7},{4,0},{5,1},{6,2},{7,3},{8,12},{9,13},{10,... | collective-permute-start | bytes 122888 | tf_op jit(solution)/shard_map/ppermute | solution.py:412
  30.9 0.1 collective-permute-start.7
  31.0 2.4 %collective-permute-start.8 = (bf16[4,8,640]{2,1,0:T(8,128)(2,1)S(1)}, bf16[4,8,640]{2,1,0:T(8,128)(2,1)S(1)}, u32[]{:S(2)}, u32[]{:S(2)}) collective-permute-start(bf16[4,8,640]{2,1,0:T(8,128)(2,1)S(1)} %get-tuple-element.30), channel_id=1, source_target_pairs={{0,12},{1,13},{2,14},{3,15},{4,8},{5,9},{6,10},{7,11},{8,4},{9,5},... | collective-permute-start | bytes 122888 | tf_op jit(solution)/shard_map/ppermute | solution.py:412
  33.4 0.1 copy.21.row_ref
  33.5 4.2 %shard_map.175 = (bf16[8,512,128]{2,1,0:T(8,128)(2,1)S(1)}, bf16[1024,5120]{1,0:T(8,128)(2,1)S(1)}) custom-call(bf16[4,8,640]{2,1,0:T(8,128)(2,1)S(1)} %get-tuple-element.25.after_ref.refs_0_, bf16[8,512,128]{2,1,0:T(8,128)(2,1)} %upward_hbm.1, bf16[1024,7168]{1,0:T(8,128)(2,1)} %bitcast.42), custom_call_target="tpu_custom_call" | custom-call | tf_op jit(solution)/shard_map/pallas_call | solution.py:352
  37.8 4.1 %shard_map.177 = (f32[8,2,7168]{2,1,0:T(2,128)S(1)}, bf16[8,2,7168]{2,1,0:T(2,128)(2,1)S(1)}) custom-call(s32[256,3]{1,0:T(8,128)S(1)} %copy.21.row_ref, s32[3,128]{1,0:T(4,128)S(1)} %pad_add_fusion.1.column_ref, s32[1,16]{1,0:T(1,128)S(1)} %iota_xor_fusion.peer_ref, bf16[8,512,128]{2,1,0:T(8,128)(2,1)S(1)} %get-tuple-element.26.upward_ref, ...), custom_call_target="tpu_custom_call" | custom-call | tf_op jit(solution)/shard_map/pallas_call | solution.py:324
  41.9 0.1 collective-permute-start.12
  42.0 1.5 %collective-permute-done.12.other_ref = bf16[8,2,7168]{2,1,0:T(2,128)(2,1)S(1)} collective-permute-done((bf16[8,2,7168]{2,1,0:T(2,128)(2,1)S(1)}, bf16[8,2,7168]{2,1,0:T(2,128)(2,1)S(1)}, u32[]{:S(2)}, u32[]{:S(2)}) %collective-permute-start.12) | collective-permute-done | bytes 229408 | tf_op jit(solution)/shard_map/ppermute | solution.py:503
  43.5 0.9 %shard_map.178 = bf16[8,2,7168]{2,1,0:T(2,128)(2,1)} custom-call(f32[8,2,7168]{2,1,0:T(2,128)S(1)} %get-tuple-element.35.keep_ref, bf16[8,2,7168]{2,1,0:T(2,128)(2,1)S(1)} %collective-permute-done.12.other_ref), custom_call_target="tpu_custom_call" | custom-call | tf_op jit(solution)/shard_map/pallas_call | solution.py:324
  44.3 4.4 %all-to-all-start.1 = ((bf16[8,2,7168]{2,1,0:T(2,128)(2,1)}), bf16[8,2,7168]{2,1,0:T(2,128)(2,1)S(1)}, u32[]{:S(2)}, u32[]{:S(2)}) async-start(bf16[8,2,7168]{2,1,0:T(2,128)(2,1)} %shard_map.178), calls=%async_computation.1 | async-start | bytes 458752 | tf_op jit(solution)/shard_map/all_to_all | solution.py:405
  48.7 0.5 collective-permute-start.14
  49.3 5.6 %all-to-all-done.1 = bf16[8,2,7168]{2,1,0:T(2,128)(2,1)S(1)} async-done(((bf16[8,2,7168]{2,1,0:T(2,128)(2,1)}), bf16[8,2,7168]{2,1,0:T(2,128)(2,1)S(1)}, u32[]{:S(2)}, u32[]{:S(2)}) %all-to-all-start.1) | async-done | bytes 229408 | tf_op jit(solution)/shard_map/all_to_all | solution.py:405
  54.9 0.2 convert_reduce_fusion
  55.1 0.2 fusion.2
  55.3 0.1 fusion.4
  55.4 0.1 broadcast_in_dim.45
  55.5 9.9 %all_to_all.20 = bf16[8,2,7168]{2,1,0:T(2,128)(2,1)S(1)} all-to-all(bf16[8,2,7168]{2,1,0:T(2,128)(2,1)S(1)} %broadcast_in_dim.45), channel_id=1, replica_groups={{8,4,10,6,12,0,14,2},{9,5,11,7,13,1,15,3},{24,20,26,22,28,16,30,18},{25..., dimensions={0} | all-to-all | bytes 458752 | tf_op jit(solution)/shard_map/all_to_all | solution.py:405
  65.4 0.1 reshape.289.rows_ref
  65.5 0.0 copy-start.7
  65.5 0.0 copy-start.9
  65.5 5.4 %shard_map.179 = bf16[8,2,7168]{2,1,0:T(2,128)(2,1)} custom-call(bf16[16,7168]{1,0:T(8,128)(2,1)S(1)} %reshape.289.rows_ref, bf16[128,7168]{1,0:T(8,128)(2,1)} %refs_0_.1, bf16[128,7168]{1,0:T(8,128)(2,1)S(1)} %collective-permute-done.13.refs_1_, bf16[128,7168]{1,0:T(8,128)(2,1)} %refs_2_.1, bf16[128,7168]{1,0:T(8,128)(2,1)} %collective-permute-done.14.refs_3_, ...), custom_call_target="tpu_custom_call" | custom-call | tf_op jit(solution)/shard_map/pallas_call | solution.py:324
  70.9 5.7 %all-to-all-start.3 = ((bf16[8,2,7168]{2,1,0:T(2,128)(2,1)}), bf16[8,2,7168]{2,1,0:T(2,128)(2,1)S(1)}, u32[]{:S(2)}, u32[]{:S(2)}) async-start(bf16[8,2,7168]{2,1,0:T(2,128)(2,1)} %shard_map.179), calls=%async_computation.3 | async-start | bytes 458752 | tf_op jit(solution)/shard_map/all_to_all | solution.py:405
  76.6 0.1 compare_select_fusion.11
  76.7 4.6 %all-to-all-done.3 = bf16[8,2,7168]{2,1,0:T(2,128)(2,1)S(1)} async-done(((bf16[8,2,7168]{2,1,0:T(2,128)(2,1)}), bf16[8,2,7168]{2,1,0:T(2,128)(2,1)S(1)}, u32[]{:S(2)}, u32[]{:S(2)}) %all-to-all-start.3) | async-done | bytes 229408 | tf_op jit(solution)/shard_map/all_to_all | solution.py:405
  81.4 0.3 multiply_reduce_fusion
  81.7 0.7 fusion.3
  (45 shorter events, 0.2 us)
Async XLA Ops:
  0.0 11.7 %copy-start.4 = (bf16[1,2,576]{2,1,0:T(2,128)(2,1)S(1)}, bf16[1,2,576]{2,1,0:T(2,128)(2,1)}, u32[]{:S(2)}) copy-start(bf16[1,2,576]{2,1,0:T(2,128)(2,1)} %param.24) | copy-start | bytes 6916
  0.0 17.4 %collective-permute-start.1 = (bf16[576,256]{1,0:T(8,128)(2,1)}, bf16[576,256]{1,0:T(8,128)(2,1)S(1)}, u32[]{:S(2)}, u32[]{:S(2)}) collective-permute-start(bf16[576,256]{1,0:T(8,128)(2,1)} %bitcast.38), channel_id=1, source_target_pairs={{0,2},{1,3},{2,0},{3,1},{4,6},{5,7},{6,4},{7,5},{8,10},{9,11},{10,... | collective-permute-start | bytes 884744 | tf_op jit(solution)/shard_map/ppermute | solution.py:412
  2.9 21.9 %collective-permute-start = (bf16[576,256]{1,0:T(8,128)(2,1)}, bf16[576,256]{1,0:T(8,128)(2,1)S(1)}, u32[]{:S(2)}, u32[]{:S(2)}) collective-permute-start(bf16[576,256]{1,0:T(8,128)(2,1)} %bitcast.39), channel_id=1, source_target_pairs={{0,1},{1,0},{2,3},{3,2},{4,5},{5,4},{6,7},{7,6},{8,9},{9,8},{10,11... | collective-permute-start | bytes 884744 | tf_op jit(solution)/shard_map/ppermute | solution.py:412
  5.0 19.8 %all-to-all-start = ((bf16[16,144,128]{2,1,0:T(8,128)(2,1)}), bf16[16,144,128]{2,1,0:T(8,128)(2,1)S(1)}, u32[]{:S(2)}, u32[]{:S(2)}) async-start(bf16[16,144,128]{2,1,0:T(8,128)(2,1)} %shard_map.172.after_ref), calls=%async_computation | async-start | bytes 1179648 | tf_op jit(solution)/shard_map/all_to_all | solution.py:405
  11.7 5.5 %copy-start.1 = (s32[16]{0:T(128)S(1)}, s32[16]{0:T(128)}, u32[]{:S(2)}) copy-start(s32[16]{0:T(128)} %dest_ref.1) | copy-start | bytes 196
  11.7 13.2 %copy-start = (bf16[1,256,576]{1,2,0:T(8,128)(2,1)S(1)}, bf16[1,256,576]{1,2,0:T(8,128)(2,1)}, u32[]{:S(2)}) copy-start(bf16[1,256,576]{1,2,0:T(8,128)(2,1)} %param.18) | copy-start | bytes 884740
  11.7 13.2 %copy-start.2 = (s32[16]{0:T(128)S(1)}, s32[16]{0:T(128)}, u32[]{:S(2)}) copy-start(s32[16]{0:T(128)} %length_ref.2) | copy-start | bytes 196
  11.7 13.1 %copy-start.3 = (s32[16]{0:T(128)S(1)}, s32[16]{0:T(128)}, u32[]{:S(2)}) copy-start(s32[16]{0:T(128)} %constant.118.clone.slot_ref) | copy-start | bytes 196
  15.2 3.1 %collective-permute-start.3 = (bf16[5,8,512]{2,1,0:T(8,128)(2,1)S(1)}, bf16[5,8,512]{2,1,0:T(8,128)(2,1)S(1)}, u32[]{:S(2)}, u32[]{:S(2)}) collective-permute-start(bf16[5,8,512]{2,1,0:T(8,128)(2,1)S(1)} %get-tuple-element.22), channel_id=1, source_target_pairs={{0,1},{1,0},{2,3},{3,2},{4,5},{5,4},{6,7},{7,6},{8,9},{9,8},{10,11... | collective-permute-start | bytes 122888 | tf_op jit(solution)/shard_map/ppermute | solution.py:412
  15.4 5.5 %collective-permute-start.4 = (bf16[5,8,512]{2,1,0:T(8,128)(2,1)S(1)}, bf16[5,8,512]{2,1,0:T(8,128)(2,1)S(1)}, u32[]{:S(2)}, u32[]{:S(2)}) collective-permute-start(bf16[5,8,512]{2,1,0:T(8,128)(2,1)S(1)} %get-tuple-element.23), channel_id=1, source_target_pairs={{0,2},{1,3},{2,0},{3,1},{4,6},{5,7},{6,4},{7,5},{8,10},{9,11},{10,... | collective-permute-start | bytes 122888 | tf_op jit(solution)/shard_map/ppermute | solution.py:412
  16.9 4.4 %collective-permute-start.5 = (bf16[5,8,512]{2,1,0:T(8,128)(2,1)S(1)}, bf16[5,8,512]{2,1,0:T(8,128)(2,1)S(1)}, u32[]{:S(2)}, u32[]{:S(2)}) collective-permute-start(bf16[5,8,512]{2,1,0:T(8,128)(2,1)S(1)} %get-tuple-element.24), channel_id=1, source_target_pairs={{0,3},{1,2},{2,1},{3,0},{4,7},{5,6},{6,5},{7,4},{8,11},{9,10},{10,... | collective-permute-start | bytes 122888 | tf_op jit(solution)/shard_map/ppermute | solution.py:412
  17.4 7.4 %collective-permute-start.2 = (bf16[576,256]{1,0:T(8,128)(2,1)S(1)}, bf16[576,256]{1,0:T(8,128)(2,1)S(1)}, u32[]{:S(2)}, u32[]{:S(2)}) collective-permute-start(bf16[576,256]{1,0:T(8,128)(2,1)S(1)} %collective-permute-done.1.refs_2_), channel_id=1, source_target_pairs={{0,1},{1,0},{2,3},{3,2},{4,5},{5,4},{6,7},{7,6},{8,9},{9,8},{10,11... | collective-permute-start | bytes 884744 | tf_op jit(solution)/shard_map/ppermute | solution.py:412
  21.3 9.8 %collective-permute-start.10 = (bf16[5,8,512]{2,1,0:T(8,128)(2,1)S(1)}, bf16[5,8,512]{2,1,0:T(8,128)(2,1)S(1)}, u32[]{:S(2)}, u32[]{:S(2)}) collective-permute-start(bf16[5,8,512]{2,1,0:T(8,128)(2,1)S(1)} %get-tuple-element.33), channel_id=1, source_target_pairs={{0,8},{1,9},{2,10},{3,11},{4,12},{5,13},{6,14},{7,15},{8,0},{9,1},... | collective-permute-start | bytes 122888 | tf_op jit(solution)/shard_map/ppermute | solution.py:412
  21.3 16.4 %collective-permute-start.11 = (bf16[5,8,512]{2,1,0:T(8,128)(2,1)S(1)}, bf16[5,8,512]{2,1,0:T(8,128)(2,1)S(1)}, u32[]{:S(2)}, u32[]{:S(2)}) collective-permute-start(bf16[5,8,512]{2,1,0:T(8,128)(2,1)S(1)} %get-tuple-element.34), channel_id=1, source_target_pairs={{0,12},{1,13},{2,14},{3,15},{4,8},{5,9},{6,10},{7,11},{8,4},{9,5},... | collective-permute-start | bytes 122888 | tf_op jit(solution)/shard_map/ppermute | solution.py:412
  23.5 14.3 %collective-permute-start.9 = (bf16[5,8,512]{2,1,0:T(8,128)(2,1)S(1)}, bf16[5,8,512]{2,1,0:T(8,128)(2,1)S(1)}, u32[]{:S(2)}, u32[]{:S(2)}) collective-permute-start(bf16[5,8,512]{2,1,0:T(8,128)(2,1)S(1)} %get-tuple-element.32), channel_id=1, source_target_pairs={{0,4},{1,5},{2,6},{3,7},{4,0},{5,1},{6,2},{7,3},{8,12},{9,13},{10,... | collective-permute-start | bytes 122888 | tf_op jit(solution)/shard_map/ppermute | solution.py:412
  26.6 11.1 %collective-permute-start.6 = (bf16[4,8,640]{2,1,0:T(8,128)(2,1)S(1)}, bf16[4,8,640]{2,1,0:T(8,128)(2,1)S(1)}, u32[]{:S(2)}, u32[]{:S(2)}) collective-permute-start(bf16[4,8,640]{2,1,0:T(8,128)(2,1)S(1)} %get-tuple-element.28), channel_id=1, source_target_pairs={{0,4},{1,5},{2,6},{3,7},{4,0},{5,1},{6,2},{7,3},{8,12},{9,13},{10,... | collective-permute-start | bytes 122888 | tf_op jit(solution)/shard_map/ppermute | solution.py:412
  30.9 6.9 %collective-permute-start.7 = (bf16[4,8,640]{2,1,0:T(8,128)(2,1)S(1)}, bf16[4,8,640]{2,1,0:T(8,128)(2,1)S(1)}, u32[]{:S(2)}, u32[]{:S(2)}) collective-permute-start(bf16[4,8,640]{2,1,0:T(8,128)(2,1)S(1)} %get-tuple-element.29), channel_id=1, source_target_pairs={{0,8},{1,9},{2,10},{3,11},{4,12},{5,13},{6,14},{7,15},{8,0},{9,1},... | collective-permute-start | bytes 122888 | tf_op jit(solution)/shard_map/ppermute | solution.py:412
  31.0 6.8 %collective-permute-start.8 = (bf16[4,8,640]{2,1,0:T(8,128)(2,1)S(1)}, bf16[4,8,640]{2,1,0:T(8,128)(2,1)S(1)}, u32[]{:S(2)}, u32[]{:S(2)}) collective-permute-start(bf16[4,8,640]{2,1,0:T(8,128)(2,1)S(1)} %get-tuple-element.30), channel_id=1, source_target_pairs={{0,12},{1,13},{2,14},{3,15},{4,8},{5,9},{6,10},{7,11},{8,4},{9,5},... | collective-permute-start | bytes 122888 | tf_op jit(solution)/shard_map/ppermute | solution.py:412
  37.8 11.4 %copy-start.6 = (bf16[7168]{0:T(1024)(128)(2,1)S(1)}, bf16[7168]{0:T(1024)(128)(2,1)}, u32[]{:S(2)}) copy-start(bf16[7168]{0:T(1024)(128)(2,1)} %param.28) | copy-start | bytes 43012
  37.8 17.2 %copy-start.5 = (bf16[1,2,7168]{2,1,0:T(2,128)(2,1)S(1)}, bf16[1,2,7168]{2,1,0:T(2,128)(2,1)}, u32[]{:S(2)}) copy-start(bf16[1,2,7168]{2,1,0:T(2,128)(2,1)} %param.25) | copy-start | bytes 86020
  41.9 1.6 %collective-permute-start.12 = (bf16[8,2,7168]{2,1,0:T(2,128)(2,1)S(1)}, bf16[8,2,7168]{2,1,0:T(2,128)(2,1)S(1)}, u32[]{:S(2)}, u32[]{:S(2)}) collective-permute-start(bf16[8,2,7168]{2,1,0:T(2,128)(2,1)S(1)} %get-tuple-element.36), channel_id=1, source_target_pairs={{0,1},{1,0},{2,3},{3,2},{4,5},{5,4},{6,7},{7,6},{8,9},{9,8},{10,11... | collective-permute-start | bytes 688136 | tf_op jit(solution)/shard_map/ppermute | solution.py:503
  44.3 10.5 %all-to-all-start.1 = ((bf16[8,2,7168]{2,1,0:T(2,128)(2,1)}), bf16[8,2,7168]{2,1,0:T(2,128)(2,1)S(1)}, u32[]{:S(2)}, u32[]{:S(2)}) async-start(bf16[8,2,7168]{2,1,0:T(2,128)(2,1)} %shard_map.178), calls=%async_computation.1 | async-start | bytes 458752 | tf_op jit(solution)/shard_map/all_to_all | solution.py:405
  48.7 16.8 %collective-permute-start.13 = (bf16[128,7168]{1,0:T(8,128)(2,1)}, bf16[128,7168]{1,0:T(8,128)(2,1)S(1)}, u32[]{:S(2)}, u32[]{:S(2)}) collective-permute-start(bf16[128,7168]{1,0:T(8,128)(2,1)} %refs_0_.1), channel_id=1, source_target_pairs={{0,1},{1,0},{2,3},{3,2},{4,5},{5,4},{6,7},{7,6},{8,9},{9,8},{10,11... | collective-permute-start | bytes 5505032 | tf_op jit(solution)/shard_map/ppermute | solution.py:513
  48.7 16.8 %collective-permute-start.14 = (bf16[128,7168]{1,0:T(8,128)(2,1)}, bf16[128,7168]{1,0:T(8,128)(2,1)}, u32[]{:S(2)}, u32[]{:S(2)}) collective-permute-start(bf16[128,7168]{1,0:T(8,128)(2,1)} %refs_2_.1), channel_id=1, source_target_pairs={{0,1},{1,0},{2,3},{3,2},{4,5},{5,4},{6,7},{7,6},{8,9},{9,8},{10,11... | collective-permute-start | bytes 5505032 | tf_op jit(solution)/shard_map/ppermute | solution.py:513
  49.2 16.3 %collective-permute-start.15 = (bf16[128,7168]{1,0:T(8,128)(2,1)}, bf16[128,7168]{1,0:T(8,128)(2,1)}, u32[]{:S(2)}, u32[]{:S(2)}) collective-permute-start(bf16[128,7168]{1,0:T(8,128)(2,1)} %refs_4_.1), channel_id=1, source_target_pairs={{0,1},{1,0},{2,3},{3,2},{4,5},{5,4},{6,7},{7,6},{8,9},{9,8},{10,11... | collective-permute-start | bytes 5505032 | tf_op jit(solution)/shard_map/ppermute | solution.py:513
  65.5 11.2 %copy-start.7 = (f32[1,2,1]{1,2,0:T(1,128)S(1)}, f32[1,2,1]{1,2,0:T(1,128)}, u32[]{:S(2)}) copy-start(f32[1,2,1]{1,2,0:T(1,128)} %param.30) | copy-start | bytes 28
  65.5 11.2 %copy-start.8 = (s32[1,2,1]{1,2,0:T(1,128)S(1)}, s32[1,2,1]{1,2,0:T(1,128)}, u32[]{:S(2)}) copy-start(s32[1,2,1]{1,2,0:T(1,128)} %param.29) | copy-start | bytes 28
  65.5 11.1 %copy-start.9 = (s32[8]{0:T(128)S(1)}, s32[8]{0:T(128)}, u32[]{:S(2)}) copy-start(s32[8]{0:T(128)} %constant.145) | copy-start | bytes 100
  70.9 10.4 %all-to-all-start.3 = ((bf16[8,2,7168]{2,1,0:T(2,128)(2,1)}), bf16[8,2,7168]{2,1,0:T(2,128)(2,1)S(1)}, u32[]{:S(2)}, u32[]{:S(2)}) async-start(bf16[8,2,7168]{2,1,0:T(2,128)(2,1)} %shard_map.179), calls=%async_computation.3 | async-start | bytes 458752 | tf_op jit(solution)/shard_map/all_to_all | solution.py:405

commit v9 on v8

--- a/solution.py
+++ b/solution.py
@@ -144,25 +144,18 @@
 
 
 def prompt_kernel(device_ref, dest_ref, length_ref, slot_ref, *refs):
-    key_refs, message_refs, query_hbm = refs[:PLANE], refs[PLANE : 2 * PLANE], refs[2 * PLANE]
-    out_refs, (stage_ref, query_ref, sems) = refs[2 * PLANE + 1 : -3], refs[-3:]
+    key_refs, message_refs, query_ref = refs[:PLANE], refs[PLANE : 2 * PLANE], refs[2 * PLANE]
+    out_refs, stage_ref = refs[2 * PLANE + 1 : -1], refs[-1]
     planes, _, per_peer, width = stage_ref.shape
     heads = planes * per_peer
     tail = key_refs[0].shape[0] - KVR
     device = device_ref[0]
-    sources = [dest_ref[device ^ at] for at in range(PLANE)] + [device ^ at for at in range(PLANE)]
-    loads = [
-        pltpu.make_async_copy(query_hbm.at[slot_ref[source]], query_ref.at[at], sems.at[at])
-        for at, source in enumerate(sources)
-    ]
-    for load in loads:
-        load.start()
-    for load in loads:
-        load.wait()
+    prompts = [slot_ref[dest_ref[device ^ at]] for at in range(PLANE)]
+    owners = [slot_ref[device ^ at] for at in range(PLANE)]
     scores = []
     for at in range(PLANE):
         prompt = device ^ at
-        latent, rest = unpack(query_ref[at], heads, tail)
+        latent, rest = unpack(query_ref[prompts[at]], heads, tail)
         score = jnp.dot(latent, key_refs[at][:KVR], preferred_element_type=f32)
         score += jnp.dot(rest, key_refs[at][KVR:], preferred_element_type=f32)
         score *= softmax_scale
@@ -186,7 +179,7 @@
         fresh = message_refs[at][planes:].astype(f32)
         fresh = fresh.reshape(fresh.shape[0] * per_peer, KVR)
         fresh, fresh_rest = fresh[0:1], fresh[1:2, :tail]
-        latent, rest = unpack(query_ref[PLANE + at], heads, tail)
+        latent, rest = unpack(query_ref[owners[at]], heads, tail)
         fresh_score = softmax_scale * (
             jnp.sum(latent.astype(f32) * fresh, axis=1, keepdims=True)
             + jnp.sum(rest.astype(f32) * fresh_rest, axis=1, keepdims=True)
@@ -462,13 +455,16 @@
     payloads = call(
         prompt_kernel,
         [((PLANE, per_peer, KVR + LANES), bf16)] * planes,
-        [own_device, handoff_dest, handoff_len, jnp.array(slots, jnp.int32), *plane_keys, *messages],
-        [spread],
         [
-            pltpu.VMEM((planes, PLANE, per_peer, KVR + LANES), bf16),
-            pltpu.VMEM((2 * PLANE, *spread_shape[1:]), bf16),
-            pltpu.SemaphoreType.DMA((2 * PLANE,)),
+            own_device,
+            handoff_dest,
+            handoff_len,
+            jnp.array(slots, jnp.int32),
+            *plane_keys,
+            *messages,
+            spread,
         ],
+        scratch=[pltpu.VMEM((planes, PLANE, per_peer, KVR + LANES), bf16)],
     )
     projection = out_proj.reshape(-1, model)
     upward, early = prefetch(payloads[0], value_upward, projection)

time: 82.8 us -> 82.4 us (level)
  transfers between devices with their start and end apart: 19 -> 19, of which waited for: 5 -> 5; matrix products, arithmetic and copies ran while one was open for 2% -> 2% of each run, Pallas kernels for 14% -> 13%
where the time goes in v9:
time: 82.4 us; the launch traced here: 81.9 us
  starting transfers between devices  32.3 us (39%)
  Pallas kernels  21.4 us (26%)
  waiting for transfers between devices  14.7 us (18%)
  blocking collectives  9.86 us (12%)
  other arithmetic  1.83 us (2%)
  between operations  1.02 us (1%)
    all_to_all x3, starting transfers between devices, exchange(): lax.all_to_all(value, 'ep', split_axis=0, concat_axis=0, tiled=True, axis...  16.1 us
    ppermute x12, starting transfers between devices, shards(): lax.ppermute(value, 'ep', [(i, i ^ bits) for i in range(devices)])  15.7 us
    pallas_call x6, Pallas kernels, call(): pl.pallas_call(kernel, out_shape=[pltpu.VMEM(shape, dtype) for shape, dty...  15.1 us
    all_to_all x3, waiting for transfers between devices, exchange(): lax.all_to_all(value, 'ep', split_axis=0, concat_axis=0, tiled=True, axis...  10.3 us
    all_to_all x1, blocking collectives, exchange(): lax.all_to_all(value, 'ep', split_axis=0, concat_axis=0, tiled=True, axis...  9.86 us
    pallas_call x1, Pallas kernels, prefetch(): pl.pallas_call(prefetch_kernel, out_shape=[pltpu.VMEM(upward.shape, bf16)...  4.23 us
    ppermute x12, waiting for transfers between devices, shards(): lax.ppermute(value, 'ep', [(i, i ^ bits) for i in range(devices)])  2.98 us
    pallas_call x1, Pallas kernels, call_far(): pl.pallas_call(kernel, out_shape=shapes, in_specs=[far] * len(operands),...  2.05 us
  transfers between devices with their start and end apart: 19, of which 5 were waited for; matrix products, arithmetic and copies ran while one was open for 2% of the time, Pallas kernels for 13%

profile of v9, /device:TPU:0, one launch (start us, length us, event | category | flops | bytes accessed | tf_op | source)
XLA Modules:
  0.0 81.9 jit_solution(8555140784832501760)
XLA Ops:
  0.0 2.9 %collective-permute-start.1 = (bf16[576,256]{1,0:T(8,128)(2,1)}, bf16[576,256]{1,0:T(8,128)(2,1)S(1)}, u32[]{:S(2)}, u32[]{:S(2)}) collective-permute-start(bf16[576,256]{1,0:T(8,128)(2,1)} %bitcast.38), channel_id=1, source_target_pairs={{0,2},{1,3},{2,0},{3,1},{4,6},{5,7},{6,4},{7,5},{8,10},{9,11},{10,... | collective-permute-start | bytes 884744 | tf_op jit(solution)/shard_map/ppermute | solution.py:405
  2.9 2.1 %shard_map.172.after_ref = bf16[16,144,128]{2,1,0:T(8,128)(2,1)} custom-call(bf16[2,576,128]{2,1,0:T(8,128)(2,1)} %bitcast.44), custom_call_target="tpu_custom_call" | custom-call | tf_op jit(solution)/shard_map/pallas_call | solution.py:333
  5.0 6.0 %all-to-all-start = ((bf16[16,144,128]{2,1,0:T(8,128)(2,1)}), bf16[16,144,128]{2,1,0:T(8,128)(2,1)S(1)}, u32[]{:S(2)}, u32[]{:S(2)}) async-start(bf16[16,144,128]{2,1,0:T(8,128)(2,1)} %shard_map.172.after_ref), calls=%async_computation | async-start | bytes 1179648 | tf_op jit(solution)/shard_map/all_to_all | solution.py:398
  11.7 0.0 copy-start
  11.7 0.0 copy-start.2
  11.7 0.0 copy-start.3
  11.7 3.4 %shard_map.173 = (bf16[5,8,512]{2,1,0:T(8,128)(2,1)S(1)}, bf16[5,8,512]{2,1,0:T(8,128)(2,1)S(1)}, bf16[5,8,512]{2,1,0:T(8,128)(2,1)S(1)}, bf16[5,8,512]{2,1,0:T(8,128)(2,1)S(1)}) custom-call(s32[1]{0:T(128)} %bitcast.2.device_ref, s32[1]{0:T(128)S(6)} %copy.22.length_ref, bf16[2,576]{1,0:T(2,128)(2,1)S(1)} %bitcast.41, ...), custom_call_target="tpu_custom_call" | custom-call | flops 6000000000 | bytes 30000000 | tf_op jit(solution)/shard_map/pallas_call | solution.py:317
  15.2 0.2 collective-permute-start.3
  15.4 1.5 %collective-permute-start.4 = (bf16[5,8,512]{2,1,0:T(8,128)(2,1)S(1)}, bf16[5,8,512]{2,1,0:T(8,128)(2,1)S(1)}, u32[]{:S(2)}, u32[]{:S(2)}) collective-permute-start(bf16[5,8,512]{2,1,0:T(8,128)(2,1)S(1)} %get-tuple-element.23), channel_id=1, source_target_pairs={{0,2},{1,3},{2,0},{3,1},{4,6},{5,7},{6,4},{7,5},{8,10},{9,11},{10,... | collective-permute-start | bytes 122888 | tf_op jit(solution)/shard_map/ppermute | solution.py:405
  16.9 0.2 collective-permute-start.5
  17.2 0.2 select_reduce_fusion
  17.4 0.5 collective-permute-start.2
  17.9 0.1 broadcast_in_dim.42
  18.0 0.1 stack_reshape.7
  18.1 0.1 broadcast_in_dim.22
  18.2 0.1 stack_reshape.6
  18.3 2.6 %collective-permute-done.4.refs_6_.refs_2_ = bf16[5,8,512]{2,1,0:T(8,128)(2,1)S(1)} collective-permute-done((bf16[5,8,512]{2,1,0:T(8,128)(2,1)S(1)}, bf16[5,8,512]{2,1,0:T(8,128)(2,1)S(1)}, u32[]{:S(2)}, u32[]{:S(2)}) %collective-permute-start.4) | collective-permute-done | bytes 40992 | tf_op jit(solution)/shard_map/ppermute | solution.py:405
  20.9 0.3 collective-permute-done.5.refs_7_.refs_3_
  21.3 0.1 collective-permute-start.10
  21.3 2.1 %collective-permute-start.11 = (bf16[5,8,512]{2,1,0:T(8,128)(2,1)S(1)}, bf16[5,8,512]{2,1,0:T(8,128)(2,1)S(1)}, u32[]{:S(2)}, u32[]{:S(2)}) collective-permute-start(bf16[5,8,512]{2,1,0:T(8,128)(2,1)S(1)} %get-tuple-element.34), channel_id=1, source_target_pairs={{0,12},{1,13},{2,14},{3,15},{4,8},{5,9},{6,10},{7,11},{8,4},{9,5},... | collective-permute-start | bytes 122888 | tf_op jit(solution)/shard_map/ppermute | solution.py:405
  23.5 1.3 %collective-permute-start.9 = (bf16[5,8,512]{2,1,0:T(8,128)(2,1)S(1)}, bf16[5,8,512]{2,1,0:T(8,128)(2,1)S(1)}, u32[]{:S(2)}, u32[]{:S(2)}) collective-permute-start(bf16[5,8,512]{2,1,0:T(8,128)(2,1)S(1)} %get-tuple-element.32), channel_id=1, source_target_pairs={{0,4},{1,5},{2,6},{3,7},{4,0},{5,1},{6,2},{7,3},{8,12},{9,13},{10,... | collective-permute-start | bytes 122888 | tf_op jit(solution)/shard_map/ppermute | solution.py:405
  24.9 1.3 %shard_map.174 = (bf16[4,8,640]{2,1,0:T(8,128)(2,1)S(1)}, bf16[4,8,640]{2,1,0:T(8,128)(2,1)S(1)}, bf16[4,8,640]{2,1,0:T(8,128)(2,1)S(1)}, bf16[4,8,640]{2,1,0:T(8,128)(2,1)S(1)}) custom-call(s32[1]{0:T(128)} %bitcast.2.device_ref, s32[16]{0:T(128)S(1)} %copy-done.1, s32[16]{0:T(128)S(1)} %copy-done.2, s32[16]{0:T(128)S(1)} %copy-done.3, ...), custom_call_target="tpu_custom_call" | custom-call | tf_op jit(solution)/shard_map/pallas_call | solution.py:317
  26.2 4.3 %collective-permute-start.6 = (bf16[4,8,640]{2,1,0:T(8,128)(2,1)S(1)}, bf16[4,8,640]{2,1,0:T(8,128)(2,1)S(1)}, u32[]{:S(2)}, u32[]{:S(2)}) collective-permute-start(bf16[4,8,640]{2,1,0:T(8,128)(2,1)S(1)} %get-tuple-element.28), channel_id=1, source_target_pairs={{0,4},{1,5},{2,6},{3,7},{4,0},{5,1},{6,2},{7,3},{8,12},{9,13},{10,... | collective-permute-start | bytes 122888 | tf_op jit(solution)/shard_map/ppermute | solution.py:405
  30.5 0.1 collective-permute-start.7
  30.5 2.4 %collective-permute-start.8 = (bf16[4,8,640]{2,1,0:T(8,128)(2,1)S(1)}, bf16[4,8,640]{2,1,0:T(8,128)(2,1)S(1)}, u32[]{:S(2)}, u32[]{:S(2)}) collective-permute-start(bf16[4,8,640]{2,1,0:T(8,128)(2,1)S(1)} %get-tuple-element.30), channel_id=1, source_target_pairs={{0,12},{1,13},{2,14},{3,15},{4,8},{5,9},{6,10},{7,11},{8,4},{9,5},... | collective-permute-start | bytes 122888 | tf_op jit(solution)/shard_map/ppermute | solution.py:405
  32.9 0.1 copy.21.row_ref
  33.0 4.2 %shard_map.175 = (bf16[8,512,128]{2,1,0:T(8,128)(2,1)S(1)}, bf16[1024,5120]{1,0:T(8,128)(2,1)S(1)}) custom-call(bf16[4,8,640]{2,1,0:T(8,128)(2,1)S(1)} %get-tuple-element.25.after_ref.refs_0_, bf16[8,512,128]{2,1,0:T(8,128)(2,1)} %upward_hbm.1, bf16[1024,7168]{1,0:T(8,128)(2,1)} %bitcast.42), custom_call_target="tpu_custom_call" | custom-call | tf_op jit(solution)/shard_map/pallas_call | solution.py:345
  37.3 0.0 copy-start.6
  37.4 4.1 %shard_map.177 = (f32[8,2,7168]{2,1,0:T(2,128)S(1)}, bf16[8,2,7168]{2,1,0:T(2,128)(2,1)S(1)}) custom-call(s32[256,3]{1,0:T(8,128)S(1)} %copy.21.row_ref, s32[3,128]{1,0:T(4,128)S(1)} %pad_add_fusion.1.column_ref, s32[1,16]{1,0:T(1,128)S(1)} %iota_xor_fusion.peer_ref, bf16[8,512,128]{2,1,0:T(8,128)(2,1)S(1)} %get-tuple-element.26.upward_ref, ...), custom_call_target="tpu_custom_call" | custom-call | tf_op jit(solution)/shard_map/pallas_call | solution.py:317
  41.4 0.1 collective-permute-start.12
  41.5 1.5 %collective-permute-done.12.other_ref = bf16[8,2,7168]{2,1,0:T(2,128)(2,1)S(1)} collective-permute-done((bf16[8,2,7168]{2,1,0:T(2,128)(2,1)S(1)}, bf16[8,2,7168]{2,1,0:T(2,128)(2,1)S(1)}, u32[]{:S(2)}, u32[]{:S(2)}) %collective-permute-start.12) | collective-permute-done | bytes 229408 | tf_op jit(solution)/shard_map/ppermute | solution.py:499
  43.0 0.9 %shard_map.178 = bf16[8,2,7168]{2,1,0:T(2,128)(2,1)} custom-call(f32[8,2,7168]{2,1,0:T(2,128)S(1)} %get-tuple-element.35.keep_ref, bf16[8,2,7168]{2,1,0:T(2,128)(2,1)S(1)} %collective-permute-done.12.other_ref), custom_call_target="tpu_custom_call" | custom-call | tf_op jit(solution)/shard_map/pallas_call | solution.py:317
  43.9 4.4 %all-to-all-start.1 = ((bf16[8,2,7168]{2,1,0:T(2,128)(2,1)}), bf16[8,2,7168]{2,1,0:T(2,128)(2,1)S(1)}, u32[]{:S(2)}, u32[]{:S(2)}) async-start(bf16[8,2,7168]{2,1,0:T(2,128)(2,1)} %shard_map.178), calls=%async_computation.1 | async-start | bytes 458752 | tf_op jit(solution)/shard_map/all_to_all | solution.py:398
  48.3 0.5 collective-permute-start.14
  48.8 5.6 %all-to-all-done.1 = bf16[8,2,7168]{2,1,0:T(2,128)(2,1)S(1)} async-done(((bf16[8,2,7168]{2,1,0:T(2,128)(2,1)}), bf16[8,2,7168]{2,1,0:T(2,128)(2,1)S(1)}, u32[]{:S(2)}, u32[]{:S(2)}) %all-to-all-start.1) | async-done | bytes 229408 | tf_op jit(solution)/shard_map/all_to_all | solution.py:398
  54.4 0.2 convert_reduce_fusion
  54.6 0.2 fusion.2
  54.8 0.1 fusion.4
  54.9 0.1 broadcast_in_dim.45
  55.0 9.9 %all_to_all.20 = bf16[8,2,7168]{2,1,0:T(2,128)(2,1)S(1)} all-to-all(bf16[8,2,7168]{2,1,0:T(2,128)(2,1)S(1)} %broadcast_in_dim.45), channel_id=1, replica_groups={{8,4,10,6,12,0,14,2},{9,5,11,7,13,1,15,3},{24,20,26,22,28,16,30,18},{25..., dimensions={0} | all-to-all | bytes 458752 | tf_op jit(solution)/shard_map/all_to_all | solution.py:398
  64.9 0.1 reshape.289.rows_ref
  65.0 0.0 copy-start.9
  65.1 5.4 %shard_map.179 = bf16[8,2,7168]{2,1,0:T(2,128)(2,1)} custom-call(bf16[16,7168]{1,0:T(8,128)(2,1)S(1)} %reshape.289.rows_ref, bf16[128,7168]{1,0:T(8,128)(2,1)} %refs_0_.1, bf16[128,7168]{1,0:T(8,128)(2,1)S(1)} %collective-permute-done.13.refs_1_, bf16[128,7168]{1,0:T(8,128)(2,1)} %refs_2_.1, bf16[128,7168]{1,0:T(8,128)(2,1)} %collective-permute-done.14.refs_3_, ...), custom_call_target="tpu_custom_call" | custom-call | tf_op jit(solution)/shard_map/pallas_call | solution.py:317
  70.4 5.7 %all-to-all-start.3 = ((bf16[8,2,7168]{2,1,0:T(2,128)(2,1)}), bf16[8,2,7168]{2,1,0:T(2,128)(2,1)S(1)}, u32[]{:S(2)}, u32[]{:S(2)}) async-start(bf16[8,2,7168]{2,1,0:T(2,128)(2,1)} %shard_map.179), calls=%async_computation.3 | async-start | bytes 458752 | tf_op jit(solution)/shard_map/all_to_all | solution.py:398
  76.2 0.1 compare_select_fusion.11
  76.2 4.6 %all-to-all-done.3 = bf16[8,2,7168]{2,1,0:T(2,128)(2,1)S(1)} async-done(((bf16[8,2,7168]{2,1,0:T(2,128)(2,1)}), bf16[8,2,7168]{2,1,0:T(2,128)(2,1)S(1)}, u32[]{:S(2)}, u32[]{:S(2)}) %all-to-all-start.3) | async-done | bytes 229408 | tf_op jit(solution)/shard_map/all_to_all | solution.py:398
  80.9 0.3 multiply_reduce_fusion
  81.2 0.7 fusion.3
  (45 shorter events, 0.2 us)
Async XLA Ops:
  0.0 11.7 %copy-start.4 = (bf16[1,2,576]{2,1,0:T(2,128)(2,1)S(1)}, bf16[1,2,576]{2,1,0:T(2,128)(2,1)}, u32[]{:S(2)}) copy-start(bf16[1,2,576]{2,1,0:T(2,128)(2,1)} %param.24) | copy-start | bytes 6916
  0.0 17.4 %collective-permute-start.1 = (bf16[576,256]{1,0:T(8,128)(2,1)}, bf16[576,256]{1,0:T(8,128)(2,1)S(1)}, u32[]{:S(2)}, u32[]{:S(2)}) collective-permute-start(bf16[576,256]{1,0:T(8,128)(2,1)} %bitcast.38), channel_id=1, source_target_pairs={{0,2},{1,3},{2,0},{3,1},{4,6},{5,7},{6,4},{7,5},{8,10},{9,11},{10,... | collective-permute-start | bytes 884744 | tf_op jit(solution)/shard_map/ppermute | solution.py:405
  2.9 21.9 %collective-permute-start = (bf16[576,256]{1,0:T(8,128)(2,1)}, bf16[576,256]{1,0:T(8,128)(2,1)S(1)}, u32[]{:S(2)}, u32[]{:S(2)}) collective-permute-start(bf16[576,256]{1,0:T(8,128)(2,1)} %bitcast.39), channel_id=1, source_target_pairs={{0,1},{1,0},{2,3},{3,2},{4,5},{5,4},{6,7},{7,6},{8,9},{9,8},{10,11... | collective-permute-start | bytes 884744 | tf_op jit(solution)/shard_map/ppermute | solution.py:405
  5.0 19.8 %all-to-all-start = ((bf16[16,144,128]{2,1,0:T(8,128)(2,1)}), bf16[16,144,128]{2,1,0:T(8,128)(2,1)S(1)}, u32[]{:S(2)}, u32[]{:S(2)}) async-start(bf16[16,144,128]{2,1,0:T(8,128)(2,1)} %shard_map.172.after_ref), calls=%async_computation | async-start | bytes 1179648 | tf_op jit(solution)/shard_map/all_to_all | solution.py:398
  11.7 5.5 %copy-start.1 = (s32[16]{0:T(128)S(1)}, s32[16]{0:T(128)}, u32[]{:S(2)}) copy-start(s32[16]{0:T(128)} %dest_ref.1) | copy-start | bytes 196
  11.7 13.2 %copy-start = (bf16[1,256,576]{1,2,0:T(8,128)(2,1)S(1)}, bf16[1,256,576]{1,2,0:T(8,128)(2,1)}, u32[]{:S(2)}) copy-start(bf16[1,256,576]{1,2,0:T(8,128)(2,1)} %param.18) | copy-start | bytes 884740
  11.7 13.2 %copy-start.2 = (s32[16]{0:T(128)S(1)}, s32[16]{0:T(128)}, u32[]{:S(2)}) copy-start(s32[16]{0:T(128)} %length_ref.2) | copy-start | bytes 196
  11.7 13.1 %copy-start.3 = (s32[16]{0:T(128)S(1)}, s32[16]{0:T(128)}, u32[]{:S(2)}) copy-start(s32[16]{0:T(128)} %constant.118.clone.slot_ref) | copy-start | bytes 196
  15.2 3.1 %collective-permute-start.3 = (bf16[5,8,512]{2,1,0:T(8,128)(2,1)S(1)}, bf16[5,8,512]{2,1,0:T(8,128)(2,1)S(1)}, u32[]{:S(2)}, u32[]{:S(2)}) collective-permute-start(bf16[5,8,512]{2,1,0:T(8,128)(2,1)S(1)} %get-tuple-element.22), channel_id=1, source_target_pairs={{0,1},{1,0},{2,3},{3,2},{4,5},{5,4},{6,7},{7,6},{8,9},{9,8},{10,11... | collective-permute-start | bytes 122888 | tf_op jit(solution)/shard_map/ppermute | solution.py:405
  15.4 5.5 %collective-permute-start.4 = (bf16[5,8,512]{2,1,0:T(8,128)(2,1)S(1)}, bf16[5,8,512]{2,1,0:T(8,128)(2,1)S(1)}, u32[]{:S(2)}, u32[]{:S(2)}) collective-permute-start(bf16[5,8,512]{2,1,0:T(8,128)(2,1)S(1)} %get-tuple-element.23), channel_id=1, source_target_pairs={{0,2},{1,3},{2,0},{3,1},{4,6},{5,7},{6,4},{7,5},{8,10},{9,11},{10,... | collective-permute-start | bytes 122888 | tf_op jit(solution)/shard_map/ppermute | solution.py:405
  16.9 4.4 %collective-permute-start.5 = (bf16[5,8,512]{2,1,0:T(8,128)(2,1)S(1)}, bf16[5,8,512]{2,1,0:T(8,128)(2,1)S(1)}, u32[]{:S(2)}, u32[]{:S(2)}) collective-permute-start(bf16[5,8,512]{2,1,0:T(8,128)(2,1)S(1)} %get-tuple-element.24), channel_id=1, source_target_pairs={{0,3},{1,2},{2,1},{3,0},{4,7},{5,6},{6,5},{7,4},{8,11},{9,10},{10,... | collective-permute-start | bytes 122888 | tf_op jit(solution)/shard_map/ppermute | solution.py:405
  17.4 7.4 %collective-permute-start.2 = (bf16[576,256]{1,0:T(8,128)(2,1)S(1)}, bf16[576,256]{1,0:T(8,128)(2,1)S(1)}, u32[]{:S(2)}, u32[]{:S(2)}) collective-permute-start(bf16[576,256]{1,0:T(8,128)(2,1)S(1)} %collective-permute-done.1.refs_2_), channel_id=1, source_target_pairs={{0,1},{1,0},{2,3},{3,2},{4,5},{5,4},{6,7},{7,6},{8,9},{9,8},{10,11... | collective-permute-start | bytes 884744 | tf_op jit(solution)/shard_map/ppermute | solution.py:405
  21.3 9.3 %collective-permute-start.10 = (bf16[5,8,512]{2,1,0:T(8,128)(2,1)S(1)}, bf16[5,8,512]{2,1,0:T(8,128)(2,1)S(1)}, u32[]{:S(2)}, u32[]{:S(2)}) collective-permute-start(bf16[5,8,512]{2,1,0:T(8,128)(2,1)S(1)} %get-tuple-element.33), channel_id=1, source_target_pairs={{0,8},{1,9},{2,10},{3,11},{4,12},{5,13},{6,14},{7,15},{8,0},{9,1},... | collective-permute-start | bytes 122888 | tf_op jit(solution)/shard_map/ppermute | solution.py:405
  21.3 15.9 %collective-permute-start.11 = (bf16[5,8,512]{2,1,0:T(8,128)(2,1)S(1)}, bf16[5,8,512]{2,1,0:T(8,128)(2,1)S(1)}, u32[]{:S(2)}, u32[]{:S(2)}) collective-permute-start(bf16[5,8,512]{2,1,0:T(8,128)(2,1)S(1)} %get-tuple-element.34), channel_id=1, source_target_pairs={{0,12},{1,13},{2,14},{3,15},{4,8},{5,9},{6,10},{7,11},{8,4},{9,5},... | collective-permute-start | bytes 122888 | tf_op jit(solution)/shard_map/ppermute | solution.py:405
  23.5 13.8 %collective-permute-start.9 = (bf16[5,8,512]{2,1,0:T(8,128)(2,1)S(1)}, bf16[5,8,512]{2,1,0:T(8,128)(2,1)S(1)}, u32[]{:S(2)}, u32[]{:S(2)}) collective-permute-start(bf16[5,8,512]{2,1,0:T(8,128)(2,1)S(1)} %get-tuple-element.32), channel_id=1, source_target_pairs={{0,4},{1,5},{2,6},{3,7},{4,0},{5,1},{6,2},{7,3},{8,12},{9,13},{10,... | collective-permute-start | bytes 122888 | tf_op jit(solution)/shard_map/ppermute | solution.py:405
  26.2 11.1 %collective-permute-start.6 = (bf16[4,8,640]{2,1,0:T(8,128)(2,1)S(1)}, bf16[4,8,640]{2,1,0:T(8,128)(2,1)S(1)}, u32[]{:S(2)}, u32[]{:S(2)}) collective-permute-start(bf16[4,8,640]{2,1,0:T(8,128)(2,1)S(1)} %get-tuple-element.28), channel_id=1, source_target_pairs={{0,4},{1,5},{2,6},{3,7},{4,0},{5,1},{6,2},{7,3},{8,12},{9,13},{10,... | collective-permute-start | bytes 122888 | tf_op jit(solution)/shard_map/ppermute | solution.py:405
  30.5 6.9 %collective-permute-start.7 = (bf16[4,8,640]{2,1,0:T(8,128)(2,1)S(1)}, bf16[4,8,640]{2,1,0:T(8,128)(2,1)S(1)}, u32[]{:S(2)}, u32[]{:S(2)}) collective-permute-start(bf16[4,8,640]{2,1,0:T(8,128)(2,1)S(1)} %get-tuple-element.29), channel_id=1, source_target_pairs={{0,8},{1,9},{2,10},{3,11},{4,12},{5,13},{6,14},{7,15},{8,0},{9,1},... | collective-permute-start | bytes 122888 | tf_op jit(solution)/shard_map/ppermute | solution.py:405
  30.5 6.8 %collective-permute-start.8 = (bf16[4,8,640]{2,1,0:T(8,128)(2,1)S(1)}, bf16[4,8,640]{2,1,0:T(8,128)(2,1)S(1)}, u32[]{:S(2)}, u32[]{:S(2)}) collective-permute-start(bf16[4,8,640]{2,1,0:T(8,128)(2,1)S(1)} %get-tuple-element.30), channel_id=1, source_target_pairs={{0,12},{1,13},{2,14},{3,15},{4,8},{5,9},{6,10},{7,11},{8,4},{9,5},... | collective-permute-start | bytes 122888 | tf_op jit(solution)/shard_map/ppermute | solution.py:405
  37.3 11.4 %copy-start.6 = (bf16[7168]{0:T(1024)(128)(2,1)S(1)}, bf16[7168]{0:T(1024)(128)(2,1)}, u32[]{:S(2)}) copy-start(bf16[7168]{0:T(1024)(128)(2,1)} %param.28) | copy-start | bytes 43012
  37.3 17.2 %copy-start.5 = (bf16[1,2,7168]{2,1,0:T(2,128)(2,1)S(1)}, bf16[1,2,7168]{2,1,0:T(2,128)(2,1)}, u32[]{:S(2)}) copy-start(bf16[1,2,7168]{2,1,0:T(2,128)(2,1)} %param.25) | copy-start | bytes 86020
  41.4 1.6 %collective-permute-start.12 = (bf16[8,2,7168]{2,1,0:T(2,128)(2,1)S(1)}, bf16[8,2,7168]{2,1,0:T(2,128)(2,1)S(1)}, u32[]{:S(2)}, u32[]{:S(2)}) collective-permute-start(bf16[8,2,7168]{2,1,0:T(2,128)(2,1)S(1)} %get-tuple-element.36), channel_id=1, source_target_pairs={{0,1},{1,0},{2,3},{3,2},{4,5},{5,4},{6,7},{7,6},{8,9},{9,8},{10,11... | collective-permute-start | bytes 688136 | tf_op jit(solution)/shard_map/ppermute | solution.py:499
  43.9 10.5 %all-to-all-start.1 = ((bf16[8,2,7168]{2,1,0:T(2,128)(2,1)}), bf16[8,2,7168]{2,1,0:T(2,128)(2,1)S(1)}, u32[]{:S(2)}, u32[]{:S(2)}) async-start(bf16[8,2,7168]{2,1,0:T(2,128)(2,1)} %shard_map.178), calls=%async_computation.1 | async-start | bytes 458752 | tf_op jit(solution)/shard_map/all_to_all | solution.py:398
  48.3 16.8 %collective-permute-start.13 = (bf16[128,7168]{1,0:T(8,128)(2,1)}, bf16[128,7168]{1,0:T(8,128)(2,1)S(1)}, u32[]{:S(2)}, u32[]{:S(2)}) collective-permute-start(bf16[128,7168]{1,0:T(8,128)(2,1)} %refs_0_.1), channel_id=1, source_target_pairs={{0,1},{1,0},{2,3},{3,2},{4,5},{5,4},{6,7},{7,6},{8,9},{9,8},{10,11... | collective-permute-start | bytes 5505032 | tf_op jit(solution)/shard_map/ppermute | solution.py:509
  48.3 16.8 %collective-permute-start.14 = (bf16[128,7168]{1,0:T(8,128)(2,1)}, bf16[128,7168]{1,0:T(8,128)(2,1)}, u32[]{:S(2)}, u32[]{:S(2)}) collective-permute-start(bf16[128,7168]{1,0:T(8,128)(2,1)} %refs_2_.1), channel_id=1, source_target_pairs={{0,1},{1,0},{2,3},{3,2},{4,5},{5,4},{6,7},{7,6},{8,9},{9,8},{10,11... | collective-permute-start | bytes 5505032 | tf_op jit(solution)/shard_map/ppermute | solution.py:509
  48.8 16.3 %collective-permute-start.15 = (bf16[128,7168]{1,0:T(8,128)(2,1)}, bf16[128,7168]{1,0:T(8,128)(2,1)}, u32[]{:S(2)}, u32[]{:S(2)}) collective-permute-start(bf16[128,7168]{1,0:T(8,128)(2,1)} %refs_4_.1), channel_id=1, source_target_pairs={{0,1},{1,0},{2,3},{3,2},{4,5},{5,4},{6,7},{7,6},{8,9},{9,8},{10,11... | collective-permute-start | bytes 5505032 | tf_op jit(solution)/shard_map/ppermute | solution.py:509
  65.0 11.2 %copy-start.7 = (f32[1,2,1]{1,2,0:T(1,128)S(1)}, f32[1,2,1]{1,2,0:T(1,128)}, u32[]{:S(2)}) copy-start(f32[1,2,1]{1,2,0:T(1,128)} %param.30) | copy-start | bytes 28
  65.0 11.2 %copy-start.8 = (s32[1,2,1]{1,2,0:T(1,128)S(1)}, s32[1,2,1]{1,2,0:T(1,128)}, u32[]{:S(2)}) copy-start(s32[1,2,1]{1,2,0:T(1,128)} %param.29) | copy-start | bytes 28
  65.0 11.1 %copy-start.9 = (s32[8]{0:T(128)S(1)}, s32[8]{0:T(128)}, u32[]{:S(2)}) copy-start(s32[8]{0:T(128)} %constant.145) | copy-start | bytes 100
  70.4 10.4 %all-to-all-start.3 = ((bf16[8,2,7168]{2,1,0:T(2,128)(2,1)}), bf16[8,2,7168]{2,1,0:T(2,128)(2,1)S(1)}, u32[]{:S(2)}, u32[]{:S(2)}) async-start(bf16[8,2,7168]{2,1,0:T(2,128)(2,1)} %shard_map.179), calls=%async_computation.3 | async-start | bytes 458752 | tf_op jit(solution)/shard_map/all_to_all | solution.py:398

commit v10 on v9

--- a/solution.py
+++ b/solution.py
@@ -386,8 +386,12 @@
     chips = devices // 2
     siblings = [(i, i ^ 1) for i in range(devices)]
     chip_order = middle_first(chips)
-    same_core = [[2 * chip + k for chip in chip_order] for k in range(2)]
-    device_order = [2 * chip + k for k in range(2) for chip in chip_order]
+    flips = [chip % 2 for chip in range(chips)]
+    chip_orders = [[chip ^ 1 for chip in chip_order], chip_order]
+    same_core = [
+        [2 * chip + (group ^ flips[chip]) for chip in chip_orders[group]] for group in range(2)
+    ]
+    device_order = same_core[1] + same_core[0]
     slots = sorted(range(devices), key=device_order.__getitem__)
     slice_count = MOE_FF // UNITS
     heads, width = queries.shape[2], queries.shape[3]
@@ -471,9 +475,12 @@
     payloads = [toward(payload, at * PLANE) for at, payload in enumerate(payloads)]
 
     row = jnp.arange(per_peer * 2 * devices, dtype=jnp.int32)
-    row_core = (row // devices % 2) ^ core
-    chip_at = jnp.array(chip_order, jnp.int32)
-    row_device = chip_at[row // 2 % chips] * 2 + row_core
+    own_group = core ^ jnp.array(flips, jnp.int32)[device // 2]
+    row_group = (row // devices % 2) ^ own_group
+    chip_at = jnp.array(chip_orders, jnp.int32)
+    flip_at = jnp.array(flips, jnp.int32)
+    row_chip = chip_at[row_group, row // 2 % chips]
+    row_device = row_chip * 2 + (row_group ^ flip_at[row_chip])
     row_table = jnp.stack([row // (2 * devices), row_device, row % 2], axis=1)
     peers = device.astype(jnp.int32) ^ jnp.arange(devices, dtype=jnp.int32)
     is_peer = peers[:, None] == jnp.arange(devices, dtype=jnp.int32)[None, :]
@@ -517,7 +524,7 @@
     )
     returned = exchange(part, same_core)
 
-    chip_expert = chip_at * 2 // slice_count
+    chip_expert = chip_at[own_group] * 2 // slice_count
     chosen = (expert_ids[0][..., None] == chip_expert).astype(f32)
     weights = jnp.sum(expert_gates[0][..., None] * chosen, axis=1)
     mixed = jnp.sum(weights.T[..., None] * returned.astype(f32), axis=0)

time: 82.4 us -> 82.4 us (level)
  local copies, waits for them, and re-layouts: 0.72 us -> 3.71 us
  waiting for transfers between devices: 14.7 us -> 11.8 us
  starting transfers between devices: 32.3 us -> 30.9 us
    ppermute x12, waiting for transfers between devices: 2.98 us -> 0.03 us  [shards(): lax.ppermute(value, 'ep', [(i, i ^ bits) for i in range(devices)])]
    gather x0 -> x1, local copies, waits for them, and re-layouts: none -> 2.43 us  [shards(): row_chip = chip_at[row_group, row // 2 % chips]]
    ppermute x12, starting transfers between devices: 15.7 us -> 13.3 us  [shards(): lax.ppermute(value, 'ep', [(i, i ^ bits) for i in range(devices)])]
    all_to_all x3, starting transfers between devices: 16.1 us -> 17 us  [exchange(): lax.all_to_all(value, 'ep', split_axis=0, concat_axis=0, tiled=True, axis...]
  transfers between devices with their start and end apart: 19 -> 19, of which waited for: 5 -> 4; matrix products, arithmetic and copies ran while one was open for 2% -> 6% of each run, Pallas kernels for 13% -> 14%
where the time goes in v10:
time: 82.4 us; the launch traced here: 81.8 us
  starting transfers between devices  30.9 us (38%)
  Pallas kernels  21.4 us (26%)
  waiting for transfers between devices  11.8 us (14%)
  blocking collectives  10.6 us (13%)
  local copies, waits for them, and re-layouts  3.71 us (5%)
  other arithmetic  1.84 us (2%)
  between operations  1.59 us (2%)
    all_to_all x3, starting transfers between devices, exchange(): lax.all_to_all(value, 'ep', split_axis=0, concat_axis=0, tiled=True, axis...  17 us
    pallas_call x6, Pallas kernels, call(): pl.pallas_call(kernel, out_shape=[pltpu.VMEM(shape, dtype) for shape, dty...  15.1 us
    ppermute x12, starting transfers between devices, shards(): lax.ppermute(value, 'ep', [(i, i ^ bits) for i in range(devices)])  13.3 us
    all_to_all x1, blocking collectives, exchange(): lax.all_to_all(value, 'ep', split_axis=0, concat_axis=0, tiled=True, axis...  10.6 us
    all_to_all x3, waiting for transfers between devices, exchange(): lax.all_to_all(value, 'ep', split_axis=0, concat_axis=0, tiled=True, axis...  10.3 us
    pallas_call x1, Pallas kernels, prefetch(): pl.pallas_call(prefetch_kernel, out_shape=[pltpu.VMEM(upward.shape, bf16)...  4.23 us
    gather x1, local copies, waits for them, and re-layouts, shards(): row_chip = chip_at[row_group, row // 2 % chips]  2.43 us
    pallas_call x1, Pallas kernels, call_far(): pl.pallas_call(kernel, out_shape=shapes, in_specs=[far] * len(operands),...  2.06 us
  transfers between devices with their start and end apart: 19, of which 4 were waited for; matrix products, arithmetic and copies ran while one was open for 6% of the time, Pallas kernels for 14%

profile of v10, /device:TPU:0, one launch (start us, length us, event | category | flops | bytes accessed | tf_op | source)
XLA Modules:
  0.0 81.8 jit_solution(9702191217018555967)
XLA Ops:
  0.0 2.9 %collective-permute-start.1 = (bf16[576,256]{1,0:T(8,128)(2,1)}, bf16[576,256]{1,0:T(8,128)(2,1)S(1)}, u32[]{:S(2)}, u32[]{:S(2)}) collective-permute-start(bf16[576,256]{1,0:T(8,128)(2,1)} %bitcast.49), channel_id=1, source_target_pairs={{0,2},{1,3},{2,0},{3,1},{4,6},{5,7},{6,4},{7,5},{8,10},{9,11},{10,... | collective-permute-start | bytes 884744 | tf_op jit(solution)/shard_map/ppermute | solution.py:409
  2.9 2.1 %shard_map.190.after_ref = bf16[16,144,128]{2,1,0:T(8,128)(2,1)} custom-call(bf16[2,576,128]{2,1,0:T(8,128)(2,1)} %bitcast.56), custom_call_target="tpu_custom_call" | custom-call | tf_op jit(solution)/shard_map/pallas_call | solution.py:333
  5.0 6.2 %all-to-all-start = ((bf16[16,144,128]{2,1,0:T(8,128)(2,1)}), bf16[16,144,128]{2,1,0:T(8,128)(2,1)S(1)}, u32[]{:S(2)}, u32[]{:S(2)}) async-start(bf16[16,144,128]{2,1,0:T(8,128)(2,1)} %shard_map.190.after_ref), calls=%async_computation | async-start | bytes 1179648 | tf_op jit(solution)/shard_map/all_to_all | solution.py:402
  11.8 0.0 copy-start.10
  11.9 0.0 copy-start.5
  11.9 0.0 copy-start
  11.9 0.0 copy-start.3
  11.9 3.4 %shard_map.191 = (bf16[5,8,512]{2,1,0:T(8,128)(2,1)S(1)}, bf16[5,8,512]{2,1,0:T(8,128)(2,1)S(1)}, bf16[5,8,512]{2,1,0:T(8,128)(2,1)S(1)}, bf16[5,8,512]{2,1,0:T(8,128)(2,1)S(1)}) custom-call(s32[1]{0:T(128)} %bitcast.5.device_ref, s32[1]{0:T(128)S(6)} %copy.28.length_ref, bf16[2,576]{1,0:T(2,128)(2,1)S(1)} %bitcast.52, ...), custom_call_target="tpu_custom_call" | custom-call | flops 6000000000 | bytes 30000000 | tf_op jit(solution)/shard_map/pallas_call | solution.py:317
  15.4 0.1 collective-permute-start.3
  15.5 1.5 %collective-permute-start.4 = (bf16[5,8,512]{2,1,0:T(8,128)(2,1)S(1)}, bf16[5,8,512]{2,1,0:T(8,128)(2,1)S(1)}, u32[]{:S(2)}, u32[]{:S(2)}) collective-permute-start(bf16[5,8,512]{2,1,0:T(8,128)(2,1)S(1)} %get-tuple-element.23), channel_id=1, source_target_pairs={{0,2},{1,3},{2,0},{3,1},{4,6},{5,7},{6,4},{7,5},{8,10},{9,11},{10,... | collective-permute-start | bytes 122888 | tf_op jit(solution)/shard_map/ppermute | solution.py:409
  17.0 0.3 collective-permute-start.5
  17.3 0.6 dynamic_slice.6
  18.5 2.4 %gather_fusion = s32[256]{0:T(256)S(1)} fusion(s32[2,8]{1,0:T(2,128)S(1)} %copy-done.5, s32[256]{0:T(256)S(1)} %bitcast.55), kind=kCustom, calls=%fused_computation | custom fusion | bytes 4096 | tf_op jit(solution)/shard_map/gather | solution.py:482
  20.9 0.2 select_reduce_fusion
  21.2 0.4 collective-permute-start.2
  21.6 0.1 broadcast_in_dim.25
  21.7 0.1 stack_reshape.7
  21.8 0.1 broadcast_in_dim.22
  21.8 0.1 stack_reshape.6
  22.0 0.5 collective-permute-start.10
  22.5 2.5 %collective-permute-start.11 = (bf16[5,8,512]{2,1,0:T(8,128)(2,1)S(1)}, bf16[5,8,512]{2,1,0:T(8,128)(2,1)S(1)}, u32[]{:S(2)}, u32[]{:S(2)}) collective-permute-start(bf16[5,8,512]{2,1,0:T(8,128)(2,1)S(1)} %get-tuple-element.34), channel_id=1, source_target_pairs={{0,12},{1,13},{2,14},{3,15},{4,8},{5,9},{6,10},{7,11},{8,4},{9,5},... | collective-permute-start | bytes 122888 | tf_op jit(solution)/shard_map/ppermute | solution.py:409
  25.0 0.6 collective-permute-start.9
  25.6 0.5 all-to-all-done.refs_8_
  26.1 1.3 %shard_map.192 = (bf16[4,8,640]{2,1,0:T(8,128)(2,1)S(1)}, bf16[4,8,640]{2,1,0:T(8,128)(2,1)S(1)}, bf16[4,8,640]{2,1,0:T(8,128)(2,1)S(1)}, bf16[4,8,640]{2,1,0:T(8,128)(2,1)S(1)}) custom-call(s32[1]{0:T(128)} %bitcast.5.device_ref, s32[16]{0:T(128)S(1)} %copy-done.1, s32[16]{0:T(128)S(1)} %copy-done.2, s32[16]{0:T(128)S(1)} %copy-done.3, ...), custom_call_target="tpu_custom_call" | custom-call | tf_op jit(solution)/shard_map/pallas_call | solution.py:317
  27.4 1.0 %collective-permute-start.6 = (bf16[4,8,640]{2,1,0:T(8,128)(2,1)S(1)}, bf16[4,8,640]{2,1,0:T(8,128)(2,1)S(1)}, u32[]{:S(2)}, u32[]{:S(2)}) collective-permute-start(bf16[4,8,640]{2,1,0:T(8,128)(2,1)S(1)} %get-tuple-element.28), channel_id=1, source_target_pairs={{0,4},{1,5},{2,6},{3,7},{4,0},{5,1},{6,2},{7,3},{8,12},{9,13},{10,... | collective-permute-start | bytes 122888 | tf_op jit(solution)/shard_map/ppermute | solution.py:409
  28.4 1.5 %collective-permute-start.7 = (bf16[4,8,640]{2,1,0:T(8,128)(2,1)S(1)}, bf16[4,8,640]{2,1,0:T(8,128)(2,1)S(1)}, u32[]{:S(2)}, u32[]{:S(2)}) collective-permute-start(bf16[4,8,640]{2,1,0:T(8,128)(2,1)S(1)} %get-tuple-element.29), channel_id=1, source_target_pairs={{0,8},{1,9},{2,10},{3,11},{4,12},{5,13},{6,14},{7,15},{8,0},{9,1},... | collective-permute-start | bytes 122888 | tf_op jit(solution)/shard_map/ppermute | solution.py:409
  29.9 1.9 %collective-permute-start.8 = (bf16[4,8,640]{2,1,0:T(8,128)(2,1)S(1)}, bf16[4,8,640]{2,1,0:T(8,128)(2,1)S(1)}, u32[]{:S(2)}, u32[]{:S(2)}) collective-permute-start(bf16[4,8,640]{2,1,0:T(8,128)(2,1)S(1)} %get-tuple-element.30), channel_id=1, source_target_pairs={{0,12},{1,13},{2,14},{3,15},{4,8},{5,9},{6,10},{7,11},{8,4},{9,5},... | collective-permute-start | bytes 122888 | tf_op jit(solution)/shard_map/ppermute | solution.py:409
  31.8 0.1 copy.27.row_ref
  32.0 4.2 %shard_map.193 = (bf16[8,512,128]{2,1,0:T(8,128)(2,1)S(1)}, bf16[1024,5120]{1,0:T(8,128)(2,1)S(1)}) custom-call(bf16[4,8,640]{2,1,0:T(8,128)(2,1)S(1)} %get-tuple-element.25.after_ref.refs_0_, bf16[8,512,128]{2,1,0:T(8,128)(2,1)} %upward_hbm.1, bf16[1024,7168]{1,0:T(8,128)(2,1)} %bitcast.53), custom_call_target="tpu_custom_call" | custom-call | tf_op jit(solution)/shard_map/pallas_call | solution.py:345
  36.3 4.1 %shard_map.195 = (f32[8,2,7168]{2,1,0:T(2,128)S(1)}, bf16[8,2,7168]{2,1,0:T(2,128)(2,1)S(1)}) custom-call(s32[256,3]{1,0:T(8,128)S(1)} %copy.27.row_ref, s32[3,128]{1,0:T(4,128)S(1)} %pad_add_fusion.1.column_ref, s32[1,16]{1,0:T(1,128)S(1)} %iota_xor_fusion.peer_ref, bf16[8,512,128]{2,1,0:T(8,128)(2,1)S(1)} %get-tuple-element.26.upward_ref, ...), custom_call_target="tpu_custom_call" | custom-call | tf_op jit(solution)/shard_map/pallas_call | solution.py:317
  40.4 0.1 collective-permute-start.12
  40.4 1.5 %collective-permute-done.12.other_ref = bf16[8,2,7168]{2,1,0:T(2,128)(2,1)S(1)} collective-permute-done((bf16[8,2,7168]{2,1,0:T(2,128)(2,1)S(1)}, bf16[8,2,7168]{2,1,0:T(2,128)(2,1)S(1)}, u32[]{:S(2)}, u32[]{:S(2)}) %collective-permute-start.12) | collective-permute-done | bytes 229408 | tf_op jit(solution)/shard_map/ppermute | solution.py:506
  41.9 0.9 %shard_map.196 = bf16[8,2,7168]{2,1,0:T(2,128)(2,1)} custom-call(f32[8,2,7168]{2,1,0:T(2,128)S(1)} %get-tuple-element.35.keep_ref, bf16[8,2,7168]{2,1,0:T(2,128)(2,1)S(1)} %collective-permute-done.12.other_ref), custom_call_target="tpu_custom_call" | custom-call | tf_op jit(solution)/shard_map/pallas_call | solution.py:317
  42.8 5.4 %all-to-all-start.1 = ((bf16[8,2,7168]{2,1,0:T(2,128)(2,1)}), bf16[8,2,7168]{2,1,0:T(2,128)(2,1)S(1)}, u32[]{:S(2)}, u32[]{:S(2)}) async-start(bf16[8,2,7168]{2,1,0:T(2,128)(2,1)} %shard_map.196), calls=%async_computation.1 | async-start | bytes 458752 | tf_op jit(solution)/shard_map/all_to_all | solution.py:402
  48.2 0.5 collective-permute-start.14
  48.7 4.7 %all-to-all-done.1 = bf16[8,2,7168]{2,1,0:T(2,128)(2,1)S(1)} async-done(((bf16[8,2,7168]{2,1,0:T(2,128)(2,1)}), bf16[8,2,7168]{2,1,0:T(2,128)(2,1)S(1)}, u32[]{:S(2)}, u32[]{:S(2)}) %all-to-all-start.1) | async-done | bytes 229408 | tf_op jit(solution)/shard_map/all_to_all | solution.py:402
  53.4 0.2 convert_reduce_fusion
  53.6 0.2 fusion.2
  53.8 0.1 fusion.4
  53.9 0.1 broadcast_in_dim.47
  54.1 10.6 %all_to_all.20 = bf16[8,2,7168]{2,1,0:T(2,128)(2,1)S(1)} all-to-all(bf16[8,2,7168]{2,1,0:T(2,128)(2,1)S(1)} %broadcast_in_dim.47), channel_id=1, replica_groups={{11,7,8,4,15,3,12,0},{9,5,10,6,13,1,14,2},{27,23,24,20,31,19,28,16},{25..., dimensions={0} | all-to-all | bytes 458752 | tf_op jit(solution)/shard_map/all_to_all | solution.py:402
  64.7 0.1 reshape.338.rows_ref
  64.8 5.4 %shard_map.197 = bf16[8,2,7168]{2,1,0:T(2,128)(2,1)} custom-call(bf16[16,7168]{1,0:T(8,128)(2,1)S(1)} %reshape.338.rows_ref, bf16[128,7168]{1,0:T(8,128)(2,1)} %refs_0_.1, bf16[128,7168]{1,0:T(8,128)(2,1)S(1)} %collective-permute-done.13.refs_1_, bf16[128,7168]{1,0:T(8,128)(2,1)} %refs_2_.1, bf16[128,7168]{1,0:T(8,128)(2,1)} %collective-permute-done.14.refs_3_, ...), custom_call_target="tpu_custom_call" | custom-call | tf_op jit(solution)/shard_map/pallas_call | solution.py:317
  70.2 5.4 %all-to-all-start.3 = ((bf16[8,2,7168]{2,1,0:T(2,128)(2,1)}), bf16[8,2,7168]{2,1,0:T(2,128)(2,1)S(1)}, u32[]{:S(2)}, u32[]{:S(2)}) async-start(bf16[8,2,7168]{2,1,0:T(2,128)(2,1)} %shard_map.197), calls=%async_computation.3 | async-start | bytes 458752 | tf_op jit(solution)/shard_map/all_to_all | solution.py:402
  75.7 0.1 compare_select_fusion.13
  75.7 5.1 %all-to-all-done.3 = bf16[8,2,7168]{2,1,0:T(2,128)(2,1)S(1)} async-done(((bf16[8,2,7168]{2,1,0:T(2,128)(2,1)}), bf16[8,2,7168]{2,1,0:T(2,128)(2,1)S(1)}, u32[]{:S(2)}, u32[]{:S(2)}) %all-to-all-start.3) | async-done | bytes 229408 | tf_op jit(solution)/shard_map/all_to_all | solution.py:402
  80.9 0.3 multiply_reduce_fusion
  81.2 0.7 fusion.3
  (51 shorter events, 0.3 us)
Async XLA Ops:
  0.0 11.8 %copy-start.4 = (bf16[1,2,576]{2,1,0:T(2,128)(2,1)S(1)}, bf16[1,2,576]{2,1,0:T(2,128)(2,1)}, u32[]{:S(2)}) copy-start(bf16[1,2,576]{2,1,0:T(2,128)(2,1)} %param.26) | copy-start | bytes 6916
  0.0 21.2 %collective-permute-start.1 = (bf16[576,256]{1,0:T(8,128)(2,1)}, bf16[576,256]{1,0:T(8,128)(2,1)S(1)}, u32[]{:S(2)}, u32[]{:S(2)}) collective-permute-start(bf16[576,256]{1,0:T(8,128)(2,1)} %bitcast.49), channel_id=1, source_target_pairs={{0,2},{1,3},{2,0},{3,1},{4,6},{5,7},{6,4},{7,5},{8,10},{9,11},{10,... | collective-permute-start | bytes 884744 | tf_op jit(solution)/shard_map/ppermute | solution.py:409
  2.9 22.6 %collective-permute-start = (bf16[576,256]{1,0:T(8,128)(2,1)}, bf16[576,256]{1,0:T(8,128)(2,1)S(1)}, u32[]{:S(2)}, u32[]{:S(2)}) collective-permute-start(bf16[576,256]{1,0:T(8,128)(2,1)} %bitcast.50), channel_id=1, source_target_pairs={{0,1},{1,0},{2,3},{3,2},{4,5},{5,4},{6,7},{7,6},{8,9},{9,8},{10,11... | collective-permute-start | bytes 884744 | tf_op jit(solution)/shard_map/ppermute | solution.py:409
  5.0 21.1 %all-to-all-start = ((bf16[16,144,128]{2,1,0:T(8,128)(2,1)}), bf16[16,144,128]{2,1,0:T(8,128)(2,1)S(1)}, u32[]{:S(2)}, u32[]{:S(2)}) async-start(bf16[16,144,128]{2,1,0:T(8,128)(2,1)} %shard_map.190.after_ref), calls=%async_computation | async-start | bytes 1179648 | tf_op jit(solution)/shard_map/all_to_all | solution.py:402
  11.8 5.5 %copy-start.10 = (s32[8]{0:T(128)S(1)}, s32[8]{0:T(128)}, u32[]{:S(2)}) copy-start(s32[8]{0:T(128)} %constant.132.clone) | copy-start | bytes 100
  11.9 6.6 %copy-start.5 = (s32[2,8]{1,0:T(2,128)S(1)}, s32[2,8]{1,0:T(2,128)}, u32[]{:S(2)}) copy-start(s32[2,8]{1,0:T(2,128)} %constant.133.clone) | copy-start | bytes 196
  11.9 9.1 %copy-start.1 = (s32[16]{0:T(128)S(1)}, s32[16]{0:T(128)}, u32[]{:S(2)}) copy-start(s32[16]{0:T(128)} %dest_ref.1) | copy-start | bytes 196
  11.9 14.2 %copy-start = (bf16[1,256,576]{1,2,0:T(8,128)(2,1)S(1)}, bf16[1,256,576]{1,2,0:T(8,128)(2,1)}, u32[]{:S(2)}) copy-start(bf16[1,256,576]{1,2,0:T(8,128)(2,1)} %param.20) | copy-start | bytes 884740
  11.9 14.2 %copy-start.2 = (s32[16]{0:T(128)S(1)}, s32[16]{0:T(128)}, u32[]{:S(2)}) copy-start(s32[16]{0:T(128)} %length_ref.2) | copy-start | bytes 196
  11.9 14.2 %copy-start.3 = (s32[16]{0:T(128)S(1)}, s32[16]{0:T(128)}, u32[]{:S(2)}) copy-start(s32[16]{0:T(128)} %constant.131.clone.slot_ref) | copy-start | bytes 196
  15.4 6.6 %collective-permute-start.3 = (bf16[5,8,512]{2,1,0:T(8,128)(2,1)S(1)}, bf16[5,8,512]{2,1,0:T(8,128)(2,1)S(1)}, u32[]{:S(2)}, u32[]{:S(2)}) collective-permute-start(bf16[5,8,512]{2,1,0:T(8,128)(2,1)S(1)} %get-tuple-element.22), channel_id=1, source_target_pairs={{0,1},{1,0},{2,3},{3,2},{4,5},{5,4},{6,7},{7,6},{8,9},{9,8},{10,11... | collective-permute-start | bytes 122888 | tf_op jit(solution)/shard_map/ppermute | solution.py:409
  15.5 6.5 %collective-permute-start.4 = (bf16[5,8,512]{2,1,0:T(8,128)(2,1)S(1)}, bf16[5,8,512]{2,1,0:T(8,128)(2,1)S(1)}, u32[]{:S(2)}, u32[]{:S(2)}) collective-permute-start(bf16[5,8,512]{2,1,0:T(8,128)(2,1)S(1)} %get-tuple-element.23), channel_id=1, source_target_pairs={{0,2},{1,3},{2,0},{3,1},{4,6},{5,7},{6,4},{7,5},{8,10},{9,11},{10,... | collective-permute-start | bytes 122888 | tf_op jit(solution)/shard_map/ppermute | solution.py:409
  17.0 5.0 %collective-permute-start.5 = (bf16[5,8,512]{2,1,0:T(8,128)(2,1)S(1)}, bf16[5,8,512]{2,1,0:T(8,128)(2,1)S(1)}, u32[]{:S(2)}, u32[]{:S(2)}) collective-permute-start(bf16[5,8,512]{2,1,0:T(8,128)(2,1)S(1)} %get-tuple-element.24), channel_id=1, source_target_pairs={{0,3},{1,2},{2,1},{3,0},{4,7},{5,6},{6,5},{7,4},{8,11},{9,10},{10,... | collective-permute-start | bytes 122888 | tf_op jit(solution)/shard_map/ppermute | solution.py:409
  21.2 4.4 %collective-permute-start.2 = (bf16[576,256]{1,0:T(8,128)(2,1)S(1)}, bf16[576,256]{1,0:T(8,128)(2,1)S(1)}, u32[]{:S(2)}, u32[]{:S(2)}) collective-permute-start(bf16[576,256]{1,0:T(8,128)(2,1)S(1)} %collective-permute-done.1.refs_2_), channel_id=1, source_target_pairs={{0,1},{1,0},{2,3},{3,2},{4,5},{5,4},{6,7},{7,6},{8,9},{9,8},{10,11... | collective-permute-start | bytes 884744 | tf_op jit(solution)/shard_map/ppermute | solution.py:409
  22.0 7.9 %collective-permute-start.10 = (bf16[5,8,512]{2,1,0:T(8,128)(2,1)S(1)}, bf16[5,8,512]{2,1,0:T(8,128)(2,1)S(1)}, u32[]{:S(2)}, u32[]{:S(2)}) collective-permute-start(bf16[5,8,512]{2,1,0:T(8,128)(2,1)S(1)} %get-tuple-element.33), channel_id=1, source_target_pairs={{0,8},{1,9},{2,10},{3,11},{4,12},{5,13},{6,14},{7,15},{8,0},{9,1},... | collective-permute-start | bytes 122888 | tf_op jit(solution)/shard_map/ppermute | solution.py:409
  22.5 13.7 %collective-permute-start.11 = (bf16[5,8,512]{2,1,0:T(8,128)(2,1)S(1)}, bf16[5,8,512]{2,1,0:T(8,128)(2,1)S(1)}, u32[]{:S(2)}, u32[]{:S(2)}) collective-permute-start(bf16[5,8,512]{2,1,0:T(8,128)(2,1)S(1)} %get-tuple-element.34), channel_id=1, source_target_pairs={{0,12},{1,13},{2,14},{3,15},{4,8},{5,9},{6,10},{7,11},{8,4},{9,5},... | collective-permute-start | bytes 122888 | tf_op jit(solution)/shard_map/ppermute | solution.py:409
  25.0 11.3 %collective-permute-start.9 = (bf16[5,8,512]{2,1,0:T(8,128)(2,1)S(1)}, bf16[5,8,512]{2,1,0:T(8,128)(2,1)S(1)}, u32[]{:S(2)}, u32[]{:S(2)}) collective-permute-start(bf16[5,8,512]{2,1,0:T(8,128)(2,1)S(1)} %get-tuple-element.32), channel_id=1, source_target_pairs={{0,4},{1,5},{2,6},{3,7},{4,0},{5,1},{6,2},{7,3},{8,12},{9,13},{10,... | collective-permute-start | bytes 122888 | tf_op jit(solution)/shard_map/ppermute | solution.py:409
  27.4 8.9 %collective-permute-start.6 = (bf16[4,8,640]{2,1,0:T(8,128)(2,1)S(1)}, bf16[4,8,640]{2,1,0:T(8,128)(2,1)S(1)}, u32[]{:S(2)}, u32[]{:S(2)}) collective-permute-start(bf16[4,8,640]{2,1,0:T(8,128)(2,1)S(1)} %get-tuple-element.28), channel_id=1, source_target_pairs={{0,4},{1,5},{2,6},{3,7},{4,0},{5,1},{6,2},{7,3},{8,12},{9,13},{10,... | collective-permute-start | bytes 122888 | tf_op jit(solution)/shard_map/ppermute | solution.py:409
  28.4 7.8 %collective-permute-start.7 = (bf16[4,8,640]{2,1,0:T(8,128)(2,1)S(1)}, bf16[4,8,640]{2,1,0:T(8,128)(2,1)S(1)}, u32[]{:S(2)}, u32[]{:S(2)}) collective-permute-start(bf16[4,8,640]{2,1,0:T(8,128)(2,1)S(1)} %get-tuple-element.29), channel_id=1, source_target_pairs={{0,8},{1,9},{2,10},{3,11},{4,12},{5,13},{6,14},{7,15},{8,0},{9,1},... | collective-permute-start | bytes 122888 | tf_op jit(solution)/shard_map/ppermute | solution.py:409
  29.9 6.4 %collective-permute-start.8 = (bf16[4,8,640]{2,1,0:T(8,128)(2,1)S(1)}, bf16[4,8,640]{2,1,0:T(8,128)(2,1)S(1)}, u32[]{:S(2)}, u32[]{:S(2)}) collective-permute-start(bf16[4,8,640]{2,1,0:T(8,128)(2,1)S(1)} %get-tuple-element.30), channel_id=1, source_target_pairs={{0,12},{1,13},{2,14},{3,15},{4,8},{5,9},{6,10},{7,11},{8,4},{9,5},... | collective-permute-start | bytes 122888 | tf_op jit(solution)/shard_map/ppermute | solution.py:409
  36.3 12.4 %copy-start.7 = (bf16[7168]{0:T(1024)(128)(2,1)S(1)}, bf16[7168]{0:T(1024)(128)(2,1)}, u32[]{:S(2)}) copy-start(bf16[7168]{0:T(1024)(128)(2,1)} %param.30) | copy-start | bytes 43012
  36.3 17.4 %copy-start.6 = (bf16[1,2,7168]{2,1,0:T(2,128)(2,1)S(1)}, bf16[1,2,7168]{2,1,0:T(2,128)(2,1)}, u32[]{:S(2)}) copy-start(bf16[1,2,7168]{2,1,0:T(2,128)(2,1)} %param.27) | copy-start | bytes 86020
  40.4 1.6 %collective-permute-start.12 = (bf16[8,2,7168]{2,1,0:T(2,128)(2,1)S(1)}, bf16[8,2,7168]{2,1,0:T(2,128)(2,1)S(1)}, u32[]{:S(2)}, u32[]{:S(2)}) collective-permute-start(bf16[8,2,7168]{2,1,0:T(2,128)(2,1)S(1)} %get-tuple-element.36), channel_id=1, source_target_pairs={{0,1},{1,0},{2,3},{3,2},{4,5},{5,4},{6,7},{7,6},{8,9},{9,8},{10,11... | collective-permute-start | bytes 688136 | tf_op jit(solution)/shard_map/ppermute | solution.py:506
  42.8 10.6 %all-to-all-start.1 = ((bf16[8,2,7168]{2,1,0:T(2,128)(2,1)}), bf16[8,2,7168]{2,1,0:T(2,128)(2,1)S(1)}, u32[]{:S(2)}, u32[]{:S(2)}) async-start(bf16[8,2,7168]{2,1,0:T(2,128)(2,1)} %shard_map.196), calls=%async_computation.1 | async-start | bytes 458752 | tf_op jit(solution)/shard_map/all_to_all | solution.py:402
  48.2 16.6 %collective-permute-start.13 = (bf16[128,7168]{1,0:T(8,128)(2,1)}, bf16[128,7168]{1,0:T(8,128)(2,1)S(1)}, u32[]{:S(2)}, u32[]{:S(2)}) collective-permute-start(bf16[128,7168]{1,0:T(8,128)(2,1)} %refs_0_.1), channel_id=1, source_target_pairs={{0,1},{1,0},{2,3},{3,2},{4,5},{5,4},{6,7},{7,6},{8,9},{9,8},{10,11... | collective-permute-start | bytes 5505032 | tf_op jit(solution)/shard_map/ppermute | solution.py:516
  48.2 16.6 %collective-permute-start.14 = (bf16[128,7168]{1,0:T(8,128)(2,1)}, bf16[128,7168]{1,0:T(8,128)(2,1)}, u32[]{:S(2)}, u32[]{:S(2)}) collective-permute-start(bf16[128,7168]{1,0:T(8,128)(2,1)} %refs_2_.1), channel_id=1, source_target_pairs={{0,1},{1,0},{2,3},{3,2},{4,5},{5,4},{6,7},{7,6},{8,9},{9,8},{10,11... | collective-permute-start | bytes 5505032 | tf_op jit(solution)/shard_map/ppermute | solution.py:516
  48.7 16.1 %collective-permute-start.15 = (bf16[128,7168]{1,0:T(8,128)(2,1)}, bf16[128,7168]{1,0:T(8,128)(2,1)}, u32[]{:S(2)}, u32[]{:S(2)}) collective-permute-start(bf16[128,7168]{1,0:T(8,128)(2,1)} %refs_4_.1), channel_id=1, source_target_pairs={{0,1},{1,0},{2,3},{3,2},{4,5},{5,4},{6,7},{7,6},{8,9},{9,8},{10,11... | collective-permute-start | bytes 5505032 | tf_op jit(solution)/shard_map/ppermute | solution.py:516
  64.8 10.9 %copy-start.8 = (f32[1,2,1]{1,2,0:T(1,128)S(1)}, f32[1,2,1]{1,2,0:T(1,128)}, u32[]{:S(2)}) copy-start(f32[1,2,1]{1,2,0:T(1,128)} %param.32) | copy-start | bytes 28
  64.8 10.9 %copy-start.9 = (s32[1,2,1]{1,2,0:T(1,128)S(1)}, s32[1,2,1]{1,2,0:T(1,128)}, u32[]{:S(2)}) copy-start(s32[1,2,1]{1,2,0:T(1,128)} %param.31) | copy-start | bytes 28
  70.2 10.7 %all-to-all-start.3 = ((bf16[8,2,7168]{2,1,0:T(2,128)(2,1)}), bf16[8,2,7168]{2,1,0:T(2,128)(2,1)S(1)}, u32[]{:S(2)}, u32[]{:S(2)}) async-start(bf16[8,2,7168]{2,1,0:T(2,128)(2,1)} %shard_map.197), calls=%async_computation.3 | async-start | bytes 458752 | tf_op jit(solution)/shard_map/all_to_all | solution.py:402
